TPU v7x, 32 devices: a whole 2x2x4 slice. The times are simulated.
32 devices in a mesh: grp: 4 (over y, x), orb: 8 (over z, core).
Axes of the slice: x: 2, y: 2, z: 4, core: 2. Of those that a mesh axis runs over, the one named last changes fastest.
Arguments:
- wavevectors: float32 [3, 1024], replicated, may hold values from -3 to 3
- coefficients: bfloat16 [2048, 1024], P(None, 'orb'), may hold values from -0.0017089844 to 0.0017089844
- inverse: float32 [32, 1024, 1024], P(('grp', 'orb')), may hold values from -0.5 to 0.5
- positions: float32 [32, 3, 1024], P(('grp', 'orb')), may hold values from 0 to 10
- displacements: float32 [2, 32, 3, 16], P(None, ('grp', 'orb')), may hold values from -0.3125 to 0.3125
- moved: int32 [2, 32, 16], P(None, ('grp', 'orb')), may hold values from 0 to 1023, as said below
- donor: int32 [8], P('orb'), may hold values from 0 to 3
- take: int32 [32], P(('grp', 'orb')), may hold values 0 or 1
- log_weight: float32 [32], P(('grp', 'orb')), may hold values from -1 to 1
Outputs:
- new_inverse: float32 [32, 1024, 1024], P(('grp', 'orb'))
- drift: float32 [2, 32, 3, 16], P(None, ('grp', 'orb'))
- laplacian: float32 [2, 32, 16], P(None, ('grp', 'orb'))
- new_weight: float32 [32], P(('grp', 'orb'))
Inputs may be any that keep to these rules, and one draw needn't show every extreme that they name: `moved`: within a walker slot the 32 entries are distinct electrons.
All inputs are finite; a program needn't handle non-finite values. No bound on the sum of `take` on one device may be relied on, other than what follows from the above.
Results may differ from a plain program's by a relative error of at most 0.004.
Values may be sent and summed in bfloat16 or wider, within the bound.
No kernel may reach another device: no remote copies, remote signals or barrier semaphores. Data moves between devices by JAX's collectives and lax.ppermute only.
A program may use at most 64 MiB of HBM per device.

v0:
```python
import math

import jax
import jax.numpy as jnp
from jax import lax
from jax.sharding import PartitionSpec as P

UPD = 2


precise = lax.Precision.HIGHEST


def spread(block, axis, owner):
    block = jnp.where(lax.axis_index(axis) == owner, block, jnp.zeros_like(block))
    return lax.psum(block, axis)


def build_tables(coefficients, wavevectors):
    coeff_f = coefficients.astype(jnp.float32)
    wave_count = wavevectors.shape[1]
    cos_part = coeff_f[:wave_count]
    sin_part = coeff_f[wave_count:]
    parts = [coeff_f]
    for component in range(3):
        scale = wavevectors[component][:, None]
        parts.append(jnp.concatenate([scale * sin_part, -scale * cos_part], 0))
    squared = (
        wavevectors[0] * wavevectors[0]
        + wavevectors[1] * wavevectors[1]
        + wavevectors[2] * wavevectors[2]
    )
    doubled = jnp.concatenate([squared, squared], 0)[:, None]
    parts.append(-doubled * coeff_f)
    return jnp.stack(parts, 1).astype(jnp.bfloat16)


def evaluate_many(points, wavevectors, coefficients, derived):
    walkers = points.shape[0]
    count = points.shape[2] // 2
    phases = points[:, 0, :, None] * wavevectors[0] + points[:, 1, :, None] * wavevectors[1]
    phases = phases + points[:, 2, :, None] * wavevectors[2]
    waves = jnp.concatenate([jnp.cos(phases), jnp.sin(phases)], 2).astype(jnp.bfloat16)
    old_rows = waves[:, :count].reshape(walkers * count, -1)
    new_rows = waves[:, count:].reshape(walkers * count, -1)
    before = jnp.dot(old_rows, coefficients, preferred_element_type=jnp.float32).reshape(
        walkers, count, -1
    )
    flat = derived.reshape(derived.shape[0], -1)
    after = jnp.dot(new_rows, flat, preferred_element_type=jnp.float32).reshape(
        walkers, count, 5, -1
    )
    change = after[:, :, 0] - before
    return jnp.concatenate([change[:, :, None], after[:, :, 1:]], 2)


def woodbury(matrix, values, chosen):
    change = values[:, 0]
    columns = matrix[:, chosen]
    ratio_matrix = jnp.eye(change.shape[0], dtype=jnp.float32) + jnp.dot(
        change, columns, precision=precise
    )
    product = jnp.dot(change, matrix, precision=precise)
    normal_matrix = jnp.dot(ratio_matrix.T, ratio_matrix, precision=precise)
    factor = jnp.linalg.cholesky(normal_matrix)
    right_side = jnp.dot(ratio_matrix.T, product, precision=precise)
    middle = lax.linalg.triangular_solve(factor, right_side, left_side=True, lower=True)
    solved = lax.linalg.triangular_solve(
        factor, middle, left_side=True, lower=True, transpose_a=True
    )
    updated = matrix - jnp.dot(columns, solved, precision=precise)
    log_ratio = jnp.sum(jnp.log(jnp.diagonal(factor)))
    fresh_columns = updated[:, chosen]
    drift = jnp.einsum("kaj,jk->ak", values[:, 1:4], fresh_columns, precision=precise)
    laplacian = jnp.einsum("kj,jk->k", values[:, 4], fresh_columns, precision=precise)
    return (updated, log_ratio, drift, laplacian)


def per_device(
    wavevectors, coefficients, inverse, positions, displacements, moved, donor, take, log_weight
):
    matrix = inverse[0]
    places = positions[0]
    weight = log_weight[0]
    derived = build_tables(coefficients, wavevectors)
    drifts = []
    laplacians = []
    for update in range(UPD):
        if update == 1:
            source = donor[0]
            group = lax.axis_index("grp")
            copied = (
                spread(matrix, "grp", source),
                spread(places, "grp", source),
                spread(weight[None], "grp", source),
            )
            taking = jnp.logical_and(take[0] == 1, group != source)
            matrix = jnp.where(taking, copied[0], matrix)
            places = jnp.where(taking, copied[1], places)
            weight = jnp.where(taking, copied[2][0], weight)
        chosen = moved[update, 0]
        before_points = places[:, chosen]
        moved_to = before_points + displacements[update, 0]
        points = jnp.concatenate([before_points, moved_to], 1)
        portion = lax.all_gather(points[None], "orb", axis=0, tiled=True)
        total = portion.shape[0]
        width = math.gcd(total, 8)
        blocks = portion.reshape((total // width, width) + portion.shape[1:])

        def single(block_points):
            return evaluate_many(block_points, wavevectors, coefficients, derived)

        result = lax.map(single, blocks)
        gathered = result.reshape((total,) + result.shape[2:])
        values = lax.all_to_all(gathered, "orb", split_axis=0, concat_axis=3, tiled=True)[0]
        matrix, log_ratio, drift, laplacian = woodbury(matrix, values, chosen)
        places = places.at[:, chosen].set(moved_to)
        weight = weight + log_ratio
        drifts.append(drift)
        laplacians.append(laplacian)
    return (matrix[None], jnp.stack(drifts)[:, None], jnp.stack(laplacians)[:, None], weight[None])


def solution(mesh):
    return jax.shard_map(
        per_device,
        mesh=mesh,
        in_specs=(
            P(),
            P(None, "orb"),
            P(("grp", "orb"), None, None),
            P(("grp", "orb"), None, None),
            P(None, ("grp", "orb"), None, None),
            P(None, ("grp", "orb"), None),
            P("orb"),
            P(("grp", "orb")),
            P(("grp", "orb")),
        ),
        out_specs=(
            P(("grp", "orb"), None, None),
            P(None, ("grp", "orb"), None, None),
            P(None, ("grp", "orb"), None),
            P(("grp", "orb")),
        ),
        check_vma=False,
    )
```

profile of v0, /device:TPU:0, one launch (start us, length us, event | category | flops | bytes accessed | tf_op | source)
XLA Modules:
  0.0 241.6 jit_solution(3163931108250645322)
XLA Ops:
  7.2 1.3 copy.74
  8.5 0.9 bitcast_dynamic-update-slice_fusion
  9.4 0.8 fusion.54
  10.3 0.7 fusion.45
  11.0 0.9 copy.72
  12.6 14.4 %all-gather.2 = f32[8,3,32]{2,1,0:T(4,128)S(1)} all-gather(f32[1,3,32]{2,1,0:T(4,128)S(1)} %maximum_bitcast_fusion.4), channel_id=2, replica_groups=mesh['grp'=4,'orb'=8] {'orb'}, dimensions={0}, use_global_device_ids=true | all-gather | bytes 3456 | tf_op jit(solution)/shard_map/all_gather | solution.py:105
  27.4 0.9 fusion.16
  28.3 0.8 fusion.17
  29.1 0.8 fusion.18
  29.9 0.9 fusion.7
  30.9 4.2 %sine_convert_fusion.1 = (bf16[8,32,1024]{2,1,0:T(8,128)(2,1)S(1)}, bf16[8,32,1024]{2,1,0:T(8,128)(2,1)S(1)}) fusion(f32[1024]{0:T(1024)S(1)} %bitcast.221, f32[8,32]{1,0:T(8,128)S(1)} %bitcast.236, f32[1024]{0:T(1024)S(1)} %bitcast.229, f32[8,32]{1,0:T(8,128)S(1)} %bitcast.235, f32[1024]{0:T(1024)S(1)} %bitcast.225, f32[8,32]{1,0:T(8,128)S(1)} %bitcast.234), kind=kLoop, calls=%fused_computation.31 | loop fusion | flops 1835008 | bytes 1063936 | tf_op jit(solution)/shard_map/convert.19
  35.1 2.7 %fusion.2 = f32[8,16,5,128]{3,1,2,0:T(8,128)S(1)} fusion(bf16[2048,5,128]{0,2,1:T(8,128)(2,1)} %fusion.7, bf16[8,32,1024]{2,1,0:T(8,128)(2,1)S(1)} %get-tuple-element.74, bf16[8,32,1024]{2,1,0:T(8,128)(2,1)S(1)} %get-tuple-element.73), kind=kOutput, calls=%fused_computation.11 | convolution fusion | flops 336592896 | bytes 3997696 | tf_op jit(solution)/shard_map/while/body/eval_jaxpr/dot_general | solution.py:50
  38.1 0.7 pad_maximum_fusion.4
  38.9 3.4 %all-to-all-start = ((f32[8,16,5,128]{3,1,2,0:T(8,128)}), f32[8,16,5,128]{3,1,2,0:T(8,128)S(1)}, u32[]{:S(2)}, u32[]{:S(2)}) async-start(f32[8,16,5,128]{3,1,2,0:T(8,128)} %pad_maximum_fusion.4), calls=%async_computation | async-start | bytes 655360 | tf_op jit(solution)/shard_map/all_to_all | solution.py:115
  42.3 5.3 %copy.71 = f32[1024,1024]{0,1:T(8,128)} copy(f32[1024,1024]{1,0:T(8,128)} %bitcast.211) | data formatting | bytes 8388608 | tf_op jit(solution)/shard_map/squeeze | solution.py:82
  47.7 2.8 %gather_fusion = f32[16,1024]{1,0:T(8,128)S(1)} fusion(f32[1024,1024]{0,1:T(8,128)} %copy.71, s32[1024]{0:T(1024)S(1)} %pad_clamp_fusion.1), kind=kCustom, calls=%fused_computation | custom fusion | bytes 131136 | tf_op jit(solution)/shard_map/gather | solution.py:59
  51.1 2.3 all-to-all-done
  53.6 4.4 %fusion.31 = f32[16,1024]{1,0:T(8,128)S(1)} fusion(f32[16,5,1024]{2,0,1:T(8,128)S(1)} %squeeze.95, f32[1,1024,1024]{2,1,0:T(8,128)} %param.16), kind=kOutput, calls=%fused_computation.79 | convolution fusion | flops 201326592 | bytes 4325376 | tf_op jit(solution)/shard_map/dot_general | solution.py:63
  58.5 1.5 cholesky.44
  60.0 0.6 compare_reduce_fusion.1
  60.6 0.6 select_bitcast_fusion.1
  61.3 1.2 custom-call.15
  63.2 7.4 %broadcast_select_fusion = (f32[1024,1024]{1,0:T(8,128)}, f32[1024,1024]{1,0:T(8,128)}) fusion(pred[]{:T(512)S(6)} %eq.19, f32[16,1024]{1,0:T(8,128)S(1)} %gather_fusion, f32[16,1024]{1,0:T(8,128)S(1)} %fusion.40, f32[1,1024,1024]{2,1,0:T(8,128)} %param.16), kind=kOutput, calls=%fused_computation.15 | convolution fusion | flops 203423744 | bytes 12713985 | tf_op jit(solution)/shard_map/dot_general | solution.py:71
  71.4 0.8 scatter_fusion
  73.0 0.7 gather_fusion.6
  74.9 43.5 %all-reduce = (f32[3,1024]{0,1:T(8,128)S(1)}, f32[]{:T(128)}) all-reduce(f32[3,1024]{0,1:T(8,128)S(1)} %broadcast_select_fusion.2, f32[]{:T(128)S(6)} %select_n.85), channel_id=1, replica_groups=mesh['grp'=4,'orb'=8] {'grp'}, use_global_device_ids=true, to_apply=%region_4.8 | all-reduce | flops 3073 | bytes 24584 | tf_op jit(solution)/shard_map/psum | solution.py:16
  119.2 12.7 %all-gather.3 = f32[8,3,32]{2,1,0:T(4,128)S(1)} all-gather(f32[1,3,32]{2,1,0:T(4,128)S(1)} %maximum_bitcast_fusion.5), channel_id=3, replica_groups=mesh['grp'=4,'orb'=8] {'orb'}, dimensions={0}, use_global_device_ids=true | all-gather | bytes 3456 | tf_op jit(solution)/shard_map/all_gather | solution.py:105
  131.9 4.2 %sine_convert_fusion = (bf16[8,32,1024]{2,1,0:T(8,128)(2,1)S(1)}, bf16[8,32,1024]{2,1,0:T(8,128)(2,1)S(1)}) fusion(f32[8,32]{1,0:T(8,128)S(1)} %bitcast.239, f32[8,32]{1,0:T(8,128)S(1)} %bitcast.238, f32[8,32]{1,0:T(8,128)S(1)} %bitcast.237, f32[1024]{0:T(1024)S(1)} %bitcast.222, f32[1024]{0:T(1024)S(1)} %bitcast.230, f32[1024]{0:T(1024)S(1)} %bitcast.226), kind=kLoop, calls=%fused_computation.27 | loop fusion | flops 1835008 | bytes 1063936 | tf_op jit(solution)/shard_map/convert.1
  136.1 2.7 %fusion = f32[8,16,5,128]{3,1,2,0:T(8,128)S(1)} fusion(bf16[2048,5,128]{0,2,1:T(8,128)(2,1)} %fusion.7, bf16[8,32,1024]{2,1,0:T(8,128)(2,1)S(1)} %get-tuple-element.72, bf16[8,32,1024]{2,1,0:T(8,128)(2,1)S(1)} %get-tuple-element.71), kind=kOutput, calls=%fused_computation.9 | convolution fusion | flops 336592896 | bytes 3997696 | tf_op jit(solution)/shard_map/while/body/eval_jaxpr/dot_general | solution.py:50
  139.1 0.8 pad_maximum_fusion.5
  139.9 3.6 %all-to-all-start.1 = ((f32[8,16,5,128]{3,1,2,0:T(8,128)}), f32[8,16,5,128]{3,1,2,0:T(8,128)S(1)}, u32[]{:S(2)}, u32[]{:S(2)}) async-start(f32[8,16,5,128]{3,1,2,0:T(8,128)} %pad_maximum_fusion.5), calls=%async_computation.1 | async-start | bytes 655360 | tf_op jit(solution)/shard_map/all_to_all | solution.py:115
  144.2 5.7 %copy.85 = f32[1024,1024]{0,1:T(8,128)} copy(f32[1024,1024]{1,0:T(8,128)} %get-tuple-element.93) | data formatting | bytes 8388608 | tf_op jit(solution)/shard_map/sub | solution.py:71
  149.9 2.9 %gather_fusion.4 = f32[16,1024]{1,0:T(8,128)S(1)} fusion(f32[1024,1024]{0,1:T(8,128)} %copy.85, s32[1024]{0:T(1024)S(1)} %pad_clamp_fusion.1), kind=kCustom, calls=%fused_computation.4 | custom fusion | bytes 131136 | tf_op jit(solution)/shard_map/gather | solution.py:73
  152.7 1.2 fusion.23
  154.8 36.2 %all-reduce.3.cloned.1.call-done = f32[1024,1024]{1,0:T(8,128)} async-done(((f32[1024,1024]{1,0:T(8,128)}), f32[1024,1024]{1,0:T(8,128)}) %all-reduce.3.cloned.1.call-update) | async-done | bytes 4194320 | tf_op jit(solution)/shard_map/psum | solution.py:16
  191.0 5.6 %broadcast_select_fusion.1 = f32[1024,1024]{1,0:T(8,128)} fusion(f32[1024,1024]{1,0:T(8,128)} %all-reduce.3.cloned.1.call-done, f32[1024,1024]{1,0:T(8,128)} %get-tuple-element.93, pred[]{:T(512)S(6)} %and.4), kind=kLoop, calls=%fused_computation.16 | loop fusion | flops 1048576 | bytes 12582913 | tf_op jit(solution)/shard_map/jit(_where)/select_n | solution.py:98
  196.6 5.3 %copy.79 = f32[1024,1024]{0,1:T(8,128)} copy(f32[1024,1024]{1,0:T(8,128)} %broadcast_select_fusion.1) | data formatting | bytes 8388608 | tf_op jit(solution)/shard_map/jit(_where)/select_n | solution.py:98
  202.0 4.3 %fusion.32 = f32[16,1024]{1,0:T(8,128)S(1)} fusion(f32[1024,1024]{1,0:T(8,128)} %broadcast_select_fusion.1, f32[16,5,1024]{2,0,1:T(8,128)S(1)} %squeeze.100), kind=kOutput, calls=%fused_computation.80 | convolution fusion | flops 201326592 | bytes 4325376 | tf_op jit(solution)/shard_map/dot_general | solution.py:63
  206.2 2.8 %gather_fusion.2 = f32[16,1024]{1,0:T(8,128)S(1)} fusion(f32[1024,1024]{0,1:T(8,128)} %copy.79, s32[1024]{0:T(1024)S(1)} %pad_clamp_fusion), kind=kCustom, calls=%fused_computation.2 | custom fusion | bytes 131136 | tf_op jit(solution)/shard_map/gather | solution.py:59
  209.5 1.5 cholesky.55
  211.0 0.6 compare_reduce_fusion
  211.7 0.6 select_bitcast_fusion
  212.3 0.7 gather_fusion.7
  213.6 1.2 custom-call.17
  215.6 6.6 %convolution_subtract_fusion = f32[1024,1024]{1,0:T(8,128)} fusion(f32[1024,1024]{1,0:T(8,128)} %broadcast_select_fusion.1, f32[16,1024]{1,0:T(8,128)S(1)} %gather_fusion.2, f32[16,1024]{1,0:T(8,128)S(1)} %fusion.35), kind=kOutput, calls=%fused_computation.13 | convolution fusion | flops 202375168 | bytes 8519680 | tf_op jit(solution)/shard_map/dot_general | solution.py:71
  222.2 5.3 %copy.86 = f32[1024,1024]{0,1:T(8,128)} copy(f32[1024,1024]{1,0:T(8,128)} %convolution_subtract_fusion) | data formatting | bytes 8388608 | tf_op jit(solution)/shard_map/sub | solution.py:71
  227.6 2.8 %gather_fusion.5 = f32[16,1024]{1,0:T(8,128)S(1)} fusion(f32[1024,1024]{0,1:T(8,128)} %copy.86, s32[1024]{0:T(1024)S(1)} %pad_clamp_fusion), kind=kCustom, calls=%fused_computation.5 | custom fusion | bytes 131136 | tf_op jit(solution)/shard_map/gather | solution.py:73
  230.5 1.2 fusion.21
  (68 shorter events, 8.9 us)
Async XLA Ops:
  7.2 5.4 %copy-start.3 = (f32[2,1,3,16]{3,1,2,0:T(1,128)S(1)}, f32[2,1,3,16]{3,1,2,0:T(1,128)}, u32[]{:S(2)}) copy-start(f32[2,1,3,16]{3,1,2,0:T(1,128)} %param.18) | copy-start | bytes 1156
  29.1 8.7 %copy-start = (bf16[2048,128]{1,0:T(8,128)(2,1)S(1)}, bf16[2048,128]{1,0:T(8,128)(2,1)}, u32[]{:S(2)}) copy-start(bf16[2048,128]{1,0:T(8,128)(2,1)} %param.15) | copy-start | bytes 1572868
  38.9 14.5 %all-to-all-start = ((f32[8,16,5,128]{3,1,2,0:T(8,128)}), f32[8,16,5,128]{3,1,2,0:T(8,128)S(1)}, u32[]{:S(2)}, u32[]{:S(2)}) async-start(f32[8,16,5,128]{3,1,2,0:T(8,128)} %pad_maximum_fusion.4), calls=%async_computation | async-start | bytes 655360 | tf_op jit(solution)/shard_map/all_to_all | solution.py:115
  42.3 148.8 %all-reduce.3.cloned.1.call-start = ((), (), s32[]{:S(2)}) async-start(), calls=%async_computation.2 | async-start | bytes 8388608 | tf_op jit(solution)/shard_map/psum | solution.py:16
  53.6 90.0 %copy-start.1 = (f32[16,5,1024]{2,0,1:T(8,128)}, f32[16,5,1024]{2,0,1:T(8,128)S(1)}, u32[]{:S(2)}) copy-start(f32[16,5,1024]{2,0,1:T(8,128)S(1)} %squeeze.95) | copy-start | bytes 983044
  139.9 14.7 %all-to-all-start.1 = ((f32[8,16,5,128]{3,1,2,0:T(8,128)}), f32[8,16,5,128]{3,1,2,0:T(8,128)S(1)}, u32[]{:S(2)}, u32[]{:S(2)}) async-start(f32[8,16,5,128]{3,1,2,0:T(8,128)} %pad_maximum_fusion.5), calls=%async_computation.1 | async-start | bytes 655360 | tf_op jit(solution)/shard_map/all_to_all | solution.py:115
  149.9 2.9 %slice-start = ((f32[16,5,1024]{2,0,1:T(8,128)}), f32[16,3,1024]{2,0,1:T(8,128)S(1)}, s32[]{:S(2)}) async-start(f32[16,5,1024]{2,0,1:T(8,128)} %copy-done.1), calls=%async_computation.3 | async-start | bytes 393216 | tf_op jit(solution)/shard_map/slice | solution.py:74
  149.9 4.2 %copy-start.2 = (f32[16,5,1024]{2,0,1:T(8,128)S(1)}, f32[16,5,1024]{2,0,1:T(8,128)}, u32[]{:S(2)}) copy-start(f32[16,5,1024]{2,0,1:T(8,128)} %copy-done.1) | copy-start | bytes 983044
Sparse Core Ops, SparseCore 0:
  70.8 120.2 all-reduce.2
where the time goes:
time: 243 us; the launch traced here: 242 us
  blocking collectives  70.5 us (29%)
  local copies, waits for them, and re-layouts  41.7 us (17%)
  waiting for transfers between devices  39 us (16%)
  matrix products  33.3 us (14%)
  other arithmetic  30.5 us (13%)
  between operations  19.4 us (8%)
  starting transfers between devices  7.08 us (3%)
    psum x1, blocking collectives, spread(): return lax.psum(block, axis)  43.5 us
    psum x1, waiting for transfers between devices, spread(): return lax.psum(block, axis)  36.2 us
    all_gather x2, blocking collectives, per_device(): portion = lax.all_gather(points[None], 'orb', axis=0, tiled=True)  27.1 us
    dot_general x2, matrix products, woodbury(): updated = matrix - jnp.dot(columns, solved, precision=precise)  14 us
    sub x2, local copies, waits for them, and re-layouts, woodbury(): updated = matrix - jnp.dot(columns, solved, precision=precise)  11 us
    another operation x3, other arithmetic  8.77 us
    dot_general x2, matrix products, woodbury(): product = jnp.dot(change, matrix, precision=precise)  8.67 us
    all_to_all x2, starting transfers between devices, per_device(): lax.all_to_all(gathered, 'orb', split_axis=0, concat_axis=3, tiled=True)[0]  7.04 us
  transfers between devices with their start and end apart: 3, of which 3 were waited for; matrix products, arithmetic and copies ran while one was open for 12% of the time, Pallas kernels for 0%

commit v1 on v0

v1 whole, which is shorter than its diff:
```python
import functools
import math

import jax
import jax.numpy as jnp
from jax import lax
from jax.experimental import pallas as pl
from jax.experimental.pallas import tpu as pltpu
from jax.sharding import PartitionSpec as P

F32 = jnp.float32
BF16 = jnp.bfloat16
LANES = 128
VMEM_BYTES = 40 * 1024 * 1024
precise = lax.Precision.HIGHEST

SIN_HALF = (4.4428679, -7.30744342, 3.59478808, -0.78437403)
COS_HALF = (1.4142135, -6.97885099, 5.73946117, -1.88356299, 0.31069819)


def dot(a, b, dims=((1,), (0,)), exact=False):
    return lax.dot_general(
        a, b, (dims, ((), ())), precision=precise if exact else None, preferred_element_type=F32
    )


def iota(shape, dim):
    return lax.broadcasted_iota(jnp.int32, shape, dim)


def call(kernel, out_shape, in_specs, out_specs, scratch=(), flops=0, moved=0):
    return pl.pallas_call(
        kernel,
        out_shape=out_shape,
        in_specs=in_specs,
        out_specs=out_specs,
        scratch_shapes=list(scratch),
        compiler_params=pltpu.CompilerParams(vmem_limit_bytes=VMEM_BYTES),
        cost_estimate=pl.CostEstimate(flops=flops, bytes_accessed=moved, transcendentals=0),
    )


VM = pl.BlockSpec(memory_space=pltpu.VMEM)
SM = pl.BlockSpec(memory_space=pltpu.SMEM)
ANY = pl.BlockSpec(memory_space=pl.ANY)


def shape(dims, dtype):
    return jax.ShapeDtypeStruct(dims, dtype)


def is_power(n):
    return n & (n - 1) == 0


def pairs(n, step):
    if is_power(n):
        return [(i, i ^ step) for i in range(n)]
    return [(i, (i + step) % n) for i in range(n)]


def distance(n, here, there):
    return here ^ there if is_power(n) else lax.rem(here - there + n, n)


def backward(n, step):
    return step if is_power(n) else (n - step) % n


def start_kernel(count, pos_ref, moved_ref, disp_ref, weight_ref, out_ref):
    electrons = pos_ref.shape[2]
    pos = jnp.concatenate([pos_ref[0], jnp.zeros((5, electrons), F32)], 0)
    pick = (iota((electrons, LANES), 0) == moved_ref[0:1, :]).astype(F32)
    block = iota((8, LANES), 1) // count
    old = dot(pos, pick, exact=True)
    disp = disp_ref[0]
    points = old + jnp.where(block % 2 == 1, disp, 0.0)
    first = jnp.where(block == 0, disp, 0.0)
    out_ref[...] = pos + dot(first, pick, ((1,), (1,)), exact=True)
    out_ref[3:6, 0:LANES] = points[0:3]
    out_ref[6:7, 0:LANES] = moved_ref[1:2, :].astype(F32)
    out_ref[7:8, 0:LANES] = jnp.full((1, LANES), weight_ref[0], F32)


def points_kernel(count, others, role_ref, *refs):
    own_ref = refs[0]
    received = refs[1 : 1 + others]
    moved_ref, disp_ref, points_ref, weight_ref = refs[1 + others :]
    role = role_ref[0]
    parent = own_ref[...]
    for step in range(others):
        parent = jnp.where(role == step + 1, received[step][...], parent)
    electrons = parent.shape[1]
    pick = (iota((electrons, LANES), 0) == moved_ref[1:2, :]).astype(F32)
    block = iota((8, LANES), 1) // count
    old = dot(parent, pick, exact=True)
    later = old + jnp.where(block % 2 == 1, disp_ref[1], 0.0)
    zeros = jnp.zeros((5, LANES), F32)
    mine = jnp.concatenate([own_ref[3:6, 0:LANES], zeros], 0)
    theirs = jnp.concatenate([parent[3:6, 0:LANES], zeros], 0)
    points = jnp.where(block < 2, mine, jnp.where(block < 4, theirs, later))
    points_ref[...] = jnp.broadcast_to(points[None], points_ref.shape)
    weight_ref[...] = parent[7:8, 0:LANES]


def columns_kernel(count, others, chunks, steps, *refs):
    chunk_refs = refs[:chunks]
    moved_ref = refs[chunks]
    received = refs[chunks + 1 : chunks + 1 + others]
    outs = refs[chunks + 1 + others :]
    depth = chunk_refs[0].shape[0]
    electrons = chunk_refs[0].shape[1]
    block = iota((1, LANES), 1) // count
    wanted = jnp.where(block == 0, moved_ref[0:1, :], moved_ref[1:2, :])
    for step in range(others):
        theirs = received[step][6:7, 0:LANES].astype(jnp.int32)
        wanted = jnp.where(block == 2 + step, theirs, wanted)
    pick = (iota((electrons, LANES), 0) == wanted).astype(F32).astype(BF16)
    for chunk in range(chunks):
        rows = slice(chunk * depth, (chunk + 1) * depth)
        found = dot(chunk_refs[chunk][...], pick)
        turned = jnp.transpose(found).astype(BF16)
        for out, step in zip(outs, steps):
            out[0:count, rows] = turned[0:count]
            out[count : 2 * count, rows] = turned[(1 + step) * count : (2 + step) * count]


def table_kernel(coeff_ref, wave_ref, out_ref):
    waves = wave_ref.shape[1]
    width = coeff_ref.shape[1]
    wave = jnp.transpose(jnp.concatenate([wave_ref[...], jnp.zeros((5, waves), F32)], 0))
    cos_part = coeff_ref[0:waves].astype(F32)
    sin_part = coeff_ref[waves:].astype(F32)
    squared = None
    for a in range(3):
        scale = wave[:, a : a + 1]
        where = slice(a * width, (a + 1) * width)
        out_ref[0:waves, where] = (scale * sin_part).astype(BF16)
        out_ref[waves:, where] = (-scale * cos_part).astype(BF16)
        squared = scale * scale if a == 0 else squared + scale * scale
    where = slice(3 * width, 4 * width)
    out_ref[0:waves, where] = (-squared * cos_part).astype(BF16)
    out_ref[waves:, where] = (-squared * sin_part).astype(BF16)


def horner(coefs, u):
    value = coefs[-1] * u + coefs[-2]
    for c in reversed(coefs[:-2]):
        value = value * u + c
    return value


def evaluate_kernel(count, points_ref, wave_ref, coeff_ref, table_ref, out_ref, diff, new):
    walkers = points_ref.shape[0]
    waves = wave_ref.shape[1]
    width = coeff_ref.shape[1]
    step = math.gcd(waves, LANES)

    def one(w, carry):
        column = jnp.transpose(points_ref[w])
        xs = [column[0 : 6 * count, a : a + 1] for a in range(3)]
        row_d = pl.multiple_of(w * (3 * count), count)
        row_n = pl.multiple_of(w * (2 * count), count)
        for at in range(0, waves, step):
            ks = [wave_ref[a : a + 1, at : at + step] * (0.5 / math.pi) for a in range(3)]
            turn = xs[0] * ks[0] + xs[1] * ks[1] + xs[2] * ks[2]
            r = turn - jnp.floor(turn + 0.5)
            u = r * r
            s = r * horner(SIN_HALF, u)
            c = horner(COS_HALF, u)
            for value, base in ((1.0 - s * s, 0), (s * c, waves)):
                where = slice(base + at, base + at + step)
                kept = value.astype(BF16)
                wide = kept.astype(F32)
                part = [wide[i * count : (i + 1) * count] for i in range(6)]
                diff[pl.ds(row_d, count), where] = (part[3] - part[2]).astype(BF16)
                diff[pl.ds(row_d + count, count), where] = (part[5] - part[4]).astype(BF16)
                diff[pl.ds(row_d + 2 * count, count), where] = (part[1] - part[0]).astype(BF16)
                new[pl.ds(row_n, count), where] = kept[5 * count : 6 * count]
                new[pl.ds(row_n + count, count), where] = kept[count : 2 * count]
        return carry

    lax.fori_loop(0, walkers, one, 0)
    change = dot(diff[...], coeff_ref[...]).astype(BF16)
    rest = dot(new[...], table_ref[...]).astype(BF16)
    for w in range(walkers):
        at = w * 3 * count
        out_ref[w, 0 : 2 * count] = change[at : at + 2 * count]
        out_ref[w, 6 * count : 7 * count] = change[at + 2 * count : at + 3 * count]
        for half, base in ((0, 2 * count), (1, 7 * count)):
            row = (2 * w + half) * count
            for a in range(4):
                out_ref[w, base + a * count : base + (a + 1) * count] = rest[
                    row : row + count, a * width : (a + 1) * width
                ]


def eliminate(matrix, size, first):
    row = iota((size, 1), 0).astype(F32)
    free = jnp.ones((size, 1), F32)
    logdet = jnp.zeros((1, 1), F32)
    for k in range(size):
        column = matrix[:, first + k : first + k + 1]
        score = jnp.where(free > 0, jnp.abs(column), -1.0)
        best = jnp.max(score, axis=0, keepdims=True)
        index = jnp.min(jnp.where(score == best, row, float(size)), axis=0, keepdims=True)
        chosen = row == index
        pivot = jnp.sum(jnp.where(chosen, column, 0.0), axis=0, keepdims=True)
        line = jnp.sum(jnp.where(chosen, matrix, 0.0), axis=0, keepdims=True) / pivot
        matrix = jnp.where(chosen, line, matrix - column * line)
        free = jnp.where(chosen, 0.0, free)
        logdet = logdet + jnp.log(jnp.abs(pivot))
    return matrix, logdet


def solve_kernel(count, others, role_ref, vals_ref, own_ref, *refs):
    received = refs[:others]
    weight_ref, change_ref, cols_ref, inv_ref, first_ref, second_ref, out_weight_ref, vals = refs[
        others:
    ]
    pieces, _, width = vals_ref.shape
    for o in range(pieces):
        vals[:, o * width : (o + 1) * width] = vals_ref[o]
    role = role_ref[0]
    cols = own_ref[...].astype(F32)
    for step in range(others):
        cols = jnp.where(role == step + 1, received[step][...].astype(F32), cols)
    cols = cols.astype(BF16)
    cols_ref[...] = cols
    change_ref[...] = vals[0 : 2 * count]
    own = own_ref[0:count]
    for sums_ref, size, matrix_in, part in (
        (first_ref, count, own, vals[6 * count : 11 * count]),
        (second_ref, 2 * count, cols, vals[0 : 6 * count]),
    ):
        wide = part.shape[0]
        products = dot(matrix_in, part, ((1,), (1,)))
        lane = iota((size, wide), 1)
        row = iota((size, wide), 0)
        matrix = jnp.where(lane < size, products, 0.0)
        matrix = matrix + jnp.where(lane == row, 1.0, 0.0) + jnp.where(lane == row + size, 1.0, 0.0)
        matrix, logdet = eliminate(matrix, size, 0)
        joined = dot(matrix, matrix, ((0,), (0,)), exact=True)[size : 2 * size, :]
        line = iota((wide, wide), 0)
        place = iota((wide, wide), 1)
        tile = jnp.where(line == size - count + place % count, 1.0, 0.0)
        spread = dot(joined, tile, exact=True)
        sums_ref[...] = jnp.sum(products * spread, axis=0, keepdims=True)[:, size:]
        if size > count:
            inv_ref[...] = joined[:, 0:size]
            out_weight_ref[...] = weight_ref[...] + logdet


def finish_kernel(sources, chunks, role_ref, change_ref, cols_ref, inv_ref, *refs):
    inputs = refs[:-5]
    out_ref, parent, staged, in_sem, out_sem = refs[-5:]
    depth = inputs[0].shape[0]
    role = role_ref[0]
    for chunk in range(chunks):
        for which, table in enumerate(sources):

            @pl.when(role == which)
            def _():
                pltpu.make_async_copy(
                    inputs[table[chunk]], parent.at[chunk], in_sem.at[chunk]
                ).start()

    total = jnp.zeros((change_ref.shape[0], inputs[0].shape[1]), F32)
    for chunk in range(chunks):
        pltpu.make_async_copy(inputs[chunk], parent.at[chunk], in_sem.at[chunk]).wait()
        total = total + dot(change_ref[:, chunk * depth : (chunk + 1) * depth], parent[chunk])
    solved = dot(inv_ref[...], total, exact=True).astype(BF16)
    copies = []
    for chunk in range(chunks):
        rows = slice(chunk * depth, (chunk + 1) * depth)
        columns = jnp.transpose(cols_ref[:, rows].astype(F32)).astype(BF16)
        staged[chunk] = parent[chunk].astype(F32) - dot(columns, solved)
        copy = pltpu.make_async_copy(staged.at[chunk], out_ref.at[rows], out_sem.at[chunk])
        copy.start()
        copies.append(copy)
    for copy in copies:
        copy.wait()


def branch(own, donor_here, n):
    chunks = len(own)
    if n == 4 and chunks == 4:
        send_x = lambda block: lax.ppermute(block, "grp", pairs(n, 1))
        send_y = lambda block: lax.ppermute(block, "grp", pairs(n, 2))
        x1, y1 = send_x(own[0]), send_y(own[3])
        x2 = send_x(jnp.where(donor_here, own[1], y1))
        y2 = send_y(jnp.where(donor_here, own[2], x1))
        x3 = send_x(jnp.where(donor_here, own[2], y2))
        y3 = send_y(jnp.where(donor_here, own[1], x2))
        arrays = list(own) + [x1, x2, x3, y1, y2, y3]
        a1, a2, a3, b1, b2, b3 = range(chunks, chunks + 6)
        return arrays, [range(chunks), (a1, a2, a3, b3), (a3, b3, b2, b1), (b2, b3, a3, a2)]
    arrays = list(own)
    table = [range(chunks)]
    for step in range(1, n):
        table.append(range(len(arrays), len(arrays) + chunks))
        arrays += [lax.ppermute(block, "grp", pairs(n, step)) for block in own]
    return arrays, table


def per_device(
    n_grp,
    n_orb,
    wavevectors,
    coefficients,
    inverse,
    positions,
    displacements,
    moved,
    donor,
    take,
    log_weight,
):
    electrons = inverse.shape[1]
    count = moved.shape[2]
    plane = coefficients.shape[0]
    local = coefficients.shape[1]
    others = n_grp - 1
    chunks = 4
    group = lax.axis_index("grp")
    source = donor[0]
    apart = distance(n_grp, group, source)
    role = jnp.where(take[0] == 1, apart, 0).astype(jnp.int32).reshape(1)

    tiled = jnp.tile(moved[:, 0], (1, LANES // count))
    disp = jnp.pad(jnp.tile(displacements[:, 0], (1, 1, LANES // count)), ((0, 0), (0, 5), (0, 0)))
    record = call(
        functools.partial(start_kernel, count),
        shape((8, electrons), F32),
        [VM, VM, VM, SM],
        VM,
    )(positions, tiled, disp, log_weight)
    records = [lax.ppermute(record, "grp", pairs(n_grp, s)) for s in range(1, n_grp)]

    depth = electrons // chunks
    own = [inverse[0, c * depth : (c + 1) * depth].astype(BF16) for c in range(chunks)]
    arrays, table = branch(own, apart == 0, n_grp)

    points, weight = call(
        functools.partial(points_kernel, count, others),
        (shape((n_orb, 8, LANES), F32), shape((1, LANES), F32)),
        [SM] + [VM] * (others + 3),
        (VM, VM),
    )(role, record, *records, tiled, disp)
    points = lax.all_to_all(points, "orb", split_axis=0, concat_axis=0, tiled=True)

    steps = [0] + [backward(n_grp, s) for s in range(1, n_grp)]
    columns = call(
        functools.partial(columns_kernel, count, others, chunks, steps),
        tuple(shape((2 * count, electrons), BF16) for _ in steps),
        [VM] * (chunks + 1 + others),
        tuple(VM for _ in steps),
        flops=2 * electrons * electrons * LANES,
        moved=2 * electrons * electrons,
    )(*own, tiled, *records)
    sent = [lax.ppermute(columns[s], "grp", pairs(n_grp, s)) for s in range(1, n_grp)]

    width = -(-local // LANES) * LANES
    coeff = jnp.pad(coefficients, ((0, 0), (0, width - local))) if width > local else coefficients
    derived = call(
        table_kernel,
        shape((plane, 4 * width), BF16),
        [VM, VM],
        VM,
        flops=8 * plane * width,
        moved=10 * plane * width,
    )(coeff, wavevectors)
    block = math.gcd(n_orb, 8)
    values = pl.pallas_call(
        functools.partial(evaluate_kernel, count),
        grid=(n_orb // block,),
        out_shape=shape((n_orb, 11 * count, width), BF16),
        in_specs=[
            pl.BlockSpec((block, 8, LANES), lambda i: (i, 0, 0)),
            pl.BlockSpec(wavevectors.shape, lambda i: (0, 0)),
            pl.BlockSpec(coeff.shape, lambda i: (0, 0)),
            pl.BlockSpec(derived.shape, lambda i: (0, 0)),
        ],
        out_specs=pl.BlockSpec((block, 11 * count, width), lambda i: (i, 0, 0)),
        scratch_shapes=[
            pltpu.VMEM((block * 3 * count, plane), BF16),
            pltpu.VMEM((block * 2 * count, plane), BF16),
        ],
        compiler_params=pltpu.CompilerParams(vmem_limit_bytes=VMEM_BYTES),
        cost_estimate=pl.CostEstimate(
            flops=2 * n_orb * count * plane * width * 11, bytes_accessed=12 * plane * width, transcendentals=0
        ),
    )(points, wavevectors, coeff, derived)
    values = values[:, :, :local]
    values = lax.all_to_all(values, "orb", split_axis=0, concat_axis=0, tiled=True)
    if width > local:
        values = values.transpose(1, 0, 2).reshape(1, 11 * count, electrons)

    change, cols, small, first, second, new_weight = call(
        functools.partial(solve_kernel, count, others),
        (
            shape((2 * count, electrons), BF16),
            shape((2 * count, electrons), BF16),
            shape((2 * count, 2 * count), F32),
            shape((1, 4 * count), F32),
            shape((1, 4 * count), F32),
            shape((1, LANES), F32),
        ),
        [SM] + [VM] * (others + 3),
        (VM,) * 6,
        scratch=[pltpu.VMEM((11 * count, electrons), BF16)],
        flops=2 * electrons * count * count * 16,
        moved=4 * 11 * count * electrons,
    )(role, values, columns[0], *sent, weight)

    updated = call(
        functools.partial(finish_kernel, table, chunks),
        shape((electrons, electrons), F32),
        [SM, VM, VM, VM] + [ANY] * len(arrays),
        ANY,
        scratch=[
            pltpu.VMEM((chunks, depth, electrons), BF16),
            pltpu.VMEM((chunks, depth, electrons), F32),
            pltpu.SemaphoreType.DMA((chunks,)),
            pltpu.SemaphoreType.DMA((chunks,)),
        ],
        flops=4 * electrons * electrons * 2 * count,
        moved=6 * electrons * electrons,
    )(role, change, cols, small, *arrays)

    both = jnp.concatenate([first, second]).reshape(2, 1, 4, count)
    return updated[None], both[:, :, :3], both[:, :, 3], new_weight[0, :1]


def solution(mesh):
    split = ("grp", "orb")
    return jax.shard_map(
        functools.partial(per_device, mesh.shape["grp"], mesh.shape["orb"]),
        mesh=mesh,
        in_specs=(
            P(),
            P(None, "orb"),
            P(split, None, None),
            P(split, None, None),
            P(None, split, None, None),
            P(None, split, None),
            P("orb"),
            P(split),
            P(split),
        ),
        out_specs=(
            P(split, None, None),
            P(None, split, None, None),
            P(None, split, None),
            P(split),
        ),
        check_vma=False,
    )
```

time: 243 us -> 116 us (0.48)
  blocking collectives: 70.5 us -> 0 us
  matrix products: 33.3 us -> 0 us
  local copies, waits for them, and re-layouts: 41.7 us -> 16.2 us
  Pallas kernels: 0 us -> 23.1 us
  other arithmetic: 30.5 us -> 8.18 us
  starting transfers between devices: 7.08 us -> 25.9 us
  between operations: 19.4 us -> 2.81 us
    psum x1 -> x0, blocking collectives: 43.5 us -> none  [spread(): return lax.psum(block, axis)]
    psum x1 -> x0, waiting for transfers between devices: 36.2 us -> none  [spread(): return lax.psum(block, axis)]
    ppermute x0 -> x12, waiting for transfers between devices: none -> 36 us  [the longest x3 11.4 us: branch(): send_x = lambda block: lax.ppermute(block, 'grp', pairs(n, 1))]
    dot_general x16 -> x0, matrix products: 32.4 us -> none  [the longest x2 14 us: woodbury(): updated = matrix - jnp.dot(columns, solved, precision=precise)]
    all_gather x2 -> x0, blocking collectives: 27.1 us -> none  [per_device(): portion = lax.all_gather(points[None], 'orb', axis=0, tiled=True)]
    pallas_call x0 -> x7, Pallas kernels: none -> 23.1 us  [the longest x1 9.56 us: per_device(): call(functools.partial(solve_kernel, count, others), (shape((2 * count, e...]
    ppermute x0 -> x12, starting transfers between devices: none -> 17.9 us  [the longest x3 5.98 us: branch(): send_y = lambda block: lax.ppermute(block, 'grp', pairs(n, 2))]
    another operation x15 -> x1, other arithmetic: 18.3 us -> 2.51 us
  transfers between devices with their start and end apart: 3 -> 14, of which waited for: 3 -> 5; matrix products, arithmetic and copies ran while one was open for 12% -> 4% of each run, Pallas kernels for 0% -> 17%
where the time goes in v1:
time: 116 us; the launch traced here: 115 us
  waiting for transfers between devices  39.2 us (34%)
  starting transfers between devices  25.9 us (22%)
  Pallas kernels  23.1 us (20%)
  local copies, waits for them, and re-layouts  16.2 us (14%)
  other arithmetic  8.18 us (7%)
  between operations  2.81 us (2%)
    unnamed x68, local copies, waits for them, and re-layouts  14.7 us
    ppermute x3, waiting for transfers between devices, branch(): send_x = lambda block: lax.ppermute(block, 'grp', pairs(n, 1))  11.4 us
    ppermute x3, waiting for transfers between devices, branch(): send_y = lambda block: lax.ppermute(block, 'grp', pairs(n, 2))  9.74 us
    pallas_call x1, Pallas kernels, per_device(): call(functools.partial(solve_kernel, count, others), (shape((2 * count, e...  9.56 us
    ppermute x3, waiting for transfers between devices, per_device(): lax.ppermute(columns[s], 'grp', pairs(n_grp, s))  8.29 us
    ppermute x3, waiting for transfers between devices, per_device(): lax.ppermute(record, 'grp', pairs(n_grp, s))  6.57 us
    pallas_call x1, Pallas kernels, per_device(): pl.pallas_call(functools.partial(evaluate_kernel, count), grid=(n_orb //...  6.39 us
    ppermute x3, starting transfers between devices, branch(): send_y = lambda block: lax.ppermute(block, 'grp', pairs(n, 2))  5.98 us
  transfers between devices with their start and end apart: 14, of which 5 were waited for; matrix products, arithmetic and copies ran while one was open for 4% of the time, Pallas kernels for 17%

profile of v1, /device:TPU:0, one launch (start us, length us, event | category | flops | bytes accessed | tf_op | source)
XLA Modules:
  0.0 115.4 jit_solution(17475284639057386823)
XLA Ops:
  0.6 2.5 %convert.6 = bf16[1,1024,1024]{2,1,0:T(8,128)(2,1)S(1)} convert(f32[1,1024,1024]{2,1,0:T(8,128)} %param.11) | non-fusion elementwise | flops 1048576 | bytes 6291456 | tf_op jit(solution)/shard_map/convert.3
  3.2 1.2 %slice_bitcast_fusion = (bf16[256,1024]{1,0:T(8,128)(2,1)S(1)}, bf16[256,1024]{1,0:T(8,128)(2,1)S(1)}, bf16[256,1024]{1,0:T(8,128)(2,1)}, bf16[256,1024]{1,0:T(8,128)(2,1)S(1)}) fusion(bf16[1,1024,1024]{2,1,0:T(8,128)(2,1)S(1)} %convert.6), kind=kLoop, calls=%fused_computation | loop fusion | bytes 4194304 | tf_op jit(solution)/shard_map/convert_element_type | solution.py:341
  4.4 3.0 %collective-permute-start.7 = (bf16[256,1024]{1,0:T(8,128)(2,1)S(1)}, bf16[256,1024]{1,0:T(8,128)(2,1)S(1)}, u32[]{:S(2)}, u32[]{:S(2)}) collective-permute-start(bf16[256,1024]{1,0:T(8,128)(2,1)S(1)} %get-tuple-element.38.refs_3_), channel_id=1, source_target_pairs={{0,16},{8,24},{16,0},{24,8},{1,17},{9,25},{17,1},{25,9},{2,18},{10... | collective-permute-start | bytes 1572872 | tf_op jit(solution)/shard_map/ppermute | solution.py:289
  7.4 1.5 %collective-permute-start.6 = (bf16[256,1024]{1,0:T(8,128)(2,1)S(1)}, bf16[256,1024]{1,0:T(8,128)(2,1)S(1)}, u32[]{:S(2)}, u32[]{:S(2)}) collective-permute-start(bf16[256,1024]{1,0:T(8,128)(2,1)S(1)} %get-tuple-element.41.refs_0_), channel_id=1, source_target_pairs={{0,8},{8,0},{16,24},{24,16},{1,9},{9,1},{17,25},{25,17},{2,10},{10... | collective-permute-start | bytes 1572872 | tf_op jit(solution)/shard_map/ppermute | solution.py:288
  9.5 9.7 %collective-permute-done.7.refs_7_ = bf16[256,1024]{1,0:T(8,128)(2,1)S(1)} collective-permute-done((bf16[256,1024]{1,0:T(8,128)(2,1)S(1)}, bf16[256,1024]{1,0:T(8,128)(2,1)S(1)}, u32[]{:S(2)}, u32[]{:S(2)}) %collective-permute-start.7) | collective-permute-done | bytes 524320 | tf_op jit(solution)/shard_map/ppermute | solution.py:289
  19.3 1.3 %broadcast_select_fusion.3 = bf16[256,1024]{1,0:T(8,128)(2,1)S(1)} fusion(bf16[256,1024]{1,0:T(8,128)(2,1)S(1)} %collective-permute-done.7.refs_7_, pred[]{:T(512)S(6)} %eq.11, bf16[1,1024,1024]{2,1,0:T(8,128)(2,1)} %copy-done.28), kind=kLoop, calls=%fused_computation.7 | loop fusion | flops 262144 | bytes 1572865 | tf_op jit(solution)/shard_map/jit(_where)/select_n | solution.py:291
  20.6 1.8 %collective-permute-start.8 = (bf16[256,1024]{1,0:T(8,128)(2,1)S(1)}, bf16[256,1024]{1,0:T(8,128)(2,1)S(1)}, u32[]{:S(2)}, u32[]{:S(2)}) collective-permute-start(bf16[256,1024]{1,0:T(8,128)(2,1)S(1)} %broadcast_select_fusion.3), channel_id=1, source_target_pairs={{0,8},{8,0},{16,24},{24,16},{1,9},{9,1},{17,25},{25,17},{2,10},{10... | collective-permute-start | bytes 1572872 | tf_op jit(solution)/shard_map/ppermute | solution.py:288
  22.4 11.4 %collective-permute-done.8.refs_5_ = bf16[256,1024]{1,0:T(8,128)(2,1)S(1)} collective-permute-done((bf16[256,1024]{1,0:T(8,128)(2,1)S(1)}, bf16[256,1024]{1,0:T(8,128)(2,1)S(1)}, u32[]{:S(2)}, u32[]{:S(2)}) %collective-permute-start.8) | collective-permute-done | bytes 524320 | tf_op jit(solution)/shard_map/ppermute | solution.py:288
  33.8 2.5 %broadcast_select_fusion = (bf16[256,1024]{1,0:T(8,128)(2,1)}, bf16[256,1024]{1,0:T(8,128)(2,1)}) fusion(bf16[256,1024]{1,0:T(8,128)(2,1)S(1)} %collective-permute-done.8.refs_5_, pred[]{:T(512)S(6)} %eq.11, bf16[1,1024,1024]{2,1,0:T(8,128)(2,1)} %copy-done.28, bf16[256,1024]{1,0:T(8,128)(2,1)S(1)} %collective-permute-done.6.refs_4_), kind=kLoop, calls=%fused_computation.4 | loop fusion | flops 524288 | bytes 3145729 | tf_op jit(solution)/shard_map/jit(_where)/select_n | solution.py:294
  36.2 1.4 %collective-permute-start.9 = (bf16[256,1024]{1,0:T(8,128)(2,1)}, bf16[256,1024]{1,0:T(8,128)(2,1)}, u32[]{:S(2)}, u32[]{:S(2)}) collective-permute-start(bf16[256,1024]{1,0:T(8,128)(2,1)} %get-tuple-element.37), channel_id=1, source_target_pairs={{0,16},{8,24},{16,0},{24,8},{1,17},{9,25},{17,1},{25,9},{2,18},{10... | collective-permute-start | bytes 1572872 | tf_op jit(solution)/shard_map/ppermute | solution.py:289
  38.5 0.8 shard_map.120.refs_0_
  39.3 1.5 %collective-permute-start = (f32[8,1024]{1,0:T(8,128)S(1)}, f32[8,1024]{1,0:T(8,128)S(1)}, u32[]{:S(2)}, u32[]{:S(2)}) collective-permute-start(f32[8,1024]{1,0:T(8,128)S(1)} %shard_map.120.refs_0_), channel_id=1, source_target_pairs={{0,8},{8,0},{16,24},{24,16},{1,9},{9,1},{17,25},{25,17},{2,10},{10... | collective-permute-start | bytes 98312 | tf_op jit(solution)/shard_map/ppermute | solution.py:338
  41.3 1.5 %collective-permute-start.2 = (f32[8,1024]{1,0:T(8,128)S(1)}, f32[8,1024]{1,0:T(8,128)S(1)}, u32[]{:S(2)}, u32[]{:S(2)}) collective-permute-start(f32[8,1024]{1,0:T(8,128)S(1)} %shard_map.120.refs_0_), channel_id=1, source_target_pairs={{0,24},{8,16},{16,8},{24,0},{1,25},{9,17},{17,9},{25,1},{2,26},{10... | collective-permute-start | bytes 98312 | tf_op jit(solution)/shard_map/ppermute | solution.py:338
  43.5 6.6 %collective-permute-done.1.refs_2_.refs_6_ = f32[8,1024]{1,0:T(8,128)S(1)} collective-permute-done((f32[8,1024]{1,0:T(8,128)S(1)}, f32[8,1024]{1,0:T(8,128)S(1)}, u32[]{:S(2)}, u32[]{:S(2)}) %collective-permute-start.1) | collective-permute-done | bytes 32800 | tf_op jit(solution)/shard_map/ppermute | solution.py:338
  50.0 1.0 shard_map.121
  51.0 4.5 %all-to-all-start = ((f32[8,8,128]{2,1,0:T(8,128)}), f32[8,8,128]{2,1,0:T(8,128)S(1)}, u32[]{:S(2)}, u32[]{:S(2)}) async-start(f32[8,8,128]{2,1,0:T(8,128)} %get-tuple-element.16), calls=%async_computation | async-start | bytes 65536 | tf_op jit(solution)/shard_map/all_to_all | solution.py:350
  55.5 1.0 copy-done.5
  56.6 1.5 %shard_map.122.table_ref = bf16[2048,512]{1,0:T(8,128)(2,1)S(1)} custom-call(bf16[2048,128]{1,0:T(8,128)(2,1)S(1)} %copy-done.5, f32[3,1024]{1,0:T(4,128)S(1)} %copy-done.19), custom_call_target="tpu_custom_call" | custom-call | flops 2097152 | bytes 2621440 | tf_op jit(solution)/shard_map/pallas_call | solution.py:365
  58.0 3.2 %all-to-all-done.points_ref = f32[8,8,128]{2,1,0:T(8,128)S(1)} async-done(((f32[8,8,128]{2,1,0:T(8,128)}), f32[8,8,128]{2,1,0:T(8,128)S(1)}, u32[]{:S(2)}, u32[]{:S(2)}) %all-to-all-start) | async-done | bytes 32800 | tf_op jit(solution)/shard_map/all_to_all | solution.py:350
  61.2 1.0 copy-done.6
  62.3 6.4 %shard_map.123 = bf16[8,176,128]{2,1,0:T(8,128)(2,1)} custom-call(f32[8,8,128]{2,1,0:T(8,128)S(1)} %all-to-all-done.points_ref, f32[3,1024]{1,0:T(4,128)S(1)} %copy-done.19, bf16[2048,128]{1,0:T(8,128)(2,1)S(1)} %copy-done.6, bf16[2048,512]{1,0:T(8,128)(2,1)S(1)} %shard_map.122.table_ref), custom_call_target="tpu_custom_call" | custom-call | flops 738197504 | bytes 3145728 | tf_op jit(solution)/shard_map/pallas_call | solution.py:374
  68.7 3.6 %all-to-all-start.1 = ((bf16[8,176,128]{2,1,0:T(8,128)(2,1)}), bf16[8,176,128]{2,1,0:T(8,128)(2,1)S(1)}, u32[]{:S(2)}, u32[]{:S(2)}) async-start(bf16[8,176,128]{2,1,0:T(8,128)(2,1)} %shard_map.123), calls=%async_computation.1 | async-start | bytes 720896 | tf_op jit(solution)/shard_map/all_to_all | solution.py:395
  72.3 1.6 %collective-permute-start.11 = (bf16[256,1024]{1,0:T(8,128)(2,1)}, bf16[256,1024]{1,0:T(8,128)(2,1)}, u32[]{:S(2)}, u32[]{:S(2)}) collective-permute-start(bf16[256,1024]{1,0:T(8,128)(2,1)} %get-tuple-element.36), channel_id=1, source_target_pairs={{0,16},{8,24},{16,0},{24,8},{1,17},{9,25},{17,1},{25,9},{2,18},{10... | collective-permute-start | bytes 1572872 | tf_op jit(solution)/shard_map/ppermute | solution.py:289
  73.9 1.9 %broadcast_select_fusion.1 = bf16[256,1024]{1,0:T(8,128)(2,1)} fusion(bf16[256,1024]{1,0:T(8,128)(2,1)} %collective-permute-done.9.refs_8_, pred[]{:T(512)S(6)} %eq.11, bf16[1,1024,1024]{2,1,0:T(8,128)(2,1)} %copy-done.28), kind=kLoop, calls=%fused_computation.5 | loop fusion | flops 262144 | bytes 1572865 | tf_op jit(solution)/shard_map/jit(_where)/select_n | solution.py:293
  75.8 1.6 %collective-permute-start.10 = (bf16[256,1024]{1,0:T(8,128)(2,1)}, bf16[256,1024]{1,0:T(8,128)(2,1)}, u32[]{:S(2)}, u32[]{:S(2)}) collective-permute-start(bf16[256,1024]{1,0:T(8,128)(2,1)} %broadcast_select_fusion.1), channel_id=1, source_target_pairs={{0,8},{8,0},{16,24},{24,16},{1,9},{9,1},{17,25},{25,17},{2,10},{10... | collective-permute-start | bytes 1572872 | tf_op jit(solution)/shard_map/ppermute | solution.py:288
  77.5 0.8 copy-done.12
  78.2 0.8 copy-done.14
  79.0 0.8 shard_map.124
  79.8 0.6 copy-done.20
  80.8 0.7 collective-permute-start.4
  81.4 2.4 %collective-permute-start.5 = (bf16[32,1024]{1,0:T(8,128)(2,1)S(1)}, bf16[32,1024]{1,0:T(8,128)(2,1)S(1)}, u32[]{:S(2)}, u32[]{:S(2)}) collective-permute-start(bf16[32,1024]{1,0:T(8,128)(2,1)S(1)} %get-tuple-element.20), channel_id=1, source_target_pairs={{0,24},{8,16},{16,8},{24,0},{1,25},{9,17},{17,9},{25,1},{2,26},{10... | collective-permute-start | bytes 196616 | tf_op jit(solution)/shard_map/ppermute | solution.py:361
  83.9 8.3 %collective-permute-done.3.refs_0_ = bf16[32,1024]{1,0:T(8,128)(2,1)S(1)} collective-permute-done((bf16[32,1024]{1,0:T(8,128)(2,1)S(1)}, bf16[32,1024]{1,0:T(8,128)(2,1)S(1)}, u32[]{:S(2)}, u32[]{:S(2)}) %collective-permute-start.3) | collective-permute-done | bytes 65568 | tf_op jit(solution)/shard_map/ppermute | solution.py:361
  92.2 0.6 copy-done.22
  92.8 0.6 copy-done.24
  93.4 0.6 copy-done.26
  94.1 0.8 copy-done.21
  94.9 0.8 copy-done.23
  95.7 0.8 copy-done.25
  96.6 0.8 copy-done.27
  97.4 9.6 %shard_map.125 = (bf16[32,1024]{1,0:T(8,128)(2,1)S(1)}, bf16[32,1024]{1,0:T(8,128)(2,1)S(1)}, f32[32,32]{1,0:T(8,128)S(1)}, f32[1,64]{1,0:T(1,128)S(1)}, f32[1,64]{1,0:T(1,128)S(1)}, /*index=5*/f32[1,128]{1,0:T(1,128)}) custom-call(s32[1]{0:T(128)} %bitcast.2.role_ref, bf16[8,176,128]{2,1,0:T(8,128)(2,1)S(1)} %all-to-all-done.1.vals_ref, ...), custom_call_target="tpu_custom_call" | custom-call | flops 8388608 | bytes 720896 | tf_op jit(solution)/shard_map/pallas_call | solution.py:399
  107.0 0.6 copy-done.15
  107.6 0.6 copy-done.17
  108.3 0.6 copy.21
  108.9 0.6 slice_bitcast_fusion.4
  109.5 1.0 copy-done.10
  110.5 0.8 copy-done.16
  111.4 0.8 copy-done.18
  112.2 3.2 %shard_map.126 = f32[1024,1024]{1,0:T(8,128)} custom-call(s32[1]{0:T(128)} %bitcast.2.role_ref, bf16[32,1024]{1,0:T(8,128)(2,1)S(1)} %copy-done.16, bf16[32,1024]{1,0:T(8,128)(2,1)S(1)} %copy-done.18, f32[32,32]{1,0:T(8,128)S(1)} %get-tuple-element.24.inv_ref, bf16[256,1024]{1,0:T(8,128)(2,1)S(1)} %copy-done.2, bf16[256,1024]{1,0:T(8,128)(2,1)S(1)} %copy-done, ...), custom_call_target="tpu_custom_call" | custom-call | flops 134217728 | bytes 6291456 | tf_op jit(solution)/shard_map/pallas_call | solution.py:416
  (68 shorter events, 1.3 us)
Async XLA Ops:
  3.1 4.2 %copy-start.28 = (bf16[1,1024,1024]{2,1,0:T(8,128)(2,1)}, bf16[1,1024,1024]{2,1,0:T(8,128)(2,1)S(1)}, u32[]{:S(2)}) copy-start(bf16[1,1024,1024]{2,1,0:T(8,128)(2,1)S(1)} %convert.6) | copy-start | bytes 6291460
  4.4 31.8 %copy-start.1 = (bf16[256,1024]{1,0:T(8,128)(2,1)}, bf16[256,1024]{1,0:T(8,128)(2,1)S(1)}, u32[]{:S(2)}) copy-start(bf16[256,1024]{1,0:T(8,128)(2,1)S(1)} %get-tuple-element.41.refs_0_) | copy-start | bytes 1572868
  4.4 14.9 %collective-permute-start.7 = (bf16[256,1024]{1,0:T(8,128)(2,1)S(1)}, bf16[256,1024]{1,0:T(8,128)(2,1)S(1)}, u32[]{:S(2)}, u32[]{:S(2)}) collective-permute-start(bf16[256,1024]{1,0:T(8,128)(2,1)S(1)} %get-tuple-element.38.refs_3_), channel_id=1, source_target_pairs={{0,16},{8,24},{16,0},{24,8},{1,17},{9,25},{17,1},{25,9},{2,18},{10... | collective-permute-start | bytes 1572872 | tf_op jit(solution)/shard_map/ppermute | solution.py:289
  7.4 15.0 %collective-permute-start.6 = (bf16[256,1024]{1,0:T(8,128)(2,1)S(1)}, bf16[256,1024]{1,0:T(8,128)(2,1)S(1)}, u32[]{:S(2)}, u32[]{:S(2)}) collective-permute-start(bf16[256,1024]{1,0:T(8,128)(2,1)S(1)} %get-tuple-element.41.refs_0_), channel_id=1, source_target_pairs={{0,8},{8,0},{16,24},{24,16},{1,9},{9,1},{17,25},{25,17},{2,10},{10... | collective-permute-start | bytes 1572872 | tf_op jit(solution)/shard_map/ppermute | solution.py:288
  9.5 28.2 %copy-start.31 = (s32[2,1,16]{2,1,0:T(1,128)S(1)}, s32[2,1,16]{2,1,0:T(1,128)}, u32[]{:S(2)}) copy-start(s32[2,1,16]{2,1,0:T(1,128)} %param.14) | copy-start | bytes 388
  9.5 28.2 %copy-start.30 = (f32[2,1,3,16]{3,1,2,0:T(1,128)S(1)}, f32[2,1,3,16]{3,1,2,0:T(1,128)}, u32[]{:S(2)}) copy-start(f32[2,1,3,16]{3,1,2,0:T(1,128)} %param.13) | copy-start | bytes 1156
  9.5 28.3 %copy-start.29 = (f32[1,3,1024]{2,0,1:T(1,128)S(1)}, f32[1,3,1024]{2,0,1:T(1,128)}, u32[]{:S(2)}) copy-start(f32[1,3,1024]{2,0,1:T(1,128)} %param.12) | copy-start | bytes 36868
  19.3 17.0 %copy-start.3 = (bf16[256,1024]{1,0:T(8,128)(2,1)}, bf16[256,1024]{1,0:T(8,128)(2,1)S(1)}, u32[]{:S(2)}) copy-start(bf16[256,1024]{1,0:T(8,128)(2,1)S(1)} %collective-permute-done.7.refs_7_) | copy-start | bytes 1572868
  20.6 34.9 %copy-start.19 = (f32[3,1024]{1,0:T(4,128)S(1)}, f32[3,1024]{1,0:T(4,128)}, u32[]{:S(2)}) copy-start(f32[3,1024]{1,0:T(4,128)} %wave_ref.3) | copy-start | bytes 36868
  20.6 13.2 %collective-permute-start.8 = (bf16[256,1024]{1,0:T(8,128)(2,1)S(1)}, bf16[256,1024]{1,0:T(8,128)(2,1)S(1)}, u32[]{:S(2)}, u32[]{:S(2)}) collective-permute-start(bf16[256,1024]{1,0:T(8,128)(2,1)S(1)} %broadcast_select_fusion.3), channel_id=1, source_target_pairs={{0,8},{8,0},{16,24},{24,16},{1,9},{9,1},{17,25},{25,17},{2,10},{10... | collective-permute-start | bytes 1572872 | tf_op jit(solution)/shard_map/ppermute | solution.py:288
  22.4 28.7 %copy-start.7 = (bf16[256,1024]{1,0:T(8,128)(2,1)}, bf16[256,1024]{1,0:T(8,128)(2,1)S(1)}, u32[]{:S(2)}) copy-start(bf16[256,1024]{1,0:T(8,128)(2,1)S(1)} %collective-permute-done.6.refs_4_) | copy-start | bytes 1572868
  33.8 17.3 %copy-start.9 = (bf16[256,1024]{1,0:T(8,128)(2,1)}, bf16[256,1024]{1,0:T(8,128)(2,1)S(1)}, u32[]{:S(2)}) copy-start(bf16[256,1024]{1,0:T(8,128)(2,1)S(1)} %collective-permute-done.8.refs_5_) | copy-start | bytes 1572868
  36.2 37.7 %collective-permute-start.9 = (bf16[256,1024]{1,0:T(8,128)(2,1)}, bf16[256,1024]{1,0:T(8,128)(2,1)}, u32[]{:S(2)}, u32[]{:S(2)}) collective-permute-start(bf16[256,1024]{1,0:T(8,128)(2,1)} %get-tuple-element.37), channel_id=1, source_target_pairs={{0,16},{8,24},{16,0},{24,8},{1,17},{9,25},{17,1},{25,9},{2,18},{10... | collective-permute-start | bytes 1572872 | tf_op jit(solution)/shard_map/ppermute | solution.py:289
  39.3 4.2 %collective-permute-start = (f32[8,1024]{1,0:T(8,128)S(1)}, f32[8,1024]{1,0:T(8,128)S(1)}, u32[]{:S(2)}, u32[]{:S(2)}) collective-permute-start(f32[8,1024]{1,0:T(8,128)S(1)} %shard_map.120.refs_0_), channel_id=1, source_target_pairs={{0,8},{8,0},{16,24},{24,16},{1,9},{9,1},{17,25},{25,17},{2,10},{10... | collective-permute-start | bytes 98312 | tf_op jit(solution)/shard_map/ppermute | solution.py:338
  40.8 9.2 %collective-permute-start.1 = (f32[8,1024]{1,0:T(8,128)S(1)}, f32[8,1024]{1,0:T(8,128)S(1)}, u32[]{:S(2)}, u32[]{:S(2)}) collective-permute-start(f32[8,1024]{1,0:T(8,128)S(1)} %shard_map.120.refs_0_), channel_id=1, source_target_pairs={{0,16},{8,24},{16,0},{24,8},{1,17},{9,25},{17,1},{25,9},{2,18},{10... | collective-permute-start | bytes 98312 | tf_op jit(solution)/shard_map/ppermute | solution.py:338
  41.3 8.7 %collective-permute-start.2 = (f32[8,1024]{1,0:T(8,128)S(1)}, f32[8,1024]{1,0:T(8,128)S(1)}, u32[]{:S(2)}, u32[]{:S(2)}) collective-permute-start(f32[8,1024]{1,0:T(8,128)S(1)} %shard_map.120.refs_0_), channel_id=1, source_target_pairs={{0,24},{8,16},{16,8},{24,0},{1,25},{9,17},{17,9},{25,1},{2,26},{10... | collective-permute-start | bytes 98312 | tf_op jit(solution)/shard_map/ppermute | solution.py:338
  50.0 18.6 %copy-start.11 = (f32[8,1024]{1,0:T(8,128)}, f32[8,1024]{1,0:T(8,128)S(1)}, u32[]{:S(2)}) copy-start(f32[8,1024]{1,0:T(8,128)S(1)} %collective-permute-done.1.refs_2_.refs_6_) | copy-start | bytes 98308
  50.0 18.6 %copy-start.13 = (f32[8,1024]{1,0:T(8,128)}, f32[8,1024]{1,0:T(8,128)S(1)}, u32[]{:S(2)}) copy-start(f32[8,1024]{1,0:T(8,128)S(1)} %collective-permute-done.2.refs_3_.refs_7_) | copy-start | bytes 98308
  51.0 10.2 %all-to-all-start = ((f32[8,8,128]{2,1,0:T(8,128)}), f32[8,8,128]{2,1,0:T(8,128)S(1)}, u32[]{:S(2)}, u32[]{:S(2)}) async-start(f32[8,8,128]{2,1,0:T(8,128)} %get-tuple-element.16), calls=%async_computation | async-start | bytes 65536 | tf_op jit(solution)/shard_map/all_to_all | solution.py:350
  55.5 1.0 copy-start.5
  61.2 1.0 copy-start.6
  68.7 8.8 %copy-start = (bf16[256,1024]{1,0:T(8,128)(2,1)S(1)}, bf16[256,1024]{1,0:T(8,128)(2,1)}, u32[]{:S(2)}) copy-start(bf16[256,1024]{1,0:T(8,128)(2,1)} %get-tuple-element.40.refs_1_) | copy-start | bytes 1572868
  68.7 8.8 %copy-start.2 = (bf16[256,1024]{1,0:T(8,128)(2,1)S(1)}, bf16[256,1024]{1,0:T(8,128)(2,1)}, u32[]{:S(2)}) copy-start(bf16[256,1024]{1,0:T(8,128)(2,1)} %copy-done.1) | copy-start | bytes 1572868
  68.7 25.4 %all-to-all-start.1 = ((bf16[8,176,128]{2,1,0:T(8,128)(2,1)}), bf16[8,176,128]{2,1,0:T(8,128)(2,1)S(1)}, u32[]{:S(2)}, u32[]{:S(2)}) async-start(bf16[8,176,128]{2,1,0:T(8,128)(2,1)} %shard_map.123), calls=%async_computation.1 | async-start | bytes 720896 | tf_op jit(solution)/shard_map/all_to_all | solution.py:395
  72.3 37.2 %copy-start.4 = (bf16[256,1024]{1,0:T(8,128)(2,1)S(1)}, bf16[256,1024]{1,0:T(8,128)(2,1)}, u32[]{:S(2)}) copy-start(bf16[256,1024]{1,0:T(8,128)(2,1)} %copy-done.3) | copy-start | bytes 1572868
  72.3 37.2 %copy-start.8 = (bf16[256,1024]{1,0:T(8,128)(2,1)S(1)}, bf16[256,1024]{1,0:T(8,128)(2,1)}, u32[]{:S(2)}) copy-start(bf16[256,1024]{1,0:T(8,128)(2,1)} %copy-done.7) | copy-start | bytes 1572868
  72.3 37.2 %collective-permute-start.11 = (bf16[256,1024]{1,0:T(8,128)(2,1)}, bf16[256,1024]{1,0:T(8,128)(2,1)}, u32[]{:S(2)}, u32[]{:S(2)}) collective-permute-start(bf16[256,1024]{1,0:T(8,128)(2,1)} %get-tuple-element.36), channel_id=1, source_target_pairs={{0,16},{8,24},{16,0},{24,8},{1,17},{9,25},{17,1},{25,9},{2,18},{10... | collective-permute-start | bytes 1572872 | tf_op jit(solution)/shard_map/ppermute | solution.py:289
  75.8 33.7 %collective-permute-start.10 = (bf16[256,1024]{1,0:T(8,128)(2,1)}, bf16[256,1024]{1,0:T(8,128)(2,1)}, u32[]{:S(2)}, u32[]{:S(2)}) collective-permute-start(bf16[256,1024]{1,0:T(8,128)(2,1)} %broadcast_select_fusion.1), channel_id=1, source_target_pairs={{0,8},{8,0},{16,24},{24,16},{1,9},{9,1},{17,25},{25,17},{2,10},{10... | collective-permute-start | bytes 1572872 | tf_op jit(solution)/shard_map/ppermute | solution.py:288
  77.5 0.8 copy-start.12
  78.2 0.8 copy-start.14
  79.7 0.6 copy-start.20
  80.4 11.8 %collective-permute-start.3 = (bf16[32,1024]{1,0:T(8,128)(2,1)S(1)}, bf16[32,1024]{1,0:T(8,128)(2,1)S(1)}, u32[]{:S(2)}, u32[]{:S(2)}) collective-permute-start(bf16[32,1024]{1,0:T(8,128)(2,1)S(1)} %get-tuple-element.18), channel_id=1, source_target_pairs={{0,8},{8,0},{16,24},{24,16},{1,9},{9,1},{17,25},{25,17},{2,10},{10... | collective-permute-start | bytes 196616 | tf_op jit(solution)/shard_map/ppermute | solution.py:361
  80.8 12.0 %collective-permute-start.4 = (bf16[32,1024]{1,0:T(8,128)(2,1)S(1)}, bf16[32,1024]{1,0:T(8,128)(2,1)S(1)}, u32[]{:S(2)}, u32[]{:S(2)}) collective-permute-start(bf16[32,1024]{1,0:T(8,128)(2,1)S(1)} %get-tuple-element.19), channel_id=1, source_target_pairs={{0,16},{8,24},{16,0},{24,8},{1,17},{9,25},{17,1},{25,9},{2,18},{10... | collective-permute-start | bytes 196616 | tf_op jit(solution)/shard_map/ppermute | solution.py:361
  81.4 12.0 %collective-permute-start.5 = (bf16[32,1024]{1,0:T(8,128)(2,1)S(1)}, bf16[32,1024]{1,0:T(8,128)(2,1)S(1)}, u32[]{:S(2)}, u32[]{:S(2)}) collective-permute-start(bf16[32,1024]{1,0:T(8,128)(2,1)S(1)} %get-tuple-element.20), channel_id=1, source_target_pairs={{0,24},{8,16},{16,8},{24,0},{1,25},{9,17},{17,9},{25,1},{2,26},{10... | collective-permute-start | bytes 196616 | tf_op jit(solution)/shard_map/ppermute | solution.py:361
  92.2 0.6 copy-start.22
  92.8 0.6 copy-start.24
  93.4 0.6 copy-start.26
  94.1 0.8 copy-start.21
  94.9 0.8 copy-start.23
  95.7 0.8 copy-start.25
  96.6 0.8 copy-start.27
  107.0 0.6 copy-start.15
  107.6 0.6 copy-start.17
  109.5 1.0 copy-start.10
  110.5 0.8 copy-start.16
  111.4 0.8 copy-start.18

commit v2 on v1

--- a/solution.py
+++ b/solution.py
@@ -11,7 +11,7 @@
 F32 = jnp.float32
 BF16 = jnp.bfloat16
 LANES = 128
-VMEM_BYTES = 40 * 1024 * 1024
+MIB = 1024 * 1024
 precise = lax.Precision.HIGHEST
 
 SIN_HALF = (4.4428679, -7.30744342, 3.59478808, -0.78437403)
@@ -28,14 +28,14 @@
     return lax.broadcasted_iota(jnp.int32, shape, dim)
 
 
-def call(kernel, out_shape, in_specs, out_specs, scratch=(), flops=0, moved=0):
+def call(kernel, out_shape, in_specs, out_specs, scratch=(), flops=0, moved=0, vmem=4):
     return pl.pallas_call(
         kernel,
         out_shape=out_shape,
         in_specs=in_specs,
         out_specs=out_specs,
         scratch_shapes=list(scratch),
-        compiler_params=pltpu.CompilerParams(vmem_limit_bytes=VMEM_BYTES),
+        compiler_params=pltpu.CompilerParams(vmem_limit_bytes=vmem * MIB),
         cost_estimate=pl.CostEstimate(flops=flops, bytes_accessed=moved, transcendentals=0),
     )
 
@@ -67,19 +67,58 @@
     return step if is_power(n) else (n - step) % n
 
 
-def start_kernel(count, pos_ref, moved_ref, disp_ref, weight_ref, out_ref):
+def start_kernel(count, pos_ref, moved_ref, disp_ref, weight_ref, out_ref, tiled_ref, shift_ref):
     electrons = pos_ref.shape[2]
+    copies = LANES // count
+    tiled = jnp.concatenate([moved_ref[:, 0, :]] * copies, 1)
+    tiled_ref[...] = tiled
+    zeros = jnp.zeros((5, LANES), F32)
+    for update in range(2):
+        shift = jnp.concatenate([disp_ref[update, 0]] * copies, 1)
+        shift_ref[update] = jnp.concatenate([shift, zeros], 0)
     pos = jnp.concatenate([pos_ref[0], jnp.zeros((5, electrons), F32)], 0)
-    pick = (iota((electrons, LANES), 0) == moved_ref[0:1, :]).astype(F32)
+    pick = (iota((electrons, LANES), 0) == tiled[0:1, :]).astype(F32)
     block = iota((8, LANES), 1) // count
     old = dot(pos, pick, exact=True)
-    disp = disp_ref[0]
+    disp = shift_ref[0]
     points = old + jnp.where(block % 2 == 1, disp, 0.0)
     first = jnp.where(block == 0, disp, 0.0)
     out_ref[...] = pos + dot(first, pick, ((1,), (1,)), exact=True)
     out_ref[3:6, 0:LANES] = points[0:3]
-    out_ref[6:7, 0:LANES] = moved_ref[1:2, :].astype(F32)
+    out_ref[6:7, 0:LANES] = tiled[1:2, :].astype(F32)
     out_ref[7:8, 0:LANES] = jnp.full((1, LANES), weight_ref[0], F32)
+
+
+def round_kernel(wanted, inverse_ref, after_ref, *refs):
+    outs = refs[: len(wanted)]
+    staged, sem = refs[len(wanted) :]
+    depth = staged.shape[1]
+    copies = []
+    for slot, chunk in enumerate(wanted):
+        rows = inverse_ref.at[0, pl.ds(chunk * depth, depth)]
+        copy = pltpu.make_async_copy(rows, staged.at[slot], sem.at[slot])
+        copy.start()
+        copies.append(copy)
+    for slot, out in enumerate(outs):
+        copies[slot].wait()
+        out[...] = staged[slot].astype(BF16)
+
+
+def relay_kernel(flag_ref, own_a, own_b, got_a, got_b, *refs):
+    out_a, out_b, token_ref = refs[-3:]
+    here = flag_ref[0] == 0
+
+    @pl.when(here)
+    def _():
+        out_a[...] = own_a[...]
+        out_b[...] = own_b[...]
+
+    @pl.when(jnp.logical_not(here))
+    def _():
+        out_a[...] = got_a[...]
+        out_b[...] = got_b[...]
+
+    token_ref[...] = jnp.zeros(token_ref.shape, F32)
 
 
 def points_kernel(count, others, role_ref, *refs):
@@ -150,7 +189,9 @@
     return value
 
 
-def evaluate_kernel(count, points_ref, wave_ref, coeff_ref, table_ref, out_ref, diff, new):
+def evaluate_kernel(
+    count, points_ref, wave_ref, coeff_ref, table_ref, after_ref, out_ref, diff, new
+):
     walkers = points_ref.shape[0]
     waves = wave_ref.shape[1]
     width = coeff_ref.shape[1]
@@ -195,29 +236,33 @@
                 ]
 
 
-def eliminate(matrix, size, first):
-    row = iota((size, 1), 0).astype(F32)
-    free = jnp.ones((size, 1), F32)
-    logdet = jnp.zeros((1, 1), F32)
-    for k in range(size):
-        column = matrix[:, first + k : first + k + 1]
-        score = jnp.where(free > 0, jnp.abs(column), -1.0)
-        best = jnp.max(score, axis=0, keepdims=True)
-        index = jnp.min(jnp.where(score == best, row, float(size)), axis=0, keepdims=True)
-        chosen = row == index
-        pivot = jnp.sum(jnp.where(chosen, column, 0.0), axis=0, keepdims=True)
-        line = jnp.sum(jnp.where(chosen, matrix, 0.0), axis=0, keepdims=True) / pivot
-        matrix = jnp.where(chosen, line, matrix - column * line)
-        free = jnp.where(chosen, 0.0, free)
-        logdet = logdet + jnp.log(jnp.abs(pivot))
-    return matrix, logdet
+def sweep(matrices):
+    matrices = list(matrices)
+    logs = [jnp.zeros((1, 1), F32) for _ in matrices]
+    for k in range(max(m.shape[0] for m in matrices)):
+        for which, matrix in enumerate(matrices):
+            size = matrix.shape[0]
+            if k >= size:
+                continue
+            pivot = matrix[k : k + 1, k : k + 1]
+            inverse = 1.0 / pivot
+            column = matrix[:, k : k + 1]
+            line = matrix[k : k + 1, :]
+            row_here = iota((size, size), 0) == k
+            lane_here = iota((size, size), 1) == k
+            scaled = line * inverse
+            reduced = matrix - column * scaled
+            matrix = jnp.where(row_here, scaled, jnp.where(lane_here, column * inverse, reduced))
+            matrix = jnp.where(jnp.logical_and(row_here, lane_here), -inverse, matrix)
+            matrices[which] = matrix
+            logs[which] = logs[which] + jnp.log(pivot)
+    return [-m for m in matrices], logs
 
 
 def solve_kernel(count, others, role_ref, vals_ref, own_ref, *refs):
     received = refs[:others]
-    weight_ref, change_ref, cols_ref, inv_ref, first_ref, second_ref, out_weight_ref, vals = refs[
-        others:
-    ]
+    weight_ref, after_ref = refs[others : others + 2]
+    change_ref, cols_ref, inv_ref, first_ref, second_ref, out_weight_ref, vals = refs[others + 2 :]
     pieces, _, width = vals_ref.shape
     for o in range(pieces):
         vals[:, o * width : (o + 1) * width] = vals_ref[o]
@@ -229,26 +274,26 @@
     cols_ref[...] = cols
     change_ref[...] = vals[0 : 2 * count]
     own = own_ref[0:count]
-    for sums_ref, size, matrix_in, part in (
-        (first_ref, count, own, vals[6 * count : 11 * count]),
-        (second_ref, 2 * count, cols, vals[0 : 6 * count]),
+    products, ratios, normal = [], [], []
+    for size, matrix, part in (
+        (count, own, vals[6 * count : 11 * count]),
+        (2 * count, cols, vals[0 : 6 * count]),
     ):
-        wide = part.shape[0]
-        products = dot(matrix_in, part, ((1,), (1,)))
-        lane = iota((size, wide), 1)
-        row = iota((size, wide), 0)
-        matrix = jnp.where(lane < size, products, 0.0)
-        matrix = matrix + jnp.where(lane == row, 1.0, 0.0) + jnp.where(lane == row + size, 1.0, 0.0)
-        matrix, logdet = eliminate(matrix, size, 0)
-        joined = dot(matrix, matrix, ((0,), (0,)), exact=True)[size : 2 * size, :]
-        line = iota((wide, wide), 0)
-        place = iota((wide, wide), 1)
-        tile = jnp.where(line == size - count + place % count, 1.0, 0.0)
-        spread = dot(joined, tile, exact=True)
-        sums_ref[...] = jnp.sum(products * spread, axis=0, keepdims=True)[:, size:]
-        if size > count:
-            inv_ref[...] = joined[:, 0:size]
-            out_weight_ref[...] = weight_ref[...] + logdet
+        product = dot(matrix, part, ((1,), (1,)))
+        ratio = product[:, 0:size] + jnp.where(iota((size, size), 0) == iota((size, size), 1), 1.0, 0.0)
+        products.append(product[:, size:])
+        ratios.append(ratio)
+        normal.append(dot(ratio, ratio, ((1,), (1,)), exact=True))
+    inverses, logs = sweep(normal)
+    for inverse, ratio, product, sums_ref in zip(inverses, ratios, products, (first_ref, second_ref)):
+        size = ratio.shape[0]
+        wide = product.shape[1]
+        small = dot(inverse, ratio, exact=True)
+        tile = jnp.where(iota((size, wide), 0) == size - count + iota((size, wide), 1) % count, 1.0, 0.0)
+        spread = dot(small, tile, exact=True)
+        sums_ref[...] = jnp.sum(product * spread, axis=0, keepdims=True)
+    inv_ref[...] = small
+    out_weight_ref[...] = weight_ref[...] + 0.5 * logs[1]
 
 
 def finish_kernel(sources, chunks, role_ref, change_ref, cols_ref, inv_ref, *refs):
@@ -280,27 +325,6 @@
         copies.append(copy)
     for copy in copies:
         copy.wait()
-
-
-def branch(own, donor_here, n):
-    chunks = len(own)
-    if n == 4 and chunks == 4:
-        send_x = lambda block: lax.ppermute(block, "grp", pairs(n, 1))
-        send_y = lambda block: lax.ppermute(block, "grp", pairs(n, 2))
-        x1, y1 = send_x(own[0]), send_y(own[3])
-        x2 = send_x(jnp.where(donor_here, own[1], y1))
-        y2 = send_y(jnp.where(donor_here, own[2], x1))
-        x3 = send_x(jnp.where(donor_here, own[2], y2))
-        y3 = send_y(jnp.where(donor_here, own[1], x2))
-        arrays = list(own) + [x1, x2, x3, y1, y2, y3]
-        a1, a2, a3, b1, b2, b3 = range(chunks, chunks + 6)
-        return arrays, [range(chunks), (a1, a2, a3, b3), (a3, b3, b2, b1), (b2, b3, a3, a2)]
-    arrays = list(own)
-    table = [range(chunks)]
-    for step in range(1, n):
-        table.append(range(len(arrays), len(arrays) + chunks))
-        arrays += [lax.ppermute(block, "grp", pairs(n, step)) for block in own]
-    return arrays, table
 
 
 def per_device(
@@ -327,19 +351,37 @@
     apart = distance(n_grp, group, source)
     role = jnp.where(take[0] == 1, apart, 0).astype(jnp.int32).reshape(1)
 
-    tiled = jnp.tile(moved[:, 0], (1, LANES // count))
-    disp = jnp.pad(jnp.tile(displacements[:, 0], (1, 1, LANES // count)), ((0, 0), (0, 5), (0, 0)))
-    record = call(
+    record, tiled, disp = call(
         functools.partial(start_kernel, count),
-        shape((8, electrons), F32),
+        (
+            shape((8, electrons), F32),
+            shape((2, LANES), jnp.int32),
+            shape((2, 8, LANES), F32),
+        ),
         [VM, VM, VM, SM],
-        VM,
-    )(positions, tiled, disp, log_weight)
+        (VM, VM, VM),
+    )(positions, moved, displacements, log_weight)
     records = [lax.ppermute(record, "grp", pairs(n_grp, s)) for s in range(1, n_grp)]
 
     depth = electrons // chunks
-    own = [inverse[0, c * depth : (c + 1) * depth].astype(BF16) for c in range(chunks)]
-    arrays, table = branch(own, apart == 0, n_grp)
+    own = [None] * chunks
+    after = record
+    for wanted in ((0, chunks - 1), tuple(range(1, chunks - 1))):
+        some = call(
+            functools.partial(round_kernel, wanted),
+            tuple(shape((depth, electrons), BF16) for _ in wanted),
+            [ANY, ANY],
+            tuple(VM for _ in wanted),
+            scratch=[
+                pltpu.VMEM((len(wanted), depth, electrons), F32),
+                pltpu.SemaphoreType.DMA((len(wanted),)),
+            ],
+            moved=6 * len(wanted) * depth * electrons,
+            vmem=6,
+        )(inverse, after)
+        for chunk, block in zip(wanted, some):
+            own[chunk] = block
+        after = some[0]
 
     points, weight = call(
         functools.partial(points_kernel, count, others),
@@ -357,6 +399,7 @@
         tuple(VM for _ in steps),
         flops=2 * electrons * electrons * LANES,
         moved=2 * electrons * electrons,
+        vmem=8,
     )(*own, tiled, *records)
     sent = [lax.ppermute(columns[s], "grp", pairs(n_grp, s)) for s in range(1, n_grp)]
 
@@ -369,7 +412,41 @@
         VM,
         flops=8 * plane * width,
         moved=10 * plane * width,
+        vmem=8,
     )(coeff, wavevectors)
+
+    apart = apart.astype(jnp.int32).reshape(1)
+    arrays = list(own)
+    if n_grp == 4:
+        send_x = lambda block: lax.ppermute(block, "grp", pairs(n_grp, 1))
+        send_y = lambda block: lax.ppermute(block, "grp", pairs(n_grp, 2))
+
+        def relay(mine, got, first):
+            kept = shape((depth, electrons), BF16)
+            return call(
+                relay_kernel,
+                (kept, kept, shape((8, LANES), F32)),
+                [SM, VM, VM, VM, VM] + [ANY] * len(first),
+                (VM, VM, VM),
+                moved=4 * depth * electrons,
+                vmem=4,
+            )(apart, *mine, *got, *first)
+
+        x1, y1 = send_x(own[0]), send_y(own[3])
+        relay_x, relay_y, token_1 = relay((own[1], own[2]), (y1, x1), (derived, columns[0]))
+        x2, y2 = send_x(relay_x), send_y(relay_y)
+        relay_x, relay_y, token_2 = relay((own[2], own[1]), (y2, x2), ())
+        x3, y3 = send_x(relay_x), send_y(relay_y)
+        arrays += [x1, x2, x3, y1, y2, y3]
+        a1, a2, a3, b1, b2, b3 = range(chunks, chunks + 6)
+        table = [range(chunks), (a1, a2, a3, b3), (a3, b3, b2, b1), (b2, b3, a3, a2)]
+    else:
+        token_1 = token_2 = jnp.zeros((8, LANES), F32)
+        table = [range(chunks)]
+        for step in range(1, n_grp):
+            table.append(range(len(arrays), len(arrays) + chunks))
+            arrays += [lax.ppermute(block, "grp", pairs(n_grp, step)) for block in own]
+
     block = math.gcd(n_orb, 8)
     values = pl.pallas_call(
         functools.partial(evaluate_kernel, count),
@@ -380,17 +457,20 @@
             pl.BlockSpec(wavevectors.shape, lambda i: (0, 0)),
             pl.BlockSpec(coeff.shape, lambda i: (0, 0)),
             pl.BlockSpec(derived.shape, lambda i: (0, 0)),
+            ANY,
         ],
         out_specs=pl.BlockSpec((block, 11 * count, width), lambda i: (i, 0, 0)),
         scratch_shapes=[
             pltpu.VMEM((block * 3 * count, plane), BF16),
             pltpu.VMEM((block * 2 * count, plane), BF16),
         ],
-        compiler_params=pltpu.CompilerParams(vmem_limit_bytes=VMEM_BYTES),
+        compiler_params=pltpu.CompilerParams(vmem_limit_bytes=16 * MIB),
         cost_estimate=pl.CostEstimate(
-            flops=2 * n_orb * count * plane * width * 11, bytes_accessed=12 * plane * width, transcendentals=0
+            flops=2 * n_orb * count * plane * width * 11,
+            bytes_accessed=12 * plane * width,
+            transcendentals=0,
         ),
-    )(points, wavevectors, coeff, derived)
+    )(points, wavevectors, coeff, derived, token_1)
     values = values[:, :, :local]
     values = lax.all_to_all(values, "orb", split_axis=0, concat_axis=0, tiled=True)
     if width > local:
@@ -406,12 +486,12 @@
             shape((1, 4 * count), F32),
             shape((1, LANES), F32),
         ),
-        [SM] + [VM] * (others + 3),
+        [SM] + [VM] * (others + 3) + [ANY],
         (VM,) * 6,
         scratch=[pltpu.VMEM((11 * count, electrons), BF16)],
         flops=2 * electrons * count * count * 16,
         moved=4 * 11 * count * electrons,
-    )(role, values, columns[0], *sent, weight)
+    )(role, values, columns[0], *sent, weight, token_2)
 
     updated = call(
         functools.partial(finish_kernel, table, chunks),
@@ -426,6 +506,7 @@
         ],
         flops=4 * electrons * electrons * 2 * count,
         moved=6 * electrons * electrons,
+        vmem=12,
     )(role, change, cols, small, *arrays)
 
     both = jnp.concatenate([first, second]).reshape(2, 1, 4, count)

time: 116 us -> 88.5 us (0.76)
  waiting for transfers between devices: 39.2 us -> 20.8 us
  other arithmetic: 8.18 us -> 0.01 us
  local copies, waits for them, and re-layouts: 16.2 us -> 10.4 us
  Pallas kernels: 23.1 us -> 27.3 us
    ppermute x6, waiting for transfers between devices: 21.1 us -> 0.34 us  [the longest x3 0.33 us: per_device(): send_x = lambda block: lax.ppermute(block, 'grp', pairs(n_grp, 1))]
    pallas_call x1 -> x5, Pallas kernels: 0.75 us -> 6.85 us  [the longest x2 4.54 us: relay(): call(relay_kernel, (kept, kept, shape((8, LANES), F32)), [SM, VM, VM, VM,...]
    select_n x3 -> x0, other arithmetic: 5.66 us -> none  [the longest x1 2.46 us: branch(): y3 = send_y(jnp.where(donor_here, own[1], x2))]
    unnamed x68 -> x20, local copies, waits for them, and re-layouts: 14.7 us -> 10.3 us
    pallas_call x1, Pallas kernels: 9.56 us -> 5.57 us  [per_device(): call(functools.partial(solve_kernel, count, others), (shape((2 * count, e...]
    ppermute x3, waiting for transfers between devices: 8.29 us -> 12 us  [per_device(): lax.ppermute(columns[s], 'grp', pairs(n_grp, s))]
    all_to_all x1, waiting for transfers between devices: 3.22 us -> 0.01 us  [per_device(): lax.all_to_all(points, 'orb', split_axis=0, concat_axis=0, tiled=True)]
    another operation x1 -> x0, other arithmetic: 2.51 us -> none
  transfers between devices with their start and end apart: 14 -> 14, of which waited for: 5 -> 5; matrix products, arithmetic and copies ran while one was open for 4% -> 1% of each run, Pallas kernels for 17% -> 24%
where the time goes in v2:
time: 88.5 us; the launch traced here: 87.8 us
  Pallas kernels  27.3 us (31%)
  starting transfers between devices  26.6 us (30%)
  waiting for transfers between devices  20.8 us (24%)
  local copies, waits for them, and re-layouts  10.4 us (12%)
  between operations  2.68 us (3%)
    ppermute x3, waiting for transfers between devices, per_device(): lax.ppermute(columns[s], 'grp', pairs(n_grp, s))  12 us
    unnamed x20, local copies, waits for them, and re-layouts  10.3 us
    ppermute x3, waiting for transfers between devices, per_device(): lax.ppermute(record, 'grp', pairs(n_grp, s))  8.51 us
    pallas_call x1, Pallas kernels, per_device(): pl.pallas_call(functools.partial(evaluate_kernel, count), grid=(n_orb //...  6.4 us
    pallas_call x1, Pallas kernels, per_device(): call(functools.partial(solve_kernel, count, others), (shape((2 * count, e...  5.57 us
    all_to_all x1, starting transfers between devices, per_device(): lax.all_to_all(values, 'orb', split_axis=0, concat_axis=0, tiled=True)  5.1 us
    ppermute x3, starting transfers between devices, per_device(): send_y = lambda block: lax.ppermute(block, 'grp', pairs(n_grp, 2))  5.06 us
    all_to_all x1, starting transfers between devices, per_device(): lax.all_to_all(points, 'orb', split_axis=0, concat_axis=0, tiled=True)  5.02 us
  transfers between devices with their start and end apart: 14, of which 5 were waited for; matrix products, arithmetic and copies ran while one was open for 1% of the time, Pallas kernels for 24%

profile of v2, /device:TPU:0, one launch (start us, length us, event | category | flops | bytes accessed | tf_op | source)
XLA Modules:
  0.0 87.8 jit_solution(17992431237050020967)
XLA Ops:
  0.6 0.7 copy.13.pos_ref
  1.3 0.7 copy.14.disp_ref
  2.7 0.0 copy-start.5
  2.7 0.7 copy-done.5
  3.4 0.8 shard_map.120
  4.2 2.2 %copy-done = f32[1,1024,1024]{2,1,0:T(8,128)S(1)} copy-done((f32[1,1024,1024]{2,1,0:T(8,128)S(1)}, f32[1,1024,1024]{2,1,0:T(8,128)}, u32[]{:S(2)}) %copy-start) | copy-done | bytes 4194328
  6.4 1.2 %shard_map.123 = (bf16[256,1024]{1,0:T(8,128)(2,1)}, bf16[256,1024]{1,0:T(8,128)(2,1)}) custom-call(f32[1,1024,1024]{2,1,0:T(8,128)S(1)} %copy-done, f32[8,1024]{1,0:T(8,128)S(1)} %get-tuple-element.29.refs_0_.after_ref), custom_call_target="tpu_custom_call" | custom-call | bytes 3145728 | tf_op jit(solution)/shard_map/pallas_call | solution.py:370
  7.6 3.0 %collective-permute-start.3 = (bf16[256,1024]{1,0:T(8,128)(2,1)}, bf16[256,1024]{1,0:T(8,128)(2,1)}, u32[]{:S(2)}, u32[]{:S(2)}) collective-permute-start(bf16[256,1024]{1,0:T(8,128)(2,1)} %get-tuple-element.36.refs_3_), channel_id=1, source_target_pairs={{0,16},{8,24},{16,0},{24,8},{1,17},{9,25},{17,1},{25,9},{2,18},{10... | collective-permute-start | bytes 1572872 | tf_op jit(solution)/shard_map/ppermute | solution.py:422
  10.6 1.5 %collective-permute-start.4 = (bf16[256,1024]{1,0:T(8,128)(2,1)}, bf16[256,1024]{1,0:T(8,128)(2,1)}, u32[]{:S(2)}, u32[]{:S(2)}) collective-permute-start(bf16[256,1024]{1,0:T(8,128)(2,1)} %get-tuple-element.33.after_ref.refs_0_), channel_id=1, source_target_pairs={{0,8},{8,0},{16,24},{24,16},{1,9},{9,1},{17,25},{25,17},{2,10},{10... | collective-permute-start | bytes 1572872 | tf_op jit(solution)/shard_map/ppermute | solution.py:421
  12.1 0.5 collective-permute-start
  12.7 0.1 collective-permute-start.1
  12.8 2.9 %collective-permute-start.2 = (f32[8,1024]{1,0:T(8,128)S(1)}, f32[8,1024]{1,0:T(8,128)S(1)}, u32[]{:S(2)}, u32[]{:S(2)}) collective-permute-start(f32[8,1024]{1,0:T(8,128)S(1)} %get-tuple-element.29.refs_0_.after_ref), channel_id=1, source_target_pairs={{0,24},{8,16},{16,8},{24,0},{1,25},{9,17},{17,9},{25,1},{2,26},{10... | collective-permute-start | bytes 98312 | tf_op jit(solution)/shard_map/ppermute | solution.py:364
  16.9 8.4 %collective-permute-done.refs_1_.refs_5_ = f32[8,1024]{1,0:T(8,128)S(1)} collective-permute-done((f32[8,1024]{1,0:T(8,128)S(1)}, f32[8,1024]{1,0:T(8,128)S(1)}, u32[]{:S(2)}, u32[]{:S(2)}) %collective-permute-start) | collective-permute-done | bytes 32800 | tf_op jit(solution)/shard_map/ppermute | solution.py:364
  25.3 0.0 collective-permute-done.1.refs_2_.refs_6_
  25.3 0.1 collective-permute-done.2.refs_3_.refs_7_
  25.4 1.0 %shard_map.121 = (f32[8,8,128]{2,1,0:T(8,128)}, f32[1,128]{1,0:T(1,128)S(1)}) custom-call(s32[1]{0:T(128)} %bitcast.2.role_ref, f32[8,1024]{1,0:T(8,128)S(1)} %get-tuple-element.29.refs_0_.after_ref, f32[8,1024]{1,0:T(8,128)S(1)} %collective-permute-done.refs_1_.refs_5_, f32[8,1024]{1,0:T(8,128)S(1)} %collective-permute-done.1.refs_2_.refs_6_, ...), custom_call_target="tpu_custom_call" | custom-call | tf_op jit(solution)/shard_map/pallas_call | solution.py:386
  26.4 5.0 %all-to-all-start = ((f32[8,8,128]{2,1,0:T(8,128)}), f32[8,8,128]{2,1,0:T(8,128)S(1)}, u32[]{:S(2)}, u32[]{:S(2)}) async-start(f32[8,8,128]{2,1,0:T(8,128)} %get-tuple-element.32), calls=%async_computation | async-start | bytes 65536 | tf_op jit(solution)/shard_map/all_to_all | solution.py:392
  31.4 2.2 %copy-done.1 = f32[1,1024,1024]{2,1,0:T(8,128)S(1)} copy-done((f32[1,1024,1024]{2,1,0:T(8,128)S(1)}, f32[1,1024,1024]{2,1,0:T(8,128)}, u32[]{:S(2)}) %copy-start.1) | copy-done | bytes 4194328
  33.6 0.3 shard_map.124
  33.9 0.0 copy-start.2
  33.9 1.0 %copy-done.2 = bf16[2048,128]{1,0:T(8,128)(2,1)S(1)} copy-done((bf16[2048,128]{1,0:T(8,128)(2,1)S(1)}, bf16[2048,128]{1,0:T(8,128)(2,1)}, u32[]{:S(2)}) %copy-start.2) | copy-done | bytes 524312
  34.9 1.5 %shard_map.122.refs_0_.table_ref = bf16[2048,512]{1,0:T(8,128)(2,1)S(1)} custom-call(bf16[2048,128]{1,0:T(8,128)(2,1)S(1)} %copy-done.2, f32[3,1024]{1,0:T(4,128)S(1)} %copy-done.4), custom_call_target="tpu_custom_call" | custom-call | flops 2097152 | bytes 2621440 | tf_op jit(solution)/shard_map/pallas_call | solution.py:408
  36.4 2.0 %shard_map.125 = (bf16[32,1024]{1,0:T(8,128)(2,1)S(1)}, bf16[32,1024]{1,0:T(8,128)(2,1)S(1)}, bf16[32,1024]{1,0:T(8,128)(2,1)S(1)}, bf16[32,1024]{1,0:T(8,128)(2,1)S(1)}) custom-call(bf16[256,1024]{1,0:T(8,128)(2,1)} %get-tuple-element.33.after_ref.refs_0_, bf16[256,1024]{1,0:T(8,128)(2,1)S(1)} %get-tuple-element.34.refs_1_.own_a.own_b, ...), custom_call_target="tpu_custom_call" | custom-call | flops 268435456 | bytes 2097152 | tf_op jit(solution)/shard_map/pallas_call | solution.py:395
  38.4 0.6 copy-done.6
  39.0 0.0 collective-permute-done.3.got_a.refs_7_
  39.0 0.0 collective-permute-done.4.got_b.refs_4_
  39.0 2.3 %shard_map.126 = (bf16[256,1024]{1,0:T(8,128)(2,1)}, bf16[256,1024]{1,0:T(8,128)(2,1)}, f32[8,128]{1,0:T(8,128)S(1)}) custom-call(s32[1]{0:T(128)} %bitcast.3.flag_ref, bf16[256,1024]{1,0:T(8,128)(2,1)S(1)} %get-tuple-element.34.refs_1_.own_a.own_b, bf16[256,1024]{1,0:T(8,128)(2,1)S(1)} %get-tuple-element.35.refs_2_.own_b.own_a, ...), custom_call_target="tpu_custom_call" | custom-call | bytes 1048576 | tf_op jit(solution)/shard_map/pallas_call | solution.py:426
  41.3 1.5 %collective-permute-start.8 = (bf16[256,1024]{1,0:T(8,128)(2,1)}, bf16[256,1024]{1,0:T(8,128)(2,1)}, u32[]{:S(2)}, u32[]{:S(2)}) collective-permute-start(bf16[256,1024]{1,0:T(8,128)(2,1)} %get-tuple-element.43), channel_id=1, source_target_pairs={{0,16},{8,24},{16,0},{24,8},{1,17},{9,25},{17,1},{25,9},{2,18},{10... | collective-permute-start | bytes 1572872 | tf_op jit(solution)/shard_map/ppermute | solution.py:422
  42.8 1.5 %collective-permute-start.9 = (bf16[256,1024]{1,0:T(8,128)(2,1)}, bf16[256,1024]{1,0:T(8,128)(2,1)}, u32[]{:S(2)}, u32[]{:S(2)}) collective-permute-start(bf16[256,1024]{1,0:T(8,128)(2,1)} %get-tuple-element.44), channel_id=1, source_target_pairs={{0,8},{8,0},{16,24},{24,16},{1,9},{9,1},{17,25},{25,17},{2,10},{10... | collective-permute-start | bytes 1572872 | tf_op jit(solution)/shard_map/ppermute | solution.py:421
  44.3 0.0 all-to-all-done.points_ref
  44.3 1.0 %copy-done.3 = bf16[2048,128]{1,0:T(8,128)(2,1)S(1)} copy-done((bf16[2048,128]{1,0:T(8,128)(2,1)S(1)}, bf16[2048,128]{1,0:T(8,128)(2,1)}, u32[]{:S(2)}) %copy-start.3) | copy-done | bytes 524312
  45.4 6.4 %shard_map.127 = bf16[8,176,128]{2,1,0:T(8,128)(2,1)} custom-call(f32[8,8,128]{2,1,0:T(8,128)S(1)} %all-to-all-done.points_ref, f32[3,1024]{1,0:T(4,128)S(1)} %copy-done.4, bf16[2048,128]{1,0:T(8,128)(2,1)S(1)} %copy-done.3, bf16[2048,512]{1,0:T(8,128)(2,1)S(1)} %shard_map.122.refs_0_.table_ref, f32[8,128]{1,0:T(8,128)S(1)} %get-tuple-element.38.after_ref), custom_call_target="tpu_custom_call" | custom-call | flops 738197504 | bytes 3145728 | tf_op jit(solution)/shard_map/pallas_call | solution.py:451
  51.8 5.1 %all-to-all-start.1 = ((bf16[8,176,128]{2,1,0:T(8,128)(2,1)}), bf16[8,176,128]{2,1,0:T(8,128)(2,1)S(1)}, u32[]{:S(2)}, u32[]{:S(2)}) async-start(bf16[8,176,128]{2,1,0:T(8,128)(2,1)} %shard_map.127), calls=%async_computation.1 | async-start | bytes 720896 | tf_op jit(solution)/shard_map/all_to_all | solution.py:475
  56.9 0.3 collective-permute-done.9.got_b.refs_5_
  57.2 2.3 %shard_map.128 = (bf16[256,1024]{1,0:T(8,128)(2,1)}, bf16[256,1024]{1,0:T(8,128)(2,1)}, f32[8,128]{1,0:T(8,128)S(1)}) custom-call(s32[1]{0:T(128)} %bitcast.3.flag_ref, bf16[256,1024]{1,0:T(8,128)(2,1)S(1)} %get-tuple-element.35.refs_2_.own_b.own_a, bf16[256,1024]{1,0:T(8,128)(2,1)S(1)} %get-tuple-element.34.refs_1_.own_a.own_b, ...), custom_call_target="tpu_custom_call" | custom-call | bytes 1048576 | tf_op jit(solution)/shard_map/pallas_call | solution.py:426
  59.5 1.5 %collective-permute-start.10 = (bf16[256,1024]{1,0:T(8,128)(2,1)}, bf16[256,1024]{1,0:T(8,128)(2,1)S(1)}, u32[]{:S(2)}, u32[]{:S(2)}) collective-permute-start(bf16[256,1024]{1,0:T(8,128)(2,1)} %get-tuple-element.49), channel_id=1, source_target_pairs={{0,8},{8,0},{16,24},{24,16},{1,9},{9,1},{17,25},{25,17},{2,10},{10... | collective-permute-start | bytes 1572872 | tf_op jit(solution)/shard_map/ppermute | solution.py:421
  61.0 0.5 collective-permute-start.11
  61.5 0.5 collective-permute-start.5
  62.0 1.5 %collective-permute-start.6 = (bf16[32,1024]{1,0:T(8,128)(2,1)S(1)}, bf16[32,1024]{1,0:T(8,128)(2,1)S(1)}, u32[]{:S(2)}, u32[]{:S(2)}) collective-permute-start(bf16[32,1024]{1,0:T(8,128)(2,1)S(1)} %get-tuple-element.40), channel_id=1, source_target_pairs={{0,16},{8,24},{16,0},{24,8},{1,17},{9,25},{17,1},{25,9},{2,18},{10... | collective-permute-start | bytes 196616 | tf_op jit(solution)/shard_map/ppermute | solution.py:404
  63.5 1.4 %collective-permute-start.7 = (bf16[32,1024]{1,0:T(8,128)(2,1)S(1)}, bf16[32,1024]{1,0:T(8,128)(2,1)S(1)}, u32[]{:S(2)}, u32[]{:S(2)}) collective-permute-start(bf16[32,1024]{1,0:T(8,128)(2,1)S(1)} %get-tuple-element.41), channel_id=1, source_target_pairs={{0,24},{8,16},{16,8},{24,0},{1,25},{9,17},{17,9},{25,1},{2,26},{10... | collective-permute-start | bytes 196616 | tf_op jit(solution)/shard_map/ppermute | solution.py:404
  65.0 10.8 %collective-permute-done.5.refs_0_ = bf16[32,1024]{1,0:T(8,128)(2,1)S(1)} collective-permute-done((bf16[32,1024]{1,0:T(8,128)(2,1)S(1)}, bf16[32,1024]{1,0:T(8,128)(2,1)S(1)}, u32[]{:S(2)}, u32[]{:S(2)}) %collective-permute-start.5) | collective-permute-done | bytes 65568 | tf_op jit(solution)/shard_map/ppermute | solution.py:404
  75.8 1.1 %collective-permute-done.6.refs_1_ = bf16[32,1024]{1,0:T(8,128)(2,1)S(1)} collective-permute-done((bf16[32,1024]{1,0:T(8,128)(2,1)S(1)}, bf16[32,1024]{1,0:T(8,128)(2,1)S(1)}, u32[]{:S(2)}, u32[]{:S(2)}) %collective-permute-start.6) | collective-permute-done | bytes 65568 | tf_op jit(solution)/shard_map/ppermute | solution.py:404
  76.9 5.6 %shard_map.129 = (bf16[32,1024]{1,0:T(8,128)(2,1)S(1)}, bf16[32,1024]{1,0:T(8,128)(2,1)S(1)}, f32[32,32]{1,0:T(8,128)S(1)}, f32[1,64]{1,0:T(1,128)S(1)}, f32[1,64]{1,0:T(1,128)S(1)}, /*index=5*/f32[1,128]{1,0:T(1,128)}) custom-call(s32[1]{0:T(128)} %bitcast.2.role_ref, bf16[8,176,128]{2,1,0:T(8,128)(2,1)S(1)} %all-to-all-done.1.vals_ref, ...), custom_call_target="tpu_custom_call" | custom-call | flops 8388608 | bytes 720896 | tf_op jit(solution)/shard_map/pallas_call | solution.py:479
  82.5 0.1 reshape.21
  82.6 0.6 copy.15
  83.2 0.6 slice_bitcast_fusion
  83.7 0.0 collective-permute-done.10.refs_6_
  83.8 4.0 %shard_map.130 = f32[1024,1024]{1,0:T(8,128)} custom-call(s32[1]{0:T(128)} %bitcast.2.role_ref, bf16[32,1024]{1,0:T(8,128)(2,1)S(1)} %get-tuple-element.46.change_ref, bf16[32,1024]{1,0:T(8,128)(2,1)S(1)} %get-tuple-element.47.cols_ref, f32[32,32]{1,0:T(8,128)S(1)} %get-tuple-element.48.inv_ref, bf16[256,1024]{1,0:T(8,128)(2,1)} %get-tuple-element.33.after_ref.refs_0_, ...), custom_call_target="tpu_custom_call" | custom-call | flops 134217728 | bytes 6291456 | tf_op jit(solution)/shard_map/pallas_call | solution.py:496
  (13 shorter events, 0.0 us)
Async XLA Ops:
  2.7 0.7 copy-start.5
  4.2 2.2 %copy-start = (f32[1,1024,1024]{2,1,0:T(8,128)S(1)}, f32[1,1024,1024]{2,1,0:T(8,128)}, u32[]{:S(2)}) copy-start(f32[1,1024,1024]{2,1,0:T(8,128)} %inverse_ref.3) | copy-start | bytes 12582916
  6.4 27.5 %copy-start.4 = (f32[3,1024]{1,0:T(4,128)S(1)}, f32[3,1024]{1,0:T(4,128)}, u32[]{:S(2)}) copy-start(f32[3,1024]{1,0:T(4,128)} %wave_ref.3) | copy-start | bytes 36868
  7.6 31.4 %collective-permute-start.3 = (bf16[256,1024]{1,0:T(8,128)(2,1)}, bf16[256,1024]{1,0:T(8,128)(2,1)}, u32[]{:S(2)}, u32[]{:S(2)}) collective-permute-start(bf16[256,1024]{1,0:T(8,128)(2,1)} %get-tuple-element.36.refs_3_), channel_id=1, source_target_pairs={{0,16},{8,24},{16,0},{24,8},{1,17},{9,25},{17,1},{25,9},{2,18},{10... | collective-permute-start | bytes 1572872 | tf_op jit(solution)/shard_map/ppermute | solution.py:422
  10.6 28.4 %collective-permute-start.4 = (bf16[256,1024]{1,0:T(8,128)(2,1)}, bf16[256,1024]{1,0:T(8,128)(2,1)}, u32[]{:S(2)}, u32[]{:S(2)}) collective-permute-start(bf16[256,1024]{1,0:T(8,128)(2,1)} %get-tuple-element.33.after_ref.refs_0_), channel_id=1, source_target_pairs={{0,8},{8,0},{16,24},{24,16},{1,9},{9,1},{17,25},{25,17},{2,10},{10... | collective-permute-start | bytes 1572872 | tf_op jit(solution)/shard_map/ppermute | solution.py:421
  12.1 13.2 %collective-permute-start = (f32[8,1024]{1,0:T(8,128)S(1)}, f32[8,1024]{1,0:T(8,128)S(1)}, u32[]{:S(2)}, u32[]{:S(2)}) collective-permute-start(f32[8,1024]{1,0:T(8,128)S(1)} %get-tuple-element.29.refs_0_.after_ref), channel_id=1, source_target_pairs={{0,8},{8,0},{16,24},{24,16},{1,9},{9,1},{17,25},{25,17},{2,10},{10... | collective-permute-start | bytes 98312 | tf_op jit(solution)/shard_map/ppermute | solution.py:364
  12.7 12.6 %collective-permute-start.1 = (f32[8,1024]{1,0:T(8,128)S(1)}, f32[8,1024]{1,0:T(8,128)S(1)}, u32[]{:S(2)}, u32[]{:S(2)}) collective-permute-start(f32[8,1024]{1,0:T(8,128)S(1)} %get-tuple-element.29.refs_0_.after_ref), channel_id=1, source_target_pairs={{0,16},{8,24},{16,0},{24,8},{1,17},{9,25},{17,1},{25,9},{2,18},{10... | collective-permute-start | bytes 98312 | tf_op jit(solution)/shard_map/ppermute | solution.py:364
  12.8 12.7 %collective-permute-start.2 = (f32[8,1024]{1,0:T(8,128)S(1)}, f32[8,1024]{1,0:T(8,128)S(1)}, u32[]{:S(2)}, u32[]{:S(2)}) collective-permute-start(f32[8,1024]{1,0:T(8,128)S(1)} %get-tuple-element.29.refs_0_.after_ref), channel_id=1, source_target_pairs={{0,24},{8,16},{16,8},{24,0},{1,25},{9,17},{17,9},{25,1},{2,26},{10... | collective-permute-start | bytes 98312 | tf_op jit(solution)/shard_map/ppermute | solution.py:364
  26.4 17.9 %all-to-all-start = ((f32[8,8,128]{2,1,0:T(8,128)}), f32[8,8,128]{2,1,0:T(8,128)S(1)}, u32[]{:S(2)}, u32[]{:S(2)}) async-start(f32[8,8,128]{2,1,0:T(8,128)} %get-tuple-element.32), calls=%async_computation | async-start | bytes 65536 | tf_op jit(solution)/shard_map/all_to_all | solution.py:392
  31.4 2.2 %copy-start.1 = (f32[1,1024,1024]{2,1,0:T(8,128)S(1)}, f32[1,1024,1024]{2,1,0:T(8,128)}, u32[]{:S(2)}) copy-start(f32[1,1024,1024]{2,1,0:T(8,128)} %inverse_ref.3) | copy-start | bytes 12582916
  33.9 1.0 %copy-start.2 = (bf16[2048,128]{1,0:T(8,128)(2,1)S(1)}, bf16[2048,128]{1,0:T(8,128)(2,1)}, u32[]{:S(2)}) copy-start(bf16[2048,128]{1,0:T(8,128)(2,1)} %coeff_ref.3) | copy-start | bytes 1572868
  38.4 0.6 copy-start.6
  39.0 22.4 %copy-start.7 = (bf16[32,1024]{1,0:T(8,128)(2,1)S(1)}, bf16[32,1024]{1,0:T(8,128)(2,1)}, u32[]{:S(2)}) copy-start(bf16[32,1024]{1,0:T(8,128)(2,1)} %copy-done.6) | copy-start | bytes 196612
  41.3 15.6 %collective-permute-start.8 = (bf16[256,1024]{1,0:T(8,128)(2,1)}, bf16[256,1024]{1,0:T(8,128)(2,1)}, u32[]{:S(2)}, u32[]{:S(2)}) collective-permute-start(bf16[256,1024]{1,0:T(8,128)(2,1)} %get-tuple-element.43), channel_id=1, source_target_pairs={{0,16},{8,24},{16,0},{24,8},{1,17},{9,25},{17,1},{25,9},{2,18},{10... | collective-permute-start | bytes 1572872 | tf_op jit(solution)/shard_map/ppermute | solution.py:422
  42.8 14.4 %collective-permute-start.9 = (bf16[256,1024]{1,0:T(8,128)(2,1)}, bf16[256,1024]{1,0:T(8,128)(2,1)}, u32[]{:S(2)}, u32[]{:S(2)}) collective-permute-start(bf16[256,1024]{1,0:T(8,128)(2,1)} %get-tuple-element.44), channel_id=1, source_target_pairs={{0,8},{8,0},{16,24},{24,16},{1,9},{9,1},{17,25},{25,17},{2,10},{10... | collective-permute-start | bytes 1572872 | tf_op jit(solution)/shard_map/ppermute | solution.py:421
  44.3 1.0 %copy-start.3 = (bf16[2048,128]{1,0:T(8,128)(2,1)S(1)}, bf16[2048,128]{1,0:T(8,128)(2,1)}, u32[]{:S(2)}) copy-start(bf16[2048,128]{1,0:T(8,128)(2,1)} %coeff_ref.3) | copy-start | bytes 1572868
  51.8 25.2 %all-to-all-start.1 = ((bf16[8,176,128]{2,1,0:T(8,128)(2,1)}), bf16[8,176,128]{2,1,0:T(8,128)(2,1)S(1)}, u32[]{:S(2)}, u32[]{:S(2)}) async-start(bf16[8,176,128]{2,1,0:T(8,128)(2,1)} %shard_map.127), calls=%async_computation.1 | async-start | bytes 720896 | tf_op jit(solution)/shard_map/all_to_all | solution.py:475
  59.5 24.3 %collective-permute-start.10 = (bf16[256,1024]{1,0:T(8,128)(2,1)}, bf16[256,1024]{1,0:T(8,128)(2,1)S(1)}, u32[]{:S(2)}, u32[]{:S(2)}) collective-permute-start(bf16[256,1024]{1,0:T(8,128)(2,1)} %get-tuple-element.49), channel_id=1, source_target_pairs={{0,8},{8,0},{16,24},{24,16},{1,9},{9,1},{17,25},{25,17},{2,10},{10... | collective-permute-start | bytes 1572872 | tf_op jit(solution)/shard_map/ppermute | solution.py:421
  61.0 22.8 %collective-permute-start.11 = (bf16[256,1024]{1,0:T(8,128)(2,1)}, bf16[256,1024]{1,0:T(8,128)(2,1)S(1)}, u32[]{:S(2)}, u32[]{:S(2)}) collective-permute-start(bf16[256,1024]{1,0:T(8,128)(2,1)} %get-tuple-element.50), channel_id=1, source_target_pairs={{0,16},{8,24},{16,0},{24,8},{1,17},{9,25},{17,1},{25,9},{2,18},{10... | collective-permute-start | bytes 1572872 | tf_op jit(solution)/shard_map/ppermute | solution.py:422
  61.5 14.3 %collective-permute-start.5 = (bf16[32,1024]{1,0:T(8,128)(2,1)S(1)}, bf16[32,1024]{1,0:T(8,128)(2,1)S(1)}, u32[]{:S(2)}, u32[]{:S(2)}) collective-permute-start(bf16[32,1024]{1,0:T(8,128)(2,1)S(1)} %copy-done.7), channel_id=1, source_target_pairs={{0,8},{8,0},{16,24},{24,16},{1,9},{9,1},{17,25},{25,17},{2,10},{10... | collective-permute-start | bytes 196616 | tf_op jit(solution)/shard_map/ppermute | solution.py:404
  62.0 14.9 %collective-permute-start.6 = (bf16[32,1024]{1,0:T(8,128)(2,1)S(1)}, bf16[32,1024]{1,0:T(8,128)(2,1)S(1)}, u32[]{:S(2)}, u32[]{:S(2)}) collective-permute-start(bf16[32,1024]{1,0:T(8,128)(2,1)S(1)} %get-tuple-element.40), channel_id=1, source_target_pairs={{0,16},{8,24},{16,0},{24,8},{1,17},{9,25},{17,1},{25,9},{2,18},{10... | collective-permute-start | bytes 196616 | tf_op jit(solution)/shard_map/ppermute | solution.py:404
  63.5 13.4 %collective-permute-start.7 = (bf16[32,1024]{1,0:T(8,128)(2,1)S(1)}, bf16[32,1024]{1,0:T(8,128)(2,1)S(1)}, u32[]{:S(2)}, u32[]{:S(2)}) collective-permute-start(bf16[32,1024]{1,0:T(8,128)(2,1)S(1)} %get-tuple-element.41), channel_id=1, source_target_pairs={{0,24},{8,16},{16,8},{24,0},{1,25},{9,17},{17,9},{25,1},{2,26},{10... | collective-permute-start | bytes 196616 | tf_op jit(solution)/shard_map/ppermute | solution.py:404

commit v3 on v2

--- a/solution.py
+++ b/solution.py
@@ -28,10 +28,13 @@
     return lax.broadcasted_iota(jnp.int32, shape, dim)
 
 
-def call(kernel, out_shape, in_specs, out_specs, scratch=(), flops=0, moved=0, vmem=4):
+def call(
+    kernel, out_shape, in_specs, out_specs, scratch=(), flops=0, moved=0, vmem=4, aliases=None
+):
     return pl.pallas_call(
         kernel,
         out_shape=out_shape,
+        input_output_aliases=aliases or {},
         in_specs=in_specs,
         out_specs=out_specs,
         scratch_shapes=list(scratch),
@@ -43,6 +46,7 @@
 VM = pl.BlockSpec(memory_space=pltpu.VMEM)
 SM = pl.BlockSpec(memory_space=pltpu.SMEM)
 ANY = pl.BlockSpec(memory_space=pl.ANY)
+HBM = pl.BlockSpec(memory_space=pltpu.HBM)
 
 
 def shape(dims, dtype):
@@ -67,18 +71,48 @@
     return step if is_power(n) else (n - step) % n
 
 
-def start_kernel(count, pos_ref, moved_ref, disp_ref, weight_ref, out_ref, tiled_ref, shift_ref):
+def start_kernel(
+    count,
+    pos_hbm,
+    moved_hbm,
+    disp_hbm,
+    weight_hbm,
+    out_ref,
+    tiled_ref,
+    shift_ref,
+    pos_ref,
+    moved_ref,
+    disp_ref,
+    weight_ref,
+    sems,
+):
+    loads = [
+        pltpu.make_async_copy(src, dst, sems.at[i])
+        for i, (src, dst) in enumerate(
+            (
+                (moved_hbm, moved_ref),
+                (disp_hbm, disp_ref),
+                (pos_hbm, pos_ref),
+                (weight_hbm, weight_ref),
+            )
+        )
+    ]
+    for load in loads:
+        load.start()
     electrons = pos_ref.shape[2]
     copies = LANES // count
+    loads[0].wait()
     tiled = jnp.concatenate([moved_ref[:, 0, :]] * copies, 1)
     tiled_ref[...] = tiled
-    zeros = jnp.zeros((5, LANES), F32)
-    for update in range(2):
-        shift = jnp.concatenate([disp_ref[update, 0]] * copies, 1)
-        shift_ref[update] = jnp.concatenate([shift, zeros], 0)
-    pos = jnp.concatenate([pos_ref[0], jnp.zeros((5, electrons), F32)], 0)
     pick = (iota((electrons, LANES), 0) == tiled[0:1, :]).astype(F32)
     block = iota((8, LANES), 1) // count
+    zeros = jnp.zeros((5, LANES), F32)
+    loads[1].wait()
+    for update in range(2):
+        shift = jnp.concatenate([disp_ref[3 * update : 3 * update + 3, 0, :]] * copies, 1)
+        shift_ref[update] = jnp.concatenate([shift, zeros], 0)
+    loads[2].wait()
+    pos = jnp.concatenate([pos_ref[:, 0, :], jnp.zeros((5, electrons), F32)], 0)
     old = dot(pos, pick, exact=True)
     disp = shift_ref[0]
     points = old + jnp.where(block % 2 == 1, disp, 0.0)
@@ -86,37 +120,43 @@
     out_ref[...] = pos + dot(first, pick, ((1,), (1,)), exact=True)
     out_ref[3:6, 0:LANES] = points[0:3]
     out_ref[6:7, 0:LANES] = tiled[1:2, :].astype(F32)
+    loads[3].wait()
     out_ref[7:8, 0:LANES] = jnp.full((1, LANES), weight_ref[0], F32)
 
 
-def round_kernel(wanted, inverse_ref, after_ref, *refs):
-    outs = refs[: len(wanted)]
-    staged, sem = refs[len(wanted) :]
+def round_kernel(inverse_ref, after_ref, *refs):
+    outs = refs[:-2]
+    staged, sem = refs[-2:]
     depth = staged.shape[1]
     copies = []
-    for slot, chunk in enumerate(wanted):
+    for chunk in range(len(outs)):
         rows = inverse_ref.at[0, pl.ds(chunk * depth, depth)]
-        copy = pltpu.make_async_copy(rows, staged.at[slot], sem.at[slot])
+        copy = pltpu.make_async_copy(rows, staged.at[chunk], sem.at[chunk])
         copy.start()
         copies.append(copy)
-    for slot, out in enumerate(outs):
-        copies[slot].wait()
-        out[...] = staged[slot].astype(BF16)
+    for chunk, out in enumerate(outs):
+        copies[chunk].wait()
+        out[...] = staged[chunk].astype(BF16)
+
+
+def gate_kernel(*refs):
+    token_ref = refs[-1]
+    token_ref[...] = jnp.zeros(token_ref.shape, F32)
 
 
 def relay_kernel(flag_ref, own_a, own_b, got_a, got_b, *refs):
-    out_a, out_b, token_ref = refs[-3:]
-    here = flag_ref[0] == 0
-
-    @pl.when(here)
+    out_a, out_b, token_ref, sems = refs[-4:]
+
+    @pl.when(flag_ref[0] == 0)
     def _():
-        out_a[...] = own_a[...]
-        out_b[...] = own_b[...]
-
-    @pl.when(jnp.logical_not(here))
-    def _():
-        out_a[...] = got_a[...]
-        out_b[...] = got_b[...]
+        copies = [
+            pltpu.make_async_copy(own_a, out_a, sems.at[0]),
+            pltpu.make_async_copy(own_b, out_b, sems.at[1]),
+        ]
+        for copy in copies:
+            copy.start()
+        for copy in copies:
+            copy.wait()
 
     token_ref[...] = jnp.zeros(token_ref.shape, F32)
 
@@ -124,7 +164,7 @@
 def points_kernel(count, others, role_ref, *refs):
     own_ref = refs[0]
     received = refs[1 : 1 + others]
-    moved_ref, disp_ref, points_ref, weight_ref = refs[1 + others :]
+    moved_ref, disp_ref, after_ref, points_ref, weight_ref = refs[1 + others :]
     role = role_ref[0]
     parent = own_ref[...]
     for step in range(others):
@@ -168,16 +208,17 @@
     waves = wave_ref.shape[1]
     width = coeff_ref.shape[1]
     wave = jnp.transpose(jnp.concatenate([wave_ref[...], jnp.zeros((5, waves), F32)], 0))
+    out_ref[:, 0:width] = coeff_ref[...]
     cos_part = coeff_ref[0:waves].astype(F32)
     sin_part = coeff_ref[waves:].astype(F32)
     squared = None
     for a in range(3):
         scale = wave[:, a : a + 1]
-        where = slice(a * width, (a + 1) * width)
+        where = slice((a + 1) * width, (a + 2) * width)
         out_ref[0:waves, where] = (scale * sin_part).astype(BF16)
         out_ref[waves:, where] = (-scale * cos_part).astype(BF16)
         squared = scale * scale if a == 0 else squared + scale * scale
-    where = slice(3 * width, 4 * width)
+    where = slice(4 * width, 5 * width)
     out_ref[0:waves, where] = (-squared * cos_part).astype(BF16)
     out_ref[waves:, where] = (-squared * sin_part).astype(BF16)
 
@@ -190,11 +231,11 @@
 
 
 def evaluate_kernel(
-    count, points_ref, wave_ref, coeff_ref, table_ref, after_ref, out_ref, diff, new
+    count, points_ref, wave_ref, table_ref, after_ref, out_ref, diff, new
 ):
     walkers = points_ref.shape[0]
     waves = wave_ref.shape[1]
-    width = coeff_ref.shape[1]
+    width = table_ref.shape[1] // 5
     step = math.gcd(waves, LANES)
 
     def one(w, carry):
@@ -222,8 +263,8 @@
         return carry
 
     lax.fori_loop(0, walkers, one, 0)
-    change = dot(diff[...], coeff_ref[...]).astype(BF16)
-    rest = dot(new[...], table_ref[...]).astype(BF16)
+    change = dot(diff[...], table_ref[:, 0:width]).astype(BF16)
+    rest = dot(new[...], table_ref[:, width:]).astype(BF16)
     for w in range(walkers):
         at = w * 3 * count
         out_ref[w, 0 : 2 * count] = change[at : at + 2 * count]
@@ -262,7 +303,7 @@
 def solve_kernel(count, others, role_ref, vals_ref, own_ref, *refs):
     received = refs[:others]
     weight_ref, after_ref = refs[others : others + 2]
-    change_ref, cols_ref, inv_ref, first_ref, second_ref, out_weight_ref, vals = refs[others + 2 :]
+    change_ref, cols_ref, inv_ref, drift_ref, lap_ref, out_weight_ref, vals = refs[others + 2 :]
     pieces, _, width = vals_ref.shape
     for o in range(pieces):
         vals[:, o * width : (o + 1) * width] = vals_ref[o]
@@ -285,13 +326,16 @@
         ratios.append(ratio)
         normal.append(dot(ratio, ratio, ((1,), (1,)), exact=True))
     inverses, logs = sweep(normal)
-    for inverse, ratio, product, sums_ref in zip(inverses, ratios, products, (first_ref, second_ref)):
+    for update, (inverse, ratio, product) in enumerate(zip(inverses, ratios, products)):
         size = ratio.shape[0]
         wide = product.shape[1]
         small = dot(inverse, ratio, exact=True)
         tile = jnp.where(iota((size, wide), 0) == size - count + iota((size, wide), 1) % count, 1.0, 0.0)
         spread = dot(small, tile, exact=True)
-        sums_ref[...] = jnp.sum(product * spread, axis=0, keepdims=True)
+        sums = jnp.sum(product * spread, axis=0, keepdims=True)
+        for a in range(3):
+            drift_ref[3 * update + a] = sums[:, a * count : (a + 1) * count]
+        lap_ref[update] = sums[:, 3 * count : 4 * count]
     inv_ref[...] = small
     out_weight_ref[...] = weight_ref[...] + 0.5 * logs[1]
 
@@ -358,37 +402,52 @@
             shape((2, LANES), jnp.int32),
             shape((2, 8, LANES), F32),
         ),
-        [VM, VM, VM, SM],
+        [HBM, HBM, HBM, HBM],
         (VM, VM, VM),
-    )(positions, moved, displacements, log_weight)
+        scratch=[
+            pltpu.VMEM((3, 1, electrons), F32),
+            pltpu.VMEM((2, 1, count), jnp.int32),
+            pltpu.VMEM((6, 1, count), F32),
+            pltpu.SMEM((1,), F32),
+            pltpu.SemaphoreType.DMA((4,)),
+        ],
+    )(
+        positions.reshape(3, 1, electrons), moved, displacements.reshape(6, 1, count), log_weight
+    )
     records = [lax.ppermute(record, "grp", pairs(n_grp, s)) for s in range(1, n_grp)]
 
     depth = electrons // chunks
-    own = [None] * chunks
-    after = record
-    for wanted in ((0, chunks - 1), tuple(range(1, chunks - 1))):
-        some = call(
-            functools.partial(round_kernel, wanted),
-            tuple(shape((depth, electrons), BF16) for _ in wanted),
-            [ANY, ANY],
-            tuple(VM for _ in wanted),
+    kept = shape((depth, electrons), BF16)
+    token = shape((8, LANES), F32)
+    own = list(
+        call(
+            round_kernel,
+            (kept,) * chunks,
+            [HBM, ANY],
+            (VM,) * chunks,
             scratch=[
-                pltpu.VMEM((len(wanted), depth, electrons), F32),
-                pltpu.SemaphoreType.DMA((len(wanted),)),
+                pltpu.VMEM((chunks, depth, electrons), F32),
+                pltpu.SemaphoreType.DMA((chunks,)),
             ],
-            moved=6 * len(wanted) * depth * electrons,
-            vmem=6,
-        )(inverse, after)
-        for chunk, block in zip(wanted, some):
-            own[chunk] = block
-        after = some[0]
+            moved=6 * electrons * electrons,
+            vmem=8,
+        )(inverse, record)
+    )
+    own[0], own[-1], token_0 = call(
+        gate_kernel,
+        (kept, kept, token),
+        [ANY] * (2 + others),
+        (ANY, ANY, VM),
+        aliases={0: 0, 1: 1},
+        vmem=1,
+    )(own[0], own[-1], *records)
 
     points, weight = call(
         functools.partial(points_kernel, count, others),
         (shape((n_orb, 8, LANES), F32), shape((1, LANES), F32)),
-        [SM] + [VM] * (others + 3),
+        [SM] + [VM] * (others + 3) + [ANY],
         (VM, VM),
-    )(role, record, *records, tiled, disp)
+    )(role, record, *records, tiled, disp, token_0)
     points = lax.all_to_all(points, "orb", split_axis=0, concat_axis=0, tiled=True)
 
     steps = [0] + [backward(n_grp, s) for s in range(1, n_grp)]
@@ -407,7 +466,7 @@
     coeff = jnp.pad(coefficients, ((0, 0), (0, width - local))) if width > local else coefficients
     derived = call(
         table_kernel,
-        shape((plane, 4 * width), BF16),
+        shape((plane, 5 * width), BF16),
         [VM, VM],
         VM,
         flops=8 * plane * width,
@@ -422,21 +481,21 @@
         send_y = lambda block: lax.ppermute(block, "grp", pairs(n_grp, 2))
 
         def relay(mine, got, first):
-            kept = shape((depth, electrons), BF16)
             return call(
                 relay_kernel,
-                (kept, kept, shape((8, LANES), F32)),
-                [SM, VM, VM, VM, VM] + [ANY] * len(first),
-                (VM, VM, VM),
-                moved=4 * depth * electrons,
-                vmem=4,
+                (kept, kept, token),
+                [SM] + [ANY] * (4 + len(first)),
+                (ANY, ANY, VM),
+                scratch=[pltpu.SemaphoreType.DMA((2,))],
+                aliases={3: 0, 4: 1},
+                vmem=1,
             )(apart, *mine, *got, *first)
 
         x1, y1 = send_x(own[0]), send_y(own[3])
-        relay_x, relay_y, token_1 = relay((own[1], own[2]), (y1, x1), (derived, columns[0]))
-        x2, y2 = send_x(relay_x), send_y(relay_y)
-        relay_x, relay_y, token_2 = relay((own[2], own[1]), (y2, x2), ())
-        x3, y3 = send_x(relay_x), send_y(relay_y)
+        y1, x1, token_1 = relay((own[1], own[2]), (y1, x1), (derived, columns[0], weight))
+        x2, y2 = send_x(y1), send_y(x1)
+        y2, x2, token_2 = relay((own[2], own[1]), (y2, x2), sent)
+        x3, y3 = send_x(y2), send_y(x2)
         arrays += [x1, x2, x3, y1, y2, y3]
         a1, a2, a3, b1, b2, b3 = range(chunks, chunks + 6)
         table = [range(chunks), (a1, a2, a3, b3), (a3, b3, b2, b1), (b2, b3, a3, a2)]
@@ -455,7 +514,6 @@
         in_specs=[
             pl.BlockSpec((block, 8, LANES), lambda i: (i, 0, 0)),
             pl.BlockSpec(wavevectors.shape, lambda i: (0, 0)),
-            pl.BlockSpec(coeff.shape, lambda i: (0, 0)),
             pl.BlockSpec(derived.shape, lambda i: (0, 0)),
             ANY,
         ],
@@ -470,20 +528,20 @@
             bytes_accessed=12 * plane * width,
             transcendentals=0,
         ),
-    )(points, wavevectors, coeff, derived, token_1)
+    )(points, wavevectors, derived, token_1)
     values = values[:, :, :local]
     values = lax.all_to_all(values, "orb", split_axis=0, concat_axis=0, tiled=True)
     if width > local:
         values = values.transpose(1, 0, 2).reshape(1, 11 * count, electrons)
 
-    change, cols, small, first, second, new_weight = call(
+    change, cols, small, drift, laplacian, new_weight = call(
         functools.partial(solve_kernel, count, others),
         (
             shape((2 * count, electrons), BF16),
             shape((2 * count, electrons), BF16),
             shape((2 * count, 2 * count), F32),
-            shape((1, 4 * count), F32),
-            shape((1, 4 * count), F32),
+            shape((6, 1, count), F32),
+            shape((2, 1, count), F32),
             shape((1, LANES), F32),
         ),
         [SM] + [VM] * (others + 3) + [ANY],
@@ -509,8 +567,7 @@
         vmem=12,
     )(role, change, cols, small, *arrays)
 
-    both = jnp.concatenate([first, second]).reshape(2, 1, 4, count)
-    return updated[None], both[:, :, :3], both[:, :, 3], new_weight[0, :1]
+    return updated[None], drift.reshape(2, 1, 3, count), laplacian, new_weight[0, :1]
 
 
 def solution(mesh):

time: 88.5 us -> 75.9 us (0.86)
  blocking collectives: 0 us -> 10.4 us
  starting transfers between devices: 26.6 us -> 16.5 us
  Pallas kernels: 27.3 us -> 20.4 us
  waiting for transfers between devices: 20.8 us -> 15.8 us
  local copies, waits for them, and re-layouts: 10.4 us -> 9.48 us
    all_to_all x0 -> x1, blocking collectives: none -> 10.4 us  [per_device(): lax.all_to_all(points, 'orb', split_axis=0, concat_axis=0, tiled=True)]
    ppermute x3, waiting for transfers between devices: 8.51 us -> 1.04 us  [per_device(): lax.ppermute(record, 'grp', pairs(n_grp, s))]
    ppermute x3, waiting for transfers between devices: 12 us -> 4.76 us  [per_device(): lax.ppermute(columns[s], 'grp', pairs(n_grp, s))]
    ppermute x3, waiting for transfers between devices: 0.01 us -> 5.87 us  [per_device(): send_y = lambda block: lax.ppermute(block, 'grp', pairs(n_grp, 2))]
    all_to_all x1 -> x0, starting transfers between devices: 5.02 us -> none  [per_device(): lax.all_to_all(points, 'orb', split_axis=0, concat_axis=0, tiled=True)]
    pallas_call x5, Pallas kernels: 7.47 us -> 3 us  [the longest x1 1.52 us: per_device(): call(table_kernel, shape((plane, 5 * width), BF16), [VM, VM], VM, flops=8...]
    ppermute x3, starting transfers between devices: 5.06 us -> 2.02 us  [per_device(): send_y = lambda block: lax.ppermute(block, 'grp', pairs(n_grp, 2))]
    all_to_all x1, waiting for transfers between devices: 0.01 us -> 2.09 us  [per_device(): lax.all_to_all(values, 'orb', split_axis=0, concat_axis=0, tiled=True)]
  transfers between devices with their start and end apart: 14 -> 13, of which waited for: 5 -> 10; matrix products, arithmetic and copies ran while one was open for 1% -> 0% of each run, Pallas kernels for 24% -> 20%
where the time goes in v3:
time: 75.9 us; the launch traced here: 75.3 us
  Pallas kernels  20.4 us (27%)
  starting transfers between devices  16.5 us (22%)
  waiting for transfers between devices  15.8 us (21%)
  blocking collectives  10.4 us (14%)
  local copies, waits for them, and re-layouts  9.48 us (12%)
  between operations  2.78 us (4%)
    all_to_all x1, blocking collectives, per_device(): lax.all_to_all(points, 'orb', split_axis=0, concat_axis=0, tiled=True)  10.4 us
    unnamed x38, local copies, waits for them, and re-layouts  9.48 us
    pallas_call x1, Pallas kernels, per_device(): pl.pallas_call(functools.partial(evaluate_kernel, count), grid=(n_orb //...  6.41 us
    ppermute x3, waiting for transfers between devices, per_device(): send_y = lambda block: lax.ppermute(block, 'grp', pairs(n_grp, 2))  5.87 us
    pallas_call x1, Pallas kernels, per_device(): call(functools.partial(solve_kernel, count, others), (shape((2 * count, e...  5.66 us
    ppermute x3, waiting for transfers between devices, per_device(): lax.ppermute(columns[s], 'grp', pairs(n_grp, s))  4.76 us
    ppermute x3, starting transfers between devices, per_device(): lax.ppermute(record, 'grp', pairs(n_grp, s))  4.6 us
    ppermute x3, starting transfers between devices, per_device(): lax.ppermute(columns[s], 'grp', pairs(n_grp, s))  3.55 us
  transfers between devices with their start and end apart: 13, of which 10 were waited for; matrix products, arithmetic and copies ran while one was open for 0% of the time, Pallas kernels for 20%

profile of v3, /device:TPU:0, one launch (start us, length us, event | category | flops | bytes accessed | tf_op | source)
XLA Modules:
  0.0 75.3 jit_solution(6997545860452757373)
XLA Ops:
  1.3 0.7 copy-done.13
  2.0 0.7 copy-done.14
  2.7 0.7 copy-done.15
  3.4 1.1 %shard_map.120 = (f32[8,1024]{1,0:T(8,128)S(1)}, s32[2,128]{1,0:T(2,128)S(1)}, f32[2,8,128]{2,1,0:T(8,128)S(1)}) custom-call(f32[3,1,1024]{2,1,0:T(1,128)S(1)} %bitcast.11, s32[2,1,16]{2,1,0:T(1,128)S(1)} %copy-done.15, f32[6,1,16]{2,1,0:T(1,128)S(1)} %bitcast.12, f32[1]{0:T(128)S(6)} %copy.27.weight_hbm), custom_call_target="tpu_custom_call" | custom-call | tf_op jit(solution)/shard_map/pallas_call | solution.py:398
  4.4 4.0 %collective-permute-start.2 = (f32[8,1024]{1,0:T(8,128)S(1)}, f32[8,1024]{1,0:T(8,128)S(1)}, u32[]{:S(2)}, u32[]{:S(2)}) collective-permute-start(f32[8,1024]{1,0:T(8,128)S(1)} %get-tuple-element.32.after_ref.refs_0_), channel_id=1, source_target_pairs={{0,24},{8,16},{16,8},{24,0},{1,25},{9,17},{17,9},{25,1},{2,26},{10... | collective-permute-start | bytes 98312 | tf_op jit(solution)/shard_map/ppermute | solution.py:417
  8.4 0.5 collective-permute-start.1
  8.9 0.1 collective-permute-start
  9.1 2.2 %copy-done = f32[1,1024,1024]{2,1,0:T(8,128)S(1)} copy-done((f32[1,1024,1024]{2,1,0:T(8,128)S(1)}, f32[1,1024,1024]{2,1,0:T(8,128)}, u32[]{:S(2)}) %copy-start) | copy-done | bytes 4194328
  11.2 0.5 shard_map.121
  11.8 0.0 collective-permute-done.2.refs_4_.refs_3_.refs_7_
  11.8 0.5 collective-permute-done.1.refs_3_.refs_2_.refs_6_
  12.3 0.5 collective-permute-done.refs_2_.refs_1_.refs_5_
  12.8 1.5 %collective-permute-start.3 = (bf16[256,1024]{1,0:T(8,128)(2,1)S(1)}, bf16[256,1024]{1,0:T(8,128)(2,1)S(1)}, u32[]{:S(2)}, u32[]{:S(2)}) collective-permute-start(bf16[256,1024]{1,0:T(8,128)(2,1)S(1)} %get-tuple-element.41.refs_3_), channel_id=1, source_target_pairs={{0,16},{8,24},{16,0},{24,8},{1,17},{9,25},{17,1},{25,9},{2,18},{10... | collective-permute-start | bytes 1572872 | tf_op jit(solution)/shard_map/ppermute | solution.py:481
  14.3 0.9 %collective-permute-start.4 = (bf16[256,1024]{1,0:T(8,128)(2,1)S(1)}, bf16[256,1024]{1,0:T(8,128)(2,1)}, u32[]{:S(2)}, u32[]{:S(2)}) collective-permute-start(bf16[256,1024]{1,0:T(8,128)(2,1)S(1)} %get-tuple-element.42.refs_0_), channel_id=1, source_target_pairs={{0,8},{8,0},{16,24},{24,16},{1,9},{9,1},{17,25},{25,17},{2,10},{10... | collective-permute-start | bytes 1572872 | tf_op jit(solution)/shard_map/ppermute | solution.py:480
  16.6 1.5 %shard_map.124.refs_0_.table_ref = bf16[2048,640]{1,0:T(8,128)(2,1)S(1)} custom-call(bf16[2048,128]{1,0:T(8,128)(2,1)S(1)} %copy-done.3, f32[3,1024]{1,0:T(4,128)S(1)} %copy-done.12), custom_call_target="tpu_custom_call" | custom-call | flops 2097152 | bytes 2621440 | tf_op jit(solution)/shard_map/pallas_call | solution.py:467
  18.1 0.4 shard_map.123
  18.5 0.8 %shard_map.125 = (bf16[32,1024]{1,0:T(8,128)(2,1)S(1)}, bf16[32,1024]{1,0:T(8,128)(2,1)S(1)}, bf16[32,1024]{1,0:T(8,128)(2,1)S(1)}, bf16[32,1024]{1,0:T(8,128)(2,1)S(1)}) custom-call(bf16[256,1024]{1,0:T(8,128)(2,1)S(1)} %get-tuple-element.42.refs_0_, bf16[256,1024]{1,0:T(8,128)(2,1)S(1)} %get-tuple-element.39.refs_1_.own_a.own_b, ...), custom_call_target="tpu_custom_call" | custom-call | flops 268435456 | bytes 2097152 | tf_op jit(solution)/shard_map/pallas_call | solution.py:454
  19.3 5.7 %collective-permute-done.3.got_a = bf16[256,1024]{1,0:T(8,128)(2,1)S(1)} collective-permute-done((bf16[256,1024]{1,0:T(8,128)(2,1)S(1)}, bf16[256,1024]{1,0:T(8,128)(2,1)S(1)}, u32[]{:S(2)}, u32[]{:S(2)}) %collective-permute-start.3) | collective-permute-done | bytes 524320 | tf_op jit(solution)/shard_map/ppermute | solution.py:481
  25.0 1.5 %collective-permute-done.4.got_b = bf16[256,1024]{1,0:T(8,128)(2,1)} collective-permute-done((bf16[256,1024]{1,0:T(8,128)(2,1)S(1)}, bf16[256,1024]{1,0:T(8,128)(2,1)}, u32[]{:S(2)}, u32[]{:S(2)}) %collective-permute-start.4) | collective-permute-done | bytes 524320 | tf_op jit(solution)/shard_map/ppermute | solution.py:480
  26.5 0.8 %shard_map.126 = (bf16[256,1024]{1,0:T(8,128)(2,1)S(1)}, bf16[256,1024]{1,0:T(8,128)(2,1)}, f32[8,128]{1,0:T(8,128)S(1)}) custom-call(s32[1]{0:T(128)} %bitcast.5.flag_ref, bf16[256,1024]{1,0:T(8,128)(2,1)S(1)} %get-tuple-element.39.refs_1_.own_a.own_b, ...), custom_call_target="tpu_custom_call", output_to_operand_aliasing={{0}: (3, {}), {1}: (4, {})} | custom-call | tf_op jit(solution)/shard_map/pallas_call | solution.py:484
  27.3 0.0 copy-start.1
  27.3 0.8 %copy-done.1 = bf16[256,1024]{1,0:T(8,128)(2,1)} copy-done((bf16[256,1024]{1,0:T(8,128)(2,1)}, bf16[256,1024]{1,0:T(8,128)(2,1)S(1)}, u32[]{:S(2)}) %copy-start.1) | copy-done | bytes 524312
  28.1 1.2 %collective-permute-start.9 = (bf16[256,1024]{1,0:T(8,128)(2,1)}, bf16[256,1024]{1,0:T(8,128)(2,1)S(1)}, u32[]{:S(2)}, u32[]{:S(2)}) collective-permute-start(bf16[256,1024]{1,0:T(8,128)(2,1)} %copy-done.1), channel_id=1, source_target_pairs={{0,8},{8,0},{16,24},{24,16},{1,9},{9,1},{17,25},{25,17},{2,10},{10... | collective-permute-start | bytes 1572872 | tf_op jit(solution)/shard_map/ppermute | solution.py:480
  29.4 10.4 %all_to_all.10.points_ref = f32[8,8,128]{2,1,0:T(8,128)S(1)} all-to-all(f32[8,8,128]{2,1,0:T(8,128)S(1)} %get-tuple-element.38), channel_id=1, replica_groups=mesh['grp'=4,'orb'=8] {'orb'}, dimensions={0} | all-to-all | bytes 65536 | tf_op jit(solution)/shard_map/all_to_all | solution.py:451
  39.8 6.4 %shard_map.127 = bf16[8,176,128]{2,1,0:T(8,128)(2,1)} custom-call(f32[8,8,128]{2,1,0:T(8,128)S(1)} %all_to_all.10.points_ref, f32[3,1024]{1,0:T(4,128)S(1)} %copy-done.12, bf16[2048,640]{1,0:T(8,128)(2,1)S(1)} %shard_map.124.refs_0_.table_ref, f32[8,128]{1,0:T(8,128)S(1)} %get-tuple-element.45.after_ref), custom_call_target="tpu_custom_call" | custom-call | flops 738197504 | bytes 3145728 | tf_op jit(solution)/shard_map/pallas_call | solution.py:510
  46.2 3.4 %all-to-all-start.1 = ((bf16[8,176,128]{2,1,0:T(8,128)(2,1)}), bf16[8,176,128]{2,1,0:T(8,128)(2,1)S(1)}, u32[]{:S(2)}, u32[]{:S(2)}) async-start(bf16[8,176,128]{2,1,0:T(8,128)(2,1)} %shard_map.127), calls=%async_computation.1 | async-start | bytes 720896 | tf_op jit(solution)/shard_map/all_to_all | solution.py:533
  49.6 0.9 %collective-permute-start.5 = (bf16[32,1024]{1,0:T(8,128)(2,1)}, bf16[32,1024]{1,0:T(8,128)(2,1)S(1)}, u32[]{:S(2)}, u32[]{:S(2)}) collective-permute-start(bf16[32,1024]{1,0:T(8,128)(2,1)} %copy-done.18), channel_id=1, source_target_pairs={{0,8},{8,0},{16,24},{24,16},{1,9},{9,1},{17,25},{25,17},{2,10},{10... | collective-permute-start | bytes 196616 | tf_op jit(solution)/shard_map/ppermute | solution.py:463
  50.6 2.0 %collective-permute-start.6 = (bf16[32,1024]{1,0:T(8,128)(2,1)}, bf16[32,1024]{1,0:T(8,128)(2,1)S(1)}, u32[]{:S(2)}, u32[]{:S(2)}) collective-permute-start(bf16[32,1024]{1,0:T(8,128)(2,1)} %copy-done.17), channel_id=1, source_target_pairs={{0,16},{8,24},{16,0},{24,8},{1,17},{9,25},{17,1},{25,9},{2,18},{10... | collective-permute-start | bytes 196616 | tf_op jit(solution)/shard_map/ppermute | solution.py:463
  52.6 0.6 collective-permute-start.7
  53.2 1.1 %collective-permute-done.5.refs_0_ = bf16[32,1024]{1,0:T(8,128)(2,1)S(1)} collective-permute-done((bf16[32,1024]{1,0:T(8,128)(2,1)}, bf16[32,1024]{1,0:T(8,128)(2,1)S(1)}, u32[]{:S(2)}, u32[]{:S(2)}) %collective-permute-start.5) | collective-permute-done | bytes 65568 | tf_op jit(solution)/shard_map/ppermute | solution.py:463
  54.2 1.9 %collective-permute-done.6.refs_1_ = bf16[32,1024]{1,0:T(8,128)(2,1)S(1)} collective-permute-done((bf16[32,1024]{1,0:T(8,128)(2,1)}, bf16[32,1024]{1,0:T(8,128)(2,1)S(1)}, u32[]{:S(2)}, u32[]{:S(2)}) %collective-permute-start.6) | collective-permute-done | bytes 65568 | tf_op jit(solution)/shard_map/ppermute | solution.py:463
  56.1 1.8 %collective-permute-done.7.refs_2_ = bf16[32,1024]{1,0:T(8,128)(2,1)S(1)} collective-permute-done((bf16[32,1024]{1,0:T(8,128)(2,1)}, bf16[32,1024]{1,0:T(8,128)(2,1)S(1)}, u32[]{:S(2)}, u32[]{:S(2)}) %collective-permute-start.7) | collective-permute-done | bytes 65568 | tf_op jit(solution)/shard_map/ppermute | solution.py:463
  57.9 0.0 collective-permute-done.8.got_a
  57.9 0.0 collective-permute-done.9.got_b
  57.9 0.1 shard_map.128
  58.1 0.5 collective-permute-start.11
  58.6 0.0 copy-done.8
  58.6 0.7 collective-permute-start.10
  59.3 2.1 %all-to-all-done.1.vals_ref = bf16[8,176,128]{2,1,0:T(8,128)(2,1)S(1)} async-done(((bf16[8,176,128]{2,1,0:T(8,128)(2,1)}), bf16[8,176,128]{2,1,0:T(8,128)(2,1)S(1)}, u32[]{:S(2)}, u32[]{:S(2)}) %all-to-all-start.1) | async-done | bytes 360480 | tf_op jit(solution)/shard_map/all_to_all | solution.py:533
  61.4 0.8 %copy-done.5 = bf16[32,1024]{1,0:T(8,128)(2,1)S(1)} copy-done((bf16[32,1024]{1,0:T(8,128)(2,1)S(1)}, bf16[32,1024]{1,0:T(8,128)(2,1)}, u32[]{:S(2)}) %copy-start.5) | copy-done | bytes 65560
  62.2 0.8 %copy-done.7 = bf16[32,1024]{1,0:T(8,128)(2,1)S(1)} copy-done((bf16[32,1024]{1,0:T(8,128)(2,1)S(1)}, bf16[32,1024]{1,0:T(8,128)(2,1)}, u32[]{:S(2)}) %copy-start.7) | copy-done | bytes 65560
  63.1 0.8 %copy-done.9 = bf16[32,1024]{1,0:T(8,128)(2,1)S(1)} copy-done((bf16[32,1024]{1,0:T(8,128)(2,1)S(1)}, bf16[32,1024]{1,0:T(8,128)(2,1)}, u32[]{:S(2)}) %copy-start.9) | copy-done | bytes 65560
  63.9 0.8 %copy-done.11 = bf16[32,1024]{1,0:T(8,128)(2,1)S(1)} copy-done((bf16[32,1024]{1,0:T(8,128)(2,1)S(1)}, bf16[32,1024]{1,0:T(8,128)(2,1)}, u32[]{:S(2)}) %copy-start.11) | copy-done | bytes 65560
  64.7 5.7 %shard_map.129 = (bf16[32,1024]{1,0:T(8,128)(2,1)S(1)}, bf16[32,1024]{1,0:T(8,128)(2,1)S(1)}, f32[32,32]{1,0:T(8,128)S(1)}, f32[6,1,16]{2,1,0:T(1,128)}, f32[2,1,16]{2,1,0:T(1,128)}, /*index=5*/f32[1,128]{1,0:T(1,128)}) custom-call(s32[1]{0:T(128)} %bitcast.2.role_ref, bf16[8,176,128]{2,1,0:T(8,128)(2,1)S(1)} %all-to-all-done.1.vals_ref, ...), custom_call_target="tpu_custom_call" | custom-call | flops 8388608 | bytes 720896 | tf_op jit(solution)/shard_map/pallas_call | solution.py:537
  70.4 0.2 collective-permute-done.11.refs_9_
  70.6 0.5 collective-permute-done.10.refs_6_
  71.1 1.0 %copy-done.2 = bf16[256,1024]{1,0:T(8,128)(2,1)S(1)} copy-done((bf16[256,1024]{1,0:T(8,128)(2,1)S(1)}, bf16[256,1024]{1,0:T(8,128)(2,1)}, u32[]{:S(2)}) %copy-start.2) | copy-done | bytes 524312
  72.2 3.2 %shard_map.130 = f32[1024,1024]{1,0:T(8,128)} custom-call(s32[1]{0:T(128)} %bitcast.2.role_ref, bf16[32,1024]{1,0:T(8,128)(2,1)S(1)} %get-tuple-element.52.change_ref, bf16[32,1024]{1,0:T(8,128)(2,1)S(1)} %get-tuple-element.53.cols_ref, f32[32,32]{1,0:T(8,128)S(1)} %get-tuple-element.54.inv_ref, bf16[256,1024]{1,0:T(8,128)(2,1)S(1)} %get-tuple-element.42.refs_0_, ...), custom_call_target="tpu_custom_call" | custom-call | flops 134217728 | bytes 6291456 | tf_op jit(solution)/shard_map/pallas_call | solution.py:554
  (28 shorter events, 0.1 us)
Async XLA Ops:
  0.6 16.0 %copy-start.12 = (f32[3,1024]{1,0:T(4,128)S(1)}, f32[3,1024]{1,0:T(4,128)}, u32[]{:S(2)}) copy-start(f32[3,1024]{1,0:T(4,128)} %wave_ref.3) | copy-start | bytes 36868
  1.3 0.7 copy-start.13
  2.0 0.7 copy-start.14
  2.7 0.7 copy-start.15
  4.4 7.3 %collective-permute-start.2 = (f32[8,1024]{1,0:T(8,128)S(1)}, f32[8,1024]{1,0:T(8,128)S(1)}, u32[]{:S(2)}, u32[]{:S(2)}) collective-permute-start(f32[8,1024]{1,0:T(8,128)S(1)} %get-tuple-element.32.after_ref.refs_0_), channel_id=1, source_target_pairs={{0,24},{8,16},{16,8},{24,0},{1,25},{9,17},{17,9},{25,1},{2,26},{10... | collective-permute-start | bytes 98312 | tf_op jit(solution)/shard_map/ppermute | solution.py:417
  8.4 3.9 %collective-permute-start.1 = (f32[8,1024]{1,0:T(8,128)S(1)}, f32[8,1024]{1,0:T(8,128)S(1)}, u32[]{:S(2)}, u32[]{:S(2)}) collective-permute-start(f32[8,1024]{1,0:T(8,128)S(1)} %get-tuple-element.32.after_ref.refs_0_), channel_id=1, source_target_pairs={{0,16},{8,24},{16,0},{24,8},{1,17},{9,25},{17,1},{25,9},{2,18},{10... | collective-permute-start | bytes 98312 | tf_op jit(solution)/shard_map/ppermute | solution.py:417
  8.9 3.9 %collective-permute-start = (f32[8,1024]{1,0:T(8,128)S(1)}, f32[8,1024]{1,0:T(8,128)S(1)}, u32[]{:S(2)}, u32[]{:S(2)}) collective-permute-start(f32[8,1024]{1,0:T(8,128)S(1)} %get-tuple-element.32.after_ref.refs_0_), channel_id=1, source_target_pairs={{0,8},{8,0},{16,24},{24,16},{1,9},{9,1},{17,25},{25,17},{2,10},{10... | collective-permute-start | bytes 98312 | tf_op jit(solution)/shard_map/ppermute | solution.py:417
  9.0 2.2 %copy-start = (f32[1,1024,1024]{2,1,0:T(8,128)S(1)}, f32[1,1024,1024]{2,1,0:T(8,128)}, u32[]{:S(2)}) copy-start(f32[1,1024,1024]{2,1,0:T(8,128)} %inverse_ref.1) | copy-start | bytes 12582916
  11.2 5.4 %copy-start.3 = (bf16[2048,128]{1,0:T(8,128)(2,1)S(1)}, bf16[2048,128]{1,0:T(8,128)(2,1)}, u32[]{:S(2)}) copy-start(bf16[2048,128]{1,0:T(8,128)(2,1)} %coeff_ref.1) | copy-start | bytes 1572868
  12.8 12.2 %collective-permute-start.3 = (bf16[256,1024]{1,0:T(8,128)(2,1)S(1)}, bf16[256,1024]{1,0:T(8,128)(2,1)S(1)}, u32[]{:S(2)}, u32[]{:S(2)}) collective-permute-start(bf16[256,1024]{1,0:T(8,128)(2,1)S(1)} %get-tuple-element.41.refs_3_), channel_id=1, source_target_pairs={{0,16},{8,24},{16,0},{24,8},{1,17},{9,25},{17,1},{25,9},{2,18},{10... | collective-permute-start | bytes 1572872 | tf_op jit(solution)/shard_map/ppermute | solution.py:481
  14.3 12.1 %collective-permute-start.4 = (bf16[256,1024]{1,0:T(8,128)(2,1)S(1)}, bf16[256,1024]{1,0:T(8,128)(2,1)}, u32[]{:S(2)}, u32[]{:S(2)}) collective-permute-start(bf16[256,1024]{1,0:T(8,128)(2,1)S(1)} %get-tuple-element.42.refs_0_), channel_id=1, source_target_pairs={{0,8},{8,0},{16,24},{24,16},{1,9},{9,1},{17,25},{25,17},{2,10},{10... | collective-permute-start | bytes 1572872 | tf_op jit(solution)/shard_map/ppermute | solution.py:480
  19.3 8.8 %copy-start.10 = (bf16[32,1024]{1,0:T(8,128)(2,1)}, bf16[32,1024]{1,0:T(8,128)(2,1)S(1)}, u32[]{:S(2)}) copy-start(bf16[32,1024]{1,0:T(8,128)(2,1)S(1)} %get-tuple-element.43.refs_1_.own_ref) | copy-start | bytes 196612
  19.3 8.8 %copy-start.16 = (bf16[32,1024]{1,0:T(8,128)(2,1)}, bf16[32,1024]{1,0:T(8,128)(2,1)S(1)}, u32[]{:S(2)}) copy-start(bf16[32,1024]{1,0:T(8,128)(2,1)S(1)} %get-tuple-element.48) | copy-start | bytes 196612
  19.3 8.8 %copy-start.17 = (bf16[32,1024]{1,0:T(8,128)(2,1)}, bf16[32,1024]{1,0:T(8,128)(2,1)S(1)}, u32[]{:S(2)}) copy-start(bf16[32,1024]{1,0:T(8,128)(2,1)S(1)} %get-tuple-element.47) | copy-start | bytes 196612
  19.3 8.8 %copy-start.18 = (bf16[32,1024]{1,0:T(8,128)(2,1)}, bf16[32,1024]{1,0:T(8,128)(2,1)S(1)}, u32[]{:S(2)}) copy-start(bf16[32,1024]{1,0:T(8,128)(2,1)S(1)} %get-tuple-element.46) | copy-start | bytes 196612
  27.3 0.8 %copy-start.1 = (bf16[256,1024]{1,0:T(8,128)(2,1)}, bf16[256,1024]{1,0:T(8,128)(2,1)S(1)}, u32[]{:S(2)}) copy-start(bf16[256,1024]{1,0:T(8,128)(2,1)S(1)} %get-tuple-element.50.refs_7_) | copy-start | bytes 1572868
  28.1 29.8 %collective-permute-start.8 = (bf16[256,1024]{1,0:T(8,128)(2,1)}, bf16[256,1024]{1,0:T(8,128)(2,1)S(1)}, u32[]{:S(2)}, u32[]{:S(2)}) collective-permute-start(bf16[256,1024]{1,0:T(8,128)(2,1)} %get-tuple-element.49.refs_4_), channel_id=1, source_target_pairs={{0,16},{8,24},{16,0},{24,8},{1,17},{9,25},{17,1},{25,9},{2,18},{10... | collective-permute-start | bytes 1572872 | tf_op jit(solution)/shard_map/ppermute | solution.py:481
  28.1 29.8 %collective-permute-start.9 = (bf16[256,1024]{1,0:T(8,128)(2,1)}, bf16[256,1024]{1,0:T(8,128)(2,1)S(1)}, u32[]{:S(2)}, u32[]{:S(2)}) collective-permute-start(bf16[256,1024]{1,0:T(8,128)(2,1)} %copy-done.1), channel_id=1, source_target_pairs={{0,8},{8,0},{16,24},{24,16},{1,9},{9,1},{17,25},{25,17},{2,10},{10... | collective-permute-start | bytes 1572872 | tf_op jit(solution)/shard_map/ppermute | solution.py:480
  46.2 15.2 %all-to-all-start.1 = ((bf16[8,176,128]{2,1,0:T(8,128)(2,1)}), bf16[8,176,128]{2,1,0:T(8,128)(2,1)S(1)}, u32[]{:S(2)}, u32[]{:S(2)}) async-start(bf16[8,176,128]{2,1,0:T(8,128)(2,1)} %shard_map.127), calls=%async_computation.1 | async-start | bytes 720896 | tf_op jit(solution)/shard_map/all_to_all | solution.py:533
  49.6 4.6 %collective-permute-start.5 = (bf16[32,1024]{1,0:T(8,128)(2,1)}, bf16[32,1024]{1,0:T(8,128)(2,1)S(1)}, u32[]{:S(2)}, u32[]{:S(2)}) collective-permute-start(bf16[32,1024]{1,0:T(8,128)(2,1)} %copy-done.18), channel_id=1, source_target_pairs={{0,8},{8,0},{16,24},{24,16},{1,9},{9,1},{17,25},{25,17},{2,10},{10... | collective-permute-start | bytes 196616 | tf_op jit(solution)/shard_map/ppermute | solution.py:463
  50.6 5.5 %collective-permute-start.6 = (bf16[32,1024]{1,0:T(8,128)(2,1)}, bf16[32,1024]{1,0:T(8,128)(2,1)S(1)}, u32[]{:S(2)}, u32[]{:S(2)}) collective-permute-start(bf16[32,1024]{1,0:T(8,128)(2,1)} %copy-done.17), channel_id=1, source_target_pairs={{0,16},{8,24},{16,0},{24,8},{1,17},{9,25},{17,1},{25,9},{2,18},{10... | collective-permute-start | bytes 196616 | tf_op jit(solution)/shard_map/ppermute | solution.py:463
  52.6 5.4 %collective-permute-start.7 = (bf16[32,1024]{1,0:T(8,128)(2,1)}, bf16[32,1024]{1,0:T(8,128)(2,1)S(1)}, u32[]{:S(2)}, u32[]{:S(2)}) collective-permute-start(bf16[32,1024]{1,0:T(8,128)(2,1)} %copy-done.16), channel_id=1, source_target_pairs={{0,24},{8,16},{16,8},{24,0},{1,25},{9,17},{17,9},{25,1},{2,26},{10... | collective-permute-start | bytes 196616 | tf_op jit(solution)/shard_map/ppermute | solution.py:463
  54.2 4.3 %copy-start.4 = (bf16[32,1024]{1,0:T(8,128)(2,1)}, bf16[32,1024]{1,0:T(8,128)(2,1)S(1)}, u32[]{:S(2)}) copy-start(bf16[32,1024]{1,0:T(8,128)(2,1)S(1)} %collective-permute-done.5.refs_0_) | copy-start | bytes 196612
  56.1 2.5 %copy-start.6 = (bf16[32,1024]{1,0:T(8,128)(2,1)}, bf16[32,1024]{1,0:T(8,128)(2,1)S(1)}, u32[]{:S(2)}) copy-start(bf16[32,1024]{1,0:T(8,128)(2,1)S(1)} %collective-permute-done.6.refs_1_) | copy-start | bytes 196612
  57.9 0.6 copy-start.8
  58.1 12.6 %collective-permute-start.11 = (bf16[256,1024]{1,0:T(8,128)(2,1)S(1)}, bf16[256,1024]{1,0:T(8,128)(2,1)}, u32[]{:S(2)}, u32[]{:S(2)}) collective-permute-start(bf16[256,1024]{1,0:T(8,128)(2,1)S(1)} %get-tuple-element.55.refs_5_), channel_id=1, source_target_pairs={{0,16},{8,24},{16,0},{24,8},{1,17},{9,25},{17,1},{25,9},{2,18},{10... | collective-permute-start | bytes 1572872 | tf_op jit(solution)/shard_map/ppermute | solution.py:481
  58.6 12.6 %collective-permute-start.10 = (bf16[256,1024]{1,0:T(8,128)(2,1)S(1)}, bf16[256,1024]{1,0:T(8,128)(2,1)}, u32[]{:S(2)}, u32[]{:S(2)}) collective-permute-start(bf16[256,1024]{1,0:T(8,128)(2,1)S(1)} %get-tuple-element.56.refs_8_), channel_id=1, source_target_pairs={{0,8},{8,0},{16,24},{24,16},{1,9},{9,1},{17,25},{25,17},{2,10},{10... | collective-permute-start | bytes 1572872 | tf_op jit(solution)/shard_map/ppermute | solution.py:480
  61.4 0.8 %copy-start.5 = (bf16[32,1024]{1,0:T(8,128)(2,1)S(1)}, bf16[32,1024]{1,0:T(8,128)(2,1)}, u32[]{:S(2)}) copy-start(bf16[32,1024]{1,0:T(8,128)(2,1)} %copy-done.4) | copy-start | bytes 196612
  62.2 0.8 %copy-start.7 = (bf16[32,1024]{1,0:T(8,128)(2,1)S(1)}, bf16[32,1024]{1,0:T(8,128)(2,1)}, u32[]{:S(2)}) copy-start(bf16[32,1024]{1,0:T(8,128)(2,1)} %copy-done.6) | copy-start | bytes 196612
  63.1 0.8 %copy-start.9 = (bf16[32,1024]{1,0:T(8,128)(2,1)S(1)}, bf16[32,1024]{1,0:T(8,128)(2,1)}, u32[]{:S(2)}) copy-start(bf16[32,1024]{1,0:T(8,128)(2,1)} %copy-done.8) | copy-start | bytes 196612
  63.9 0.8 %copy-start.11 = (bf16[32,1024]{1,0:T(8,128)(2,1)S(1)}, bf16[32,1024]{1,0:T(8,128)(2,1)}, u32[]{:S(2)}) copy-start(bf16[32,1024]{1,0:T(8,128)(2,1)} %copy-done.10) | copy-start | bytes 196612
  71.1 1.0 %copy-start.2 = (bf16[256,1024]{1,0:T(8,128)(2,1)S(1)}, bf16[256,1024]{1,0:T(8,128)(2,1)}, u32[]{:S(2)}) copy-start(bf16[256,1024]{1,0:T(8,128)(2,1)} %copy-done.1) | copy-start | bytes 1572868

commit v4 on v3

--- a/solution.py
+++ b/solution.py
@@ -53,6 +53,10 @@
     return jax.ShapeDtypeStruct(dims, dtype)
 
 
+def in_hbm(*arrays):
+    return tuple(pltpu.with_memory_space_constraint(a, pltpu.HBM) for a in arrays)
+
+
 def is_power(n):
     return n & (n - 1) == 0
 
@@ -76,14 +80,13 @@
     pos_hbm,
     moved_hbm,
     disp_hbm,
-    weight_hbm,
+    weight_ref,
     out_ref,
     tiled_ref,
     shift_ref,
     pos_ref,
     moved_ref,
     disp_ref,
-    weight_ref,
     sems,
 ):
     loads = [
@@ -93,7 +96,6 @@
                 (moved_hbm, moved_ref),
                 (disp_hbm, disp_ref),
                 (pos_hbm, pos_ref),
-                (weight_hbm, weight_ref),
             )
         )
     ]
@@ -120,7 +122,6 @@
     out_ref[...] = pos + dot(first, pick, ((1,), (1,)), exact=True)
     out_ref[3:6, 0:LANES] = points[0:3]
     out_ref[6:7, 0:LANES] = tiled[1:2, :].astype(F32)
-    loads[3].wait()
     out_ref[7:8, 0:LANES] = jnp.full((1, LANES), weight_ref[0], F32)
 
 
@@ -204,7 +205,15 @@
             out[count : 2 * count, rows] = turned[(1 + step) * count : (2 + step) * count]
 
 
-def table_kernel(coeff_ref, wave_ref, out_ref):
+def table_kernel(coeff_hbm, wave_hbm, out_ref, coeff_ref, wave_ref, sems):
+    loads = [
+        pltpu.make_async_copy(wave_hbm, wave_ref, sems.at[0]),
+        pltpu.make_async_copy(coeff_hbm, coeff_ref, sems.at[1]),
+    ]
+    for load in loads:
+        load.start()
+    for load in loads:
+        load.wait()
     waves = wave_ref.shape[1]
     width = coeff_ref.shape[1]
     wave = jnp.transpose(jnp.concatenate([wave_ref[...], jnp.zeros((5, waves), F32)], 0))
@@ -402,17 +411,19 @@
             shape((2, LANES), jnp.int32),
             shape((2, 8, LANES), F32),
         ),
-        [HBM, HBM, HBM, HBM],
+        [HBM, HBM, HBM, SM],
         (VM, VM, VM),
         scratch=[
             pltpu.VMEM((3, 1, electrons), F32),
             pltpu.VMEM((2, 1, count), jnp.int32),
             pltpu.VMEM((6, 1, count), F32),
-            pltpu.SMEM((1,), F32),
-            pltpu.SemaphoreType.DMA((4,)),
+            pltpu.SemaphoreType.DMA((3,)),
         ],
     )(
-        positions.reshape(3, 1, electrons), moved, displacements.reshape(6, 1, count), log_weight
+        *in_hbm(
+            positions.reshape(3, 1, electrons), moved, displacements.reshape(6, 1, count)
+        ),
+        log_weight,
     )
     records = [lax.ppermute(record, "grp", pairs(n_grp, s)) for s in range(1, n_grp)]
 
@@ -431,7 +442,7 @@
             ],
             moved=6 * electrons * electrons,
             vmem=8,
-        )(inverse, record)
+        )(*in_hbm(inverse), record)
     )
     own[0], own[-1], token_0 = call(
         gate_kernel,
@@ -467,12 +478,17 @@
     derived = call(
         table_kernel,
         shape((plane, 5 * width), BF16),
-        [VM, VM],
+        [HBM, HBM],
         VM,
+        scratch=[
+            pltpu.VMEM((plane, width), BF16),
+            pltpu.VMEM(wavevectors.shape, F32),
+            pltpu.SemaphoreType.DMA((2,)),
+        ],
         flops=8 * plane * width,
         moved=10 * plane * width,
         vmem=8,
-    )(coeff, wavevectors)
+    )(*in_hbm(coeff, wavevectors))
 
     apart = apart.astype(jnp.int32).reshape(1)
     arrays = list(own)
@@ -492,9 +508,9 @@
             )(apart, *mine, *got, *first)
 
         x1, y1 = send_x(own[0]), send_y(own[3])
-        y1, x1, token_1 = relay((own[1], own[2]), (y1, x1), (derived, columns[0], weight))
+        y1, x1, token_1 = relay((own[1], own[2]), (y1, x1), (derived, points, *sent))
         x2, y2 = send_x(y1), send_y(x1)
-        y2, x2, token_2 = relay((own[2], own[1]), (y2, x2), sent)
+        y2, x2, token_2 = relay((own[2], own[1]), (y2, x2), ())
         x3, y3 = send_x(y2), send_y(x2)
         arrays += [x1, x2, x3, y1, y2, y3]
         a1, a2, a3, b1, b2, b3 = range(chunks, chunks + 6)

time: 75.9 us -> 70.5 us (0.929); the launches traced: 75.3 us -> 70.9 us
  blocking collectives: 10.4 us -> 0 us
  Pallas kernels: 20.4 us -> 27.4 us
  local copies, waits for them, and re-layouts: 9.48 us -> 3.13 us
  starting transfers between devices: 16.5 us -> 22.5 us
    all_to_all x1 -> x0, blocking collectives: 10.4 us -> none  [per_device(): lax.all_to_all(points, 'orb', split_axis=0, concat_axis=0, tiled=True)]
    unnamed x38 -> x10, local copies, waits for them, and re-layouts: 9.48 us -> 3.13 us
    all_to_all x0 -> x1, starting transfers between devices: none -> 4.88 us  [per_device(): lax.all_to_all(points, 'orb', split_axis=0, concat_axis=0, tiled=True)]
    ppermute x3, waiting for transfers between devices: 4.76 us -> 0.01 us  [per_device(): lax.ppermute(columns[s], 'grp', pairs(n_grp, s))]
    all_to_all x1, waiting for transfers between devices: 2.09 us -> 5.74 us  [per_device(): lax.all_to_all(values, 'orb', split_axis=0, concat_axis=0, tiled=True)]
    all_to_all x0 -> x1, waiting for transfers between devices: none -> 3.1 us  [per_device(): lax.all_to_all(points, 'orb', split_axis=0, concat_axis=0, tiled=True)]
    pallas_call x1, Pallas kernels: 0.53 us -> 3.2 us  [per_device(): call(round_kernel, (kept,) * chunks, [HBM, ANY], (VM,) * chunks, scratch=...]
    ppermute x3, waiting for transfers between devices: 5.87 us -> 3.35 us  [per_device(): send_y = lambda block: lax.ppermute(block, 'grp', pairs(n_grp, 2))]
  transfers between devices with their start and end apart: 13 -> 14, of which waited for: 10 -> 7; matrix products, arithmetic and copies ran while one was open for 0% -> 0% of each run, Pallas kernels for 20% -> 30%
where the time goes in v4:
time: 70.5 us; the launch traced here: 70.9 us
  Pallas kernels  27.4 us (39%)
  starting transfers between devices  22.5 us (32%)
  waiting for transfers between devices  15.2 us (22%)
  local copies, waits for them, and re-layouts  3.13 us (4%)
  between operations  2.69 us (4%)
    pallas_call x1, Pallas kernels, per_device(): pl.pallas_call(functools.partial(evaluate_kernel, count), grid=(n_orb //...  6.4 us
    all_to_all x1, waiting for transfers between devices, per_device(): lax.all_to_all(values, 'orb', split_axis=0, concat_axis=0, tiled=True)  5.74 us
    pallas_call x1, Pallas kernels, per_device(): call(functools.partial(solve_kernel, count, others), (shape((2 * count, e...  5.65 us
    all_to_all x1, starting transfers between devices, per_device(): lax.all_to_all(points, 'orb', split_axis=0, concat_axis=0, tiled=True)  4.88 us
    ppermute x3, starting transfers between devices, per_device(): lax.ppermute(record, 'grp', pairs(n_grp, s))  4.6 us
    pallas_call x1, Pallas kernels, per_device(): call(functools.partial(finish_kernel, table, chunks), shape((electrons, e...  4.17 us
    ppermute x3, starting transfers between devices, per_device(): lax.ppermute(columns[s], 'grp', pairs(n_grp, s))  3.49 us
    all_to_all x1, starting transfers between devices, per_device(): lax.all_to_all(values, 'orb', split_axis=0, concat_axis=0, tiled=True)  3.44 us
  transfers between devices with their start and end apart: 14, of which 7 were waited for; matrix products, arithmetic and copies ran while one was open for 0% of the time, Pallas kernels for 30%

profile of v4, /device:TPU:0, one launch (start us, length us, event | category | flops | bytes accessed | tf_op | source)
XLA Modules:
  0.0 70.9 jit_solution(9746877620188267021)
XLA Ops:
  1.3 1.7 %shard_map.120 = (f32[8,1024]{1,0:T(8,128)S(1)}, s32[2,128]{1,0:T(2,128)S(1)}, f32[2,8,128]{2,1,0:T(8,128)S(1)}) custom-call(f32[3,1,1024]{2,1,0:T(1,128)} %bitcast.12, s32[2,1,16]{2,1,0:T(1,128)} %moved_hbm.1, f32[6,1,16]{2,1,0:T(1,128)} %bitcast.13, f32[1]{0:T(128)S(6)} %copy.27.weight_ref), custom_call_target="tpu_custom_call" | custom-call | tf_op jit(solution)/shard_map/pallas_call | solution.py:407
  3.0 4.0 %collective-permute-start.2 = (f32[8,1024]{1,0:T(8,128)S(1)}, f32[8,1024]{1,0:T(8,128)S(1)}, u32[]{:S(2)}, u32[]{:S(2)}) collective-permute-start(f32[8,1024]{1,0:T(8,128)S(1)} %get-tuple-element.32.after_ref.refs_0_), channel_id=1, source_target_pairs={{0,24},{8,16},{16,8},{24,0},{1,25},{9,17},{17,9},{25,1},{2,26},{10... | collective-permute-start | bytes 98312 | tf_op jit(solution)/shard_map/ppermute | solution.py:428
  7.0 0.5 collective-permute-start.1
  7.5 0.1 collective-permute-start
  7.6 3.2 %shard_map.121 = (bf16[256,1024]{1,0:T(8,128)(2,1)}, bf16[256,1024]{1,0:T(8,128)(2,1)S(1)}, bf16[256,1024]{1,0:T(8,128)(2,1)S(1)}, bf16[256,1024]{1,0:T(8,128)(2,1)}) custom-call(f32[1,1024,1024]{2,1,0:T(8,128)} %inverse_ref.1, f32[8,1024]{1,0:T(8,128)S(1)} %get-tuple-element.32.after_ref.refs_0_), custom_call_target="tpu_custom_call" | custom-call | bytes 6291456 | tf_op jit(solution)/shard_map/pallas_call | solution.py:434
  10.8 0.0 copy-start
  10.8 0.0 collective-permute-done.2.refs_4_.refs_3_.refs_7_
  10.8 0.0 collective-permute-done.1.refs_3_.refs_2_.refs_6_
  10.9 0.5 collective-permute-done.refs_2_.refs_1_.refs_5_
  11.4 1.5 %collective-permute-start.3 = (bf16[256,1024]{1,0:T(8,128)(2,1)}, bf16[256,1024]{1,0:T(8,128)(2,1)}, u32[]{:S(2)}, u32[]{:S(2)}) collective-permute-start(bf16[256,1024]{1,0:T(8,128)(2,1)} %get-tuple-element.41.refs_3_), channel_id=1, source_target_pairs={{0,16},{8,24},{16,0},{24,8},{1,17},{9,25},{17,1},{25,9},{2,18},{10... | collective-permute-start | bytes 1572872 | tf_op jit(solution)/shard_map/ppermute | solution.py:497
  12.9 1.4 %collective-permute-start.4 = (bf16[256,1024]{1,0:T(8,128)(2,1)}, bf16[256,1024]{1,0:T(8,128)(2,1)}, u32[]{:S(2)}, u32[]{:S(2)}) collective-permute-start(bf16[256,1024]{1,0:T(8,128)(2,1)} %get-tuple-element.42.refs_0_), channel_id=1, source_target_pairs={{0,8},{8,0},{16,24},{24,16},{1,9},{9,1},{17,25},{25,17},{2,10},{10... | collective-permute-start | bytes 1572872 | tf_op jit(solution)/shard_map/ppermute | solution.py:496
  14.3 0.0 copy-done
  14.3 2.6 %shard_map.125 = (bf16[32,1024]{1,0:T(8,128)(2,1)S(1)}, bf16[32,1024]{1,0:T(8,128)(2,1)}, bf16[32,1024]{1,0:T(8,128)(2,1)}, bf16[32,1024]{1,0:T(8,128)(2,1)S(1)}) custom-call(bf16[256,1024]{1,0:T(8,128)(2,1)} %get-tuple-element.42.refs_0_, bf16[256,1024]{1,0:T(8,128)(2,1)S(1)} %get-tuple-element.39.refs_1_.own_a.own_b, ...), custom_call_target="tpu_custom_call" | custom-call | flops 268435456 | bytes 2097152 | tf_op jit(solution)/shard_map/pallas_call | solution.py:465
  17.0 0.0 copy-start.4
  17.0 0.6 collective-permute-start.5
  17.5 0.5 collective-permute-start.6
  18.1 2.4 %collective-permute-start.7 = (bf16[32,1024]{1,0:T(8,128)(2,1)S(1)}, bf16[32,1024]{1,0:T(8,128)(2,1)S(1)}, u32[]{:S(2)}, u32[]{:S(2)}) collective-permute-start(bf16[32,1024]{1,0:T(8,128)(2,1)S(1)} %get-tuple-element.45), channel_id=1, source_target_pairs={{0,24},{8,16},{16,8},{24,0},{1,25},{9,17},{17,9},{25,1},{2,26},{10... | collective-permute-start | bytes 196616 | tf_op jit(solution)/shard_map/ppermute | solution.py:474
  21.7 1.0 %shard_map.123 = (f32[8,8,128]{2,1,0:T(8,128)}, f32[1,128]{1,0:T(1,128)S(1)}) custom-call(s32[1]{0:T(128)} %bitcast.2.role_ref, f32[8,1024]{1,0:T(8,128)S(1)} %get-tuple-element.32.after_ref.refs_0_, f32[8,1024]{1,0:T(8,128)S(1)} %collective-permute-done.refs_2_.refs_1_.refs_5_, f32[8,1024]{1,0:T(8,128)S(1)} %collective-permute-done.1.refs_3_.refs_2_.refs_6_, ...), custom_call_target="tpu_custom_call" | custom-call | tf_op jit(solution)/shard_map/pallas_call | solution.py:456
  22.7 4.9 %all-to-all-start = ((f32[8,8,128]{2,1,0:T(8,128)}), f32[8,8,128]{2,1,0:T(8,128)S(1)}, u32[]{:S(2)}, u32[]{:S(2)}) async-start(f32[8,8,128]{2,1,0:T(8,128)} %get-tuple-element.38), calls=%async_computation | async-start | bytes 65536 | tf_op jit(solution)/shard_map/all_to_all | solution.py:462
  27.6 2.6 %shard_map.124.refs_0_.table_ref = bf16[2048,640]{1,0:T(8,128)(2,1)S(1)} custom-call(bf16[2048,128]{1,0:T(8,128)(2,1)} %coeff_hbm.1, f32[3,1024]{1,0:T(4,128)} %wave_ref.1), custom_call_target="tpu_custom_call" | custom-call | flops 2097152 | bytes 2621440 | tf_op jit(solution)/shard_map/pallas_call | solution.py:478
  30.3 3.1 %all-to-all-done.refs_1_.points_ref = f32[8,8,128]{2,1,0:T(8,128)S(1)} async-done(((f32[8,8,128]{2,1,0:T(8,128)}), f32[8,8,128]{2,1,0:T(8,128)S(1)}, u32[]{:S(2)}, u32[]{:S(2)}) %all-to-all-start) | async-done | bytes 32800 | tf_op jit(solution)/shard_map/all_to_all | solution.py:462
  33.4 0.0 collective-permute-done.5.refs_2_.refs_0_
  33.4 0.0 collective-permute-done.6.refs_3_.refs_1_
  33.4 0.0 collective-permute-done.7.refs_4_.refs_2_
  33.4 0.0 collective-permute-done.3.got_a
  33.4 0.0 collective-permute-done.4.got_b
  33.4 0.0 copy-start.1
  33.4 1.0 %copy-done.1 = bf16[256,1024]{1,0:T(8,128)(2,1)S(1)} copy-done((bf16[256,1024]{1,0:T(8,128)(2,1)S(1)}, bf16[256,1024]{1,0:T(8,128)(2,1)}, u32[]{:S(2)}) %copy-start.1) | copy-done | bytes 524312
  34.5 0.6 collective-permute-start.8
  35.0 1.2 %collective-permute-start.9 = (bf16[256,1024]{1,0:T(8,128)(2,1)}, bf16[256,1024]{1,0:T(8,128)(2,1)}, u32[]{:S(2)}, u32[]{:S(2)}) collective-permute-start(bf16[256,1024]{1,0:T(8,128)(2,1)} %get-tuple-element.50.refs_7_), channel_id=1, source_target_pairs={{0,8},{8,0},{16,24},{24,16},{1,9},{9,1},{17,25},{25,17},{2,10},{10... | collective-permute-start | bytes 1572872 | tf_op jit(solution)/shard_map/ppermute | solution.py:496
  36.2 0.0 copy-done.4
  36.2 6.4 %shard_map.127 = bf16[8,176,128]{2,1,0:T(8,128)(2,1)} custom-call(f32[8,8,128]{2,1,0:T(8,128)S(1)} %all-to-all-done.refs_1_.points_ref, f32[3,1024]{1,0:T(4,128)S(1)} %copy-done.4, bf16[2048,640]{1,0:T(8,128)(2,1)S(1)} %shard_map.124.refs_0_.table_ref, f32[8,128]{1,0:T(8,128)S(1)} %get-tuple-element.46.after_ref), custom_call_target="tpu_custom_call" | custom-call | flops 738197504 | bytes 3145728 | tf_op jit(solution)/shard_map/pallas_call | solution.py:526
  42.6 3.4 %all-to-all-start.1 = ((bf16[8,176,128]{2,1,0:T(8,128)(2,1)}), bf16[8,176,128]{2,1,0:T(8,128)(2,1)S(1)}, u32[]{:S(2)}, u32[]{:S(2)}) async-start(bf16[8,176,128]{2,1,0:T(8,128)(2,1)} %shard_map.127), calls=%async_computation.1 | async-start | bytes 720896 | tf_op jit(solution)/shard_map/all_to_all | solution.py:549
  46.1 2.3 %collective-permute-done.8.got_a = bf16[256,1024]{1,0:T(8,128)(2,1)} collective-permute-done((bf16[256,1024]{1,0:T(8,128)(2,1)}, bf16[256,1024]{1,0:T(8,128)(2,1)}, u32[]{:S(2)}, u32[]{:S(2)}) %collective-permute-start.8) | collective-permute-done | bytes 524320 | tf_op jit(solution)/shard_map/ppermute | solution.py:497
  48.4 1.2 %collective-permute-done.9.got_b = bf16[256,1024]{1,0:T(8,128)(2,1)} collective-permute-done((bf16[256,1024]{1,0:T(8,128)(2,1)}, bf16[256,1024]{1,0:T(8,128)(2,1)}, u32[]{:S(2)}, u32[]{:S(2)}) %collective-permute-start.9) | collective-permute-done | bytes 524320 | tf_op jit(solution)/shard_map/ppermute | solution.py:496
  49.6 0.0 copy-start.2
  49.6 1.0 %copy-done.2 = bf16[256,1024]{1,0:T(8,128)(2,1)S(1)} copy-done((bf16[256,1024]{1,0:T(8,128)(2,1)S(1)}, bf16[256,1024]{1,0:T(8,128)(2,1)}, u32[]{:S(2)}) %copy-start.2) | copy-done | bytes 524312
  50.7 0.6 collective-permute-start.11
  51.3 0.8 %collective-permute-start.10 = (bf16[256,1024]{1,0:T(8,128)(2,1)}, bf16[256,1024]{1,0:T(8,128)(2,1)S(1)}, u32[]{:S(2)}, u32[]{:S(2)}) collective-permute-start(bf16[256,1024]{1,0:T(8,128)(2,1)} %get-tuple-element.56.refs_8_), channel_id=1, source_target_pairs={{0,8},{8,0},{16,24},{24,16},{1,9},{9,1},{17,25},{25,17},{2,10},{10... | collective-permute-start | bytes 1572872 | tf_op jit(solution)/shard_map/ppermute | solution.py:496
  52.1 5.7 %all-to-all-done.1.vals_ref = bf16[8,176,128]{2,1,0:T(8,128)(2,1)S(1)} async-done(((bf16[8,176,128]{2,1,0:T(8,128)(2,1)}), bf16[8,176,128]{2,1,0:T(8,128)(2,1)S(1)}, u32[]{:S(2)}, u32[]{:S(2)}) %all-to-all-start.1) | async-done | bytes 360480 | tf_op jit(solution)/shard_map/all_to_all | solution.py:549
  57.8 5.7 %shard_map.129 = (bf16[32,1024]{1,0:T(8,128)(2,1)S(1)}, bf16[32,1024]{1,0:T(8,128)(2,1)S(1)}, f32[32,32]{1,0:T(8,128)S(1)}, f32[6,1,16]{2,1,0:T(1,128)}, f32[2,1,16]{2,1,0:T(1,128)}, /*index=5*/f32[1,128]{1,0:T(1,128)}) custom-call(s32[1]{0:T(128)} %bitcast.2.role_ref, bf16[8,176,128]{2,1,0:T(8,128)(2,1)S(1)} %all-to-all-done.1.vals_ref, ...), custom_call_target="tpu_custom_call" | custom-call | flops 8388608 | bytes 720896 | tf_op jit(solution)/shard_map/pallas_call | solution.py:553
  63.5 1.0 %collective-permute-done.11.refs_9_ = bf16[256,1024]{1,0:T(8,128)(2,1)S(1)} collective-permute-done((bf16[256,1024]{1,0:T(8,128)(2,1)}, bf16[256,1024]{1,0:T(8,128)(2,1)S(1)}, u32[]{:S(2)}, u32[]{:S(2)}) %collective-permute-start.11) | collective-permute-done | bytes 524320 | tf_op jit(solution)/shard_map/ppermute | solution.py:497
  64.5 1.2 %collective-permute-done.10.refs_6_ = bf16[256,1024]{1,0:T(8,128)(2,1)S(1)} collective-permute-done((bf16[256,1024]{1,0:T(8,128)(2,1)}, bf16[256,1024]{1,0:T(8,128)(2,1)S(1)}, u32[]{:S(2)}, u32[]{:S(2)}) %collective-permute-start.10) | collective-permute-done | bytes 524320 | tf_op jit(solution)/shard_map/ppermute | solution.py:496
  65.7 0.0 copy-start.3
  65.7 1.0 %copy-done.3 = bf16[256,1024]{1,0:T(8,128)(2,1)S(1)} copy-done((bf16[256,1024]{1,0:T(8,128)(2,1)S(1)}, bf16[256,1024]{1,0:T(8,128)(2,1)}, u32[]{:S(2)}) %copy-start.3) | copy-done | bytes 524312
  66.7 4.2 %shard_map.130 = f32[1024,1024]{1,0:T(8,128)} custom-call(s32[1]{0:T(128)} %bitcast.2.role_ref, bf16[32,1024]{1,0:T(8,128)(2,1)S(1)} %get-tuple-element.52.change_ref, bf16[32,1024]{1,0:T(8,128)(2,1)S(1)} %get-tuple-element.53.cols_ref, f32[32,32]{1,0:T(8,128)S(1)} %get-tuple-element.54.inv_ref, bf16[256,1024]{1,0:T(8,128)(2,1)} %get-tuple-element.42.refs_0_, ...), custom_call_target="tpu_custom_call" | custom-call | flops 134217728 | bytes 6291456 | tf_op jit(solution)/shard_map/pallas_call | solution.py:570
  (3 shorter events, 0.0 us)
Async XLA Ops:
  3.0 7.8 %collective-permute-start.2 = (f32[8,1024]{1,0:T(8,128)S(1)}, f32[8,1024]{1,0:T(8,128)S(1)}, u32[]{:S(2)}, u32[]{:S(2)}) collective-permute-start(f32[8,1024]{1,0:T(8,128)S(1)} %get-tuple-element.32.after_ref.refs_0_), channel_id=1, source_target_pairs={{0,24},{8,16},{16,8},{24,0},{1,25},{9,17},{17,9},{25,1},{2,26},{10... | collective-permute-start | bytes 98312 | tf_op jit(solution)/shard_map/ppermute | solution.py:428
  7.0 3.9 %collective-permute-start.1 = (f32[8,1024]{1,0:T(8,128)S(1)}, f32[8,1024]{1,0:T(8,128)S(1)}, u32[]{:S(2)}, u32[]{:S(2)}) collective-permute-start(f32[8,1024]{1,0:T(8,128)S(1)} %get-tuple-element.32.after_ref.refs_0_), channel_id=1, source_target_pairs={{0,16},{8,24},{16,0},{24,8},{1,17},{9,25},{17,1},{25,9},{2,18},{10... | collective-permute-start | bytes 98312 | tf_op jit(solution)/shard_map/ppermute | solution.py:428
  7.5 3.9 %collective-permute-start = (f32[8,1024]{1,0:T(8,128)S(1)}, f32[8,1024]{1,0:T(8,128)S(1)}, u32[]{:S(2)}, u32[]{:S(2)}) collective-permute-start(f32[8,1024]{1,0:T(8,128)S(1)} %get-tuple-element.32.after_ref.refs_0_), channel_id=1, source_target_pairs={{0,8},{8,0},{16,24},{24,16},{1,9},{9,1},{17,25},{25,17},{2,10},{10... | collective-permute-start | bytes 98312 | tf_op jit(solution)/shard_map/ppermute | solution.py:428
  10.8 3.5 %copy-start = (bf16[256,1024]{1,0:T(8,128)(2,1)}, bf16[256,1024]{1,0:T(8,128)(2,1)S(1)}, u32[]{:S(2)}) copy-start(bf16[256,1024]{1,0:T(8,128)(2,1)S(1)} %get-tuple-element.40.refs_2_.own_b.own_a) | copy-start | bytes 1572868
  11.4 22.0 %collective-permute-start.3 = (bf16[256,1024]{1,0:T(8,128)(2,1)}, bf16[256,1024]{1,0:T(8,128)(2,1)}, u32[]{:S(2)}, u32[]{:S(2)}) collective-permute-start(bf16[256,1024]{1,0:T(8,128)(2,1)} %get-tuple-element.41.refs_3_), channel_id=1, source_target_pairs={{0,16},{8,24},{16,0},{24,8},{1,17},{9,25},{17,1},{25,9},{2,18},{10... | collective-permute-start | bytes 1572872 | tf_op jit(solution)/shard_map/ppermute | solution.py:497
  12.9 20.5 %collective-permute-start.4 = (bf16[256,1024]{1,0:T(8,128)(2,1)}, bf16[256,1024]{1,0:T(8,128)(2,1)}, u32[]{:S(2)}, u32[]{:S(2)}) collective-permute-start(bf16[256,1024]{1,0:T(8,128)(2,1)} %get-tuple-element.42.refs_0_), channel_id=1, source_target_pairs={{0,8},{8,0},{16,24},{24,16},{1,9},{9,1},{17,25},{25,17},{2,10},{10... | collective-permute-start | bytes 1572872 | tf_op jit(solution)/shard_map/ppermute | solution.py:496
  17.0 19.3 %copy-start.4 = (f32[3,1024]{1,0:T(4,128)S(1)}, f32[3,1024]{1,0:T(4,128)}, u32[]{:S(2)}) copy-start(f32[3,1024]{1,0:T(4,128)} %wave_ref.1) | copy-start | bytes 36868
  17.0 16.4 %collective-permute-start.5 = (bf16[32,1024]{1,0:T(8,128)(2,1)}, bf16[32,1024]{1,0:T(8,128)(2,1)S(1)}, u32[]{:S(2)}, u32[]{:S(2)}) collective-permute-start(bf16[32,1024]{1,0:T(8,128)(2,1)} %get-tuple-element.43), channel_id=1, source_target_pairs={{0,8},{8,0},{16,24},{24,16},{1,9},{9,1},{17,25},{25,17},{2,10},{10... | collective-permute-start | bytes 196616 | tf_op jit(solution)/shard_map/ppermute | solution.py:474
  17.5 15.8 %collective-permute-start.6 = (bf16[32,1024]{1,0:T(8,128)(2,1)}, bf16[32,1024]{1,0:T(8,128)(2,1)S(1)}, u32[]{:S(2)}, u32[]{:S(2)}) collective-permute-start(bf16[32,1024]{1,0:T(8,128)(2,1)} %get-tuple-element.44), channel_id=1, source_target_pairs={{0,16},{8,24},{16,0},{24,8},{1,17},{9,25},{17,1},{25,9},{2,18},{10... | collective-permute-start | bytes 196616 | tf_op jit(solution)/shard_map/ppermute | solution.py:474
  18.1 15.3 %collective-permute-start.7 = (bf16[32,1024]{1,0:T(8,128)(2,1)S(1)}, bf16[32,1024]{1,0:T(8,128)(2,1)S(1)}, u32[]{:S(2)}, u32[]{:S(2)}) collective-permute-start(bf16[32,1024]{1,0:T(8,128)(2,1)S(1)} %get-tuple-element.45), channel_id=1, source_target_pairs={{0,24},{8,16},{16,8},{24,0},{1,25},{9,17},{17,9},{25,1},{2,26},{10... | collective-permute-start | bytes 196616 | tf_op jit(solution)/shard_map/ppermute | solution.py:474
  22.7 10.6 %all-to-all-start = ((f32[8,8,128]{2,1,0:T(8,128)}), f32[8,8,128]{2,1,0:T(8,128)S(1)}, u32[]{:S(2)}, u32[]{:S(2)}) async-start(f32[8,8,128]{2,1,0:T(8,128)} %get-tuple-element.38), calls=%async_computation | async-start | bytes 65536 | tf_op jit(solution)/shard_map/all_to_all | solution.py:462
  33.4 1.0 %copy-start.1 = (bf16[256,1024]{1,0:T(8,128)(2,1)S(1)}, bf16[256,1024]{1,0:T(8,128)(2,1)}, u32[]{:S(2)}) copy-start(bf16[256,1024]{1,0:T(8,128)(2,1)} %copy-done) | copy-start | bytes 1572868
  34.5 13.9 %collective-permute-start.8 = (bf16[256,1024]{1,0:T(8,128)(2,1)}, bf16[256,1024]{1,0:T(8,128)(2,1)}, u32[]{:S(2)}, u32[]{:S(2)}) collective-permute-start(bf16[256,1024]{1,0:T(8,128)(2,1)} %get-tuple-element.49.refs_4_), channel_id=1, source_target_pairs={{0,16},{8,24},{16,0},{24,8},{1,17},{9,25},{17,1},{25,9},{2,18},{10... | collective-permute-start | bytes 1572872 | tf_op jit(solution)/shard_map/ppermute | solution.py:497
  35.0 14.6 %collective-permute-start.9 = (bf16[256,1024]{1,0:T(8,128)(2,1)}, bf16[256,1024]{1,0:T(8,128)(2,1)}, u32[]{:S(2)}, u32[]{:S(2)}) collective-permute-start(bf16[256,1024]{1,0:T(8,128)(2,1)} %get-tuple-element.50.refs_7_), channel_id=1, source_target_pairs={{0,8},{8,0},{16,24},{24,16},{1,9},{9,1},{17,25},{25,17},{2,10},{10... | collective-permute-start | bytes 1572872 | tf_op jit(solution)/shard_map/ppermute | solution.py:496
  42.6 15.2 %all-to-all-start.1 = ((bf16[8,176,128]{2,1,0:T(8,128)(2,1)}), bf16[8,176,128]{2,1,0:T(8,128)(2,1)S(1)}, u32[]{:S(2)}, u32[]{:S(2)}) async-start(bf16[8,176,128]{2,1,0:T(8,128)(2,1)} %shard_map.127), calls=%async_computation.1 | async-start | bytes 720896 | tf_op jit(solution)/shard_map/all_to_all | solution.py:549
  49.6 1.0 %copy-start.2 = (bf16[256,1024]{1,0:T(8,128)(2,1)S(1)}, bf16[256,1024]{1,0:T(8,128)(2,1)}, u32[]{:S(2)}) copy-start(bf16[256,1024]{1,0:T(8,128)(2,1)} %copy-done) | copy-start | bytes 1572868
  50.7 13.8 %collective-permute-start.11 = (bf16[256,1024]{1,0:T(8,128)(2,1)}, bf16[256,1024]{1,0:T(8,128)(2,1)S(1)}, u32[]{:S(2)}, u32[]{:S(2)}) collective-permute-start(bf16[256,1024]{1,0:T(8,128)(2,1)} %get-tuple-element.55.refs_5_), channel_id=1, source_target_pairs={{0,16},{8,24},{16,0},{24,8},{1,17},{9,25},{17,1},{25,9},{2,18},{10... | collective-permute-start | bytes 1572872 | tf_op jit(solution)/shard_map/ppermute | solution.py:497
  51.3 14.4 %collective-permute-start.10 = (bf16[256,1024]{1,0:T(8,128)(2,1)}, bf16[256,1024]{1,0:T(8,128)(2,1)S(1)}, u32[]{:S(2)}, u32[]{:S(2)}) collective-permute-start(bf16[256,1024]{1,0:T(8,128)(2,1)} %get-tuple-element.56.refs_8_), channel_id=1, source_target_pairs={{0,8},{8,0},{16,24},{24,16},{1,9},{9,1},{17,25},{25,17},{2,10},{10... | collective-permute-start | bytes 1572872 | tf_op jit(solution)/shard_map/ppermute | solution.py:496
  65.7 1.0 %copy-start.3 = (bf16[256,1024]{1,0:T(8,128)(2,1)S(1)}, bf16[256,1024]{1,0:T(8,128)(2,1)}, u32[]{:S(2)}) copy-start(bf16[256,1024]{1,0:T(8,128)(2,1)} %copy-done) | copy-start | bytes 1572868

commit v5 on v4

--- a/solution.py
+++ b/solution.py
@@ -11,6 +11,7 @@
 F32 = jnp.float32
 BF16 = jnp.bfloat16
 LANES = 128
+ROWS = 16
 MIB = 1024 * 1024
 precise = lax.Precision.HIGHEST
 
@@ -125,19 +126,29 @@
     out_ref[7:8, 0:LANES] = jnp.full((1, LANES), weight_ref[0], F32)
 
 
-def round_kernel(inverse_ref, after_ref, *refs):
-    outs = refs[:-2]
-    staged, sem = refs[-2:]
+def rows_of(ref, chunk, depth):
+    return ref.at[0, pl.ds(chunk * depth, depth)]
+
+
+def round_kernel(wanted, inverse_hbm, after_ref, *refs):
+    outs = refs[: len(wanted)]
+    staged, rounded, in_sem, out_sem = refs[len(wanted) :]
     depth = staged.shape[1]
-    copies = []
-    for chunk in range(len(outs)):
-        rows = inverse_ref.at[0, pl.ds(chunk * depth, depth)]
-        copy = pltpu.make_async_copy(rows, staged.at[chunk], sem.at[chunk])
-        copy.start()
-        copies.append(copy)
-    for chunk, out in enumerate(outs):
-        copies[chunk].wait()
-        out[...] = staged[chunk].astype(BF16)
+    loads, stores = [], []
+    for slot, chunk in enumerate(wanted):
+        load = pltpu.make_async_copy(
+            rows_of(inverse_hbm, chunk, depth), staged.at[slot], in_sem.at[slot]
+        )
+        load.start()
+        loads.append(load)
+    for slot, out in enumerate(outs):
+        loads[slot].wait()
+        rounded[slot] = staged[slot].astype(BF16)
+        store = pltpu.make_async_copy(rounded.at[slot], out, out_sem.at[slot])
+        store.start()
+        stores.append(store)
+    for store in stores:
+        store.wait()
 
 
 def gate_kernel(*refs):
@@ -147,17 +158,18 @@
 
 def relay_kernel(flag_ref, own_a, own_b, got_a, got_b, *refs):
     out_a, out_b, token_ref, sems = refs[-4:]
-
-    @pl.when(flag_ref[0] == 0)
-    def _():
-        copies = [
-            pltpu.make_async_copy(own_a, out_a, sems.at[0]),
-            pltpu.make_async_copy(own_b, out_b, sems.at[1]),
-        ]
-        for copy in copies:
-            copy.start()
-        for copy in copies:
-            copy.wait()
+    for here, pair in ((True, (own_a, own_b)), (False, (got_a, got_b))):
+
+        @pl.when((flag_ref[0] == 0) == here)
+        def _():
+            copies = [
+                pltpu.make_async_copy(pair[0], out_a, sems.at[0]),
+                pltpu.make_async_copy(pair[1], out_b, sems.at[1]),
+            ]
+            for copy in copies:
+                copy.start()
+            for copy in copies:
+                copy.wait()
 
     token_ref[...] = jnp.zeros(token_ref.shape, F32)
 
@@ -179,41 +191,12 @@
     mine = jnp.concatenate([own_ref[3:6, 0:LANES], zeros], 0)
     theirs = jnp.concatenate([parent[3:6, 0:LANES], zeros], 0)
     points = jnp.where(block < 2, mine, jnp.where(block < 4, theirs, later))
+    points = jnp.concatenate([points, jnp.zeros((ROWS - 8, LANES), F32)], 0)
     points_ref[...] = jnp.broadcast_to(points[None], points_ref.shape)
     weight_ref[...] = parent[7:8, 0:LANES]
 
 
-def columns_kernel(count, others, chunks, steps, *refs):
-    chunk_refs = refs[:chunks]
-    moved_ref = refs[chunks]
-    received = refs[chunks + 1 : chunks + 1 + others]
-    outs = refs[chunks + 1 + others :]
-    depth = chunk_refs[0].shape[0]
-    electrons = chunk_refs[0].shape[1]
-    block = iota((1, LANES), 1) // count
-    wanted = jnp.where(block == 0, moved_ref[0:1, :], moved_ref[1:2, :])
-    for step in range(others):
-        theirs = received[step][6:7, 0:LANES].astype(jnp.int32)
-        wanted = jnp.where(block == 2 + step, theirs, wanted)
-    pick = (iota((electrons, LANES), 0) == wanted).astype(F32).astype(BF16)
-    for chunk in range(chunks):
-        rows = slice(chunk * depth, (chunk + 1) * depth)
-        found = dot(chunk_refs[chunk][...], pick)
-        turned = jnp.transpose(found).astype(BF16)
-        for out, step in zip(outs, steps):
-            out[0:count, rows] = turned[0:count]
-            out[count : 2 * count, rows] = turned[(1 + step) * count : (2 + step) * count]
-
-
-def table_kernel(coeff_hbm, wave_hbm, out_ref, coeff_ref, wave_ref, sems):
-    loads = [
-        pltpu.make_async_copy(wave_hbm, wave_ref, sems.at[0]),
-        pltpu.make_async_copy(coeff_hbm, coeff_ref, sems.at[1]),
-    ]
-    for load in loads:
-        load.start()
-    for load in loads:
-        load.wait()
+def derive(coeff_ref, wave_ref, out_ref):
     waves = wave_ref.shape[1]
     width = coeff_ref.shape[1]
     wave = jnp.transpose(jnp.concatenate([wave_ref[...], jnp.zeros((5, waves), F32)], 0))
@@ -232,6 +215,52 @@
     out_ref[waves:, where] = (-squared * sin_part).astype(BF16)
 
 
+def prepare_kernel(
+    count, others, chunks, wanted, steps, coeff_hbm, wave_hbm, inverse_hbm, moved_ref, *refs
+):
+    received = refs[:others]
+    table_ref = refs[others + 1]
+    outs = refs[others + 2 : others + 2 + len(wanted)]
+    columns = refs[others + 2 + len(wanted) : -7]
+    coeff_ref, wave_ref, staged, rounded, small_sem, in_sem, out_sem = refs[-7:]
+    depth, electrons = staged.shape[1:]
+    wave_load = pltpu.make_async_copy(wave_hbm, wave_ref, small_sem.at[0])
+    coeff_load = pltpu.make_async_copy(coeff_hbm, coeff_ref, small_sem.at[1])
+    wave_load.start()
+    coeff_load.start()
+    loads, stores = [], []
+    for chunk in range(chunks):
+        load = pltpu.make_async_copy(
+            rows_of(inverse_hbm, chunk, depth), staged.at[chunk], in_sem.at[chunk]
+        )
+        load.start()
+        loads.append(load)
+    block = iota((1, LANES), 1) // count
+    number = jnp.where(block == 0, moved_ref[0:1, :], moved_ref[1:2, :])
+    for step in range(others):
+        theirs = received[step][6:7, 0:LANES].astype(jnp.int32)
+        number = jnp.where(block == 2 + step, theirs, number)
+    pick = (iota((electrons, LANES), 0) == number).astype(F32).astype(BF16)
+    wave_load.wait()
+    coeff_load.wait()
+    derive(coeff_ref, wave_ref, table_ref)
+    for chunk in range(chunks):
+        rows = slice(chunk * depth, (chunk + 1) * depth)
+        loads[chunk].wait()
+        rounded[chunk] = staged[chunk].astype(BF16)
+        if chunk in wanted:
+            slot = wanted.index(chunk)
+            store = pltpu.make_async_copy(rounded.at[chunk], outs[slot], out_sem.at[slot])
+            store.start()
+            stores.append(store)
+        turned = jnp.transpose(dot(rounded[chunk], pick)).astype(BF16)
+        for out, step in zip(columns, steps):
+            out[0:count, rows] = turned[0:count]
+            out[count : 2 * count, rows] = turned[(1 + step) * count : (2 + step) * count]
+    for store in stores:
+        store.wait()
+
+
 def horner(coefs, u):
     value = coefs[-1] * u + coefs[-2]
     for c in reversed(coefs[:-2]):
@@ -239,16 +268,15 @@
     return value
 
 
-def evaluate_kernel(
-    count, points_ref, wave_ref, table_ref, after_ref, out_ref, diff, new
-):
+def evaluate_kernel(count, points_ref, wave_ref, table_ref, *refs):
+    out_ref, diff, new = refs[-3:]
     walkers = points_ref.shape[0]
     waves = wave_ref.shape[1]
     width = table_ref.shape[1] // 5
     step = math.gcd(waves, LANES)
 
     def one(w, carry):
-        column = jnp.transpose(points_ref[w])
+        column = jnp.transpose(points_ref[w, 0:8])
         xs = [column[0 : 6 * count, a : a + 1] for a in range(3)]
         row_d = pl.multiple_of(w * (3 * count), count)
         row_n = pl.multiple_of(w * (2 * count), count)
@@ -428,22 +456,25 @@
     records = [lax.ppermute(record, "grp", pairs(n_grp, s)) for s in range(1, n_grp)]
 
     depth = electrons // chunks
-    kept = shape((depth, electrons), BF16)
+    kept = pltpu.HBM((depth, electrons), BF16)
     token = shape((8, LANES), F32)
-    own = list(
-        call(
-            round_kernel,
-            (kept,) * chunks,
-            [HBM, ANY],
-            (VM,) * chunks,
-            scratch=[
-                pltpu.VMEM((chunks, depth, electrons), F32),
-                pltpu.SemaphoreType.DMA((chunks,)),
-            ],
-            moved=6 * electrons * electrons,
-            vmem=8,
-        )(*in_hbm(inverse), record)
-    )
+    own = [None] * chunks
+    ends = (0, chunks - 1)
+    middle = tuple(range(1, chunks - 1))
+    own[0], own[-1] = call(
+        functools.partial(round_kernel, ends),
+        (kept,) * 2,
+        [HBM, ANY],
+        (HBM,) * 2,
+        scratch=[
+            pltpu.VMEM((2, depth, electrons), F32),
+            pltpu.VMEM((2, depth, electrons), BF16),
+            pltpu.SemaphoreType.DMA((2,)),
+            pltpu.SemaphoreType.DMA((2,)),
+        ],
+        moved=3 * electrons * electrons,
+        vmem=6,
+    )(*in_hbm(inverse), record)
     own[0], own[-1], token_0 = call(
         gate_kernel,
         (kept, kept, token),
@@ -451,44 +482,43 @@
         (ANY, ANY, VM),
         aliases={0: 0, 1: 1},
         vmem=1,
-    )(own[0], own[-1], *records)
+    )(*in_hbm(own[0], own[-1]), *records)
 
     points, weight = call(
         functools.partial(points_kernel, count, others),
-        (shape((n_orb, 8, LANES), F32), shape((1, LANES), F32)),
+        (shape((n_orb, ROWS, LANES), F32), shape((1, LANES), F32)),
         [SM] + [VM] * (others + 3) + [ANY],
         (VM, VM),
     )(role, record, *records, tiled, disp, token_0)
     points = lax.all_to_all(points, "orb", split_axis=0, concat_axis=0, tiled=True)
 
-    steps = [0] + [backward(n_grp, s) for s in range(1, n_grp)]
-    columns = call(
-        functools.partial(columns_kernel, count, others, chunks, steps),
-        tuple(shape((2 * count, electrons), BF16) for _ in steps),
-        [VM] * (chunks + 1 + others),
-        tuple(VM for _ in steps),
-        flops=2 * electrons * electrons * LANES,
-        moved=2 * electrons * electrons,
-        vmem=8,
-    )(*own, tiled, *records)
-    sent = [lax.ppermute(columns[s], "grp", pairs(n_grp, s)) for s in range(1, n_grp)]
-
     width = -(-local // LANES) * LANES
     coeff = jnp.pad(coefficients, ((0, 0), (0, width - local))) if width > local else coefficients
-    derived = call(
-        table_kernel,
-        shape((plane, 5 * width), BF16),
-        [HBM, HBM],
-        VM,
+    steps = [0] + [backward(n_grp, s) for s in range(1, n_grp)]
+    derived, *prepared = call(
+        functools.partial(prepare_kernel, count, others, chunks, middle, steps),
+        (shape((plane, 5 * width), BF16),)
+        + (kept,) * len(middle)
+        + tuple(shape((2 * count, electrons), BF16) for _ in steps),
+        [HBM, HBM, HBM] + [VM] * (1 + others) + [ANY],
+        (VM,) + (HBM,) * len(middle) + (VM,) * len(steps),
         scratch=[
             pltpu.VMEM((plane, width), BF16),
             pltpu.VMEM(wavevectors.shape, F32),
+            pltpu.VMEM((chunks, depth, electrons), F32),
+            pltpu.VMEM((chunks, depth, electrons), BF16),
             pltpu.SemaphoreType.DMA((2,)),
+            pltpu.SemaphoreType.DMA((chunks,)),
+            pltpu.SemaphoreType.DMA((len(middle),)),
         ],
-        flops=8 * plane * width,
-        moved=10 * plane * width,
-        vmem=8,
-    )(*in_hbm(coeff, wavevectors))
+        flops=2 * electrons * electrons * LANES + 8 * plane * width,
+        moved=6 * electrons * electrons + 10 * plane * width,
+        vmem=16,
+    )(*in_hbm(coeff, wavevectors, inverse), tiled, *records, weight)
+    for chunk, block in zip(middle, prepared):
+        own[chunk] = block
+    columns = prepared[len(middle) :]
+    sent = [lax.ppermute(columns[s], "grp", pairs(n_grp, s)) for s in range(1, n_grp)]
 
     apart = apart.astype(jnp.int32).reshape(1)
     arrays = list(own)
@@ -501,22 +531,23 @@
                 relay_kernel,
                 (kept, kept, token),
                 [SM] + [ANY] * (4 + len(first)),
-                (ANY, ANY, VM),
+                (HBM, HBM, VM),
                 scratch=[pltpu.SemaphoreType.DMA((2,))],
-                aliases={3: 0, 4: 1},
                 vmem=1,
-            )(apart, *mine, *got, *first)
+            )(apart, *in_hbm(*mine), *got, *first)
 
         x1, y1 = send_x(own[0]), send_y(own[3])
         y1, x1, token_1 = relay((own[1], own[2]), (y1, x1), (derived, points, *sent))
         x2, y2 = send_x(y1), send_y(x1)
         y2, x2, token_2 = relay((own[2], own[1]), (y2, x2), ())
         x3, y3 = send_x(y2), send_y(x2)
-        arrays += [x1, x2, x3, y1, y2, y3]
-        a1, a2, a3, b1, b2, b3 = range(chunks, chunks + 6)
+        arrays += [x1, x2, y1, y2, x3, y3]
+        settled = len(arrays) - 2
+        a1, a2, b1, b2, a3, b3 = range(chunks, chunks + 6)
         table = [range(chunks), (a1, a2, a3, b3), (a3, b3, b2, b1), (b2, b3, a3, a2)]
     else:
         token_1 = token_2 = jnp.zeros((8, LANES), F32)
+        settled = chunks
         table = [range(chunks)]
         for step in range(1, n_grp):
             table.append(range(len(arrays), len(arrays) + chunks))
@@ -528,11 +559,11 @@
         grid=(n_orb // block,),
         out_shape=shape((n_orb, 11 * count, width), BF16),
         in_specs=[
-            pl.BlockSpec((block, 8, LANES), lambda i: (i, 0, 0)),
+            pl.BlockSpec((block, ROWS, LANES), lambda i: (i, 0, 0)),
             pl.BlockSpec(wavevectors.shape, lambda i: (0, 0)),
             pl.BlockSpec(derived.shape, lambda i: (0, 0)),
-            ANY,
-        ],
+        ]
+        + [ANY],
         out_specs=pl.BlockSpec((block, 11 * count, width), lambda i: (i, 0, 0)),
         scratch_shapes=[
             pltpu.VMEM((block * 3 * count, plane), BF16),
@@ -571,7 +602,7 @@
         functools.partial(finish_kernel, table, chunks),
         shape((electrons, electrons), F32),
         [SM, VM, VM, VM] + [ANY] * len(arrays),
-        ANY,
+        HBM,
         scratch=[
             pltpu.VMEM((chunks, depth, electrons), BF16),
             pltpu.VMEM((chunks, depth, electrons), F32),
@@ -581,7 +612,7 @@
         flops=4 * electrons * electrons * 2 * count,
         moved=6 * electrons * electrons,
         vmem=12,
-    )(role, change, cols, small, *arrays)
+    )(role, change, cols, small, *in_hbm(*arrays[:settled]), *arrays[settled:])
 
     return updated[None], drift.reshape(2, 1, 3, count), laplacian, new_weight[0, :1]
 

time: 70.5 us -> 131 us (1.86)
  Pallas kernels: 27.4 us -> 60.5 us
  starting transfers between devices: 22.5 us -> 55.4 us
  waiting for transfers between devices: 15.2 us -> 12 us
  local copies, waits for them, and re-layouts: 3.13 us -> 0.01 us
    pallas_call x2, Pallas kernels: 0.04 us -> 34 us  [relay(): call(relay_kernel, (kept, kept, token), [SM] + [ANY] * (4 + len(first)),...]
    ppermute x3, starting transfers between devices: 3.41 us -> 33.3 us  [per_device(): send_x = lambda block: lax.ppermute(block, 'grp', pairs(n_grp, 1))]
    all_to_all x1, waiting for transfers between devices: 5.74 us -> 0.01 us  [per_device(): lax.all_to_all(values, 'orb', split_axis=0, concat_axis=0, tiled=True)]
    ppermute x3, waiting for transfers between devices: 2.41 us -> 7.02 us  [per_device(): send_x = lambda block: lax.ppermute(block, 'grp', pairs(n_grp, 1))]
    ppermute x3, waiting for transfers between devices: 0.01 us -> 3.57 us  [per_device(): lax.ppermute(columns[s], 'grp', pairs(n_grp, s))]
    ppermute x3, waiting for transfers between devices: 3.35 us -> 0.01 us  [per_device(): send_y = lambda block: lax.ppermute(block, 'grp', pairs(n_grp, 2))]
    unnamed x10 -> x2, local copies, waits for them, and re-layouts: 3.13 us -> 0.01 us
    all_to_all x1, waiting for transfers between devices: 3.1 us -> 0.01 us  [per_device(): lax.all_to_all(points, 'orb', split_axis=0, concat_axis=0, tiled=True)]
  transfers between devices with their start and end apart: 14 -> 14, of which waited for: 7 -> 7; matrix products, arithmetic and copies ran while one was open for 0% -> 0% of each run, Pallas kernels for 30% -> 29%
where the time goes in v5:
time: 131 us
  Pallas kernels  60.5 us (46%)
  starting transfers between devices  55.4 us (42%)
  waiting for transfers between devices  12 us (9%)
  between operations  2.65 us (2%)
    pallas_call x2, Pallas kernels, relay(): call(relay_kernel, (kept, kept, token), [SM] + [ANY] * (4 + len(first)),...  34 us
    ppermute x3, starting transfers between devices, per_device(): send_x = lambda block: lax.ppermute(block, 'grp', pairs(n_grp, 1))  33.3 us
    ppermute x3, waiting for transfers between devices, per_device(): send_x = lambda block: lax.ppermute(block, 'grp', pairs(n_grp, 1))  7.02 us
    pallas_call x1, Pallas kernels, per_device(): pl.pallas_call(functools.partial(evaluate_kernel, count), grid=(n_orb //...  6.4 us
    pallas_call x1, Pallas kernels, per_device(): call(functools.partial(solve_kernel, count, others), (shape((2 * count, e...  5.65 us
    pallas_call x1, Pallas kernels, per_device(): call(functools.partial(prepare_kernel, count, others, chunks, middle, ste...  5.27 us
    all_to_all x1, starting transfers between devices, per_device(): lax.all_to_all(points, 'orb', split_axis=0, concat_axis=0, tiled=True)  4.88 us
    ppermute x3, starting transfers between devices, per_device(): send_y = lambda block: lax.ppermute(block, 'grp', pairs(n_grp, 2))  4.84 us
  transfers between devices with their start and end apart: 14, of which 7 were waited for; matrix products, arithmetic and copies ran while one was open for 0% of the time, Pallas kernels for 29%

profile of v5, /device:TPU:0, one launch (start us, length us, event | category | flops | bytes accessed | tf_op | source)
XLA Modules:
  0.0 130.5 jit_solution(14809971084842750578)
XLA Ops:
  1.3 1.7 %shard_map.120 = (f32[8,1024]{1,0:T(8,128)S(1)}, s32[2,128]{1,0:T(2,128)S(1)}, f32[2,8,128]{2,1,0:T(8,128)S(1)}) custom-call(f32[3,1,1024]{2,1,0:T(1,128)} %bitcast.12, s32[2,1,16]{2,1,0:T(1,128)} %moved_hbm.1, f32[6,1,16]{2,1,0:T(1,128)} %bitcast.13, f32[1]{0:T(128)S(6)} %copy.19.weight_ref), custom_call_target="tpu_custom_call" | custom-call | tf_op jit(solution)/shard_map/pallas_call | solution.py:435
  3.0 4.0 %collective-permute-start.2 = (f32[8,1024]{1,0:T(8,128)S(1)}, f32[8,1024]{1,0:T(8,128)S(1)}, u32[]{:S(2)}, u32[]{:S(2)}) collective-permute-start(f32[8,1024]{1,0:T(8,128)S(1)} %get-tuple-element.33.after_ref.refs_0_), channel_id=1, source_target_pairs={{0,24},{8,16},{16,8},{24,0},{1,25},{9,17},{17,9},{25,1},{2,26},{10... | collective-permute-start | bytes 98312 | tf_op jit(solution)/shard_map/ppermute | solution.py:456
  7.0 0.5 collective-permute-start.1
  7.5 0.1 collective-permute-start
  7.6 2.4 %shard_map.121 = (bf16[256,1024]{1,0:T(8,128)(2,1)}, bf16[256,1024]{1,0:T(8,128)(2,1)}) custom-call(f32[1,1024,1024]{2,1,0:T(8,128)} %inverse_hbm.3, f32[8,1024]{1,0:T(8,128)S(1)} %get-tuple-element.33.after_ref.refs_0_), custom_call_target="tpu_custom_call" | custom-call | bytes 3145728 | tf_op jit(solution)/shard_map/pallas_call | solution.py:464
  10.0 0.0 collective-permute-done.2.refs_4_.refs_3_.refs_2_
  10.0 0.8 collective-permute-done.1.refs_3_.refs_2_.refs_1_
  10.9 0.5 collective-permute-done.refs_2_.refs_1_.refs_0_
  11.4 1.5 %collective-permute-start.3 = (bf16[256,1024]{1,0:T(8,128)(2,1)}, bf16[256,1024]{1,0:T(8,128)(2,1)S(1)}, u32[]{:S(2)}, u32[]{:S(2)}) collective-permute-start(bf16[256,1024]{1,0:T(8,128)(2,1)} %get-tuple-element.44.refs_3_), channel_id=1, source_target_pairs={{0,16},{8,24},{16,0},{24,8},{1,17},{9,25},{17,1},{25,9},{2,18},{10... | collective-permute-start | bytes 1572872 | tf_op jit(solution)/shard_map/ppermute | solution.py:527
  12.9 0.6 collective-permute-start.4
  14.8 1.0 shard_map.123
  15.8 4.9 %all-to-all-start = ((f32[8,16,128]{2,1,0:T(8,128)}), f32[8,16,128]{2,1,0:T(8,128)S(1)}, u32[]{:S(2)}, u32[]{:S(2)}) async-start(f32[8,16,128]{2,1,0:T(8,128)} %get-tuple-element.39), calls=%async_computation | async-start | bytes 131072 | tf_op jit(solution)/shard_map/all_to_all | solution.py:493
  20.7 0.0 copy-start
  20.7 5.3 %shard_map.124 = (bf16[2048,640]{1,0:T(8,128)(2,1)S(1)}, bf16[256,1024]{1,0:T(8,128)(2,1)}, bf16[256,1024]{1,0:T(8,128)(2,1)}, bf16[32,1024]{1,0:T(8,128)(2,1)S(...) custom-call(bf16[2048,128]{1,0:T(8,128)(2,1)} %coeff_hbm.1, ...), custom_call_target="tpu_custom_call" | custom-call | flops 270532608 | bytes 8912896 | tf_op jit(solution)/shard_map/pallas_call | solution.py:498
  26.0 1.5 %collective-permute-start.5 = (bf16[32,1024]{1,0:T(8,128)(2,1)S(1)}, bf16[32,1024]{1,0:T(8,128)(2,1)S(1)}, u32[]{:S(2)}, u32[]{:S(2)}) collective-permute-start(bf16[32,1024]{1,0:T(8,128)(2,1)S(1)} %get-tuple-element.46), channel_id=1, source_target_pairs={{0,8},{8,0},{16,24},{24,16},{1,9},{9,1},{17,25},{25,17},{2,10},{10... | collective-permute-start | bytes 196616 | tf_op jit(solution)/shard_map/ppermute | solution.py:521
  27.5 0.5 collective-permute-start.6
  28.0 1.6 %collective-permute-start.7 = (bf16[32,1024]{1,0:T(8,128)(2,1)S(1)}, bf16[32,1024]{1,0:T(8,128)(2,1)S(1)}, u32[]{:S(2)}, u32[]{:S(2)}) collective-permute-start(bf16[32,1024]{1,0:T(8,128)(2,1)S(1)} %get-tuple-element.48), channel_id=1, source_target_pairs={{0,24},{8,16},{16,8},{24,0},{1,25},{9,17},{17,9},{25,1},{2,26},{10... | collective-permute-start | bytes 196616 | tf_op jit(solution)/shard_map/ppermute | solution.py:521
  29.6 1.0 collective-permute-done.5.refs_2_.refs_0_
  30.6 1.9 %collective-permute-done.6.refs_3_.refs_1_ = bf16[32,1024]{1,0:T(8,128)(2,1)S(1)} collective-permute-done((bf16[32,1024]{1,0:T(8,128)(2,1)S(1)}, bf16[32,1024]{1,0:T(8,128)(2,1)S(1)}, u32[]{:S(2)}, u32[]{:S(2)}) %collective-permute-start.6) | collective-permute-done | bytes 65568 | tf_op jit(solution)/shard_map/ppermute | solution.py:521
  32.4 0.7 collective-permute-done.7.refs_4_.refs_2_
  33.1 0.0 all-to-all-done.refs_1_.points_ref
  33.1 0.0 collective-permute-done.3.got_a
  33.1 0.0 collective-permute-done.4.got_b
  33.2 17.0 %shard_map.125 = (bf16[256,1024]{1,0:T(8,128)(2,1)}, bf16[256,1024]{1,0:T(8,128)(2,1)}, f32[8,128]{1,0:T(8,128)S(1)}) custom-call(s32[1]{0:T(128)} %bitcast.5.flag_ref, bf16[256,1024]{1,0:T(8,128)(2,1)} %get-tuple-element.42.own_a.own_b.refs_1_, bf16[256,1024]{1,0:T(8,128)(2,1)} %get-tuple-element.43.own_b.own_a.refs_2_, ...), custom_call_target="tpu_custom_call" | custom-call | tf_op jit(solution)/shard_map/pallas_call | solution.py:530
  50.2 1.6 %collective-permute-start.8 = (bf16[256,1024]{1,0:T(8,128)(2,1)}, bf16[256,1024]{1,0:T(8,128)(2,1)S(1)}, u32[]{:S(2)}, u32[]{:S(2)}) collective-permute-start(bf16[256,1024]{1,0:T(8,128)(2,1)} %get-tuple-element.51.refs_4_), channel_id=1, source_target_pairs={{0,16},{8,24},{16,0},{24,8},{1,17},{9,25},{17,1},{25,9},{2,18},{10... | collective-permute-start | bytes 1572872 | tf_op jit(solution)/shard_map/ppermute | solution.py:527
  51.8 16.5 %collective-permute-start.9 = (bf16[256,1024]{1,0:T(8,128)(2,1)}, bf16[256,1024]{1,0:T(8,128)(2,1)}, u32[]{:S(2)}, u32[]{:S(2)}) collective-permute-start(bf16[256,1024]{1,0:T(8,128)(2,1)} %get-tuple-element.52.refs_6_), channel_id=1, source_target_pairs={{0,8},{8,0},{16,24},{24,16},{1,9},{9,1},{17,25},{25,17},{2,10},{10... | collective-permute-start | bytes 1572872 | tf_op jit(solution)/shard_map/ppermute | solution.py:526
  68.3 0.0 copy-done
  68.3 6.4 %shard_map.126 = bf16[8,176,128]{2,1,0:T(8,128)(2,1)} custom-call(f32[8,16,128]{2,1,0:T(8,128)S(1)} %all-to-all-done.refs_1_.points_ref, f32[3,1024]{1,0:T(4,128)S(1)} %copy-done, bf16[2048,640]{1,0:T(8,128)(2,1)S(1)} %get-tuple-element.41.refs_0_.table_ref, f32[8,128]{1,0:T(8,128)S(1)} %get-tuple-element.49.refs_0_), custom_call_target="tpu_custom_call" | custom-call | flops 738197504 | bytes 3145728 | tf_op jit(solution)/shard_map/pallas_call | solution.py:557
  74.7 4.2 %all-to-all-start.1 = ((bf16[8,176,128]{2,1,0:T(8,128)(2,1)}), bf16[8,176,128]{2,1,0:T(8,128)(2,1)S(1)}, u32[]{:S(2)}, u32[]{:S(2)}) async-start(bf16[8,176,128]{2,1,0:T(8,128)(2,1)} %shard_map.126), calls=%async_computation.1 | async-start | bytes 720896 | tf_op jit(solution)/shard_map/all_to_all | solution.py:580
  78.9 0.0 collective-permute-done.8.got_a
  78.9 0.4 collective-permute-done.9.got_b
  79.2 17.0 %shard_map.127 = (bf16[256,1024]{1,0:T(8,128)(2,1)}, bf16[256,1024]{1,0:T(8,128)(2,1)}, f32[8,128]{1,0:T(8,128)S(1)}) custom-call(s32[1]{0:T(128)} %bitcast.5.flag_ref, bf16[256,1024]{1,0:T(8,128)(2,1)} %get-tuple-element.43.own_b.own_a.refs_2_, bf16[256,1024]{1,0:T(8,128)(2,1)} %get-tuple-element.42.own_a.own_b.refs_1_, ...), custom_call_target="tpu_custom_call" | custom-call | tf_op jit(solution)/shard_map/pallas_call | solution.py:530
  96.3 1.7 %collective-permute-start.11 = (bf16[256,1024]{1,0:T(8,128)(2,1)}, bf16[256,1024]{1,0:T(8,128)(2,1)S(1)}, u32[]{:S(2)}, u32[]{:S(2)}) collective-permute-start(bf16[256,1024]{1,0:T(8,128)(2,1)} %get-tuple-element.57.refs_5_), channel_id=1, source_target_pairs={{0,16},{8,24},{16,0},{24,8},{1,17},{9,25},{17,1},{25,9},{2,18},{10... | collective-permute-start | bytes 1572872 | tf_op jit(solution)/shard_map/ppermute | solution.py:527
  98.0 16.2 %collective-permute-start.10 = (bf16[256,1024]{1,0:T(8,128)(2,1)}, bf16[256,1024]{1,0:T(8,128)(2,1)S(1)}, u32[]{:S(2)}, u32[]{:S(2)}) collective-permute-start(bf16[256,1024]{1,0:T(8,128)(2,1)} %get-tuple-element.58.refs_7_), channel_id=1, source_target_pairs={{0,8},{8,0},{16,24},{24,16},{1,9},{9,1},{17,25},{25,17},{2,10},{10... | collective-permute-start | bytes 1572872 | tf_op jit(solution)/shard_map/ppermute | solution.py:526
  114.1 0.0 all-to-all-done.1.vals_ref
  114.2 5.7 %shard_map.128 = (bf16[32,1024]{1,0:T(8,128)(2,1)S(1)}, bf16[32,1024]{1,0:T(8,128)(2,1)S(1)}, f32[32,32]{1,0:T(8,128)S(1)}, f32[6,1,16]{2,1,0:T(1,128)}, f32[2,1,16]{2,1,0:T(1,128)}, /*index=5*/f32[1,128]{1,0:T(1,128)}) custom-call(s32[1]{0:T(128)} %bitcast.2.role_ref, bf16[8,176,128]{2,1,0:T(8,128)(2,1)S(1)} %all-to-all-done.1.vals_ref, ...), custom_call_target="tpu_custom_call" | custom-call | flops 8388608 | bytes 720896 | tf_op jit(solution)/shard_map/pallas_call | solution.py:584
  119.8 0.0 collective-permute-done.11.refs_9_
  119.8 6.7 %collective-permute-done.10.refs_8_ = bf16[256,1024]{1,0:T(8,128)(2,1)S(1)} collective-permute-done((bf16[256,1024]{1,0:T(8,128)(2,1)}, bf16[256,1024]{1,0:T(8,128)(2,1)S(1)}, u32[]{:S(2)}, u32[]{:S(2)}) %collective-permute-start.10) | collective-permute-done | bytes 524320 | tf_op jit(solution)/shard_map/ppermute | solution.py:526
  126.5 4.0 %shard_map.129 = f32[1024,1024]{1,0:T(8,128)} custom-call(s32[1]{0:T(128)} %bitcast.2.role_ref, bf16[32,1024]{1,0:T(8,128)(2,1)S(1)} %get-tuple-element.54.change_ref, bf16[32,1024]{1,0:T(8,128)(2,1)S(1)} %get-tuple-element.55.cols_ref, f32[32,32]{1,0:T(8,128)S(1)} %get-tuple-element.56.inv_ref, bf16[256,1024]{1,0:T(8,128)(2,1)} %get-tuple-element.45.refs_0_, ...), custom_call_target="tpu_custom_call" | custom-call | flops 134217728 | bytes 6291456 | tf_op jit(solution)/shard_map/pallas_call | solution.py:601
  (1 shorter events, 0.0 us)
Async XLA Ops:
  3.0 7.0 %collective-permute-start.2 = (f32[8,1024]{1,0:T(8,128)S(1)}, f32[8,1024]{1,0:T(8,128)S(1)}, u32[]{:S(2)}, u32[]{:S(2)}) collective-permute-start(f32[8,1024]{1,0:T(8,128)S(1)} %get-tuple-element.33.after_ref.refs_0_), channel_id=1, source_target_pairs={{0,24},{8,16},{16,8},{24,0},{1,25},{9,17},{17,9},{25,1},{2,26},{10... | collective-permute-start | bytes 98312 | tf_op jit(solution)/shard_map/ppermute | solution.py:456
  7.0 3.9 %collective-permute-start.1 = (f32[8,1024]{1,0:T(8,128)S(1)}, f32[8,1024]{1,0:T(8,128)S(1)}, u32[]{:S(2)}, u32[]{:S(2)}) collective-permute-start(f32[8,1024]{1,0:T(8,128)S(1)} %get-tuple-element.33.after_ref.refs_0_), channel_id=1, source_target_pairs={{0,16},{8,24},{16,0},{24,8},{1,17},{9,25},{17,1},{25,9},{2,18},{10... | collective-permute-start | bytes 98312 | tf_op jit(solution)/shard_map/ppermute | solution.py:456
  7.5 3.9 %collective-permute-start = (f32[8,1024]{1,0:T(8,128)S(1)}, f32[8,1024]{1,0:T(8,128)S(1)}, u32[]{:S(2)}, u32[]{:S(2)}) collective-permute-start(f32[8,1024]{1,0:T(8,128)S(1)} %get-tuple-element.33.after_ref.refs_0_), channel_id=1, source_target_pairs={{0,8},{8,0},{16,24},{24,16},{1,9},{9,1},{17,25},{25,17},{2,10},{10... | collective-permute-start | bytes 98312 | tf_op jit(solution)/shard_map/ppermute | solution.py:456
  11.4 21.8 %collective-permute-start.3 = (bf16[256,1024]{1,0:T(8,128)(2,1)}, bf16[256,1024]{1,0:T(8,128)(2,1)S(1)}, u32[]{:S(2)}, u32[]{:S(2)}) collective-permute-start(bf16[256,1024]{1,0:T(8,128)(2,1)} %get-tuple-element.44.refs_3_), channel_id=1, source_target_pairs={{0,16},{8,24},{16,0},{24,8},{1,17},{9,25},{17,1},{25,9},{2,18},{10... | collective-permute-start | bytes 1572872 | tf_op jit(solution)/shard_map/ppermute | solution.py:527
  12.9 20.2 %collective-permute-start.4 = (bf16[256,1024]{1,0:T(8,128)(2,1)}, bf16[256,1024]{1,0:T(8,128)(2,1)}, u32[]{:S(2)}, u32[]{:S(2)}) collective-permute-start(bf16[256,1024]{1,0:T(8,128)(2,1)} %get-tuple-element.45.refs_0_), channel_id=1, source_target_pairs={{0,8},{8,0},{16,24},{24,16},{1,9},{9,1},{17,25},{25,17},{2,10},{10... | collective-permute-start | bytes 1572872 | tf_op jit(solution)/shard_map/ppermute | solution.py:526
  15.8 17.3 %all-to-all-start = ((f32[8,16,128]{2,1,0:T(8,128)}), f32[8,16,128]{2,1,0:T(8,128)S(1)}, u32[]{:S(2)}, u32[]{:S(2)}) async-start(f32[8,16,128]{2,1,0:T(8,128)} %get-tuple-element.39), calls=%async_computation | async-start | bytes 131072 | tf_op jit(solution)/shard_map/all_to_all | solution.py:493
  20.7 47.5 %copy-start = (f32[3,1024]{1,0:T(4,128)S(1)}, f32[3,1024]{1,0:T(4,128)}, u32[]{:S(2)}) copy-start(f32[3,1024]{1,0:T(4,128)} %wave_ref.1) | copy-start | bytes 36868
  26.0 4.6 %collective-permute-start.5 = (bf16[32,1024]{1,0:T(8,128)(2,1)S(1)}, bf16[32,1024]{1,0:T(8,128)(2,1)S(1)}, u32[]{:S(2)}, u32[]{:S(2)}) collective-permute-start(bf16[32,1024]{1,0:T(8,128)(2,1)S(1)} %get-tuple-element.46), channel_id=1, source_target_pairs={{0,8},{8,0},{16,24},{24,16},{1,9},{9,1},{17,25},{25,17},{2,10},{10... | collective-permute-start | bytes 196616 | tf_op jit(solution)/shard_map/ppermute | solution.py:521
  27.5 5.0 %collective-permute-start.6 = (bf16[32,1024]{1,0:T(8,128)(2,1)S(1)}, bf16[32,1024]{1,0:T(8,128)(2,1)S(1)}, u32[]{:S(2)}, u32[]{:S(2)}) collective-permute-start(bf16[32,1024]{1,0:T(8,128)(2,1)S(1)} %get-tuple-element.47), channel_id=1, source_target_pairs={{0,16},{8,24},{16,0},{24,8},{1,17},{9,25},{17,1},{25,9},{2,18},{10... | collective-permute-start | bytes 196616 | tf_op jit(solution)/shard_map/ppermute | solution.py:521
  28.0 5.2 %collective-permute-start.7 = (bf16[32,1024]{1,0:T(8,128)(2,1)S(1)}, bf16[32,1024]{1,0:T(8,128)(2,1)S(1)}, u32[]{:S(2)}, u32[]{:S(2)}) collective-permute-start(bf16[32,1024]{1,0:T(8,128)(2,1)S(1)} %get-tuple-element.48), channel_id=1, source_target_pairs={{0,24},{8,16},{16,8},{24,0},{1,25},{9,17},{17,9},{25,1},{2,26},{10... | collective-permute-start | bytes 196616 | tf_op jit(solution)/shard_map/ppermute | solution.py:521
  50.2 28.7 %collective-permute-start.8 = (bf16[256,1024]{1,0:T(8,128)(2,1)}, bf16[256,1024]{1,0:T(8,128)(2,1)S(1)}, u32[]{:S(2)}, u32[]{:S(2)}) collective-permute-start(bf16[256,1024]{1,0:T(8,128)(2,1)} %get-tuple-element.51.refs_4_), channel_id=1, source_target_pairs={{0,16},{8,24},{16,0},{24,8},{1,17},{9,25},{17,1},{25,9},{2,18},{10... | collective-permute-start | bytes 1572872 | tf_op jit(solution)/shard_map/ppermute | solution.py:527
  51.8 27.5 %collective-permute-start.9 = (bf16[256,1024]{1,0:T(8,128)(2,1)}, bf16[256,1024]{1,0:T(8,128)(2,1)}, u32[]{:S(2)}, u32[]{:S(2)}) collective-permute-start(bf16[256,1024]{1,0:T(8,128)(2,1)} %get-tuple-element.52.refs_6_), channel_id=1, source_target_pairs={{0,8},{8,0},{16,24},{24,16},{1,9},{9,1},{17,25},{25,17},{2,10},{10... | collective-permute-start | bytes 1572872 | tf_op jit(solution)/shard_map/ppermute | solution.py:526
  74.7 39.5 %all-to-all-start.1 = ((bf16[8,176,128]{2,1,0:T(8,128)(2,1)}), bf16[8,176,128]{2,1,0:T(8,128)(2,1)S(1)}, u32[]{:S(2)}, u32[]{:S(2)}) async-start(bf16[8,176,128]{2,1,0:T(8,128)(2,1)} %shard_map.126), calls=%async_computation.1 | async-start | bytes 720896 | tf_op jit(solution)/shard_map/all_to_all | solution.py:580
  96.3 23.6 %collective-permute-start.11 = (bf16[256,1024]{1,0:T(8,128)(2,1)}, bf16[256,1024]{1,0:T(8,128)(2,1)S(1)}, u32[]{:S(2)}, u32[]{:S(2)}) collective-permute-start(bf16[256,1024]{1,0:T(8,128)(2,1)} %get-tuple-element.57.refs_5_), channel_id=1, source_target_pairs={{0,16},{8,24},{16,0},{24,8},{1,17},{9,25},{17,1},{25,9},{2,18},{10... | collective-permute-start | bytes 1572872 | tf_op jit(solution)/shard_map/ppermute | solution.py:527
  98.0 28.5 %collective-permute-start.10 = (bf16[256,1024]{1,0:T(8,128)(2,1)}, bf16[256,1024]{1,0:T(8,128)(2,1)S(1)}, u32[]{:S(2)}, u32[]{:S(2)}) collective-permute-start(bf16[256,1024]{1,0:T(8,128)(2,1)} %get-tuple-element.58.refs_7_), channel_id=1, source_target_pairs={{0,8},{8,0},{16,24},{24,16},{1,9},{9,1},{17,25},{25,17},{2,10},{10... | collective-permute-start | bytes 1572872 | tf_op jit(solution)/shard_map/ppermute | solution.py:526

commit v6 on v5

--- a/solution.py
+++ b/solution.py
@@ -157,19 +157,28 @@
 
 
 def relay_kernel(flag_ref, own_a, own_b, got_a, got_b, *refs):
-    out_a, out_b, token_ref, sems = refs[-4:]
-    for here, pair in ((True, (own_a, own_b)), (False, (got_a, got_b))):
-
-        @pl.when((flag_ref[0] == 0) == here)
-        def _():
-            copies = [
-                pltpu.make_async_copy(pair[0], out_a, sems.at[0]),
-                pltpu.make_async_copy(pair[1], out_b, sems.at[1]),
-            ]
-            for copy in copies:
-                copy.start()
-            for copy in copies:
-                copy.wait()
+    out_a, out_b, token_ref, staged, in_sem, out_sem = refs[-6:]
+    pieces, depth, _ = staged.shape
+
+    @pl.when(flag_ref[0] == 0)
+    def _():
+        loads, stores = [], []
+        for piece in range(pieces):
+            own, out = (own_a, out_a) if piece < pieces // 2 else (own_b, out_b)
+            rows = pl.ds(piece % (pieces // 2) * depth, depth)
+            loads.append(
+                pltpu.make_async_copy(own.at[rows], staged.at[piece], in_sem.at[piece])
+            )
+            stores.append(
+                pltpu.make_async_copy(staged.at[piece], out.at[rows], out_sem.at[piece])
+            )
+        for load in loads:
+            load.start()
+        for load, store in zip(loads, stores):
+            load.wait()
+            store.start()
+        for store in stores:
+            store.wait()
 
     token_ref[...] = jnp.zeros(token_ref.shape, F32)
 
@@ -456,7 +465,7 @@
     records = [lax.ppermute(record, "grp", pairs(n_grp, s)) for s in range(1, n_grp)]
 
     depth = electrons // chunks
-    kept = pltpu.HBM((depth, electrons), BF16)
+    kept = shape((depth, electrons), BF16)
     token = shape((8, LANES), F32)
     own = [None] * chunks
     ends = (0, chunks - 1)
@@ -465,7 +474,7 @@
         functools.partial(round_kernel, ends),
         (kept,) * 2,
         [HBM, ANY],
-        (HBM,) * 2,
+        (ANY,) * 2,
         scratch=[
             pltpu.VMEM((2, depth, electrons), F32),
             pltpu.VMEM((2, depth, electrons), BF16),
@@ -482,7 +491,7 @@
         (ANY, ANY, VM),
         aliases={0: 0, 1: 1},
         vmem=1,
-    )(*in_hbm(own[0], own[-1]), *records)
+    )(own[0], own[-1], *records)
 
     points, weight = call(
         functools.partial(points_kernel, count, others),
@@ -498,10 +507,10 @@
     derived, *prepared = call(
         functools.partial(prepare_kernel, count, others, chunks, middle, steps),
         (shape((plane, 5 * width), BF16),)
-        + (kept,) * len(middle)
+        + (pltpu.HBM((depth, electrons), BF16),) * len(middle)
         + tuple(shape((2 * count, electrons), BF16) for _ in steps),
         [HBM, HBM, HBM] + [VM] * (1 + others) + [ANY],
-        (VM,) + (HBM,) * len(middle) + (VM,) * len(steps),
+        (VM,) + (ANY,) * len(middle) + (VM,) * len(steps),
         scratch=[
             pltpu.VMEM((plane, width), BF16),
             pltpu.VMEM(wavevectors.shape, F32),
@@ -531,9 +540,14 @@
                 relay_kernel,
                 (kept, kept, token),
                 [SM] + [ANY] * (4 + len(first)),
-                (HBM, HBM, VM),
-                scratch=[pltpu.SemaphoreType.DMA((2,))],
-                vmem=1,
+                (ANY, ANY, VM),
+                scratch=[
+                    pltpu.VMEM((4, depth // 2, electrons), BF16),
+                    pltpu.SemaphoreType.DMA((4,)),
+                    pltpu.SemaphoreType.DMA((4,)),
+                ],
+                aliases={3: 0, 4: 1},
+                vmem=2,
             )(apart, *in_hbm(*mine), *got, *first)
 
         x1, y1 = send_x(own[0]), send_y(own[3])
@@ -542,12 +556,10 @@
         y2, x2, token_2 = relay((own[2], own[1]), (y2, x2), ())
         x3, y3 = send_x(y2), send_y(x2)
         arrays += [x1, x2, y1, y2, x3, y3]
-        settled = len(arrays) - 2
         a1, a2, b1, b2, a3, b3 = range(chunks, chunks + 6)
         table = [range(chunks), (a1, a2, a3, b3), (a3, b3, b2, b1), (b2, b3, a3, a2)]
     else:
         token_1 = token_2 = jnp.zeros((8, LANES), F32)
-        settled = chunks
         table = [range(chunks)]
         for step in range(1, n_grp):
             table.append(range(len(arrays), len(arrays) + chunks))
@@ -569,7 +581,7 @@
             pltpu.VMEM((block * 3 * count, plane), BF16),
             pltpu.VMEM((block * 2 * count, plane), BF16),
         ],
-        compiler_params=pltpu.CompilerParams(vmem_limit_bytes=16 * MIB),
+        compiler_params=pltpu.CompilerParams(vmem_limit_bytes=8 * MIB),
         cost_estimate=pl.CostEstimate(
             flops=2 * n_orb * count * plane * width * 11,
             bytes_accessed=12 * plane * width,
@@ -612,7 +624,7 @@
         flops=4 * electrons * electrons * 2 * count,
         moved=6 * electrons * electrons,
         vmem=12,
-    )(role, change, cols, small, *in_hbm(*arrays[:settled]), *arrays[settled:])
+    )(role, change, cols, small, *in_hbm(*own), *arrays[chunks:])
 
     return updated[None], drift.reshape(2, 1, 3, count), laplacian, new_weight[0, :1]
 

time: 131 us -> 70.3 us (0.54)
  Pallas kernels: 60.5 us -> 26.8 us
  starting transfers between devices: 55.4 us -> 27.9 us
    pallas_call x2, Pallas kernels: 34 us -> 0.17 us  [relay(): call(relay_kernel, (kept, kept, token), [SM] + [ANY] * (4 + len(first)),...]
    ppermute x3, starting transfers between devices: 33.3 us -> 5.69 us  [per_device(): send_x = lambda block: lax.ppermute(block, 'grp', pairs(n_grp, 1))]
    all_to_all x1, waiting for transfers between devices: 0.01 us -> 7.65 us  [per_device(): lax.all_to_all(values, 'orb', split_axis=0, concat_axis=0, tiled=True)]
    ppermute x3, waiting for transfers between devices: 7.02 us -> 0.01 us  [per_device(): send_x = lambda block: lax.ppermute(block, 'grp', pairs(n_grp, 1))]
  transfers between devices with their start and end apart: 14 -> 14, of which waited for: 7 -> 6; matrix products, arithmetic and copies ran while one was open for 0% -> 0% of each run, Pallas kernels for 29% -> 30%
where the time goes in v6:
time: 70.3 us; the launch traced here: 69.9 us
  starting transfers between devices  27.9 us (40%)
  Pallas kernels  26.8 us (38%)
  waiting for transfers between devices  12.6 us (18%)
  between operations  2.65 us (4%)
    all_to_all x1, waiting for transfers between devices, per_device(): lax.all_to_all(values, 'orb', split_axis=0, concat_axis=0, tiled=True)  7.65 us
    pallas_call x1, Pallas kernels, per_device(): pl.pallas_call(functools.partial(evaluate_kernel, count), grid=(n_orb //...  6.4 us
    ppermute x3, starting transfers between devices, per_device(): send_x = lambda block: lax.ppermute(block, 'grp', pairs(n_grp, 1))  5.69 us
    pallas_call x1, Pallas kernels, per_device(): call(functools.partial(solve_kernel, count, others), (shape((2 * count, e...  5.65 us
    pallas_call x1, Pallas kernels, per_device(): call(functools.partial(prepare_kernel, count, others, chunks, middle, ste...  5.27 us
    all_to_all x1, starting transfers between devices, per_device(): lax.all_to_all(points, 'orb', split_axis=0, concat_axis=0, tiled=True)  4.88 us
    ppermute x3, starting transfers between devices, per_device(): send_y = lambda block: lax.ppermute(block, 'grp', pairs(n_grp, 2))  4.69 us
    ppermute x3, starting transfers between devices, per_device(): lax.ppermute(record, 'grp', pairs(n_grp, s))  4.6 us
  transfers between devices with their start and end apart: 14, of which 6 were waited for; matrix products, arithmetic and copies ran while one was open for 0% of the time, Pallas kernels for 30%

profile of v6, /device:TPU:0, one launch (start us, length us, event | category | flops | bytes accessed | tf_op | source)
XLA Modules:
  0.0 69.9 jit_solution(16455618280450651813)
XLA Ops:
  1.3 1.7 %shard_map.120 = (f32[8,1024]{1,0:T(8,128)S(1)}, s32[2,128]{1,0:T(2,128)S(1)}, f32[2,8,128]{2,1,0:T(8,128)S(1)}) custom-call(f32[3,1,1024]{2,1,0:T(1,128)} %bitcast.12, s32[2,1,16]{2,1,0:T(1,128)} %moved_hbm.1, f32[6,1,16]{2,1,0:T(1,128)} %bitcast.13, f32[1]{0:T(128)S(6)} %copy.27.weight_ref), custom_call_target="tpu_custom_call" | custom-call | tf_op jit(solution)/shard_map/pallas_call | solution.py:444
  3.0 4.0 %collective-permute-start.2 = (f32[8,1024]{1,0:T(8,128)S(1)}, f32[8,1024]{1,0:T(8,128)S(1)}, u32[]{:S(2)}, u32[]{:S(2)}) collective-permute-start(f32[8,1024]{1,0:T(8,128)S(1)} %get-tuple-element.33.after_ref.refs_0_), channel_id=1, source_target_pairs={{0,24},{8,16},{16,8},{24,0},{1,25},{9,17},{17,9},{25,1},{2,26},{10... | collective-permute-start | bytes 98312 | tf_op jit(solution)/shard_map/ppermute | solution.py:465
  7.0 0.5 collective-permute-start.1
  7.5 0.1 collective-permute-start
  7.6 2.4 %shard_map.121 = (bf16[256,1024]{1,0:T(8,128)(2,1)}, bf16[256,1024]{1,0:T(8,128)(2,1)}) custom-call(f32[1,1024,1024]{2,1,0:T(8,128)} %inverse_hbm.3, f32[8,1024]{1,0:T(8,128)S(1)} %get-tuple-element.33.after_ref.refs_0_), custom_call_target="tpu_custom_call" | custom-call | bytes 3145728 | tf_op jit(solution)/shard_map/pallas_call | solution.py:473
  10.0 0.0 collective-permute-done.2.refs_4_.refs_3_.refs_2_
  10.0 0.8 %collective-permute-done.1.refs_3_.refs_2_.refs_1_ = f32[8,1024]{1,0:T(8,128)S(1)} collective-permute-done((f32[8,1024]{1,0:T(8,128)S(1)}, f32[8,1024]{1,0:T(8,128)S(1)}, u32[]{:S(2)}, u32[]{:S(2)}) %collective-permute-start.1) | collective-permute-done | bytes 32800 | tf_op jit(solution)/shard_map/ppermute | solution.py:465
  10.9 0.5 collective-permute-done.refs_2_.refs_1_.refs_0_
  11.4 1.5 %collective-permute-start.3 = (bf16[256,1024]{1,0:T(8,128)(2,1)}, bf16[256,1024]{1,0:T(8,128)(2,1)S(1)}, u32[]{:S(2)}, u32[]{:S(2)}) collective-permute-start(bf16[256,1024]{1,0:T(8,128)(2,1)} %get-tuple-element.44.refs_3_), channel_id=1, source_target_pairs={{0,16},{8,24},{16,0},{24,8},{1,17},{9,25},{17,1},{25,9},{2,18},{10... | collective-permute-start | bytes 1572872 | tf_op jit(solution)/shard_map/ppermute | solution.py:536
  12.9 0.6 collective-permute-start.4
  14.9 1.0 %shard_map.123 = (f32[8,16,128]{2,1,0:T(8,128)}, f32[1,128]{1,0:T(1,128)S(1)}) custom-call(s32[1]{0:T(128)} %bitcast.2.role_ref, f32[8,1024]{1,0:T(8,128)S(1)} %get-tuple-element.33.after_ref.refs_0_, f32[8,1024]{1,0:T(8,128)S(1)} %collective-permute-done.refs_2_.refs_1_.refs_0_, f32[8,1024]{1,0:T(8,128)S(1)} %collective-permute-done.1.refs_3_.refs_2_.refs_1_, ...), custom_call_target="tpu_custom_call" | custom-call | tf_op jit(solution)/shard_map/pallas_call | solution.py:496
  15.9 4.9 %all-to-all-start = ((f32[8,16,128]{2,1,0:T(8,128)}), f32[8,16,128]{2,1,0:T(8,128)S(1)}, u32[]{:S(2)}, u32[]{:S(2)}) async-start(f32[8,16,128]{2,1,0:T(8,128)} %get-tuple-element.39), calls=%async_computation | async-start | bytes 131072 | tf_op jit(solution)/shard_map/all_to_all | solution.py:502
  20.7 0.0 copy-start
  20.7 5.3 %shard_map.124 = (bf16[2048,640]{1,0:T(8,128)(2,1)S(1)}, bf16[256,1024]{1,0:T(8,128)(2,1)}, bf16[256,1024]{1,0:T(8,128)(2,1)}, bf16[32,1024]{1,0:T(8,128)(2,1)S(...) custom-call(bf16[2048,128]{1,0:T(8,128)(2,1)} %coeff_hbm.1, ...), custom_call_target="tpu_custom_call" | custom-call | flops 270532608 | bytes 8912896 | tf_op jit(solution)/shard_map/pallas_call | solution.py:507
  26.0 1.4 %collective-permute-start.5 = (bf16[32,1024]{1,0:T(8,128)(2,1)S(1)}, bf16[32,1024]{1,0:T(8,128)(2,1)S(1)}, u32[]{:S(2)}, u32[]{:S(2)}) collective-permute-start(bf16[32,1024]{1,0:T(8,128)(2,1)S(1)} %get-tuple-element.46), channel_id=1, source_target_pairs={{0,8},{8,0},{16,24},{24,16},{1,9},{9,1},{17,25},{25,17},{2,10},{10... | collective-permute-start | bytes 196616 | tf_op jit(solution)/shard_map/ppermute | solution.py:530
  27.5 0.5 collective-permute-start.6
  28.0 1.6 %collective-permute-start.7 = (bf16[32,1024]{1,0:T(8,128)(2,1)S(1)}, bf16[32,1024]{1,0:T(8,128)(2,1)S(1)}, u32[]{:S(2)}, u32[]{:S(2)}) collective-permute-start(bf16[32,1024]{1,0:T(8,128)(2,1)S(1)} %get-tuple-element.48), channel_id=1, source_target_pairs={{0,24},{8,16},{16,8},{24,0},{1,25},{9,17},{17,9},{25,1},{2,26},{10... | collective-permute-start | bytes 196616 | tf_op jit(solution)/shard_map/ppermute | solution.py:530
  29.6 1.0 %collective-permute-done.5.refs_2_.refs_0_ = bf16[32,1024]{1,0:T(8,128)(2,1)S(1)} collective-permute-done((bf16[32,1024]{1,0:T(8,128)(2,1)S(1)}, bf16[32,1024]{1,0:T(8,128)(2,1)S(1)}, u32[]{:S(2)}, u32[]{:S(2)}) %collective-permute-start.5) | collective-permute-done | bytes 65568 | tf_op jit(solution)/shard_map/ppermute | solution.py:530
  30.6 1.8 %collective-permute-done.6.refs_3_.refs_1_ = bf16[32,1024]{1,0:T(8,128)(2,1)S(1)} collective-permute-done((bf16[32,1024]{1,0:T(8,128)(2,1)S(1)}, bf16[32,1024]{1,0:T(8,128)(2,1)S(1)}, u32[]{:S(2)}, u32[]{:S(2)}) %collective-permute-start.6) | collective-permute-done | bytes 65568 | tf_op jit(solution)/shard_map/ppermute | solution.py:530
  32.4 0.7 %collective-permute-done.7.refs_4_.refs_2_ = bf16[32,1024]{1,0:T(8,128)(2,1)S(1)} collective-permute-done((bf16[32,1024]{1,0:T(8,128)(2,1)S(1)}, bf16[32,1024]{1,0:T(8,128)(2,1)S(1)}, u32[]{:S(2)}, u32[]{:S(2)}) %collective-permute-start.7) | collective-permute-done | bytes 65568 | tf_op jit(solution)/shard_map/ppermute | solution.py:530
  33.1 0.0 all-to-all-done.refs_1_.points_ref
  33.1 0.0 collective-permute-done.3.got_a
  33.1 0.0 collective-permute-done.4.got_b
  33.2 0.1 shard_map.125
  33.2 1.6 %collective-permute-start.8 = (bf16[256,1024]{1,0:T(8,128)(2,1)}, bf16[256,1024]{1,0:T(8,128)(2,1)}, u32[]{:S(2)}, u32[]{:S(2)}) collective-permute-start(bf16[256,1024]{1,0:T(8,128)(2,1)} %get-tuple-element.51.refs_4_), channel_id=1, source_target_pairs={{0,16},{8,24},{16,0},{24,8},{1,17},{9,25},{17,1},{25,9},{2,18},{10... | collective-permute-start | bytes 1572872 | tf_op jit(solution)/shard_map/ppermute | solution.py:536
  34.8 2.5 %collective-permute-start.9 = (bf16[256,1024]{1,0:T(8,128)(2,1)S(1)}, bf16[256,1024]{1,0:T(8,128)(2,1)}, u32[]{:S(2)}, u32[]{:S(2)}) collective-permute-start(bf16[256,1024]{1,0:T(8,128)(2,1)S(1)} %get-tuple-element.52.refs_6_), channel_id=1, source_target_pairs={{0,8},{8,0},{16,24},{24,16},{1,9},{9,1},{17,25},{25,17},{2,10},{10... | collective-permute-start | bytes 1572872 | tf_op jit(solution)/shard_map/ppermute | solution.py:535
  37.4 0.0 copy-done
  37.4 6.4 %shard_map.126 = bf16[8,176,128]{2,1,0:T(8,128)(2,1)} custom-call(f32[8,16,128]{2,1,0:T(8,128)S(1)} %all-to-all-done.refs_1_.points_ref, f32[3,1024]{1,0:T(4,128)S(1)} %copy-done, bf16[2048,640]{1,0:T(8,128)(2,1)S(1)} %get-tuple-element.41.refs_0_.table_ref, f32[8,128]{1,0:T(8,128)S(1)} %get-tuple-element.49.refs_0_), custom_call_target="tpu_custom_call" | custom-call | flops 738197504 | bytes 3145728 | tf_op jit(solution)/shard_map/pallas_call | solution.py:569
  43.8 4.5 %all-to-all-start.1 = ((bf16[8,176,128]{2,1,0:T(8,128)(2,1)}), bf16[8,176,128]{2,1,0:T(8,128)(2,1)S(1)}, u32[]{:S(2)}, u32[]{:S(2)}) async-start(bf16[8,176,128]{2,1,0:T(8,128)(2,1)} %shard_map.126), calls=%async_computation.1 | async-start | bytes 720896 | tf_op jit(solution)/shard_map/all_to_all | solution.py:592
  48.2 0.0 collective-permute-done.8.got_a
  48.2 0.0 collective-permute-done.9.got_b
  48.3 0.1 shard_map.127
  48.3 1.6 %collective-permute-start.11 = (bf16[256,1024]{1,0:T(8,128)(2,1)}, bf16[256,1024]{1,0:T(8,128)(2,1)S(1)}, u32[]{:S(2)}, u32[]{:S(2)}) collective-permute-start(bf16[256,1024]{1,0:T(8,128)(2,1)} %get-tuple-element.57.refs_5_), channel_id=1, source_target_pairs={{0,16},{8,24},{16,0},{24,8},{1,17},{9,25},{17,1},{25,9},{2,18},{10... | collective-permute-start | bytes 1572872 | tf_op jit(solution)/shard_map/ppermute | solution.py:536
  49.9 2.5 %collective-permute-start.10 = (bf16[256,1024]{1,0:T(8,128)(2,1)}, bf16[256,1024]{1,0:T(8,128)(2,1)S(1)}, u32[]{:S(2)}, u32[]{:S(2)}) collective-permute-start(bf16[256,1024]{1,0:T(8,128)(2,1)} %get-tuple-element.58.refs_7_), channel_id=1, source_target_pairs={{0,8},{8,0},{16,24},{24,16},{1,9},{9,1},{17,25},{25,17},{2,10},{10... | collective-permute-start | bytes 1572872 | tf_op jit(solution)/shard_map/ppermute | solution.py:535
  52.4 7.6 %all-to-all-done.1.vals_ref = bf16[8,176,128]{2,1,0:T(8,128)(2,1)S(1)} async-done(((bf16[8,176,128]{2,1,0:T(8,128)(2,1)}), bf16[8,176,128]{2,1,0:T(8,128)(2,1)S(1)}, u32[]{:S(2)}, u32[]{:S(2)}) %all-to-all-start.1) | async-done | bytes 360480 | tf_op jit(solution)/shard_map/all_to_all | solution.py:592
  60.1 5.7 %shard_map.128 = (bf16[32,1024]{1,0:T(8,128)(2,1)S(1)}, bf16[32,1024]{1,0:T(8,128)(2,1)S(1)}, f32[32,32]{1,0:T(8,128)S(1)}, f32[6,1,16]{2,1,0:T(1,128)}, f32[2,1,16]{2,1,0:T(1,128)}, /*index=5*/f32[1,128]{1,0:T(1,128)}) custom-call(s32[1]{0:T(128)} %bitcast.2.role_ref, bf16[8,176,128]{2,1,0:T(8,128)(2,1)S(1)} %all-to-all-done.1.vals_ref, ...), custom_call_target="tpu_custom_call" | custom-call | flops 8388608 | bytes 720896 | tf_op jit(solution)/shard_map/pallas_call | solution.py:596
  65.7 0.0 collective-permute-done.11.refs_9_
  65.7 0.0 collective-permute-done.10.refs_8_
  65.7 4.2 %shard_map.129 = f32[1024,1024]{1,0:T(8,128)} custom-call(s32[1]{0:T(128)} %bitcast.2.role_ref, bf16[32,1024]{1,0:T(8,128)(2,1)S(1)} %get-tuple-element.54.change_ref, bf16[32,1024]{1,0:T(8,128)(2,1)S(1)} %get-tuple-element.55.cols_ref, f32[32,32]{1,0:T(8,128)S(1)} %get-tuple-element.56.inv_ref, bf16[256,1024]{1,0:T(8,128)(2,1)} %get-tuple-element.45.refs_0_, ...), custom_call_target="tpu_custom_call" | custom-call | flops 134217728 | bytes 6291456 | tf_op jit(solution)/shard_map/pallas_call | solution.py:613
  (1 shorter events, 0.0 us)
Async XLA Ops:
  3.0 7.0 %collective-permute-start.2 = (f32[8,1024]{1,0:T(8,128)S(1)}, f32[8,1024]{1,0:T(8,128)S(1)}, u32[]{:S(2)}, u32[]{:S(2)}) collective-permute-start(f32[8,1024]{1,0:T(8,128)S(1)} %get-tuple-element.33.after_ref.refs_0_), channel_id=1, source_target_pairs={{0,24},{8,16},{16,8},{24,0},{1,25},{9,17},{17,9},{25,1},{2,26},{10... | collective-permute-start | bytes 98312 | tf_op jit(solution)/shard_map/ppermute | solution.py:465
  7.0 3.9 %collective-permute-start.1 = (f32[8,1024]{1,0:T(8,128)S(1)}, f32[8,1024]{1,0:T(8,128)S(1)}, u32[]{:S(2)}, u32[]{:S(2)}) collective-permute-start(f32[8,1024]{1,0:T(8,128)S(1)} %get-tuple-element.33.after_ref.refs_0_), channel_id=1, source_target_pairs={{0,16},{8,24},{16,0},{24,8},{1,17},{9,25},{17,1},{25,9},{2,18},{10... | collective-permute-start | bytes 98312 | tf_op jit(solution)/shard_map/ppermute | solution.py:465
  7.5 3.9 %collective-permute-start = (f32[8,1024]{1,0:T(8,128)S(1)}, f32[8,1024]{1,0:T(8,128)S(1)}, u32[]{:S(2)}, u32[]{:S(2)}) collective-permute-start(f32[8,1024]{1,0:T(8,128)S(1)} %get-tuple-element.33.after_ref.refs_0_), channel_id=1, source_target_pairs={{0,8},{8,0},{16,24},{24,16},{1,9},{9,1},{17,25},{25,17},{2,10},{10... | collective-permute-start | bytes 98312 | tf_op jit(solution)/shard_map/ppermute | solution.py:465
  11.4 21.8 %collective-permute-start.3 = (bf16[256,1024]{1,0:T(8,128)(2,1)}, bf16[256,1024]{1,0:T(8,128)(2,1)S(1)}, u32[]{:S(2)}, u32[]{:S(2)}) collective-permute-start(bf16[256,1024]{1,0:T(8,128)(2,1)} %get-tuple-element.44.refs_3_), channel_id=1, source_target_pairs={{0,16},{8,24},{16,0},{24,8},{1,17},{9,25},{17,1},{25,9},{2,18},{10... | collective-permute-start | bytes 1572872 | tf_op jit(solution)/shard_map/ppermute | solution.py:536
  12.9 20.2 %collective-permute-start.4 = (bf16[256,1024]{1,0:T(8,128)(2,1)}, bf16[256,1024]{1,0:T(8,128)(2,1)}, u32[]{:S(2)}, u32[]{:S(2)}) collective-permute-start(bf16[256,1024]{1,0:T(8,128)(2,1)} %get-tuple-element.45.refs_0_), channel_id=1, source_target_pairs={{0,8},{8,0},{16,24},{24,16},{1,9},{9,1},{17,25},{25,17},{2,10},{10... | collective-permute-start | bytes 1572872 | tf_op jit(solution)/shard_map/ppermute | solution.py:535
  15.9 17.3 %all-to-all-start = ((f32[8,16,128]{2,1,0:T(8,128)}), f32[8,16,128]{2,1,0:T(8,128)S(1)}, u32[]{:S(2)}, u32[]{:S(2)}) async-start(f32[8,16,128]{2,1,0:T(8,128)} %get-tuple-element.39), calls=%async_computation | async-start | bytes 131072 | tf_op jit(solution)/shard_map/all_to_all | solution.py:502
  20.7 16.6 %copy-start = (f32[3,1024]{1,0:T(4,128)S(1)}, f32[3,1024]{1,0:T(4,128)}, u32[]{:S(2)}) copy-start(f32[3,1024]{1,0:T(4,128)} %wave_ref.1) | copy-start | bytes 36868
  26.0 4.6 %collective-permute-start.5 = (bf16[32,1024]{1,0:T(8,128)(2,1)S(1)}, bf16[32,1024]{1,0:T(8,128)(2,1)S(1)}, u32[]{:S(2)}, u32[]{:S(2)}) collective-permute-start(bf16[32,1024]{1,0:T(8,128)(2,1)S(1)} %get-tuple-element.46), channel_id=1, source_target_pairs={{0,8},{8,0},{16,24},{24,16},{1,9},{9,1},{17,25},{25,17},{2,10},{10... | collective-permute-start | bytes 196616 | tf_op jit(solution)/shard_map/ppermute | solution.py:530
  27.5 5.0 %collective-permute-start.6 = (bf16[32,1024]{1,0:T(8,128)(2,1)S(1)}, bf16[32,1024]{1,0:T(8,128)(2,1)S(1)}, u32[]{:S(2)}, u32[]{:S(2)}) collective-permute-start(bf16[32,1024]{1,0:T(8,128)(2,1)S(1)} %get-tuple-element.47), channel_id=1, source_target_pairs={{0,16},{8,24},{16,0},{24,8},{1,17},{9,25},{17,1},{25,9},{2,18},{10... | collective-permute-start | bytes 196616 | tf_op jit(solution)/shard_map/ppermute | solution.py:530
  28.0 5.2 %collective-permute-start.7 = (bf16[32,1024]{1,0:T(8,128)(2,1)S(1)}, bf16[32,1024]{1,0:T(8,128)(2,1)S(1)}, u32[]{:S(2)}, u32[]{:S(2)}) collective-permute-start(bf16[32,1024]{1,0:T(8,128)(2,1)S(1)} %get-tuple-element.48), channel_id=1, source_target_pairs={{0,24},{8,16},{16,8},{24,0},{1,25},{9,17},{17,9},{25,1},{2,26},{10... | collective-permute-start | bytes 196616 | tf_op jit(solution)/shard_map/ppermute | solution.py:530
  33.2 15.0 %collective-permute-start.8 = (bf16[256,1024]{1,0:T(8,128)(2,1)}, bf16[256,1024]{1,0:T(8,128)(2,1)}, u32[]{:S(2)}, u32[]{:S(2)}) collective-permute-start(bf16[256,1024]{1,0:T(8,128)(2,1)} %get-tuple-element.51.refs_4_), channel_id=1, source_target_pairs={{0,16},{8,24},{16,0},{24,8},{1,17},{9,25},{17,1},{25,9},{2,18},{10... | collective-permute-start | bytes 1572872 | tf_op jit(solution)/shard_map/ppermute | solution.py:536
  34.8 13.4 %collective-permute-start.9 = (bf16[256,1024]{1,0:T(8,128)(2,1)S(1)}, bf16[256,1024]{1,0:T(8,128)(2,1)}, u32[]{:S(2)}, u32[]{:S(2)}) collective-permute-start(bf16[256,1024]{1,0:T(8,128)(2,1)S(1)} %get-tuple-element.52.refs_6_), channel_id=1, source_target_pairs={{0,8},{8,0},{16,24},{24,16},{1,9},{9,1},{17,25},{25,17},{2,10},{10... | collective-permute-start | bytes 1572872 | tf_op jit(solution)/shard_map/ppermute | solution.py:535
  43.8 16.3 %all-to-all-start.1 = ((bf16[8,176,128]{2,1,0:T(8,128)(2,1)}), bf16[8,176,128]{2,1,0:T(8,128)(2,1)S(1)}, u32[]{:S(2)}, u32[]{:S(2)}) async-start(bf16[8,176,128]{2,1,0:T(8,128)(2,1)} %shard_map.126), calls=%async_computation.1 | async-start | bytes 720896 | tf_op jit(solution)/shard_map/all_to_all | solution.py:592
  48.3 17.4 %collective-permute-start.11 = (bf16[256,1024]{1,0:T(8,128)(2,1)}, bf16[256,1024]{1,0:T(8,128)(2,1)S(1)}, u32[]{:S(2)}, u32[]{:S(2)}) collective-permute-start(bf16[256,1024]{1,0:T(8,128)(2,1)} %get-tuple-element.57.refs_5_), channel_id=1, source_target_pairs={{0,16},{8,24},{16,0},{24,8},{1,17},{9,25},{17,1},{25,9},{2,18},{10... | collective-permute-start | bytes 1572872 | tf_op jit(solution)/shard_map/ppermute | solution.py:536
  49.9 15.8 %collective-permute-start.10 = (bf16[256,1024]{1,0:T(8,128)(2,1)}, bf16[256,1024]{1,0:T(8,128)(2,1)S(1)}, u32[]{:S(2)}, u32[]{:S(2)}) collective-permute-start(bf16[256,1024]{1,0:T(8,128)(2,1)} %get-tuple-element.58.refs_7_), channel_id=1, source_target_pairs={{0,8},{8,0},{16,24},{24,16},{1,9},{9,1},{17,25},{25,17},{2,10},{10... | collective-permute-start | bytes 1572872 | tf_op jit(solution)/shard_map/ppermute | solution.py:535

commit v7 on v6

--- a/solution.py
+++ b/solution.py
@@ -12,6 +12,8 @@
 BF16 = jnp.bfloat16
 LANES = 128
 ROWS = 16
+DIRECT_POINTS = False
+DIRECT_VALUES = False
 MIB = 1024 * 1024
 precise = lax.Precision.HIGHEST
 
@@ -122,7 +124,7 @@
     first = jnp.where(block == 0, disp, 0.0)
     out_ref[...] = pos + dot(first, pick, ((1,), (1,)), exact=True)
     out_ref[3:6, 0:LANES] = points[0:3]
-    out_ref[6:7, 0:LANES] = tiled[1:2, :].astype(F32)
+    out_ref[6:7, 0:LANES] = tiled[0:1, :].astype(F32)
     out_ref[7:8, 0:LANES] = jnp.full((1, LANES), weight_ref[0], F32)
 
 
@@ -186,7 +188,7 @@
 def points_kernel(count, others, role_ref, *refs):
     own_ref = refs[0]
     received = refs[1 : 1 + others]
-    moved_ref, disp_ref, after_ref, points_ref, weight_ref = refs[1 + others :]
+    moved_ref, disp_ref, after_ref, points_ref, weight_ref, number_ref = refs[1 + others :]
     role = role_ref[0]
     parent = own_ref[...]
     for step in range(others):
@@ -200,9 +202,16 @@
     mine = jnp.concatenate([own_ref[3:6, 0:LANES], zeros], 0)
     theirs = jnp.concatenate([parent[3:6, 0:LANES], zeros], 0)
     points = jnp.where(block < 2, mine, jnp.where(block < 4, theirs, later))
-    points = jnp.concatenate([points, jnp.zeros((ROWS - 8, LANES), F32)], 0)
-    points_ref[...] = jnp.broadcast_to(points[None], points_ref.shape)
+    if len(points_ref.shape) == 2:
+        points_ref[...] = points
+    else:
+        points = jnp.concatenate([points, jnp.zeros((ROWS - 8, LANES), F32)], 0)
+        points_ref[...] = jnp.broadcast_to(points[None], points_ref.shape)
     weight_ref[...] = parent[7:8, 0:LANES]
+    before = parent[6:7, 0:LANES].astype(jnp.int32)
+    number_ref[...] = jnp.where(
+        block[0:1] == 0, before, jnp.where(block[0:1] == 1, moved_ref[1:2, :], -1)
+    )
 
 
 def derive(coeff_ref, wave_ref, out_ref):
@@ -224,48 +233,30 @@
     out_ref[waves:, where] = (-squared * sin_part).astype(BF16)
 
 
-def prepare_kernel(
-    count, others, chunks, wanted, steps, coeff_hbm, wave_hbm, inverse_hbm, moved_ref, *refs
-):
-    received = refs[:others]
-    table_ref = refs[others + 1]
-    outs = refs[others + 2 : others + 2 + len(wanted)]
-    columns = refs[others + 2 + len(wanted) : -7]
-    coeff_ref, wave_ref, staged, rounded, small_sem, in_sem, out_sem = refs[-7:]
-    depth, electrons = staged.shape[1:]
+def prepare_kernel(wanted, coeff_hbm, wave_hbm, inverse_hbm, after_ref, table_ref, *refs):
+    outs = refs[: len(wanted)]
+    coeff_ref, wave_ref, staged, rounded, small_sem, in_sem, out_sem = refs[len(wanted) :]
+    depth = staged.shape[1]
     wave_load = pltpu.make_async_copy(wave_hbm, wave_ref, small_sem.at[0])
     coeff_load = pltpu.make_async_copy(coeff_hbm, coeff_ref, small_sem.at[1])
     wave_load.start()
     coeff_load.start()
     loads, stores = [], []
-    for chunk in range(chunks):
+    for slot, chunk in enumerate(wanted):
         load = pltpu.make_async_copy(
-            rows_of(inverse_hbm, chunk, depth), staged.at[chunk], in_sem.at[chunk]
+            rows_of(inverse_hbm, chunk, depth), staged.at[slot], in_sem.at[slot]
         )
         load.start()
         loads.append(load)
-    block = iota((1, LANES), 1) // count
-    number = jnp.where(block == 0, moved_ref[0:1, :], moved_ref[1:2, :])
-    for step in range(others):
-        theirs = received[step][6:7, 0:LANES].astype(jnp.int32)
-        number = jnp.where(block == 2 + step, theirs, number)
-    pick = (iota((electrons, LANES), 0) == number).astype(F32).astype(BF16)
     wave_load.wait()
     coeff_load.wait()
     derive(coeff_ref, wave_ref, table_ref)
-    for chunk in range(chunks):
-        rows = slice(chunk * depth, (chunk + 1) * depth)
-        loads[chunk].wait()
-        rounded[chunk] = staged[chunk].astype(BF16)
-        if chunk in wanted:
-            slot = wanted.index(chunk)
-            store = pltpu.make_async_copy(rounded.at[chunk], outs[slot], out_sem.at[slot])
-            store.start()
-            stores.append(store)
-        turned = jnp.transpose(dot(rounded[chunk], pick)).astype(BF16)
-        for out, step in zip(columns, steps):
-            out[0:count, rows] = turned[0:count]
-            out[count : 2 * count, rows] = turned[(1 + step) * count : (2 + step) * count]
+    for slot, out in enumerate(outs):
+        loads[slot].wait()
+        rounded[slot] = staged[slot].astype(BF16)
+        store = pltpu.make_async_copy(rounded.at[slot], out, out_sem.at[slot])
+        store.start()
+        stores.append(store)
     for store in stores:
         store.wait()
 
@@ -277,15 +268,20 @@
     return value
 
 
-def evaluate_kernel(count, points_ref, wave_ref, table_ref, *refs):
-    out_ref, diff, new = refs[-3:]
-    walkers = points_ref.shape[0]
+def evaluate_kernel(count, sources, targets, *refs):
+    points = refs[:sources]
+    wave_ref, table_ref = refs[sources : sources + 2]
+    outs = refs[sources + 3 : -3]
+    diff, new, gathered = refs[-3:]
+    walkers = gathered.shape[0]
+    for w in range(walkers):
+        gathered[w] = points[w][...] if sources > 1 else points[0][w, 0:8]
     waves = wave_ref.shape[1]
     width = table_ref.shape[1] // 5
     step = math.gcd(waves, LANES)
 
     def one(w, carry):
-        column = jnp.transpose(points_ref[w, 0:8])
+        column = jnp.transpose(gathered[w])
         xs = [column[0 : 6 * count, a : a + 1] for a in range(3)]
         row_d = pl.multiple_of(w * (3 * count), count)
         row_n = pl.multiple_of(w * (2 * count), count)
@@ -312,84 +308,89 @@
     change = dot(diff[...], table_ref[:, 0:width]).astype(BF16)
     rest = dot(new[...], table_ref[:, width:]).astype(BF16)
     for w in range(walkers):
+        out_ref = outs[w] if targets > 1 else outs[0].at[w]
         at = w * 3 * count
-        out_ref[w, 0 : 2 * count] = change[at : at + 2 * count]
-        out_ref[w, 6 * count : 7 * count] = change[at + 2 * count : at + 3 * count]
+        out_ref[0 : 2 * count] = change[at : at + 2 * count]
+        out_ref[6 * count : 7 * count] = change[at + 2 * count : at + 3 * count]
         for half, base in ((0, 2 * count), (1, 7 * count)):
             row = (2 * w + half) * count
             for a in range(4):
-                out_ref[w, base + a * count : base + (a + 1) * count] = rest[
+                out_ref[base + a * count : base + (a + 1) * count] = rest[
                     row : row + count, a * width : (a + 1) * width
                 ]
 
 
-def sweep(matrices):
-    matrices = list(matrices)
-    logs = [jnp.zeros((1, 1), F32) for _ in matrices]
-    for k in range(max(m.shape[0] for m in matrices)):
-        for which, matrix in enumerate(matrices):
-            size = matrix.shape[0]
-            if k >= size:
-                continue
-            pivot = matrix[k : k + 1, k : k + 1]
-            inverse = 1.0 / pivot
-            column = matrix[:, k : k + 1]
-            line = matrix[k : k + 1, :]
-            row_here = iota((size, size), 0) == k
-            lane_here = iota((size, size), 1) == k
-            scaled = line * inverse
-            reduced = matrix - column * scaled
-            matrix = jnp.where(row_here, scaled, jnp.where(lane_here, column * inverse, reduced))
-            matrix = jnp.where(jnp.logical_and(row_here, lane_here), -inverse, matrix)
-            matrices[which] = matrix
-            logs[which] = logs[which] + jnp.log(pivot)
-    return [-m for m in matrices], logs
-
-
-def solve_kernel(count, others, role_ref, vals_ref, own_ref, *refs):
-    received = refs[:others]
-    weight_ref, after_ref = refs[others : others + 2]
-    change_ref, cols_ref, inv_ref, drift_ref, lap_ref, out_weight_ref, vals = refs[others + 2 :]
-    pieces, _, width = vals_ref.shape
-    for o in range(pieces):
-        vals[:, o * width : (o + 1) * width] = vals_ref[o]
-    role = role_ref[0]
-    cols = own_ref[...].astype(F32)
-    for step in range(others):
-        cols = jnp.where(role == step + 1, received[step][...].astype(F32), cols)
-    cols = cols.astype(BF16)
-    cols_ref[...] = cols
-    change_ref[...] = vals[0 : 2 * count]
-    own = own_ref[0:count]
-    products, ratios, normal = [], [], []
-    for size, matrix, part in (
-        (count, own, vals[6 * count : 11 * count]),
-        (2 * count, cols, vals[0 : 6 * count]),
-    ):
-        product = dot(matrix, part, ((1,), (1,)))
-        ratio = product[:, 0:size] + jnp.where(iota((size, size), 0) == iota((size, size), 1), 1.0, 0.0)
-        products.append(product[:, size:])
-        ratios.append(ratio)
-        normal.append(dot(ratio, ratio, ((1,), (1,)), exact=True))
-    inverses, logs = sweep(normal)
-    for update, (inverse, ratio, product) in enumerate(zip(inverses, ratios, products)):
-        size = ratio.shape[0]
-        wide = product.shape[1]
-        small = dot(inverse, ratio, exact=True)
-        tile = jnp.where(iota((size, wide), 0) == size - count + iota((size, wide), 1) % count, 1.0, 0.0)
-        spread = dot(small, tile, exact=True)
-        sums = jnp.sum(product * spread, axis=0, keepdims=True)
-        for a in range(3):
-            drift_ref[3 * update + a] = sums[:, a * count : (a + 1) * count]
-        lap_ref[update] = sums[:, 3 * count : 4 * count]
-    inv_ref[...] = small
-    out_weight_ref[...] = weight_ref[...] + 0.5 * logs[1]
-
-
-def finish_kernel(sources, chunks, role_ref, change_ref, cols_ref, inv_ref, *refs):
-    inputs = refs[:-5]
-    out_ref, parent, staged, in_sem, out_sem = refs[-5:]
-    depth = inputs[0].shape[0]
+def sweep(matrix):
+    size = matrix.shape[0]
+    log = jnp.zeros((1, 1), F32)
+    for k in range(size):
+        pivot = matrix[k : k + 1, k : k + 1]
+        inverse = 1.0 / pivot
+        column = matrix[:, k : k + 1]
+        line = matrix[k : k + 1, :]
+        row_here = iota((size, size), 0) == k
+        lane_here = iota((size, size), 1) == k
+        scaled = line * inverse
+        reduced = matrix - column * scaled
+        matrix = jnp.where(row_here, scaled, jnp.where(lane_here, column * inverse, reduced))
+        matrix = jnp.where(jnp.logical_and(row_here, lane_here), -inverse, matrix)
+        log = log + jnp.log(pivot)
+    return -matrix, log
+
+
+def ratio_of(products, size):
+    eye = jnp.where(iota((size, size), 0) == iota((size, size), 1), 1.0, 0.0)
+    ratio = products[0:size, 0:size] + eye
+    inverse, log = sweep(dot(ratio, ratio, ((0,), (0,)), exact=True))
+    return ratio, inverse, 0.5 * log
+
+
+def moved_sums(products, ratio, inverse, count):
+    size = ratio.shape[0]
+    turned = dot(ratio, inverse, exact=True)[size - count :]
+    tile = jnp.concatenate([turned] * 4, 0)
+    part = products[size : size + 4 * count, 0:size] * tile
+    return dot(jnp.ones((8, size), F32), part, ((1,), (1,)), exact=True)[0:1]
+
+
+def first_kernel(count, sources, me_ref, moved_ref, *refs):
+    values = refs[:sources]
+    blocks = refs[sources:-6]
+    drift_ref, lap_ref, later_ref, vals, columns = refs[-5:]
+    rows = later_ref.shape[0]
+    if sources > 1:
+        width = values[0].shape[1]
+        for step in range(sources):
+            at = pl.multiple_of((me_ref[0] ^ step) * width, width)
+            later_ref[:, pl.ds(at, width)] = values[step][0:rows]
+            vals[:, pl.ds(at, width)] = values[step][rows:]
+    else:
+        pieces, _, width = values[0].shape
+        for piece in range(pieces):
+            where = slice(piece * width, (piece + 1) * width)
+            later_ref[:, where] = values[0][piece, 0:rows]
+            vals[:, where] = values[0][piece, rows:]
+    depth, electrons = blocks[0].shape
+    block = iota((1, LANES), 1) // count
+    number = jnp.where(block == 0, moved_ref[0:1, :], -1)
+    pick = (iota((electrons, LANES), 0) == number).astype(F32).astype(BF16)
+    for chunk, ref in enumerate(blocks):
+        columns[chunk * depth : (chunk + 1) * depth] = dot(ref[...], pick).astype(BF16)
+    products = dot(vals[...], columns[...])
+    ratio, inverse, _ = ratio_of(products, count)
+    sums = moved_sums(products, ratio, inverse, count)
+    for a in range(3):
+        drift_ref[a] = sums[:, a * count : (a + 1) * count]
+    lap_ref[0] = sums[:, 3 * count : 4 * count]
+
+
+def finish_kernel(
+    count, sources, chunks, role_ref, number_ref, later_ref, weight_ref, drift_in, lap_in, *refs
+):
+    inputs = refs[:-9]
+    out_ref, drift_ref, lap_ref, out_weight_ref, parent, staged, columns, in_sem, out_sem = refs[-9:]
+    depth, electrons = inputs[0].shape
+    size = 2 * count
     role = role_ref[0]
     for chunk in range(chunks):
         for which, table in enumerate(sources):
@@ -400,19 +401,32 @@
                     inputs[table[chunk]], parent.at[chunk], in_sem.at[chunk]
                 ).start()
 
-    total = jnp.zeros((change_ref.shape[0], inputs[0].shape[1]), F32)
+    pick = (iota((electrons, LANES), 0) == number_ref[...]).astype(F32).astype(BF16)
+    total = jnp.zeros((size, electrons), F32)
     for chunk in range(chunks):
+        rows = slice(chunk * depth, (chunk + 1) * depth)
         pltpu.make_async_copy(inputs[chunk], parent.at[chunk], in_sem.at[chunk]).wait()
-        total = total + dot(change_ref[:, chunk * depth : (chunk + 1) * depth], parent[chunk])
-    solved = dot(inv_ref[...], total, exact=True).astype(BF16)
+        columns[rows] = dot(parent[chunk], pick).astype(BF16)
+        total = total + dot(later_ref[0:size, rows], parent[chunk])
+    products = dot(later_ref[...], columns[...])
+    ratio, inverse, log = ratio_of(products, size)
+    small = dot(inverse, ratio, ((1,), (1,)), exact=True)
+    solved = dot(small, total, exact=True).astype(BF16)
+    solved = jnp.concatenate([solved, jnp.zeros((LANES - size, electrons), BF16)], 0)
     copies = []
     for chunk in range(chunks):
         rows = slice(chunk * depth, (chunk + 1) * depth)
-        columns = jnp.transpose(cols_ref[:, rows].astype(F32)).astype(BF16)
-        staged[chunk] = parent[chunk].astype(F32) - dot(columns, solved)
+        staged[chunk] = parent[chunk].astype(F32) - dot(columns[rows], solved)
         copy = pltpu.make_async_copy(staged.at[chunk], out_ref.at[rows], out_sem.at[chunk])
         copy.start()
         copies.append(copy)
+    sums = moved_sums(products, ratio, inverse, count)
+    drift_ref[0:3] = drift_in[...]
+    lap_ref[0:1] = lap_in[...]
+    for a in range(3):
+        drift_ref[3 + a] = sums[:, a * count : (a + 1) * count]
+    lap_ref[1] = sums[:, 3 * count : 4 * count]
+    out_weight_ref[...] = weight_ref[...] + log
     for copy in copies:
         copy.wait()
 
@@ -493,41 +507,47 @@
         vmem=1,
     )(own[0], own[-1], *records)
 
-    points, weight = call(
+    few = is_power(n_orb) and local % LANES == 0
+    direct = few and DIRECT_POINTS
+    sources = n_orb if direct else 1
+    points, weight, number = call(
         functools.partial(points_kernel, count, others),
-        (shape((n_orb, ROWS, LANES), F32), shape((1, LANES), F32)),
+        (
+            shape((8, LANES) if direct else (n_orb, ROWS, LANES), F32),
+            shape((1, LANES), F32),
+            shape((1, LANES), jnp.int32),
+        ),
         [SM] + [VM] * (others + 3) + [ANY],
-        (VM, VM),
+        (VM, VM, VM),
     )(role, record, *records, tiled, disp, token_0)
-    points = lax.all_to_all(points, "orb", split_axis=0, concat_axis=0, tiled=True)
+    if direct:
+        points = [points] + [lax.ppermute(points, "orb", pairs(n_orb, s)) for s in range(1, n_orb)]
+    else:
+        points = [lax.all_to_all(points, "orb", split_axis=0, concat_axis=0, tiled=True)]
 
     width = -(-local // LANES) * LANES
     coeff = jnp.pad(coefficients, ((0, 0), (0, width - local))) if width > local else coefficients
-    steps = [0] + [backward(n_grp, s) for s in range(1, n_grp)]
     derived, *prepared = call(
-        functools.partial(prepare_kernel, count, others, chunks, middle, steps),
+        functools.partial(prepare_kernel, middle),
         (shape((plane, 5 * width), BF16),)
-        + (pltpu.HBM((depth, electrons), BF16),) * len(middle)
-        + tuple(shape((2 * count, electrons), BF16) for _ in steps),
-        [HBM, HBM, HBM] + [VM] * (1 + others) + [ANY],
-        (VM,) + (ANY,) * len(middle) + (VM,) * len(steps),
+        + (pltpu.HBM((depth, electrons), BF16),) * len(middle),
+        [HBM, HBM, HBM, ANY],
+        (VM,) + (ANY,) * len(middle),
         scratch=[
             pltpu.VMEM((plane, width), BF16),
             pltpu.VMEM(wavevectors.shape, F32),
-            pltpu.VMEM((chunks, depth, electrons), F32),
-            pltpu.VMEM((chunks, depth, electrons), BF16),
+            pltpu.VMEM((len(middle), depth, electrons), F32),
+            pltpu.VMEM((len(middle), depth, electrons), BF16),
             pltpu.SemaphoreType.DMA((2,)),
-            pltpu.SemaphoreType.DMA((chunks,)),
+            pltpu.SemaphoreType.DMA((len(middle),)),
             pltpu.SemaphoreType.DMA((len(middle),)),
         ],
-        flops=2 * electrons * electrons * LANES + 8 * plane * width,
-        moved=6 * electrons * electrons + 10 * plane * width,
-        vmem=16,
-    )(*in_hbm(coeff, wavevectors, inverse), tiled, *records, weight)
-    for chunk, block in zip(middle, prepared):
-        own[chunk] = block
-    columns = prepared[len(middle) :]
-    sent = [lax.ppermute(columns[s], "grp", pairs(n_grp, s)) for s in range(1, n_grp)]
+        flops=8 * plane * width,
+        moved=3 * electrons * electrons + 10 * plane * width,
+        vmem=12,
+    )(*in_hbm(coeff, wavevectors, inverse), weight)
+    for chunk, ready in zip(middle, prepared):
+        own[chunk] = ready
 
     apart = apart.astype(jnp.int32).reshape(1)
     arrays = list(own)
@@ -551,13 +571,8 @@
             )(apart, *in_hbm(*mine), *got, *first)
 
         x1, y1 = send_x(own[0]), send_y(own[3])
-        y1, x1, token_1 = relay((own[1], own[2]), (y1, x1), (derived, points, *sent))
+        y1, x1, token_1 = relay((own[1], own[2]), (y1, x1), (derived, *points))
         x2, y2 = send_x(y1), send_y(x1)
-        y2, x2, token_2 = relay((own[2], own[1]), (y2, x2), ())
-        x3, y3 = send_x(y2), send_y(x2)
-        arrays += [x1, x2, y1, y2, x3, y3]
-        a1, a2, b1, b2, a3, b3 = range(chunks, chunks + 6)
-        table = [range(chunks), (a1, a2, a3, b3), (a3, b3, b2, b1), (b2, b3, a3, a2)]
     else:
         token_1 = token_2 = jnp.zeros((8, LANES), F32)
         table = [range(chunks)]
@@ -565,21 +580,31 @@
             table.append(range(len(arrays), len(arrays) + chunks))
             arrays += [lax.ppermute(block, "grp", pairs(n_grp, step)) for block in own]
 
-    block = math.gcd(n_orb, 8)
+    height = 11 * count
+    spread = few and DIRECT_VALUES
+    targets = n_orb if spread else 1
+    block = n_orb if few else math.gcd(n_orb, 8)
+    whole = lambda array: pl.BlockSpec(array.shape, lambda i: (0,) * array.ndim)
+    if direct:
+        point_specs = [whole(p) for p in points]
+    else:
+        point_specs = [pl.BlockSpec((block, ROWS, LANES), lambda i: (i, 0, 0))]
+    if spread:
+        out_shapes = (shape((height, width), BF16),) * n_orb
+        out_specs = tuple(whole(o) for o in out_shapes)
+    else:
+        out_shapes = (shape((n_orb, height, width), BF16),)
+        out_specs = (pl.BlockSpec((block, height, width), lambda i: (i, 0, 0)),)
     values = pl.pallas_call(
-        functools.partial(evaluate_kernel, count),
+        functools.partial(evaluate_kernel, count, sources, targets),
         grid=(n_orb // block,),
-        out_shape=shape((n_orb, 11 * count, width), BF16),
-        in_specs=[
-            pl.BlockSpec((block, ROWS, LANES), lambda i: (i, 0, 0)),
-            pl.BlockSpec(wavevectors.shape, lambda i: (0, 0)),
-            pl.BlockSpec(derived.shape, lambda i: (0, 0)),
-        ]
-        + [ANY],
-        out_specs=pl.BlockSpec((block, 11 * count, width), lambda i: (i, 0, 0)),
+        out_shape=out_shapes,
+        in_specs=point_specs + [whole(wavevectors), whole(derived), ANY],
+        out_specs=out_specs,
         scratch_shapes=[
             pltpu.VMEM((block * 3 * count, plane), BF16),
             pltpu.VMEM((block * 2 * count, plane), BF16),
+            pltpu.VMEM((block, 8, LANES), F32),
         ],
         compiler_params=pltpu.CompilerParams(vmem_limit_bytes=8 * MIB),
         cost_estimate=pl.CostEstimate(
@@ -587,44 +612,66 @@
             bytes_accessed=12 * plane * width,
             transcendentals=0,
         ),
-    )(points, wavevectors, derived, token_1)
-    values = values[:, :, :local]
-    values = lax.all_to_all(values, "orb", split_axis=0, concat_axis=0, tiled=True)
-    if width > local:
-        values = values.transpose(1, 0, 2).reshape(1, 11 * count, electrons)
-
-    change, cols, small, drift, laplacian, new_weight = call(
-        functools.partial(solve_kernel, count, others),
+    )(*points, wavevectors, derived, token_1)
+    computed = values[0]
+    if spread:
+        values = [values[0]] + [
+            lax.ppermute(values[s], "orb", pairs(n_orb, s)) for s in range(1, n_orb)
+        ]
+    else:
+        values = values[0][:, :, :local]
+        values = lax.all_to_all(values, "orb", split_axis=0, concat_axis=0, tiled=True)
+        if width > local:
+            values = values.transpose(1, 0, 2).reshape(1, height, electrons)
+        values = [values]
+
+    if n_grp == 4:
+        y2, x2, token_2 = relay((own[2], own[1]), (y2, x2), (computed,))
+        x3, y3 = send_x(y2), send_y(x2)
+        arrays += [x1, x2, y1, y2, x3, y3]
+        a1, a2, b1, b2, a3, b3 = range(chunks, chunks + 6)
+        table = [range(chunks), (a1, a2, a3, b3), (a3, b3, b2, b1), (b2, b3, a3, a2)]
+
+    here = lax.axis_index("orb").astype(jnp.int32).reshape(1)
+    drift, laplacian, later = call(
+        functools.partial(first_kernel, count, targets),
         (
-            shape((2 * count, electrons), BF16),
-            shape((2 * count, electrons), BF16),
-            shape((2 * count, 2 * count), F32),
+            shape((3, 1, count), F32),
+            shape((1, 1, count), F32),
+            shape((6 * count, electrons), BF16),
+        ),
+        [SM, VM] + [VM] * (targets + chunks) + [ANY],
+        (VM, VM, VM),
+        scratch=[
+            pltpu.VMEM((5 * count, electrons), BF16),
+            pltpu.VMEM((electrons, LANES), BF16),
+        ],
+        flops=2 * electrons * electrons * LANES,
+        moved=2 * electrons * electrons,
+        vmem=8,
+    )(here, tiled, *values, *own, token_2)
+
+    updated, drift, laplacian, new_weight = call(
+        functools.partial(finish_kernel, count, table, chunks),
+        (
+            shape((electrons, electrons), F32),
             shape((6, 1, count), F32),
             shape((2, 1, count), F32),
             shape((1, LANES), F32),
         ),
-        [SM] + [VM] * (others + 3) + [ANY],
-        (VM,) * 6,
-        scratch=[pltpu.VMEM((11 * count, electrons), BF16)],
-        flops=2 * electrons * count * count * 16,
-        moved=4 * 11 * count * electrons,
-    )(role, values, columns[0], *sent, weight, token_2)
-
-    updated = call(
-        functools.partial(finish_kernel, table, chunks),
-        shape((electrons, electrons), F32),
-        [SM, VM, VM, VM] + [ANY] * len(arrays),
-        HBM,
+        [SM] + [VM] * 5 + [ANY] * len(arrays),
+        (HBM, VM, VM, VM),
         scratch=[
             pltpu.VMEM((chunks, depth, electrons), BF16),
             pltpu.VMEM((chunks, depth, electrons), F32),
+            pltpu.VMEM((electrons, LANES), BF16),
             pltpu.SemaphoreType.DMA((chunks,)),
             pltpu.SemaphoreType.DMA((chunks,)),
         ],
         flops=4 * electrons * electrons * 2 * count,
         moved=6 * electrons * electrons,
         vmem=12,
-    )(role, change, cols, small, *in_hbm(*own), *arrays[chunks:])
+    )(role, number, later, weight, drift, laplacian, *in_hbm(*own), *arrays[chunks:])
 
     return updated[None], drift.reshape(2, 1, 3, count), laplacian, new_weight[0, :1]
 

time: 70.3 us -> 69.3 us (0.986)
  starting transfers between devices: 27.9 us -> 22.9 us
  Pallas kernels: 26.8 us -> 30.2 us
  local copies, waits for them, and re-layouts: 0.01 us -> 2.09 us
  waiting for transfers between devices: 12.6 us -> 10.9 us
    ppermute x3 -> x0, waiting for transfers between devices: 3.56 us -> none  [per_device(): lax.ppermute(columns[s], 'grp', pairs(n_grp, s))]
    ppermute x3 -> x0, starting transfers between devices: 3.55 us -> none  [per_device(): lax.ppermute(columns[s], 'grp', pairs(n_grp, s))]
    pallas_call x5, Pallas kernels: 22.5 us -> 25.9 us  [the longest x1 9.93 us: per_device(): call(functools.partial(finish_kernel, count, table, chunks), (shape((elec...]
    unnamed x2 -> x10, local copies, waits for them, and re-layouts: 0.01 us -> 2.09 us
    all_to_all x1, waiting for transfers between devices: 7.65 us -> 5.63 us  [per_device(): lax.all_to_all(values, 'orb', split_axis=0, concat_axis=0, tiled=True)]
    all_to_all x1, waiting for transfers between devices: 0.01 us -> 1.83 us  [per_device(): lax.all_to_all(points, 'orb', split_axis=0, concat_axis=0, tiled=True)]
    ppermute x3, starting transfers between devices: 4.69 us -> 3.19 us  [per_device(): send_y = lambda block: lax.ppermute(block, 'grp', pairs(n_grp, 2))]
    ppermute x3, waiting for transfers between devices: 0.01 us -> 1.22 us  [per_device(): send_x = lambda block: lax.ppermute(block, 'grp', pairs(n_grp, 1))]
  transfers between devices with their start and end apart: 14 -> 11, of which waited for: 6 -> 6; matrix products, arithmetic and copies ran while one was open for 0% -> 0% of each run, Pallas kernels for 30% -> 27%
where the time goes in v7:
time: 69.3 us; the launch traced here: 68.8 us
  Pallas kernels  30.2 us (44%)
  starting transfers between devices  22.9 us (33%)
  waiting for transfers between devices  10.9 us (16%)
  between operations  2.67 us (4%)
  local copies, waits for them, and re-layouts  2.09 us (3%)
    pallas_call x1, Pallas kernels, per_device(): call(functools.partial(finish_kernel, count, table, chunks), (shape((elec...  9.93 us
    ppermute x3, starting transfers between devices, per_device(): send_x = lambda block: lax.ppermute(block, 'grp', pairs(n_grp, 1))  6.77 us
    pallas_call x1, Pallas kernels, per_device(): pl.pallas_call(functools.partial(evaluate_kernel, count, sources, targets...  6.42 us
    all_to_all x1, waiting for transfers between devices, per_device(): lax.all_to_all(values, 'orb', split_axis=0, concat_axis=0, tiled=True)  5.63 us
    all_to_all x1, starting transfers between devices, per_device(): lax.all_to_all(points, 'orb', split_axis=0, concat_axis=0, tiled=True)  4.88 us
    ppermute x3, starting transfers between devices, per_device(): lax.ppermute(record, 'grp', pairs(n_grp, s))  4.6 us
    pallas_call x1, Pallas kernels, per_device(): call(functools.partial(first_kernel, count, targets), (shape((3, 1, count...  4.48 us
    pallas_call x1, Pallas kernels, per_device(): call(functools.partial(prepare_kernel, middle), (shape((plane, 5 * width)...  4.08 us
  transfers between devices with their start and end apart: 11, of which 6 were waited for; matrix products, arithmetic and copies ran while one was open for 0% of the time, Pallas kernels for 27%

profile of v7, /device:TPU:0, one launch (start us, length us, event | category | flops | bytes accessed | tf_op | source)
XLA Modules:
  0.0 68.8 jit_solution(3488317304136699758)
XLA Ops:
  1.3 1.7 %shard_map.120 = (f32[8,1024]{1,0:T(8,128)S(1)}, s32[2,128]{1,0:T(2,128)S(1)}, f32[2,8,128]{2,1,0:T(8,128)S(1)}) custom-call(f32[3,1,1024]{2,1,0:T(1,128)} %bitcast.12, s32[2,1,16]{2,1,0:T(1,128)} %moved_hbm.1, f32[6,1,16]{2,1,0:T(1,128)} %bitcast.13, f32[1]{0:T(128)S(6)} %copy.27.weight_ref), custom_call_target="tpu_custom_call" | custom-call | tf_op jit(solution)/shard_map/pallas_call | solution.py:458
  3.0 4.0 %collective-permute-start.2 = (f32[8,1024]{1,0:T(8,128)S(1)}, f32[8,1024]{1,0:T(8,128)S(1)}, u32[]{:S(2)}, u32[]{:S(2)}) collective-permute-start(f32[8,1024]{1,0:T(8,128)S(1)} %get-tuple-element.31.after_ref.refs_0_), channel_id=1, source_target_pairs={{0,24},{8,16},{16,8},{24,0},{1,25},{9,17},{17,9},{25,1},{2,26},{10... | collective-permute-start | bytes 98312 | tf_op jit(solution)/shard_map/ppermute | solution.py:479
  7.0 0.5 collective-permute-start.1
  7.5 0.1 collective-permute-start
  7.6 2.4 %shard_map.121 = (bf16[256,1024]{1,0:T(8,128)(2,1)S(1)}, bf16[256,1024]{1,0:T(8,128)(2,1)}) custom-call(f32[1,1024,1024]{2,1,0:T(8,128)} %inverse_hbm.3, f32[8,1024]{1,0:T(8,128)S(1)} %get-tuple-element.31.after_ref.refs_0_), custom_call_target="tpu_custom_call" | custom-call | bytes 3145728 | tf_op jit(solution)/shard_map/pallas_call | solution.py:487
  10.0 0.0 collective-permute-done.2.refs_4_.refs_3_
  10.0 0.9 %collective-permute-done.1.refs_3_.refs_2_ = f32[8,1024]{1,0:T(8,128)S(1)} collective-permute-done((f32[8,1024]{1,0:T(8,128)S(1)}, f32[8,1024]{1,0:T(8,128)S(1)}, u32[]{:S(2)}, u32[]{:S(2)}) %collective-permute-start.1) | collective-permute-done | bytes 32800 | tf_op jit(solution)/shard_map/ppermute | solution.py:479
  10.9 0.5 collective-permute-done.refs_2_.refs_1_
  11.4 0.0 copy-start.2
  11.4 1.5 %collective-permute-start.3 = (bf16[256,1024]{1,0:T(8,128)(2,1)}, bf16[256,1024]{1,0:T(8,128)(2,1)}, u32[]{:S(2)}, u32[]{:S(2)}) collective-permute-start(bf16[256,1024]{1,0:T(8,128)(2,1)} %get-tuple-element.43.refs_4_.refs_3_), channel_id=1, source_target_pairs={{0,16},{8,24},{16,0},{24,8},{1,17},{9,25},{17,1},{25,9},{2,18},{10... | collective-permute-start | bytes 1572872 | tf_op jit(solution)/shard_map/ppermute | solution.py:556
  12.9 0.6 collective-permute-start.4
  14.8 1.0 %shard_map.123 = (f32[8,16,128]{2,1,0:T(8,128)}, f32[1,128]{1,0:T(1,128)S(1)}, s32[1,128]{1,0:T(1,128)S(1)}) custom-call(s32[1]{0:T(128)} %bitcast.2.role_ref, f32[8,1024]{1,0:T(8,128)S(1)} %get-tuple-element.31.after_ref.refs_0_, f32[8,1024]{1,0:T(8,128)S(1)} %collective-permute-done.refs_2_.refs_1_, f32[8,1024]{1,0:T(8,128)S(1)} %collective-permute-done.1.refs_3_.refs_2_, ...), custom_call_target="tpu_custom_call" | custom-call | tf_op jit(solution)/shard_map/pallas_call | solution.py:513
  15.8 4.9 %all-to-all-start = ((f32[8,16,128]{2,1,0:T(8,128)}), f32[8,16,128]{2,1,0:T(8,128)S(1)}, u32[]{:S(2)}, u32[]{:S(2)}) async-start(f32[8,16,128]{2,1,0:T(8,128)} %get-tuple-element.38), calls=%async_computation | async-start | bytes 131072 | tf_op jit(solution)/shard_map/all_to_all | solution.py:526
  20.7 0.0 copy-start.4
  20.7 4.1 %shard_map.124 = (bf16[2048,640]{1,0:T(8,128)(2,1)S(1)}, bf16[256,1024]{1,0:T(8,128)(2,1)}, bf16[256,1024]{1,0:T(8,128)(2,1)}) custom-call(bf16[2048,128]{1,0:T(8,128)(2,1)} %coeff_hbm.1, f32[3,1024]{1,0:T(4,128)} %refs_1_.1, f32[1,1024,1024]{2,1,0:T(8,128)} %inverse_hbm.3, f32[1,128]{1,0:T(1,128)S(1)} %get-tuple-element.39.after_ref.weight_ref), custom_call_target="tpu_custom_call" | custom-call | flops 2097152 | bytes 5767168 | tf_op jit(solution)/shard_map/pallas_call | solution.py:530
  24.8 1.8 %all-to-all-done.refs_1_.refs_0_ = f32[8,16,128]{2,1,0:T(8,128)S(1)} async-done(((f32[8,16,128]{2,1,0:T(8,128)}), f32[8,16,128]{2,1,0:T(8,128)S(1)}, u32[]{:S(2)}, u32[]{:S(2)}) %all-to-all-start) | async-done | bytes 65568 | tf_op jit(solution)/shard_map/all_to_all | solution.py:526
  26.6 0.0 collective-permute-done.3.got_a
  26.6 0.0 collective-permute-done.4.got_b
  26.7 0.0 copy-done.2
  26.7 0.1 shard_map.125
  26.8 0.0 copy-start
  26.8 0.6 collective-permute-start.5
  27.3 3.3 %collective-permute-start.6 = (bf16[256,1024]{1,0:T(8,128)(2,1)}, bf16[256,1024]{1,0:T(8,128)(2,1)}, u32[]{:S(2)}, u32[]{:S(2)}) collective-permute-start(bf16[256,1024]{1,0:T(8,128)(2,1)} %get-tuple-element.47.refs_6_), channel_id=1, source_target_pairs={{0,8},{8,0},{16,24},{24,16},{1,9},{9,1},{17,25},{25,17},{2,10},{10... | collective-permute-start | bytes 1572872 | tf_op jit(solution)/shard_map/ppermute | solution.py:555
  30.6 0.0 copy-done.4
  30.6 6.4 %shard_map.126.refs_0_ = bf16[8,176,128]{2,1,0:T(8,128)(2,1)} custom-call(f32[8,16,128]{2,1,0:T(8,128)S(1)} %all-to-all-done.refs_1_.refs_0_, f32[3,1024]{1,0:T(4,128)S(1)} %copy-done.4, bf16[2048,640]{1,0:T(8,128)(2,1)S(1)} %get-tuple-element.40.refs_0_.refs_2_, f32[8,128]{1,0:T(8,128)S(1)} %get-tuple-element.45.refs_3_), custom_call_target="tpu_custom_call" | custom-call | flops 738197504 | bytes 3145728 | tf_op jit(solution)/shard_map/pallas_call | solution.py:598
  37.1 3.4 %all-to-all-start.1 = ((bf16[8,176,128]{2,1,0:T(8,128)(2,1)}), bf16[8,176,128]{2,1,0:T(8,128)(2,1)S(1)}, u32[]{:S(2)}, u32[]{:S(2)}) async-start(bf16[8,176,128]{2,1,0:T(8,128)(2,1)} %shard_map.126.refs_0_), calls=%async_computation.1 | async-start | bytes 720896 | tf_op jit(solution)/shard_map/all_to_all | solution.py:623
  40.5 0.9 %collective-permute-done.5.got_a = bf16[256,1024]{1,0:T(8,128)(2,1)} collective-permute-done((bf16[256,1024]{1,0:T(8,128)(2,1)}, bf16[256,1024]{1,0:T(8,128)(2,1)}, u32[]{:S(2)}, u32[]{:S(2)}) %collective-permute-start.5) | collective-permute-done | bytes 524320 | tf_op jit(solution)/shard_map/ppermute | solution.py:556
  41.4 1.2 %collective-permute-done.6.got_b = bf16[256,1024]{1,0:T(8,128)(2,1)} collective-permute-done((bf16[256,1024]{1,0:T(8,128)(2,1)}, bf16[256,1024]{1,0:T(8,128)(2,1)}, u32[]{:S(2)}, u32[]{:S(2)}) %collective-permute-start.6) | collective-permute-done | bytes 524320 | tf_op jit(solution)/shard_map/ppermute | solution.py:555
  42.6 0.1 shard_map.127
  42.7 1.1 %collective-permute-start.8 = (bf16[256,1024]{1,0:T(8,128)(2,1)}, bf16[256,1024]{1,0:T(8,128)(2,1)S(1)}, u32[]{:S(2)}, u32[]{:S(2)}) collective-permute-start(bf16[256,1024]{1,0:T(8,128)(2,1)} %get-tuple-element.52.refs_5_), channel_id=1, source_target_pairs={{0,16},{8,24},{16,0},{24,8},{1,17},{9,25},{17,1},{25,9},{2,18},{10... | collective-permute-start | bytes 1572872 | tf_op jit(solution)/shard_map/ppermute | solution.py:556
  43.8 2.8 %collective-permute-start.7 = (bf16[256,1024]{1,0:T(8,128)(2,1)}, bf16[256,1024]{1,0:T(8,128)(2,1)S(1)}, u32[]{:S(2)}, u32[]{:S(2)}) collective-permute-start(bf16[256,1024]{1,0:T(8,128)(2,1)} %get-tuple-element.53.refs_7_), channel_id=1, source_target_pairs={{0,8},{8,0},{16,24},{24,16},{1,9},{9,1},{17,25},{25,17},{2,10},{10... | collective-permute-start | bytes 1572872 | tf_op jit(solution)/shard_map/ppermute | solution.py:555
  46.6 5.6 %all-to-all-done.1.refs_0_ = bf16[8,176,128]{2,1,0:T(8,128)(2,1)S(1)} async-done(((bf16[8,176,128]{2,1,0:T(8,128)(2,1)}), bf16[8,176,128]{2,1,0:T(8,128)(2,1)S(1)}, u32[]{:S(2)}, u32[]{:S(2)}) %all-to-all-start.1) | async-done | bytes 360480 | tf_op jit(solution)/shard_map/all_to_all | solution.py:623
  52.3 0.0 copy-done
  52.3 0.0 copy-start.1
  52.3 1.0 %copy-done.1 = bf16[256,1024]{1,0:T(8,128)(2,1)S(1)} copy-done((bf16[256,1024]{1,0:T(8,128)(2,1)S(1)}, bf16[256,1024]{1,0:T(8,128)(2,1)}, u32[]{:S(2)}) %copy-start.1) | copy-done | bytes 524312
  53.3 0.0 copy-start.3
  53.3 1.0 %copy-done.3 = bf16[256,1024]{1,0:T(8,128)(2,1)S(1)} copy-done((bf16[256,1024]{1,0:T(8,128)(2,1)S(1)}, bf16[256,1024]{1,0:T(8,128)(2,1)}, u32[]{:S(2)}) %copy-start.3) | copy-done | bytes 524312
  54.4 4.5 %shard_map.128 = (f32[3,1,16]{2,1,0:T(1,128)S(1)}, f32[1,1,16]{2,1,0:T(1,128)S(1)}, bf16[96,1024]{1,0:T(8,128)(2,1)S(1)}) custom-call(s32[1]{0:T(128)} %bitcast.5.me_ref, s32[2,128]{1,0:T(2,128)S(1)} %get-tuple-element.32.refs_4_.moved_ref, bf16[8,176,128]{2,1,0:T(8,128)(2,1)S(1)} %all-to-all-done.1.refs_0_, bf16[256,1024]{1,0:T(8,128)(2,1)S(1)} %copy-done.3, ...), custom_call_target="tpu_custom_call" | custom-call | flops 268435456 | bytes 2097152 | tf_op jit(solution)/shard_map/pallas_call | solution.py:636
  58.8 0.0 collective-permute-done.8.refs_9_
  58.8 0.0 collective-permute-done.7.refs_8_
  58.9 9.9 %shard_map.129 = (f32[1024,1024]{1,0:T(8,128)}, f32[6,1,16]{2,1,0:T(1,128)}, f32[2,1,16]{2,1,0:T(1,128)}, f32[1,128]{1,0:T(1,128)}) custom-call(s32[1]{0:T(128)} %bitcast.2.role_ref, s32[1,128]{1,0:T(1,128)S(1)} %get-tuple-element.37.number_ref, bf16[96,1024]{1,0:T(8,128)(2,1)S(1)} %get-tuple-element.49.later_ref, ...), custom_call_target="tpu_custom_call" | custom-call | flops 134217728 | bytes 6291456 | tf_op jit(solution)/shard_map/pallas_call | solution.py:654
  (1 shorter events, 0.0 us)
Async XLA Ops:
  3.0 7.0 %collective-permute-start.2 = (f32[8,1024]{1,0:T(8,128)S(1)}, f32[8,1024]{1,0:T(8,128)S(1)}, u32[]{:S(2)}, u32[]{:S(2)}) collective-permute-start(f32[8,1024]{1,0:T(8,128)S(1)} %get-tuple-element.31.after_ref.refs_0_), channel_id=1, source_target_pairs={{0,24},{8,16},{16,8},{24,0},{1,25},{9,17},{17,9},{25,1},{2,26},{10... | collective-permute-start | bytes 98312 | tf_op jit(solution)/shard_map/ppermute | solution.py:479
  7.0 3.9 %collective-permute-start.1 = (f32[8,1024]{1,0:T(8,128)S(1)}, f32[8,1024]{1,0:T(8,128)S(1)}, u32[]{:S(2)}, u32[]{:S(2)}) collective-permute-start(f32[8,1024]{1,0:T(8,128)S(1)} %get-tuple-element.31.after_ref.refs_0_), channel_id=1, source_target_pairs={{0,16},{8,24},{16,0},{24,8},{1,17},{9,25},{17,1},{25,9},{2,18},{10... | collective-permute-start | bytes 98312 | tf_op jit(solution)/shard_map/ppermute | solution.py:479
  7.5 3.9 %collective-permute-start = (f32[8,1024]{1,0:T(8,128)S(1)}, f32[8,1024]{1,0:T(8,128)S(1)}, u32[]{:S(2)}, u32[]{:S(2)}) collective-permute-start(f32[8,1024]{1,0:T(8,128)S(1)} %get-tuple-element.31.after_ref.refs_0_), channel_id=1, source_target_pairs={{0,8},{8,0},{16,24},{24,16},{1,9},{9,1},{17,25},{25,17},{2,10},{10... | collective-permute-start | bytes 98312 | tf_op jit(solution)/shard_map/ppermute | solution.py:479
  11.4 15.3 %copy-start.2 = (bf16[256,1024]{1,0:T(8,128)(2,1)}, bf16[256,1024]{1,0:T(8,128)(2,1)S(1)}, u32[]{:S(2)}) copy-start(bf16[256,1024]{1,0:T(8,128)(2,1)S(1)} %get-tuple-element.44.refs_1_.refs_0_) | copy-start | bytes 1572868
  11.4 15.3 %collective-permute-start.3 = (bf16[256,1024]{1,0:T(8,128)(2,1)}, bf16[256,1024]{1,0:T(8,128)(2,1)}, u32[]{:S(2)}, u32[]{:S(2)}) collective-permute-start(bf16[256,1024]{1,0:T(8,128)(2,1)} %get-tuple-element.43.refs_4_.refs_3_), channel_id=1, source_target_pairs={{0,16},{8,24},{16,0},{24,8},{1,17},{9,25},{17,1},{25,9},{2,18},{10... | collective-permute-start | bytes 1572872 | tf_op jit(solution)/shard_map/ppermute | solution.py:556
  12.9 13.7 %collective-permute-start.4 = (bf16[256,1024]{1,0:T(8,128)(2,1)S(1)}, bf16[256,1024]{1,0:T(8,128)(2,1)}, u32[]{:S(2)}, u32[]{:S(2)}) collective-permute-start(bf16[256,1024]{1,0:T(8,128)(2,1)S(1)} %get-tuple-element.44.refs_1_.refs_0_), channel_id=1, source_target_pairs={{0,8},{8,0},{16,24},{24,16},{1,9},{9,1},{17,25},{25,17},{2,10},{10... | collective-permute-start | bytes 1572872 | tf_op jit(solution)/shard_map/ppermute | solution.py:555
  15.8 10.8 %all-to-all-start = ((f32[8,16,128]{2,1,0:T(8,128)}), f32[8,16,128]{2,1,0:T(8,128)S(1)}, u32[]{:S(2)}, u32[]{:S(2)}) async-start(f32[8,16,128]{2,1,0:T(8,128)} %get-tuple-element.38), calls=%async_computation | async-start | bytes 131072 | tf_op jit(solution)/shard_map/all_to_all | solution.py:526
  20.7 9.9 %copy-start.4 = (f32[3,1024]{1,0:T(4,128)S(1)}, f32[3,1024]{1,0:T(4,128)}, u32[]{:S(2)}) copy-start(f32[3,1024]{1,0:T(4,128)} %refs_1_.1) | copy-start | bytes 36868
  26.8 25.5 %copy-start = (bf16[256,1024]{1,0:T(8,128)(2,1)S(1)}, bf16[256,1024]{1,0:T(8,128)(2,1)}, u32[]{:S(2)}) copy-start(bf16[256,1024]{1,0:T(8,128)(2,1)} %get-tuple-element.41.own_a.own_b.refs_2_.refs_1_) | copy-start | bytes 1572868
  26.8 14.6 %collective-permute-start.5 = (bf16[256,1024]{1,0:T(8,128)(2,1)}, bf16[256,1024]{1,0:T(8,128)(2,1)}, u32[]{:S(2)}, u32[]{:S(2)}) collective-permute-start(bf16[256,1024]{1,0:T(8,128)(2,1)} %get-tuple-element.46.refs_4_), channel_id=1, source_target_pairs={{0,16},{8,24},{16,0},{24,8},{1,17},{9,25},{17,1},{25,9},{2,18},{10... | collective-permute-start | bytes 1572872 | tf_op jit(solution)/shard_map/ppermute | solution.py:556
  27.3 15.3 %collective-permute-start.6 = (bf16[256,1024]{1,0:T(8,128)(2,1)}, bf16[256,1024]{1,0:T(8,128)(2,1)}, u32[]{:S(2)}, u32[]{:S(2)}) collective-permute-start(bf16[256,1024]{1,0:T(8,128)(2,1)} %get-tuple-element.47.refs_6_), channel_id=1, source_target_pairs={{0,8},{8,0},{16,24},{24,16},{1,9},{9,1},{17,25},{25,17},{2,10},{10... | collective-permute-start | bytes 1572872 | tf_op jit(solution)/shard_map/ppermute | solution.py:555
  37.1 15.2 %all-to-all-start.1 = ((bf16[8,176,128]{2,1,0:T(8,128)(2,1)}), bf16[8,176,128]{2,1,0:T(8,128)(2,1)S(1)}, u32[]{:S(2)}, u32[]{:S(2)}) async-start(bf16[8,176,128]{2,1,0:T(8,128)(2,1)} %shard_map.126.refs_0_), calls=%async_computation.1 | async-start | bytes 720896 | tf_op jit(solution)/shard_map/all_to_all | solution.py:623
  42.7 16.1 %collective-permute-start.8 = (bf16[256,1024]{1,0:T(8,128)(2,1)}, bf16[256,1024]{1,0:T(8,128)(2,1)S(1)}, u32[]{:S(2)}, u32[]{:S(2)}) collective-permute-start(bf16[256,1024]{1,0:T(8,128)(2,1)} %get-tuple-element.52.refs_5_), channel_id=1, source_target_pairs={{0,16},{8,24},{16,0},{24,8},{1,17},{9,25},{17,1},{25,9},{2,18},{10... | collective-permute-start | bytes 1572872 | tf_op jit(solution)/shard_map/ppermute | solution.py:556
  43.8 15.0 %collective-permute-start.7 = (bf16[256,1024]{1,0:T(8,128)(2,1)}, bf16[256,1024]{1,0:T(8,128)(2,1)S(1)}, u32[]{:S(2)}, u32[]{:S(2)}) collective-permute-start(bf16[256,1024]{1,0:T(8,128)(2,1)} %get-tuple-element.53.refs_7_), channel_id=1, source_target_pairs={{0,8},{8,0},{16,24},{24,16},{1,9},{9,1},{17,25},{25,17},{2,10},{10... | collective-permute-start | bytes 1572872 | tf_op jit(solution)/shard_map/ppermute | solution.py:555
  52.3 1.0 %copy-start.1 = (bf16[256,1024]{1,0:T(8,128)(2,1)S(1)}, bf16[256,1024]{1,0:T(8,128)(2,1)}, u32[]{:S(2)}) copy-start(bf16[256,1024]{1,0:T(8,128)(2,1)} %get-tuple-element.42.own_b.own_a.refs_3_.refs_2_) | copy-start | bytes 1572868
  53.3 1.0 %copy-start.3 = (bf16[256,1024]{1,0:T(8,128)(2,1)S(1)}, bf16[256,1024]{1,0:T(8,128)(2,1)}, u32[]{:S(2)}) copy-start(bf16[256,1024]{1,0:T(8,128)(2,1)} %copy-done.2) | copy-start | bytes 1572868

commit v8 on v7

--- a/solution.py
+++ b/solution.py
@@ -323,18 +323,28 @@
 def sweep(matrix):
     size = matrix.shape[0]
     log = jnp.zeros((1, 1), F32)
-    for k in range(size):
-        pivot = matrix[k : k + 1, k : k + 1]
-        inverse = 1.0 / pivot
-        column = matrix[:, k : k + 1]
-        line = matrix[k : k + 1, :]
-        row_here = iota((size, size), 0) == k
-        lane_here = iota((size, size), 1) == k
-        scaled = line * inverse
-        reduced = matrix - column * scaled
-        matrix = jnp.where(row_here, scaled, jnp.where(lane_here, column * inverse, reduced))
-        matrix = jnp.where(jnp.logical_and(row_here, lane_here), -inverse, matrix)
-        log = log + jnp.log(pivot)
+    row = iota((size, size), 0)
+    lane = iota((size, size), 1)
+    place = iota((1, size), 1)
+    for k in range(0, size, 2):
+        a = matrix[k : k + 1, k : k + 1]
+        b = matrix[k : k + 1, k + 1 : k + 2]
+        d = matrix[k + 1 : k + 2, k + 1 : k + 2]
+        column_0, column_1 = matrix[:, k : k + 1], matrix[:, k + 1 : k + 2]
+        line_0, line_1 = matrix[k : k + 1, :], matrix[k + 1 : k + 2, :]
+        det = a * d - b * b
+        scale = 1.0 / det
+        a, b, d = a * scale, b * scale, d * scale
+        scaled_0 = d * line_0 - b * line_1
+        scaled_1 = a * line_1 - b * line_0
+        reduced = matrix - column_0 * scaled_0 - column_1 * scaled_1
+        edge_0 = d * column_0 - b * column_1
+        edge_1 = a * column_1 - b * column_0
+        scaled_0 = jnp.where(place == k, -d, jnp.where(place == k + 1, b, scaled_0))
+        scaled_1 = jnp.where(place == k, b, jnp.where(place == k + 1, -a, scaled_1))
+        matrix = jnp.where(lane == k, edge_0, jnp.where(lane == k + 1, edge_1, reduced))
+        matrix = jnp.where(row == k, scaled_0, jnp.where(row == k + 1, scaled_1, matrix))
+        log = log + jnp.log(det)
     return -matrix, log
 
 
@@ -353,10 +363,27 @@
     return dot(jnp.ones((8, size), F32), part, ((1,), (1,)), exact=True)[0:1]
 
 
-def first_kernel(count, sources, me_ref, moved_ref, *refs):
+def columns_kernel(count, inverse_hbm, moved_ref, after_ref, out_ref, staged, sem):
+    chunks, depth, electrons = staged.shape
+    loads = []
+    for chunk in range(chunks):
+        load = pltpu.make_async_copy(
+            rows_of(inverse_hbm, chunk, depth), staged.at[chunk], sem.at[chunk]
+        )
+        load.start()
+        loads.append(load)
+    block = iota((1, LANES), 1) // count
+    number = jnp.where(block == 0, moved_ref[0:1, :], -1)
+    pick = (iota((electrons, LANES), 0) == number).astype(F32).astype(BF16)
+    for chunk in range(chunks):
+        loads[chunk].wait()
+        found = dot(staged[chunk].astype(BF16), pick)
+        out_ref[chunk * depth : (chunk + 1) * depth] = found.astype(BF16)
+
+
+def first_kernel(count, sources, me_ref, *refs):
     values = refs[:sources]
-    blocks = refs[sources:-6]
-    drift_ref, lap_ref, later_ref, vals, columns = refs[-5:]
+    columns, drift_ref, lap_ref, later_ref, vals = refs[sources:]
     rows = later_ref.shape[0]
     if sources > 1:
         width = values[0].shape[1]
@@ -370,12 +397,6 @@
             where = slice(piece * width, (piece + 1) * width)
             later_ref[:, where] = values[0][piece, 0:rows]
             vals[:, where] = values[0][piece, rows:]
-    depth, electrons = blocks[0].shape
-    block = iota((1, LANES), 1) // count
-    number = jnp.where(block == 0, moved_ref[0:1, :], -1)
-    pick = (iota((electrons, LANES), 0) == number).astype(F32).astype(BF16)
-    for chunk, ref in enumerate(blocks):
-        columns[chunk * depth : (chunk + 1) * depth] = dot(ref[...], pick).astype(BF16)
     products = dot(vals[...], columns[...])
     ratio, inverse, _ = ratio_of(products, count)
     sums = moved_sums(products, ratio, inverse, count)
@@ -385,38 +406,68 @@
 
 
 def finish_kernel(
-    count, sources, chunks, role_ref, number_ref, later_ref, weight_ref, drift_in, lap_in, *refs
+    count,
+    sources,
+    role_ref,
+    number_ref,
+    later_ref,
+    weight_ref,
+    drift_in,
+    lap_in,
+    inverse_hbm,
+    *refs,
 ):
     inputs = refs[:-9]
     out_ref, drift_ref, lap_ref, out_weight_ref, parent, staged, columns, in_sem, out_sem = refs[-9:]
-    depth, electrons = inputs[0].shape
+    chunks, depth, electrons = parent.shape
     size = 2 * count
     role = role_ref[0]
+    mine = role == 0
     for chunk in range(chunks):
+        own = pltpu.make_async_copy(
+            rows_of(inverse_hbm, chunk, depth), staged.at[chunk], in_sem.at[chunk]
+        )
+        pl.when(mine)(own.start)
         for which, table in enumerate(sources):
-
-            @pl.when(role == which)
-            def _():
-                pltpu.make_async_copy(
+            if which:
+                sent = pltpu.make_async_copy(
                     inputs[table[chunk]], parent.at[chunk], in_sem.at[chunk]
-                ).start()
+                )
+                pl.when(role == which)(sent.start)
 
     pick = (iota((electrons, LANES), 0) == number_ref[...]).astype(F32).astype(BF16)
+    for chunk in range(chunks):
+        own = pltpu.make_async_copy(
+            rows_of(inverse_hbm, chunk, depth), staged.at[chunk], in_sem.at[chunk]
+        )
+        sent = pltpu.make_async_copy(inputs[0], parent.at[chunk], in_sem.at[chunk])
+
+        @pl.when(mine)
+        def _():
+            own.wait()
+            parent[chunk] = staged[chunk].astype(BF16)
+
+        @pl.when(jnp.logical_not(mine))
+        def _():
+            sent.wait()
+            staged[chunk] = parent[chunk].astype(F32)
+
+    for chunk in range(chunks):
+        rows = slice(chunk * depth, (chunk + 1) * depth)
+        columns[rows] = dot(parent[chunk], pick).astype(BF16)
+    products = dot(later_ref[...], columns[...])
+    ratio, inverse, log = ratio_of(products, size)
     total = jnp.zeros((size, electrons), F32)
     for chunk in range(chunks):
         rows = slice(chunk * depth, (chunk + 1) * depth)
-        pltpu.make_async_copy(inputs[chunk], parent.at[chunk], in_sem.at[chunk]).wait()
-        columns[rows] = dot(parent[chunk], pick).astype(BF16)
         total = total + dot(later_ref[0:size, rows], parent[chunk])
-    products = dot(later_ref[...], columns[...])
-    ratio, inverse, log = ratio_of(products, size)
     small = dot(inverse, ratio, ((1,), (1,)), exact=True)
     solved = dot(small, total, exact=True).astype(BF16)
     solved = jnp.concatenate([solved, jnp.zeros((LANES - size, electrons), BF16)], 0)
     copies = []
     for chunk in range(chunks):
         rows = slice(chunk * depth, (chunk + 1) * depth)
-        staged[chunk] = parent[chunk].astype(F32) - dot(columns[rows], solved)
+        staged[chunk] = staged[chunk] - dot(columns[rows], solved)
         copy = pltpu.make_async_copy(staged.at[chunk], out_ref.at[rows], out_sem.at[chunk])
         copy.start()
         copies.append(copy)
@@ -550,7 +601,7 @@
         own[chunk] = ready
 
     apart = apart.astype(jnp.int32).reshape(1)
-    arrays = list(own)
+    arrays = []
     if n_grp == 4:
         send_x = lambda block: lax.ppermute(block, "grp", pairs(n_grp, 1))
         send_y = lambda block: lax.ppermute(block, "grp", pairs(n_grp, 2))
@@ -575,7 +626,7 @@
         x2, y2 = send_x(y1), send_y(x1)
     else:
         token_1 = token_2 = jnp.zeros((8, LANES), F32)
-        table = [range(chunks)]
+        table = [()]
         for step in range(1, n_grp):
             table.append(range(len(arrays), len(arrays) + chunks))
             arrays += [lax.ppermute(block, "grp", pairs(n_grp, step)) for block in own]
@@ -629,8 +680,22 @@
         y2, x2, token_2 = relay((own[2], own[1]), (y2, x2), (computed,))
         x3, y3 = send_x(y2), send_y(x2)
         arrays += [x1, x2, y1, y2, x3, y3]
-        a1, a2, b1, b2, a3, b3 = range(chunks, chunks + 6)
-        table = [range(chunks), (a1, a2, a3, b3), (a3, b3, b2, b1), (b2, b3, a3, a2)]
+        a1, a2, b1, b2, a3, b3 = range(6)
+        table = [(), (a1, a2, a3, b3), (a3, b3, b2, b1), (b2, b3, a3, a2)]
+
+    columns = call(
+        functools.partial(columns_kernel, count),
+        shape((electrons, LANES), BF16),
+        [HBM, VM, ANY],
+        VM,
+        scratch=[
+            pltpu.VMEM((chunks, depth, electrons), F32),
+            pltpu.SemaphoreType.DMA((chunks,)),
+        ],
+        flops=2 * electrons * electrons * LANES,
+        moved=4 * electrons * electrons,
+        vmem=8,
+    )(*in_hbm(inverse), tiled, token_2)
 
     here = lax.axis_index("orb").astype(jnp.int32).reshape(1)
     drift, laplacian, later = call(
@@ -640,26 +705,22 @@
             shape((1, 1, count), F32),
             shape((6 * count, electrons), BF16),
         ),
-        [SM, VM] + [VM] * (targets + chunks) + [ANY],
+        [SM] + [VM] * (targets + 1),
         (VM, VM, VM),
-        scratch=[
-            pltpu.VMEM((5 * count, electrons), BF16),
-            pltpu.VMEM((electrons, LANES), BF16),
-        ],
-        flops=2 * electrons * electrons * LANES,
-        moved=2 * electrons * electrons,
-        vmem=8,
-    )(here, tiled, *values, *own, token_2)
+        scratch=[pltpu.VMEM((5 * count, electrons), BF16)],
+        flops=2 * electrons * 11 * count * LANES,
+        moved=44 * count * electrons,
+    )(here, *values, columns)
 
     updated, drift, laplacian, new_weight = call(
-        functools.partial(finish_kernel, count, table, chunks),
+        functools.partial(finish_kernel, count, table),
         (
             shape((electrons, electrons), F32),
             shape((6, 1, count), F32),
             shape((2, 1, count), F32),
             shape((1, LANES), F32),
         ),
-        [SM] + [VM] * 5 + [ANY] * len(arrays),
+        [SM] + [VM] * 5 + [HBM] + [ANY] * len(arrays),
         (HBM, VM, VM, VM),
         scratch=[
             pltpu.VMEM((chunks, depth, electrons), BF16),
@@ -671,7 +732,7 @@
         flops=4 * electrons * electrons * 2 * count,
         moved=6 * electrons * electrons,
         vmem=12,
-    )(role, number, later, weight, drift, laplacian, *in_hbm(*own), *arrays[chunks:])
+    )(role, number, later, weight, drift, laplacian, *in_hbm(inverse), *arrays)
 
     return updated[None], drift.reshape(2, 1, 3, count), laplacian, new_weight[0, :1]
 

time: 69.3 us -> 69.6 us (level)
  Pallas kernels: 30.2 us -> 36.6 us
  starting transfers between devices: 22.9 us -> 18.4 us
  local copies, waits for them, and re-layouts: 2.09 us -> 0.01 us
  waiting for transfers between devices: 10.9 us -> 11.9 us
    ppermute x3, starting transfers between devices: 6.77 us -> 2.21 us  [per_device(): send_x = lambda block: lax.ppermute(block, 'grp', pairs(n_grp, 1))]
    pallas_call x1 -> x2, Pallas kernels: 9.93 us -> 13.9 us  [the longest x1 11.4 us: per_device(): call(functools.partial(finish_kernel, count, table), (shape((electrons, e...]
    pallas_call x2, Pallas kernels: 0.17 us -> 3.96 us  [relay(): call(relay_kernel, (kept, kept, token), [SM] + [ANY] * (4 + len(first)),...]
    ppermute x3, waiting for transfers between devices: 1.22 us -> 4.14 us  [per_device(): send_x = lambda block: lax.ppermute(block, 'grp', pairs(n_grp, 1))]
    unnamed x10 -> x2, local copies, waits for them, and re-layouts: 2.09 us -> 0.01 us
    all_to_all x1, starting transfers between devices: 3.44 us -> 5.04 us  [per_device(): lax.all_to_all(values, 'orb', split_axis=0, concat_axis=0, tiled=True)]
    all_to_all x1, waiting for transfers between devices: 5.63 us -> 4.06 us  [per_device(): lax.all_to_all(values, 'orb', split_axis=0, concat_axis=0, tiled=True)]
    ppermute x3, starting transfers between devices: 3.19 us -> 1.66 us  [per_device(): send_y = lambda block: lax.ppermute(block, 'grp', pairs(n_grp, 2))]
  transfers between devices with their start and end apart: 11 -> 11, of which waited for: 6 -> 8; matrix products, arithmetic and copies ran while one was open for 0% -> 0% of each run, Pallas kernels for 27% -> 31%
where the time goes in v8:
time: 69.6 us
  Pallas kernels  36.6 us (53%)
  starting transfers between devices  18.4 us (26%)
  waiting for transfers between devices  11.9 us (17%)
  between operations  2.68 us (4%)
    pallas_call x1, Pallas kernels, per_device(): call(functools.partial(finish_kernel, count, table), (shape((electrons, e...  11.4 us
    pallas_call x1, Pallas kernels, per_device(): pl.pallas_call(functools.partial(evaluate_kernel, count, sources, targets...  6.42 us
    all_to_all x1, starting transfers between devices, per_device(): lax.all_to_all(values, 'orb', split_axis=0, concat_axis=0, tiled=True)  5.04 us
    all_to_all x1, starting transfers between devices, per_device(): lax.all_to_all(points, 'orb', split_axis=0, concat_axis=0, tiled=True)  4.88 us
    ppermute x3, starting transfers between devices, per_device(): lax.ppermute(record, 'grp', pairs(n_grp, s))  4.6 us
    ppermute x3, waiting for transfers between devices, per_device(): send_x = lambda block: lax.ppermute(block, 'grp', pairs(n_grp, 1))  4.14 us
    all_to_all x1, waiting for transfers between devices, per_device(): lax.all_to_all(values, 'orb', split_axis=0, concat_axis=0, tiled=True)  4.06 us
    pallas_call x1, Pallas kernels, per_device(): call(functools.partial(prepare_kernel, middle), (shape((plane, 5 * width)...  4.05 us
  transfers between devices with their start and end apart: 11, of which 8 were waited for; matrix products, arithmetic and copies ran while one was open for 0% of the time, Pallas kernels for 31%

profile of v8, /device:TPU:0, one launch (start us, length us, event | category | flops | bytes accessed | tf_op | source)
XLA Modules:
  0.0 69.6 jit_solution(14387545200187564593)
XLA Ops:
  1.3 1.7 %shard_map.120 = (f32[8,1024]{1,0:T(8,128)S(1)}, s32[2,128]{1,0:T(2,128)S(1)}, f32[2,8,128]{2,1,0:T(8,128)S(1)}) custom-call(f32[3,1,1024]{2,1,0:T(1,128)} %bitcast.12, s32[2,1,16]{2,1,0:T(1,128)} %moved_hbm.1, f32[6,1,16]{2,1,0:T(1,128)} %bitcast.13, f32[1]{0:T(128)S(6)} %copy.27.weight_ref), custom_call_target="tpu_custom_call" | custom-call | tf_op jit(solution)/shard_map/pallas_call | solution.py:509
  3.0 4.0 %collective-permute-start.2 = (f32[8,1024]{1,0:T(8,128)S(1)}, f32[8,1024]{1,0:T(8,128)S(1)}, u32[]{:S(2)}, u32[]{:S(2)}) collective-permute-start(f32[8,1024]{1,0:T(8,128)S(1)} %get-tuple-element.31.after_ref.refs_0_), channel_id=1, source_target_pairs={{0,24},{8,16},{16,8},{24,0},{1,25},{9,17},{17,9},{25,1},{2,26},{10... | collective-permute-start | bytes 98312 | tf_op jit(solution)/shard_map/ppermute | solution.py:530
  7.0 0.5 collective-permute-start.1
  7.5 0.1 collective-permute-start
  7.6 2.4 %shard_map.121 = (bf16[256,1024]{1,0:T(8,128)(2,1)}, bf16[256,1024]{1,0:T(8,128)(2,1)}) custom-call(f32[1,1024,1024]{2,1,0:T(8,128)} %inverse_hbm.7, f32[8,1024]{1,0:T(8,128)S(1)} %get-tuple-element.31.after_ref.refs_0_), custom_call_target="tpu_custom_call" | custom-call | bytes 3145728 | tf_op jit(solution)/shard_map/pallas_call | solution.py:538
  10.1 0.0 collective-permute-done.2.refs_4_.refs_3_
  10.1 0.8 %collective-permute-done.1.refs_3_.refs_2_ = f32[8,1024]{1,0:T(8,128)S(1)} collective-permute-done((f32[8,1024]{1,0:T(8,128)S(1)}, f32[8,1024]{1,0:T(8,128)S(1)}, u32[]{:S(2)}, u32[]{:S(2)}) %collective-permute-start.1) | collective-permute-done | bytes 32800 | tf_op jit(solution)/shard_map/ppermute | solution.py:530
  10.9 0.5 collective-permute-done.refs_2_.refs_1_
  11.4 1.5 %collective-permute-start.3 = (bf16[256,1024]{1,0:T(8,128)(2,1)}, bf16[256,1024]{1,0:T(8,128)(2,1)S(1)}, u32[]{:S(2)}, u32[]{:S(2)}) collective-permute-start(bf16[256,1024]{1,0:T(8,128)(2,1)} %get-tuple-element.43), channel_id=1, source_target_pairs={{0,16},{8,24},{16,0},{24,8},{1,17},{9,25},{17,1},{25,9},{2,18},{10... | collective-permute-start | bytes 1572872 | tf_op jit(solution)/shard_map/ppermute | solution.py:607
  12.9 0.7 collective-permute-start.4
  14.9 1.0 %shard_map.123 = (f32[8,16,128]{2,1,0:T(8,128)}, f32[1,128]{1,0:T(1,128)S(1)}, s32[1,128]{1,0:T(1,128)S(1)}) custom-call(s32[1]{0:T(128)} %bitcast.2.role_ref, f32[8,1024]{1,0:T(8,128)S(1)} %get-tuple-element.31.after_ref.refs_0_, f32[8,1024]{1,0:T(8,128)S(1)} %collective-permute-done.refs_2_.refs_1_, f32[8,1024]{1,0:T(8,128)S(1)} %collective-permute-done.1.refs_3_.refs_2_, ...), custom_call_target="tpu_custom_call" | custom-call | tf_op jit(solution)/shard_map/pallas_call | solution.py:564
  15.9 4.9 %all-to-all-start = ((f32[8,16,128]{2,1,0:T(8,128)}), f32[8,16,128]{2,1,0:T(8,128)S(1)}, u32[]{:S(2)}, u32[]{:S(2)}) async-start(f32[8,16,128]{2,1,0:T(8,128)} %get-tuple-element.38), calls=%async_computation | async-start | bytes 131072 | tf_op jit(solution)/shard_map/all_to_all | solution.py:577
  20.7 0.0 copy-start
  20.7 4.1 %shard_map.124 = (bf16[2048,640]{1,0:T(8,128)(2,1)S(1)}, bf16[256,1024]{1,0:T(8,128)(2,1)}, bf16[256,1024]{1,0:T(8,128)(2,1)}) custom-call(bf16[2048,128]{1,0:T(8,128)(2,1)} %coeff_hbm.1, f32[3,1024]{1,0:T(4,128)} %refs_1_.1, f32[1,1024,1024]{2,1,0:T(8,128)} %inverse_hbm.7, f32[1,128]{1,0:T(1,128)S(1)} %get-tuple-element.39.after_ref.weight_ref), custom_call_target="tpu_custom_call" | custom-call | flops 2097152 | bytes 5767168 | tf_op jit(solution)/shard_map/pallas_call | solution.py:581
  24.8 1.9 %all-to-all-done.refs_1_.refs_0_ = f32[8,16,128]{2,1,0:T(8,128)S(1)} async-done(((f32[8,16,128]{2,1,0:T(8,128)}), f32[8,16,128]{2,1,0:T(8,128)S(1)}, u32[]{:S(2)}, u32[]{:S(2)}) %all-to-all-start) | async-done | bytes 65568 | tf_op jit(solution)/shard_map/all_to_all | solution.py:577
  26.7 0.0 collective-permute-done.3.got_a
  26.7 0.0 collective-permute-done.4.got_b
  26.7 2.0 %shard_map.125 = (bf16[256,1024]{1,0:T(8,128)(2,1)S(1)}, bf16[256,1024]{1,0:T(8,128)(2,1)}, f32[8,128]{1,0:T(8,128)S(1)}) custom-call(s32[1]{0:T(128)} %bitcast.6.flag_ref, bf16[256,1024]{1,0:T(8,128)(2,1)} %get-tuple-element.41.own_a.own_b, bf16[256,1024]{1,0:T(8,128)(2,1)} %get-tuple-element.42.own_b.own_a, ...), custom_call_target="tpu_custom_call", output_to_operand_aliasing={{0}: (3, {}), {1}: (4, {})} | custom-call | tf_op jit(solution)/shard_map/pallas_call | solution.py:610
  28.6 0.1 collective-permute-start.5
  28.7 0.1 collective-permute-start.6
  28.8 0.0 copy-done
  28.8 6.4 %shard_map.126.refs_0_ = bf16[8,176,128]{2,1,0:T(8,128)(2,1)} custom-call(f32[8,16,128]{2,1,0:T(8,128)S(1)} %all-to-all-done.refs_1_.refs_0_, f32[3,1024]{1,0:T(4,128)S(1)} %copy-done, bf16[2048,640]{1,0:T(8,128)(2,1)S(1)} %get-tuple-element.40.refs_0_.refs_2_, f32[8,128]{1,0:T(8,128)S(1)} %get-tuple-element.45.refs_3_), custom_call_target="tpu_custom_call" | custom-call | flops 738197504 | bytes 3145728 | tf_op jit(solution)/shard_map/pallas_call | solution.py:649
  35.2 5.0 %all-to-all-start.1 = ((bf16[8,176,128]{2,1,0:T(8,128)(2,1)}), bf16[8,176,128]{2,1,0:T(8,128)(2,1)S(1)}, u32[]{:S(2)}, u32[]{:S(2)}) async-start(bf16[8,176,128]{2,1,0:T(8,128)(2,1)} %shard_map.126.refs_0_), calls=%async_computation.1 | async-start | bytes 720896 | tf_op jit(solution)/shard_map/all_to_all | solution.py:674
  40.3 0.3 collective-permute-done.5.got_a
  40.6 1.4 %collective-permute-done.6.got_b = bf16[256,1024]{1,0:T(8,128)(2,1)} collective-permute-done((bf16[256,1024]{1,0:T(8,128)(2,1)S(1)}, bf16[256,1024]{1,0:T(8,128)(2,1)}, u32[]{:S(2)}, u32[]{:S(2)}) %collective-permute-start.6) | collective-permute-done | bytes 524320 | tf_op jit(solution)/shard_map/ppermute | solution.py:606
  42.0 2.0 %shard_map.127 = (bf16[256,1024]{1,0:T(8,128)(2,1)}, bf16[256,1024]{1,0:T(8,128)(2,1)}, f32[8,128]{1,0:T(8,128)S(1)}) custom-call(s32[1]{0:T(128)} %bitcast.6.flag_ref, bf16[256,1024]{1,0:T(8,128)(2,1)} %get-tuple-element.42.own_b.own_a, bf16[256,1024]{1,0:T(8,128)(2,1)} %get-tuple-element.41.own_a.own_b, ...), custom_call_target="tpu_custom_call", output_to_operand_aliasing={{0}: (3, {}), {1}: (4, {})} | custom-call | tf_op jit(solution)/shard_map/pallas_call | solution.py:610
  44.0 0.1 collective-permute-start.8
  44.1 1.5 %collective-permute-start.7 = (bf16[256,1024]{1,0:T(8,128)(2,1)}, bf16[256,1024]{1,0:T(8,128)(2,1)S(1)}, u32[]{:S(2)}, u32[]{:S(2)}) collective-permute-start(bf16[256,1024]{1,0:T(8,128)(2,1)} %get-tuple-element.53.refs_3_), channel_id=1, source_target_pairs={{0,8},{8,0},{16,24},{24,16},{1,9},{9,1},{17,25},{25,17},{2,10},{10... | collective-permute-start | bytes 1572872 | tf_op jit(solution)/shard_map/ppermute | solution.py:606
  45.6 2.5 %shard_map.128.refs_1_ = bf16[1024,128]{1,0:T(8,128)(2,1)S(1)} custom-call(f32[1,1024,1024]{2,1,0:T(8,128)} %inverse_hbm.7, s32[2,128]{1,0:T(2,128)S(1)} %get-tuple-element.32.refs_4_.moved_ref, f32[8,128]{1,0:T(8,128)S(1)} %get-tuple-element.48.after_ref), custom_call_target="tpu_custom_call" | custom-call | flops 268435456 | bytes 4194304 | tf_op jit(solution)/shard_map/pallas_call | solution.py:686
  48.1 4.1 %all-to-all-done.1.refs_0_ = bf16[8,176,128]{2,1,0:T(8,128)(2,1)S(1)} async-done(((bf16[8,176,128]{2,1,0:T(8,128)(2,1)}), bf16[8,176,128]{2,1,0:T(8,128)(2,1)S(1)}, u32[]{:S(2)}, u32[]{:S(2)}) %all-to-all-start.1) | async-done | bytes 360480 | tf_op jit(solution)/shard_map/all_to_all | solution.py:674
  52.1 3.1 %shard_map.129 = (f32[3,1,16]{2,1,0:T(1,128)S(1)}, f32[1,1,16]{2,1,0:T(1,128)S(1)}, bf16[96,1024]{1,0:T(8,128)(2,1)S(1)}) custom-call(s32[1]{0:T(128)} %bitcast.5.me_ref, bf16[8,176,128]{2,1,0:T(8,128)(2,1)S(1)} %all-to-all-done.1.refs_0_, bf16[1024,128]{1,0:T(8,128)(2,1)S(1)} %shard_map.128.refs_1_), custom_call_target="tpu_custom_call" | custom-call | flops 46137344 | bytes 720896 | tf_op jit(solution)/shard_map/pallas_call | solution.py:701
  55.3 0.2 collective-permute-done.8.refs_5_
  55.5 2.7 %collective-permute-done.7.refs_4_ = bf16[256,1024]{1,0:T(8,128)(2,1)S(1)} collective-permute-done((bf16[256,1024]{1,0:T(8,128)(2,1)}, bf16[256,1024]{1,0:T(8,128)(2,1)S(1)}, u32[]{:S(2)}, u32[]{:S(2)}) %collective-permute-start.7) | collective-permute-done | bytes 524320 | tf_op jit(solution)/shard_map/ppermute | solution.py:606
  58.2 11.4 %shard_map.130 = (f32[1024,1024]{1,0:T(8,128)}, f32[6,1,16]{2,1,0:T(1,128)}, f32[2,1,16]{2,1,0:T(1,128)}, f32[1,128]{1,0:T(1,128)}) custom-call(s32[1]{0:T(128)} %bitcast.2.role_ref, s32[1,128]{1,0:T(1,128)S(1)} %get-tuple-element.37.number_ref, bf16[96,1024]{1,0:T(8,128)(2,1)S(1)} %get-tuple-element.49.later_ref, ...), custom_call_target="tpu_custom_call" | custom-call | flops 134217728 | bytes 6291456 | tf_op jit(solution)/shard_map/pallas_call | solution.py:715
  (1 shorter events, 0.0 us)
Async XLA Ops:
  3.0 7.1 %collective-permute-start.2 = (f32[8,1024]{1,0:T(8,128)S(1)}, f32[8,1024]{1,0:T(8,128)S(1)}, u32[]{:S(2)}, u32[]{:S(2)}) collective-permute-start(f32[8,1024]{1,0:T(8,128)S(1)} %get-tuple-element.31.after_ref.refs_0_), channel_id=1, source_target_pairs={{0,24},{8,16},{16,8},{24,0},{1,25},{9,17},{17,9},{25,1},{2,26},{10... | collective-permute-start | bytes 98312 | tf_op jit(solution)/shard_map/ppermute | solution.py:530
  7.0 3.9 %collective-permute-start.1 = (f32[8,1024]{1,0:T(8,128)S(1)}, f32[8,1024]{1,0:T(8,128)S(1)}, u32[]{:S(2)}, u32[]{:S(2)}) collective-permute-start(f32[8,1024]{1,0:T(8,128)S(1)} %get-tuple-element.31.after_ref.refs_0_), channel_id=1, source_target_pairs={{0,16},{8,24},{16,0},{24,8},{1,17},{9,25},{17,1},{25,9},{2,18},{10... | collective-permute-start | bytes 98312 | tf_op jit(solution)/shard_map/ppermute | solution.py:530
  7.5 3.9 %collective-permute-start = (f32[8,1024]{1,0:T(8,128)S(1)}, f32[8,1024]{1,0:T(8,128)S(1)}, u32[]{:S(2)}, u32[]{:S(2)}) collective-permute-start(f32[8,1024]{1,0:T(8,128)S(1)} %get-tuple-element.31.after_ref.refs_0_), channel_id=1, source_target_pairs={{0,8},{8,0},{16,24},{24,16},{1,9},{9,1},{17,25},{25,17},{2,10},{10... | collective-permute-start | bytes 98312 | tf_op jit(solution)/shard_map/ppermute | solution.py:530
  11.4 15.3 %collective-permute-start.3 = (bf16[256,1024]{1,0:T(8,128)(2,1)}, bf16[256,1024]{1,0:T(8,128)(2,1)S(1)}, u32[]{:S(2)}, u32[]{:S(2)}) collective-permute-start(bf16[256,1024]{1,0:T(8,128)(2,1)} %get-tuple-element.43), channel_id=1, source_target_pairs={{0,16},{8,24},{16,0},{24,8},{1,17},{9,25},{17,1},{25,9},{2,18},{10... | collective-permute-start | bytes 1572872 | tf_op jit(solution)/shard_map/ppermute | solution.py:607
  12.9 13.8 %collective-permute-start.4 = (bf16[256,1024]{1,0:T(8,128)(2,1)}, bf16[256,1024]{1,0:T(8,128)(2,1)}, u32[]{:S(2)}, u32[]{:S(2)}) collective-permute-start(bf16[256,1024]{1,0:T(8,128)(2,1)} %get-tuple-element.44), channel_id=1, source_target_pairs={{0,8},{8,0},{16,24},{24,16},{1,9},{9,1},{17,25},{25,17},{2,10},{10... | collective-permute-start | bytes 1572872 | tf_op jit(solution)/shard_map/ppermute | solution.py:606
  15.9 10.8 %all-to-all-start = ((f32[8,16,128]{2,1,0:T(8,128)}), f32[8,16,128]{2,1,0:T(8,128)S(1)}, u32[]{:S(2)}, u32[]{:S(2)}) async-start(f32[8,16,128]{2,1,0:T(8,128)} %get-tuple-element.38), calls=%async_computation | async-start | bytes 131072 | tf_op jit(solution)/shard_map/all_to_all | solution.py:577
  20.7 8.1 %copy-start = (f32[3,1024]{1,0:T(4,128)S(1)}, f32[3,1024]{1,0:T(4,128)}, u32[]{:S(2)}) copy-start(f32[3,1024]{1,0:T(4,128)} %refs_1_.1) | copy-start | bytes 36868
  28.6 12.0 %collective-permute-start.5 = (bf16[256,1024]{1,0:T(8,128)(2,1)}, bf16[256,1024]{1,0:T(8,128)(2,1)}, u32[]{:S(2)}, u32[]{:S(2)}) collective-permute-start(bf16[256,1024]{1,0:T(8,128)(2,1)} %get-tuple-element.46.refs_0_), channel_id=1, source_target_pairs={{0,16},{8,24},{16,0},{24,8},{1,17},{9,25},{17,1},{25,9},{2,18},{10... | collective-permute-start | bytes 1572872 | tf_op jit(solution)/shard_map/ppermute | solution.py:607
  28.7 13.3 %collective-permute-start.6 = (bf16[256,1024]{1,0:T(8,128)(2,1)S(1)}, bf16[256,1024]{1,0:T(8,128)(2,1)}, u32[]{:S(2)}, u32[]{:S(2)}) collective-permute-start(bf16[256,1024]{1,0:T(8,128)(2,1)S(1)} %get-tuple-element.47.refs_2_), channel_id=1, source_target_pairs={{0,8},{8,0},{16,24},{24,16},{1,9},{9,1},{17,25},{25,17},{2,10},{10... | collective-permute-start | bytes 1572872 | tf_op jit(solution)/shard_map/ppermute | solution.py:606
  35.2 16.9 %all-to-all-start.1 = ((bf16[8,176,128]{2,1,0:T(8,128)(2,1)}), bf16[8,176,128]{2,1,0:T(8,128)(2,1)S(1)}, u32[]{:S(2)}, u32[]{:S(2)}) async-start(bf16[8,176,128]{2,1,0:T(8,128)(2,1)} %shard_map.126.refs_0_), calls=%async_computation.1 | async-start | bytes 720896 | tf_op jit(solution)/shard_map/all_to_all | solution.py:674
  44.0 11.5 %collective-permute-start.8 = (bf16[256,1024]{1,0:T(8,128)(2,1)}, bf16[256,1024]{1,0:T(8,128)(2,1)S(1)}, u32[]{:S(2)}, u32[]{:S(2)}) collective-permute-start(bf16[256,1024]{1,0:T(8,128)(2,1)} %get-tuple-element.52.refs_1_), channel_id=1, source_target_pairs={{0,16},{8,24},{16,0},{24,8},{1,17},{9,25},{17,1},{25,9},{2,18},{10... | collective-permute-start | bytes 1572872 | tf_op jit(solution)/shard_map/ppermute | solution.py:607
  44.1 14.1 %collective-permute-start.7 = (bf16[256,1024]{1,0:T(8,128)(2,1)}, bf16[256,1024]{1,0:T(8,128)(2,1)S(1)}, u32[]{:S(2)}, u32[]{:S(2)}) collective-permute-start(bf16[256,1024]{1,0:T(8,128)(2,1)} %get-tuple-element.53.refs_3_), channel_id=1, source_target_pairs={{0,8},{8,0},{16,24},{24,16},{1,9},{9,1},{17,25},{25,17},{2,10},{10... | collective-permute-start | bytes 1572872 | tf_op jit(solution)/shard_map/ppermute | solution.py:606

commit v9 on v8

--- a/solution.py
+++ b/solution.py
@@ -405,70 +405,121 @@
     lap_ref[0] = sums[:, 3 * count : 4 * count]
 
 
+def pick_from(number_ref, electrons):
+    return (iota((electrons, LANES), 0) == number_ref[...]).astype(F32).astype(BF16)
+
+
+def chunk_at(plan, role, slot):
+    chunk = jnp.int32(plan[0][slot][0])
+    for which in range(1, len(plan)):
+        chunk = jnp.where(role == which, plan[which][slot][0], chunk)
+    return chunk
+
+
+def load_slots(plan, slots, role, inverse_hbm, inputs, parent, staged, sem):
+    depth = parent.shape[1]
+    for slot in slots:
+        own = pltpu.make_async_copy(
+            rows_of(inverse_hbm, plan[0][slot][0], depth), staged.at[slot], sem.at[slot]
+        )
+        pl.when(role == 0)(own.start)
+        for which in range(1, len(plan)):
+            sent = pltpu.make_async_copy(
+                inputs[plan[which][slot][1]], parent.at[slot], sem.at[slot]
+            )
+            pl.when(role == which)(sent.start)
+
+
+def settle_slots(plan, slots, role, inverse_hbm, inputs, parent, staged, sem):
+    depth = parent.shape[1]
+    for slot in slots:
+        own = pltpu.make_async_copy(
+            rows_of(inverse_hbm, plan[0][slot][0], depth), staged.at[slot], sem.at[slot]
+        )
+        sent = pltpu.make_async_copy(inputs[0], parent.at[slot], sem.at[slot])
+
+        @pl.when(role == 0)
+        def _():
+            own.wait()
+            parent[slot] = staged[slot].astype(BF16)
+
+        @pl.when(role != 0)
+        def _():
+            sent.wait()
+            staged[slot] = parent[slot].astype(F32)
+
+
+def early_kernel(count, plan, role_ref, number_ref, later_ref, inverse_hbm, *refs):
+    inputs = refs[:-6]
+    columns_ref, products_ref, total_ref, parent, staged, sem = refs[-6:]
+    slots, depth, electrons = parent.shape
+    role = role_ref[0]
+    load_slots(plan, range(slots), role, inverse_hbm, inputs, parent, staged, sem)
+    pick = pick_from(number_ref, electrons)
+    settle_slots(plan, range(slots), role, inverse_hbm, inputs, parent, staged, sem)
+    products, total = None, None
+    for slot in range(slots):
+        columns = dot(parent[slot], pick).astype(BF16)
+        columns_ref[slot] = columns
+        at = pl.multiple_of(chunk_at(plan, role, slot) * depth, depth)
+        rows = later_ref[:, pl.ds(at, depth)]
+        part = dot(rows, columns)
+        more = dot(rows[0 : 2 * count], parent[slot])
+        products = part if slot == 0 else products + part
+        total = more if slot == 0 else total + more
+    products_ref[...] = products
+    total_ref[...] = total
+
+
 def finish_kernel(
     count,
-    sources,
+    plan,
     role_ref,
     number_ref,
     later_ref,
     weight_ref,
     drift_in,
     lap_in,
+    early_ref,
+    products_ref,
+    total_ref,
     inverse_hbm,
     *refs,
 ):
-    inputs = refs[:-9]
-    out_ref, drift_ref, lap_ref, out_weight_ref, parent, staged, columns, in_sem, out_sem = refs[-9:]
+    inputs = refs[:-8]
+    out_ref, drift_ref, lap_ref, out_weight_ref, parent, staged, in_sem, out_sem = refs[-8:]
     chunks, depth, electrons = parent.shape
+    done = early_ref.shape[0]
+    late = range(done, chunks)
     size = 2 * count
     role = role_ref[0]
-    mine = role == 0
-    for chunk in range(chunks):
-        own = pltpu.make_async_copy(
-            rows_of(inverse_hbm, chunk, depth), staged.at[chunk], in_sem.at[chunk]
-        )
-        pl.when(mine)(own.start)
-        for which, table in enumerate(sources):
-            if which:
-                sent = pltpu.make_async_copy(
-                    inputs[table[chunk]], parent.at[chunk], in_sem.at[chunk]
-                )
-                pl.when(role == which)(sent.start)
-
-    pick = (iota((electrons, LANES), 0) == number_ref[...]).astype(F32).astype(BF16)
-    for chunk in range(chunks):
-        own = pltpu.make_async_copy(
-            rows_of(inverse_hbm, chunk, depth), staged.at[chunk], in_sem.at[chunk]
-        )
-        sent = pltpu.make_async_copy(inputs[0], parent.at[chunk], in_sem.at[chunk])
-
-        @pl.when(mine)
-        def _():
-            own.wait()
-            parent[chunk] = staged[chunk].astype(BF16)
-
-        @pl.when(jnp.logical_not(mine))
-        def _():
-            sent.wait()
-            staged[chunk] = parent[chunk].astype(F32)
-
-    for chunk in range(chunks):
-        rows = slice(chunk * depth, (chunk + 1) * depth)
-        columns[rows] = dot(parent[chunk], pick).astype(BF16)
-    products = dot(later_ref[...], columns[...])
+    loads = (role, inverse_hbm, inputs, parent, staged, in_sem)
+    load_slots(plan, list(late) + list(range(done)), *loads)
+    pick = pick_from(number_ref, electrons)
+    settle_slots(plan, late, *loads)
+    columns = [early_ref[slot] for slot in range(done)]
+    products = products_ref[...]
+    rows = []
+    for slot in late:
+        columns.append(dot(parent[slot], pick).astype(BF16))
+        at = pl.multiple_of(chunk_at(plan, role, slot) * depth, depth)
+        rows.append(later_ref[:, pl.ds(at, depth)])
+        products = products + dot(rows[-1], columns[-1])
+    settle_slots(plan, range(done), *loads)
     ratio, inverse, log = ratio_of(products, size)
-    total = jnp.zeros((size, electrons), F32)
-    for chunk in range(chunks):
-        rows = slice(chunk * depth, (chunk + 1) * depth)
-        total = total + dot(later_ref[0:size, rows], parent[chunk])
+    total = total_ref[...]
+    for slot, part in zip(late, rows):
+        total = total + dot(part[0:size], parent[slot])
     small = dot(inverse, ratio, ((1,), (1,)), exact=True)
     solved = dot(small, total, exact=True).astype(BF16)
     solved = jnp.concatenate([solved, jnp.zeros((LANES - size, electrons), BF16)], 0)
     copies = []
-    for chunk in range(chunks):
-        rows = slice(chunk * depth, (chunk + 1) * depth)
-        staged[chunk] = staged[chunk] - dot(columns[rows], solved)
-        copy = pltpu.make_async_copy(staged.at[chunk], out_ref.at[rows], out_sem.at[chunk])
+    for slot in range(chunks):
+        staged[slot] = staged[slot] - dot(columns[slot], solved)
+        at = pl.multiple_of(chunk_at(plan, role, slot) * depth, depth)
+        copy = pltpu.make_async_copy(
+            staged.at[slot], out_ref.at[pl.ds(at, depth)], out_sem.at[slot]
+        )
         copy.start()
         copies.append(copy)
     sums = moved_sums(products, ratio, inverse, count)
@@ -501,11 +552,9 @@
     local = coefficients.shape[1]
     others = n_grp - 1
     chunks = 4
-    group = lax.axis_index("grp")
-    source = donor[0]
-    apart = distance(n_grp, group, source)
-    role = jnp.where(take[0] == 1, apart, 0).astype(jnp.int32).reshape(1)
-
+
+    apart = distance(n_grp, lax.axis_index("grp"), donor[0]).astype(jnp.int32).reshape(1)
+    role = jnp.where(take == 1, apart, 0)
     record, tiled, disp = call(
         functools.partial(start_kernel, count),
         (
@@ -523,7 +572,9 @@
         ],
     )(
         *in_hbm(
-            positions.reshape(3, 1, electrons), moved, displacements.reshape(6, 1, count)
+            positions.reshape(3, 1, electrons),
+            moved,
+            displacements.reshape(6, 1, count),
         ),
         log_weight,
     )
@@ -552,11 +603,11 @@
     own[0], own[-1], token_0 = call(
         gate_kernel,
         (kept, kept, token),
-        [ANY] * (2 + others),
+        [ANY] * (2 + others) + [SM, SM],
         (ANY, ANY, VM),
         aliases={0: 0, 1: 1},
         vmem=1,
-    )(own[0], own[-1], *records)
+    )(own[0], own[-1], *records, role, apart)
 
     few = is_power(n_orb) and local % LANES == 0
     direct = few and DIRECT_POINTS
@@ -600,7 +651,6 @@
     for chunk, ready in zip(middle, prepared):
         own[chunk] = ready
 
-    apart = apart.astype(jnp.int32).reshape(1)
     arrays = []
     if n_grp == 4:
         send_x = lambda block: lax.ppermute(block, "grp", pairs(n_grp, 1))
@@ -626,10 +676,11 @@
         x2, y2 = send_x(y1), send_y(x1)
     else:
         token_1 = token_2 = jnp.zeros((8, LANES), F32)
-        table = [()]
+        plan = [tuple((chunk, 0) for chunk in range(chunks))]
         for step in range(1, n_grp):
-            table.append(range(len(arrays), len(arrays) + chunks))
+            plan.append(tuple((chunk, len(arrays) + chunk) for chunk in range(chunks)))
             arrays += [lax.ppermute(block, "grp", pairs(n_grp, step)) for block in own]
+        settled = len(arrays)
 
     height = 11 * count
     spread = few and DIRECT_VALUES
@@ -679,9 +730,16 @@
     if n_grp == 4:
         y2, x2, token_2 = relay((own[2], own[1]), (y2, x2), (computed,))
         x3, y3 = send_x(y2), send_y(x2)
-        arrays += [x1, x2, y1, y2, x3, y3]
+        arrays = [x1, x2, y1, y2, x3, y3]
         a1, a2, b1, b2, a3, b3 = range(6)
-        table = [(), (a1, a2, a3, b3), (a3, b3, b2, b1), (b2, b3, a3, a2)]
+        first, second, third, fourth = range(chunks)
+        plan = [
+            tuple((chunk, 0) for chunk in range(chunks)),
+            ((first, a1), (second, a2), (third, a3), (fourth, b3)),
+            ((fourth, b1), (third, b2), (first, a3), (second, b3)),
+            ((fourth, a2), (first, b2), (third, a3), (second, b3)),
+        ]
+        settled = 4
 
     columns = call(
         functools.partial(columns_kernel, count),
@@ -712,27 +770,59 @@
         moved=44 * count * electrons,
     )(here, *values, columns)
 
+    early = 2
+    work = 2 * electrons * 2 * count
+    early_columns, products, total = call(
+        functools.partial(early_kernel, count, plan),
+        (
+            shape((early, depth, LANES), BF16),
+            shape((6 * count, LANES), F32),
+            shape((2 * count, electrons), F32),
+        ),
+        [SM, VM, VM, HBM] + [ANY] * settled,
+        (VM, VM, VM),
+        scratch=[
+            pltpu.VMEM((early, depth, electrons), BF16),
+            pltpu.VMEM((early, depth, electrons), F32),
+            pltpu.SemaphoreType.DMA((early,)),
+        ],
+        flops=early * depth * work,
+        moved=2 * early * depth * electrons,
+        vmem=8,
+    )(role, number, later, *in_hbm(inverse), *arrays[:settled])
+
     updated, drift, laplacian, new_weight = call(
-        functools.partial(finish_kernel, count, table),
+        functools.partial(finish_kernel, count, plan),
         (
             shape((electrons, electrons), F32),
             shape((6, 1, count), F32),
             shape((2, 1, count), F32),
             shape((1, LANES), F32),
         ),
-        [SM] + [VM] * 5 + [HBM] + [ANY] * len(arrays),
+        [SM] + [VM] * 8 + [HBM] + [ANY] * len(arrays),
         (HBM, VM, VM, VM),
         scratch=[
             pltpu.VMEM((chunks, depth, electrons), BF16),
             pltpu.VMEM((chunks, depth, electrons), F32),
-            pltpu.VMEM((electrons, LANES), BF16),
             pltpu.SemaphoreType.DMA((chunks,)),
             pltpu.SemaphoreType.DMA((chunks,)),
         ],
-        flops=4 * electrons * electrons * 2 * count,
+        flops=2 * electrons * work,
         moved=6 * electrons * electrons,
         vmem=12,
-    )(role, number, later, weight, drift, laplacian, *in_hbm(inverse), *arrays)
+    )(
+        role,
+        number,
+        later,
+        weight,
+        drift,
+        laplacian,
+        early_columns,
+        products,
+        total,
+        *in_hbm(inverse),
+        *arrays,
+    )
 
     return updated[None], drift.reshape(2, 1, 3, count), laplacian, new_weight[0, :1]
 

time: 69.6 us -> 69.2 us (level)
  waiting for transfers between devices: 11.9 us -> 9.07 us
  Pallas kernels: 36.6 us -> 38.2 us
  starting transfers between devices: 18.4 us -> 19.6 us
    ppermute x3, waiting for transfers between devices: 4.14 us -> 0.01 us  [per_device(): send_x = lambda block: lax.ppermute(block, 'grp', pairs(n_grp, 1))]
    all_to_all x1, waiting for transfers between devices: 4.06 us -> 6.26 us  [per_device(): lax.all_to_all(values, 'orb', split_axis=0, concat_axis=0, tiled=True)]
    pallas_call x2 -> x3, Pallas kernels: 11.4 us -> 13 us  [the longest x1 10.7 us: per_device(): call(functools.partial(finish_kernel, count, plan), (shape((electrons, el...]
    ppermute x3, waiting for transfers between devices: 1.32 us -> 0.01 us  [per_device(): lax.ppermute(record, 'grp', pairs(n_grp, s))]
    all_to_all x1, starting transfers between devices: 5.04 us -> 6.35 us  [per_device(): lax.all_to_all(values, 'orb', split_axis=0, concat_axis=0, tiled=True)]
  transfers between devices with their start and end apart: 11 -> 11, of which waited for: 8 -> 3; matrix products, arithmetic and copies ran while one was open for 0% -> 0% of each run, Pallas kernels for 31% -> 34%
where the time goes in v9:
time: 69.2 us; the launch traced here: 69.6 us
  Pallas kernels  38.2 us (55%)
  starting transfers between devices  19.6 us (28%)
  waiting for transfers between devices  9.07 us (13%)
  between operations  2.74 us (4%)
    pallas_call x1, Pallas kernels, per_device(): call(functools.partial(finish_kernel, count, plan), (shape((electrons, el...  10.7 us
    pallas_call x1, Pallas kernels, per_device(): pl.pallas_call(functools.partial(evaluate_kernel, count, sources, targets...  6.42 us
    all_to_all x1, starting transfers between devices, per_device(): lax.all_to_all(values, 'orb', split_axis=0, concat_axis=0, tiled=True)  6.35 us
    all_to_all x1, waiting for transfers between devices, per_device(): lax.all_to_all(values, 'orb', split_axis=0, concat_axis=0, tiled=True)  6.26 us
    all_to_all x1, starting transfers between devices, per_device(): lax.all_to_all(points, 'orb', split_axis=0, concat_axis=0, tiled=True)  4.88 us
    ppermute x3, starting transfers between devices, per_device(): lax.ppermute(record, 'grp', pairs(n_grp, s))  4.6 us
    pallas_call x1, Pallas kernels, per_device(): call(functools.partial(prepare_kernel, middle), (shape((plane, 5 * width)...  4.05 us
    pallas_call x2, Pallas kernels, relay(): call(relay_kernel, (kept, kept, token), [SM] + [ANY] * (4 + len(first)),...  3.97 us
  transfers between devices with their start and end apart: 11, of which 3 were waited for; matrix products, arithmetic and copies ran while one was open for 0% of the time, Pallas kernels for 34%

profile of v9, /device:TPU:0, one launch (start us, length us, event | category | flops | bytes accessed | tf_op | source)
XLA Modules:
  0.0 69.6 jit_solution(10108620145507235892)
XLA Ops:
  1.3 1.7 %shard_map.120 = (f32[8,1024]{1,0:T(8,128)S(1)}, s32[2,128]{1,0:T(2,128)S(1)}, f32[2,8,128]{2,1,0:T(8,128)S(1)}) custom-call(f32[3,1,1024]{2,1,0:T(1,128)} %bitcast.10, s32[2,1,16]{2,1,0:T(1,128)} %moved_hbm.1, f32[6,1,16]{2,1,0:T(1,128)} %bitcast.11, f32[1]{0:T(128)S(6)} %copy.27.weight_ref), custom_call_target="tpu_custom_call" | custom-call | tf_op jit(solution)/shard_map/pallas_call | solution.py:558
  3.0 4.0 %collective-permute-start.2 = (f32[8,1024]{1,0:T(8,128)S(1)}, f32[8,1024]{1,0:T(8,128)S(1)}, u32[]{:S(2)}, u32[]{:S(2)}) collective-permute-start(f32[8,1024]{1,0:T(8,128)S(1)} %get-tuple-element.34.after_ref.refs_0_), channel_id=1, source_target_pairs={{0,24},{8,16},{16,8},{24,0},{1,25},{9,17},{17,9},{25,1},{2,26},{10... | collective-permute-start | bytes 98312 | tf_op jit(solution)/shard_map/ppermute | solution.py:581
  7.0 0.5 collective-permute-start.1
  7.5 0.1 collective-permute-start
  8.9 2.4 %shard_map.121 = (bf16[256,1024]{1,0:T(8,128)(2,1)}, bf16[256,1024]{1,0:T(8,128)(2,1)}) custom-call(f32[1,1024,1024]{2,1,0:T(8,128)} %inverse_hbm.9, f32[8,1024]{1,0:T(8,128)S(1)} %get-tuple-element.34.after_ref.refs_0_), custom_call_target="tpu_custom_call" | custom-call | bytes 3145728 | tf_op jit(solution)/shard_map/pallas_call | solution.py:589
  11.4 0.0 collective-permute-done.2.refs_4_.refs_3_
  11.4 0.0 collective-permute-done.1.refs_3_.refs_2_
  11.4 0.0 collective-permute-done.refs_2_.refs_1_
  11.4 2.0 %collective-permute-start.3 = (bf16[256,1024]{1,0:T(8,128)(2,1)}, bf16[256,1024]{1,0:T(8,128)(2,1)S(1)}, u32[]{:S(2)}, u32[]{:S(2)}) collective-permute-start(bf16[256,1024]{1,0:T(8,128)(2,1)} %get-tuple-element.46), channel_id=1, source_target_pairs={{0,16},{8,24},{16,0},{24,8},{1,17},{9,25},{17,1},{25,9},{2,18},{10... | collective-permute-start | bytes 1572872 | tf_op jit(solution)/shard_map/ppermute | solution.py:657
  13.4 1.5 %collective-permute-start.4 = (bf16[256,1024]{1,0:T(8,128)(2,1)}, bf16[256,1024]{1,0:T(8,128)(2,1)}, u32[]{:S(2)}, u32[]{:S(2)}) collective-permute-start(bf16[256,1024]{1,0:T(8,128)(2,1)} %get-tuple-element.47), channel_id=1, source_target_pairs={{0,8},{8,0},{16,24},{24,16},{1,9},{9,1},{17,25},{25,17},{2,10},{10... | collective-permute-start | bytes 1572872 | tf_op jit(solution)/shard_map/ppermute | solution.py:656
  14.9 1.0 %shard_map.123 = (f32[8,16,128]{2,1,0:T(8,128)}, f32[1,128]{1,0:T(1,128)S(1)}, s32[1,128]{1,0:T(1,128)S(1)}) custom-call(s32[1]{0:T(128)S(6)} %select_n.4.refs_5_.role_ref, f32[8,1024]{1,0:T(8,128)S(1)} %get-tuple-element.34.after_ref.refs_0_, f32[8,1024]{1,0:T(8,128)S(1)} %collective-permute-done.refs_2_.refs_1_, ...), custom_call_target="tpu_custom_call" | custom-call | tf_op jit(solution)/shard_map/pallas_call | solution.py:615
  15.9 4.9 %all-to-all-start = ((f32[8,16,128]{2,1,0:T(8,128)}), f32[8,16,128]{2,1,0:T(8,128)S(1)}, u32[]{:S(2)}, u32[]{:S(2)}) async-start(f32[8,16,128]{2,1,0:T(8,128)} %get-tuple-element.41), calls=%async_computation | async-start | bytes 131072 | tf_op jit(solution)/shard_map/all_to_all | solution.py:628
  20.7 0.0 copy-start
  20.8 4.0 %shard_map.124 = (bf16[2048,640]{1,0:T(8,128)(2,1)S(1)}, bf16[256,1024]{1,0:T(8,128)(2,1)}, bf16[256,1024]{1,0:T(8,128)(2,1)}) custom-call(bf16[2048,128]{1,0:T(8,128)(2,1)} %coeff_hbm.1, f32[3,1024]{1,0:T(4,128)} %refs_1_.1, f32[1,1024,1024]{2,1,0:T(8,128)} %inverse_hbm.9, f32[1,128]{1,0:T(1,128)S(1)} %get-tuple-element.42.after_ref.weight_ref), custom_call_target="tpu_custom_call" | custom-call | flops 2097152 | bytes 5767168 | tf_op jit(solution)/shard_map/pallas_call | solution.py:632
  24.8 1.9 %all-to-all-done.refs_1_.refs_0_ = f32[8,16,128]{2,1,0:T(8,128)S(1)} async-done(((f32[8,16,128]{2,1,0:T(8,128)}), f32[8,16,128]{2,1,0:T(8,128)S(1)}, u32[]{:S(2)}, u32[]{:S(2)}) %all-to-all-start) | async-done | bytes 65568 | tf_op jit(solution)/shard_map/all_to_all | solution.py:628
  26.7 0.0 collective-permute-done.3.got_a
  26.7 0.0 collective-permute-done.4.got_b
  26.7 2.0 %shard_map.125 = (bf16[256,1024]{1,0:T(8,128)(2,1)S(1)}, bf16[256,1024]{1,0:T(8,128)(2,1)}, f32[8,128]{1,0:T(8,128)S(1)}) custom-call(s32[1]{0:T(128)} %bitcast.1.refs_6_.flag_ref, bf16[256,1024]{1,0:T(8,128)(2,1)} %get-tuple-element.44.own_a.own_b, bf16[256,1024]{1,0:T(8,128)(2,1)} %get-tuple-element.45.own_b.own_a, ...), custom_call_target="tpu_custom_call", output_to_operand_aliasing={{0}: (3, {}), {1}: (4, {})} | custom-call | tf_op jit(solution)/shard_map/pallas_call | solution.py:660
  28.7 0.1 collective-permute-start.5
  28.7 0.1 collective-permute-start.6
  28.8 0.0 copy-done
  28.8 6.4 %shard_map.126.refs_0_ = bf16[8,176,128]{2,1,0:T(8,128)(2,1)} custom-call(f32[8,16,128]{2,1,0:T(8,128)S(1)} %all-to-all-done.refs_1_.refs_0_, f32[3,1024]{1,0:T(4,128)S(1)} %copy-done, bf16[2048,640]{1,0:T(8,128)(2,1)S(1)} %get-tuple-element.43.refs_0_.refs_2_, f32[8,128]{1,0:T(8,128)S(1)} %get-tuple-element.48.refs_3_), custom_call_target="tpu_custom_call" | custom-call | flops 738197504 | bytes 3145728 | tf_op jit(solution)/shard_map/pallas_call | solution.py:700
  35.2 6.4 %all-to-all-start.1 = ((bf16[8,176,128]{2,1,0:T(8,128)(2,1)}), bf16[8,176,128]{2,1,0:T(8,128)(2,1)S(1)}, u32[]{:S(2)}, u32[]{:S(2)}) async-start(bf16[8,176,128]{2,1,0:T(8,128)(2,1)} %shard_map.126.refs_0_), calls=%async_computation.1 | async-start | bytes 720896 | tf_op jit(solution)/shard_map/all_to_all | solution.py:725
  41.6 0.9 %collective-permute-done.5.got_a = bf16[256,1024]{1,0:T(8,128)(2,1)} collective-permute-done((bf16[256,1024]{1,0:T(8,128)(2,1)}, bf16[256,1024]{1,0:T(8,128)(2,1)}, u32[]{:S(2)}, u32[]{:S(2)}) %collective-permute-start.5) | collective-permute-done | bytes 524320 | tf_op jit(solution)/shard_map/ppermute | solution.py:657
  42.5 0.0 collective-permute-done.6.got_b
  42.5 2.0 %shard_map.127 = (bf16[256,1024]{1,0:T(8,128)(2,1)}, bf16[256,1024]{1,0:T(8,128)(2,1)}, f32[8,128]{1,0:T(8,128)S(1)}) custom-call(s32[1]{0:T(128)} %bitcast.1.refs_6_.flag_ref, bf16[256,1024]{1,0:T(8,128)(2,1)} %get-tuple-element.45.own_b.own_a, bf16[256,1024]{1,0:T(8,128)(2,1)} %get-tuple-element.44.own_a.own_b, ...), custom_call_target="tpu_custom_call", output_to_operand_aliasing={{0}: (3, {}), {1}: (4, {})} | custom-call | tf_op jit(solution)/shard_map/pallas_call | solution.py:660
  44.5 0.1 collective-permute-start.8
  44.6 0.1 collective-permute-start.7
  44.7 2.5 %shard_map.128.refs_1_ = bf16[1024,128]{1,0:T(8,128)(2,1)S(1)} custom-call(f32[1,1024,1024]{2,1,0:T(8,128)} %inverse_hbm.9, s32[2,128]{1,0:T(2,128)S(1)} %get-tuple-element.35.refs_4_.moved_ref, f32[8,128]{1,0:T(8,128)S(1)} %get-tuple-element.51.after_ref), custom_call_target="tpu_custom_call" | custom-call | flops 268435456 | bytes 4194304 | tf_op jit(solution)/shard_map/pallas_call | solution.py:744
  47.2 6.3 %all-to-all-done.1.refs_0_ = bf16[8,176,128]{2,1,0:T(8,128)(2,1)S(1)} async-done(((bf16[8,176,128]{2,1,0:T(8,128)(2,1)}), bf16[8,176,128]{2,1,0:T(8,128)(2,1)S(1)}, u32[]{:S(2)}, u32[]{:S(2)}) %all-to-all-start.1) | async-done | bytes 360480 | tf_op jit(solution)/shard_map/all_to_all | solution.py:725
  53.5 3.1 %shard_map.129 = (f32[3,1,16]{2,1,0:T(1,128)S(1)}, f32[1,1,16]{2,1,0:T(1,128)S(1)}, bf16[96,1024]{1,0:T(8,128)(2,1)S(1)}) custom-call(s32[1]{0:T(128)} %bitcast.4.me_ref, bf16[8,176,128]{2,1,0:T(8,128)(2,1)S(1)} %all-to-all-done.1.refs_0_, bf16[1024,128]{1,0:T(8,128)(2,1)S(1)} %shard_map.128.refs_1_), custom_call_target="tpu_custom_call" | custom-call | flops 46137344 | bytes 720896 | tf_op jit(solution)/shard_map/pallas_call | solution.py:759
  56.6 2.3 %shard_map.130 = (bf16[2,256,128]{2,1,0:T(8,128)(2,1)S(1)}, f32[96,128]{1,0:T(8,128)S(1)}, f32[32,1024]{1,0:T(8,128)S(1)}) custom-call(s32[1]{0:T(128)S(6)} %select_n.4.refs_5_.role_ref, s32[1,128]{1,0:T(1,128)S(1)} %get-tuple-element.40.number_ref, bf16[96,1024]{1,0:T(8,128)(2,1)S(1)} %get-tuple-element.52.later_ref, f32[1,1024,1024]{2,1,0:T(8,128)} %inverse_hbm.9, ...), custom_call_target="tpu_custom_call" | custom-call | flops 33554432 | bytes 1048576 | tf_op jit(solution)/shard_map/pallas_call | solution.py:775
  58.9 0.0 collective-permute-done.8.refs_5_
  58.9 0.0 collective-permute-done.7.refs_4_
  58.9 10.7 %shard_map.131 = (f32[1024,1024]{1,0:T(8,128)}, f32[6,1,16]{2,1,0:T(1,128)}, f32[2,1,16]{2,1,0:T(1,128)}, f32[1,128]{1,0:T(1,128)}) custom-call(s32[1]{0:T(128)S(6)} %select_n.4.refs_5_.role_ref, s32[1,128]{1,0:T(1,128)S(1)} %get-tuple-element.40.number_ref, bf16[96,1024]{1,0:T(8,128)(2,1)S(1)} %get-tuple-element.52.later_ref, ...), custom_call_target="tpu_custom_call" | custom-call | flops 134217728 | bytes 6291456 | tf_op jit(solution)/shard_map/pallas_call | solution.py:794
  (1 shorter events, 0.0 us)
Async XLA Ops:
  3.0 8.4 %collective-permute-start.2 = (f32[8,1024]{1,0:T(8,128)S(1)}, f32[8,1024]{1,0:T(8,128)S(1)}, u32[]{:S(2)}, u32[]{:S(2)}) collective-permute-start(f32[8,1024]{1,0:T(8,128)S(1)} %get-tuple-element.34.after_ref.refs_0_), channel_id=1, source_target_pairs={{0,24},{8,16},{16,8},{24,0},{1,25},{9,17},{17,9},{25,1},{2,26},{10... | collective-permute-start | bytes 98312 | tf_op jit(solution)/shard_map/ppermute | solution.py:581
  7.0 4.4 %collective-permute-start.1 = (f32[8,1024]{1,0:T(8,128)S(1)}, f32[8,1024]{1,0:T(8,128)S(1)}, u32[]{:S(2)}, u32[]{:S(2)}) collective-permute-start(f32[8,1024]{1,0:T(8,128)S(1)} %get-tuple-element.34.after_ref.refs_0_), channel_id=1, source_target_pairs={{0,16},{8,24},{16,0},{24,8},{1,17},{9,25},{17,1},{25,9},{2,18},{10... | collective-permute-start | bytes 98312 | tf_op jit(solution)/shard_map/ppermute | solution.py:581
  7.5 3.9 %collective-permute-start = (f32[8,1024]{1,0:T(8,128)S(1)}, f32[8,1024]{1,0:T(8,128)S(1)}, u32[]{:S(2)}, u32[]{:S(2)}) collective-permute-start(f32[8,1024]{1,0:T(8,128)S(1)} %get-tuple-element.34.after_ref.refs_0_), channel_id=1, source_target_pairs={{0,8},{8,0},{16,24},{24,16},{1,9},{9,1},{17,25},{25,17},{2,10},{10... | collective-permute-start | bytes 98312 | tf_op jit(solution)/shard_map/ppermute | solution.py:581
  11.4 15.3 %collective-permute-start.3 = (bf16[256,1024]{1,0:T(8,128)(2,1)}, bf16[256,1024]{1,0:T(8,128)(2,1)S(1)}, u32[]{:S(2)}, u32[]{:S(2)}) collective-permute-start(bf16[256,1024]{1,0:T(8,128)(2,1)} %get-tuple-element.46), channel_id=1, source_target_pairs={{0,16},{8,24},{16,0},{24,8},{1,17},{9,25},{17,1},{25,9},{2,18},{10... | collective-permute-start | bytes 1572872 | tf_op jit(solution)/shard_map/ppermute | solution.py:657
  13.4 13.3 %collective-permute-start.4 = (bf16[256,1024]{1,0:T(8,128)(2,1)}, bf16[256,1024]{1,0:T(8,128)(2,1)}, u32[]{:S(2)}, u32[]{:S(2)}) collective-permute-start(bf16[256,1024]{1,0:T(8,128)(2,1)} %get-tuple-element.47), channel_id=1, source_target_pairs={{0,8},{8,0},{16,24},{24,16},{1,9},{9,1},{17,25},{25,17},{2,10},{10... | collective-permute-start | bytes 1572872 | tf_op jit(solution)/shard_map/ppermute | solution.py:656
  15.9 10.8 %all-to-all-start = ((f32[8,16,128]{2,1,0:T(8,128)}), f32[8,16,128]{2,1,0:T(8,128)S(1)}, u32[]{:S(2)}, u32[]{:S(2)}) async-start(f32[8,16,128]{2,1,0:T(8,128)} %get-tuple-element.41), calls=%async_computation | async-start | bytes 131072 | tf_op jit(solution)/shard_map/all_to_all | solution.py:628
  20.7 8.1 %copy-start = (f32[3,1024]{1,0:T(4,128)S(1)}, f32[3,1024]{1,0:T(4,128)}, u32[]{:S(2)}) copy-start(f32[3,1024]{1,0:T(4,128)} %refs_1_.1) | copy-start | bytes 36868
  28.7 13.9 %collective-permute-start.5 = (bf16[256,1024]{1,0:T(8,128)(2,1)}, bf16[256,1024]{1,0:T(8,128)(2,1)}, u32[]{:S(2)}, u32[]{:S(2)}) collective-permute-start(bf16[256,1024]{1,0:T(8,128)(2,1)} %get-tuple-element.49.refs_0_), channel_id=1, source_target_pairs={{0,16},{8,24},{16,0},{24,8},{1,17},{9,25},{17,1},{25,9},{2,18},{10... | collective-permute-start | bytes 1572872 | tf_op jit(solution)/shard_map/ppermute | solution.py:657
  28.7 13.8 %collective-permute-start.6 = (bf16[256,1024]{1,0:T(8,128)(2,1)S(1)}, bf16[256,1024]{1,0:T(8,128)(2,1)}, u32[]{:S(2)}, u32[]{:S(2)}) collective-permute-start(bf16[256,1024]{1,0:T(8,128)(2,1)S(1)} %get-tuple-element.50.refs_2_), channel_id=1, source_target_pairs={{0,8},{8,0},{16,24},{24,16},{1,9},{9,1},{17,25},{25,17},{2,10},{10... | collective-permute-start | bytes 1572872 | tf_op jit(solution)/shard_map/ppermute | solution.py:656
  35.2 18.2 %all-to-all-start.1 = ((bf16[8,176,128]{2,1,0:T(8,128)(2,1)}), bf16[8,176,128]{2,1,0:T(8,128)(2,1)S(1)}, u32[]{:S(2)}, u32[]{:S(2)}) async-start(bf16[8,176,128]{2,1,0:T(8,128)(2,1)} %shard_map.126.refs_0_), calls=%async_computation.1 | async-start | bytes 720896 | tf_op jit(solution)/shard_map/all_to_all | solution.py:725
  44.5 14.4 %collective-permute-start.8 = (bf16[256,1024]{1,0:T(8,128)(2,1)}, bf16[256,1024]{1,0:T(8,128)(2,1)S(1)}, u32[]{:S(2)}, u32[]{:S(2)}) collective-permute-start(bf16[256,1024]{1,0:T(8,128)(2,1)} %get-tuple-element.55.refs_1_), channel_id=1, source_target_pairs={{0,16},{8,24},{16,0},{24,8},{1,17},{9,25},{17,1},{25,9},{2,18},{10... | collective-permute-start | bytes 1572872 | tf_op jit(solution)/shard_map/ppermute | solution.py:657
  44.6 14.3 %collective-permute-start.7 = (bf16[256,1024]{1,0:T(8,128)(2,1)}, bf16[256,1024]{1,0:T(8,128)(2,1)S(1)}, u32[]{:S(2)}, u32[]{:S(2)}) collective-permute-start(bf16[256,1024]{1,0:T(8,128)(2,1)} %get-tuple-element.56.refs_3_), channel_id=1, source_target_pairs={{0,8},{8,0},{16,24},{24,16},{1,9},{9,1},{17,25},{25,17},{2,10},{10... | collective-permute-start | bytes 1572872 | tf_op jit(solution)/shard_map/ppermute | solution.py:656

commit v10 on v9

--- a/solution.py
+++ b/solution.py
@@ -185,11 +185,15 @@
     token_ref[...] = jnp.zeros(token_ref.shape, F32)
 
 
-def points_kernel(count, others, role_ref, *refs):
+def points_kernel(count, others, donor_ref, take_ref, *refs):
     own_ref = refs[0]
     received = refs[1 : 1 + others]
-    moved_ref, disp_ref, after_ref, points_ref, weight_ref, number_ref = refs[1 + others :]
-    role = role_ref[0]
+    moved_ref, disp_ref, after_ref, points_ref, weight_ref, number_ref = refs[1 + others : -2]
+    role_ref, apart_ref = refs[-2:]
+    apart = distance(others + 1, lax.axis_index("grp"), donor_ref[0, 0])
+    role = jnp.where(take_ref[0, 0] == 1, apart, 0)
+    apart_ref[0] = apart
+    role_ref[0] = role
     parent = own_ref[...]
     for step in range(others):
         parent = jnp.where(role == step + 1, received[step][...], parent)
@@ -320,31 +324,57 @@
                 ]
 
 
+def pair_inverse(a, b, d):
+    det = a * d - b * b
+    scale = 1.0 / det
+    return d * scale, -b * scale, a * scale, det
+
+
 def sweep(matrix):
     size = matrix.shape[0]
     log = jnp.zeros((1, 1), F32)
     row = iota((size, size), 0)
     lane = iota((size, size), 1)
     place = iota((1, size), 1)
-    for k in range(0, size, 2):
-        a = matrix[k : k + 1, k : k + 1]
-        b = matrix[k : k + 1, k + 1 : k + 2]
-        d = matrix[k + 1 : k + 2, k + 1 : k + 2]
-        column_0, column_1 = matrix[:, k : k + 1], matrix[:, k + 1 : k + 2]
-        line_0, line_1 = matrix[k : k + 1, :], matrix[k + 1 : k + 2, :]
-        det = a * d - b * b
-        scale = 1.0 / det
-        a, b, d = a * scale, b * scale, d * scale
-        scaled_0 = d * line_0 - b * line_1
-        scaled_1 = a * line_1 - b * line_0
-        reduced = matrix - column_0 * scaled_0 - column_1 * scaled_1
-        edge_0 = d * column_0 - b * column_1
-        edge_1 = a * column_1 - b * column_0
-        scaled_0 = jnp.where(place == k, -d, jnp.where(place == k + 1, b, scaled_0))
-        scaled_1 = jnp.where(place == k, b, jnp.where(place == k + 1, -a, scaled_1))
-        matrix = jnp.where(lane == k, edge_0, jnp.where(lane == k + 1, edge_1, reduced))
-        matrix = jnp.where(row == k, scaled_0, jnp.where(row == k + 1, scaled_1, matrix))
-        log = log + jnp.log(det)
+    for k in range(0, size, 4):
+        columns = [jnp.broadcast_to(matrix[:, k + j : k + j + 1], (size, size)) for j in range(4)]
+        lines = [matrix[k + i : k + i + 1, :] for i in range(4)]
+        at = lambda i, j: columns[j][k + i : k + i + 1, :]
+        a00, a01, a11, det_a = pair_inverse(at(0, 0), at(0, 1), at(1, 1))
+        b00, b01, b10, b11 = at(0, 2), at(0, 3), at(1, 2), at(1, 3)
+        t00, t01 = a00 * b00 + a01 * b10, a00 * b01 + a01 * b11
+        t10, t11 = a01 * b00 + a11 * b10, a01 * b01 + a11 * b11
+        d00 = at(2, 2) - (b00 * t00 + b10 * t10)
+        d01 = at(2, 3) - (b00 * t01 + b10 * t11)
+        d11 = at(3, 3) - (b01 * t01 + b11 * t11)
+        s00, s01, s11, det_s = pair_inverse(d00, d01, d11)
+        u00, u01 = -(t00 * s00 + t01 * s01), -(t00 * s01 + t01 * s11)
+        u10, u11 = -(t10 * s00 + t11 * s01), -(t10 * s01 + t11 * s11)
+        q00, q01 = a00 - (u00 * t00 + u01 * t01), a01 - (u00 * t10 + u01 * t11)
+        q11 = a11 - (u10 * t10 + u11 * t11)
+        pivot = (
+            (q00, q01, u00, u01),
+            (q01, q11, u10, u11),
+            (u00, u10, s00, s01),
+            (u01, u11, s01, s11),
+        )
+        reduced = matrix
+        scaled, edges = [], []
+        for i in range(4):
+            line = pivot[i][0] * lines[0] + pivot[i][1] * lines[1]
+            line = line + (pivot[i][2] * lines[2] + pivot[i][3] * lines[3])
+            reduced = reduced - columns[i] * line
+            for j in range(4):
+                line = jnp.where(place == k + j, -pivot[i][j], line)
+            scaled.append(line)
+            edge = pivot[i][0] * columns[0] + pivot[i][1] * columns[1]
+            edges.append(edge + (pivot[i][2] * columns[2] + pivot[i][3] * columns[3]))
+        matrix = reduced
+        for i in range(4):
+            matrix = jnp.where(lane == k + i, edges[i], matrix)
+        for i in range(4):
+            matrix = jnp.where(row == k + i, scaled[i], matrix)
+        log = log + (jnp.log(det_a[:, 0:1]) + jnp.log(det_s[:, 0:1]))
     return -matrix, log
 
 
@@ -446,7 +476,6 @@
         @pl.when(role != 0)
         def _():
             sent.wait()
-            staged[slot] = parent[slot].astype(F32)
 
 
 def early_kernel(count, plan, role_ref, number_ref, later_ref, inverse_hbm, *refs):
@@ -505,23 +534,32 @@
         at = pl.multiple_of(chunk_at(plan, role, slot) * depth, depth)
         rows.append(later_ref[:, pl.ds(at, depth)])
         products = products + dot(rows[-1], columns[-1])
-    settle_slots(plan, range(done), *loads)
     ratio, inverse, log = ratio_of(products, size)
     total = total_ref[...]
     for slot, part in zip(late, rows):
         total = total + dot(part[0:size], parent[slot])
     small = dot(inverse, ratio, ((1,), (1,)), exact=True)
-    solved = dot(small, total, exact=True).astype(BF16)
+    high = small.astype(BF16)
+    halves = jnp.concatenate([high, (small - high.astype(F32)).astype(BF16)], 1)
+    rounded = total.astype(BF16)
+    solved = dot(halves, jnp.concatenate([rounded, rounded], 0)).astype(BF16)
     solved = jnp.concatenate([solved, jnp.zeros((LANES - size, electrons), BF16)], 0)
+    settle_slots(plan, range(done), *loads)
     copies = []
-    for slot in range(chunks):
-        staged[slot] = staged[slot] - dot(columns[slot], solved)
+    for slot in list(late) + list(range(done)):
         at = pl.multiple_of(chunk_at(plan, role, slot) * depth, depth)
         copy = pltpu.make_async_copy(
             staged.at[slot], out_ref.at[pl.ds(at, depth)], out_sem.at[slot]
         )
-        copy.start()
-        copies.append(copy)
+        copies.append((slot, copy))
+
+    def write(before):
+        for slot, copy in copies:
+            staged[slot] = before(slot) - dot(columns[slot], solved)
+            copy.start()
+
+    pl.when(role == 0)(lambda: write(lambda slot: staged[slot]))
+    pl.when(role != 0)(lambda: write(lambda slot: parent[slot].astype(F32)))
     sums = moved_sums(products, ratio, inverse, count)
     drift_ref[0:3] = drift_in[...]
     lap_ref[0:1] = lap_in[...]
@@ -529,7 +567,7 @@
         drift_ref[3 + a] = sums[:, a * count : (a + 1) * count]
     lap_ref[1] = sums[:, 3 * count : 4 * count]
     out_weight_ref[...] = weight_ref[...] + log
-    for copy in copies:
+    for _, copy in copies:
         copy.wait()
 
 
@@ -553,8 +591,6 @@
     others = n_grp - 1
     chunks = 4
 
-    apart = distance(n_grp, lax.axis_index("grp"), donor[0]).astype(jnp.int32).reshape(1)
-    role = jnp.where(take == 1, apart, 0)
     record, tiled, disp = call(
         functools.partial(start_kernel, count),
         (
@@ -603,25 +639,27 @@
     own[0], own[-1], token_0 = call(
         gate_kernel,
         (kept, kept, token),
-        [ANY] * (2 + others) + [SM, SM],
+        [ANY] * (2 + others),
         (ANY, ANY, VM),
         aliases={0: 0, 1: 1},
         vmem=1,
-    )(own[0], own[-1], *records, role, apart)
+    )(own[0], own[-1], *records)
 
     few = is_power(n_orb) and local % LANES == 0
     direct = few and DIRECT_POINTS
     sources = n_orb if direct else 1
-    points, weight, number = call(
+    points, weight, number, role, apart = call(
         functools.partial(points_kernel, count, others),
         (
             shape((8, LANES) if direct else (n_orb, ROWS, LANES), F32),
             shape((1, LANES), F32),
             shape((1, LANES), jnp.int32),
+            shape((1,), jnp.int32),
+            shape((1,), jnp.int32),
         ),
-        [SM] + [VM] * (others + 3) + [ANY],
-        (VM, VM, VM),
-    )(role, record, *records, tiled, disp, token_0)
+        [VM, VM] + [VM] * (others + 3) + [ANY],
+        (VM, VM, VM, SM, SM),
+    )(donor.reshape(1, 1), take.reshape(1, 1), record, *records, tiled, disp, token_0)
     if direct:
         points = [points] + [lax.ppermute(points, "orb", pairs(n_orb, s)) for s in range(1, n_orb)]
     else:
@@ -663,9 +701,9 @@
                 [SM] + [ANY] * (4 + len(first)),
                 (ANY, ANY, VM),
                 scratch=[
-                    pltpu.VMEM((4, depth // 2, electrons), BF16),
-                    pltpu.SemaphoreType.DMA((4,)),
-                    pltpu.SemaphoreType.DMA((4,)),
+                    pltpu.VMEM((8, depth // 4, electrons), BF16),
+                    pltpu.SemaphoreType.DMA((8,)),
+                    pltpu.SemaphoreType.DMA((8,)),
                 ],
                 aliases={3: 0, 4: 1},
                 vmem=2,

time: 69.2 us -> 68.2 us (0.986)
  waiting for transfers between devices: 9.07 us -> 13.6 us
  starting transfers between devices: 19.6 us -> 15.4 us
  Pallas kernels: 38.2 us -> 36.2 us
    ppermute x3, waiting for transfers between devices: 0.93 us -> 5.23 us  [per_device(): send_y = lambda block: lax.ppermute(block, 'grp', pairs(n_grp, 2))]
    all_to_all x1, waiting for transfers between devices: 6.26 us -> 2.51 us  [per_device(): lax.all_to_all(values, 'orb', split_axis=0, concat_axis=0, tiled=True)]
    all_to_all x1, starting transfers between devices: 6.35 us -> 3.44 us  [per_device(): lax.all_to_all(values, 'orb', split_axis=0, concat_axis=0, tiled=True)]
    pallas_call x1, Pallas kernels: 10.7 us -> 7.83 us  [per_device(): call(functools.partial(finish_kernel, count, plan), (shape((electrons, el...]
    ppermute x3, waiting for transfers between devices: 0.01 us -> 2.71 us  [per_device(): send_x = lambda block: lax.ppermute(block, 'grp', pairs(n_grp, 1))]
    pallas_call x2, Pallas kernels: 3.97 us -> 5.87 us  [relay(): call(relay_kernel, (kept, kept, token), [SM] + [ANY] * (4 + len(first)),...]
    pallas_call x1, Pallas kernels: 3.13 us -> 1.41 us  [per_device(): call(functools.partial(first_kernel, count, targets), (shape((3, 1, count...]
    ppermute x3, waiting for transfers between devices: 0.01 us -> 1.33 us  [per_device(): lax.ppermute(record, 'grp', pairs(n_grp, s))]
  transfers between devices with their start and end apart: 11 -> 11, of which waited for: 3 -> 8; matrix products, arithmetic and copies ran while one was open for 0% -> 0% of each run, Pallas kernels for 34% -> 35%
where the time goes in v10:
time: 68.2 us; the launch traced here: 68 us
  Pallas kernels  36.2 us (53%)
  starting transfers between devices  15.4 us (23%)
  waiting for transfers between devices  13.6 us (20%)
  between operations  2.71 us (4%)
    pallas_call x1, Pallas kernels, per_device(): call(functools.partial(finish_kernel, count, plan), (shape((electrons, el...  7.83 us
    pallas_call x1, Pallas kernels, per_device(): pl.pallas_call(functools.partial(evaluate_kernel, count, sources, targets...  6.42 us
    pallas_call x2, Pallas kernels, relay(): call(relay_kernel, (kept, kept, token), [SM] + [ANY] * (4 + len(first)),...  5.87 us
    ppermute x3, waiting for transfers between devices, per_device(): send_y = lambda block: lax.ppermute(block, 'grp', pairs(n_grp, 2))  5.23 us
    all_to_all x1, starting transfers between devices, per_device(): lax.all_to_all(points, 'orb', split_axis=0, concat_axis=0, tiled=True)  4.89 us
    ppermute x3, starting transfers between devices, per_device(): lax.ppermute(record, 'grp', pairs(n_grp, s))  4.6 us
    pallas_call x1, Pallas kernels, per_device(): call(functools.partial(prepare_kernel, middle), (shape((plane, 5 * width)...  4.05 us
    all_to_all x1, starting transfers between devices, per_device(): lax.all_to_all(values, 'orb', split_axis=0, concat_axis=0, tiled=True)  3.44 us
  transfers between devices with their start and end apart: 11, of which 8 were waited for; matrix products, arithmetic and copies ran while one was open for 0% of the time, Pallas kernels for 35%

profile of v10, /device:TPU:0, one launch (start us, length us, event | category | flops | bytes accessed | tf_op | source)
XLA Modules:
  0.0 68.0 jit_solution(3272925234946796567)
XLA Ops:
  1.3 1.7 %shard_map.120 = (f32[8,1024]{1,0:T(8,128)S(1)}, s32[2,128]{1,0:T(2,128)S(1)}, f32[2,8,128]{2,1,0:T(8,128)S(1)}) custom-call(f32[3,1,1024]{2,1,0:T(1,128)} %bitcast.11, s32[2,1,16]{2,1,0:T(1,128)} %moved_hbm.1, f32[6,1,16]{2,1,0:T(1,128)} %bitcast.12, f32[1]{0:T(128)S(6)} %copy.27.weight_ref), custom_call_target="tpu_custom_call" | custom-call | tf_op jit(solution)/shard_map/pallas_call | solution.py:594
  3.0 4.0 %collective-permute-start.2 = (f32[8,1024]{1,0:T(8,128)S(1)}, f32[8,1024]{1,0:T(8,128)S(1)}, u32[]{:S(2)}, u32[]{:S(2)}) collective-permute-start(f32[8,1024]{1,0:T(8,128)S(1)} %get-tuple-element.36.after_ref.refs_0_), channel_id=1, source_target_pairs={{0,24},{8,16},{16,8},{24,0},{1,25},{9,17},{17,9},{25,1},{2,26},{10... | collective-permute-start | bytes 98312 | tf_op jit(solution)/shard_map/ppermute | solution.py:617
  7.0 0.5 collective-permute-start.1
  7.5 0.1 collective-permute-start
  7.6 2.4 %shard_map.121 = (bf16[256,1024]{1,0:T(8,128)(2,1)}, bf16[256,1024]{1,0:T(8,128)(2,1)}) custom-call(f32[1,1024,1024]{2,1,0:T(8,128)} %inverse_hbm.9, f32[8,1024]{1,0:T(8,128)S(1)} %get-tuple-element.36.after_ref.refs_0_), custom_call_target="tpu_custom_call" | custom-call | bytes 3145728 | tf_op jit(solution)/shard_map/pallas_call | solution.py:625
  10.0 0.0 collective-permute-done.2.refs_4_.refs_3_
  10.1 0.8 %collective-permute-done.1.refs_3_.refs_2_ = f32[8,1024]{1,0:T(8,128)S(1)} collective-permute-done((f32[8,1024]{1,0:T(8,128)S(1)}, f32[8,1024]{1,0:T(8,128)S(1)}, u32[]{:S(2)}, u32[]{:S(2)}) %collective-permute-start.1) | collective-permute-done | bytes 32800 | tf_op jit(solution)/shard_map/ppermute | solution.py:617
  10.9 0.5 collective-permute-done.refs_2_.refs_1_
  11.4 1.5 %collective-permute-start.3 = (bf16[256,1024]{1,0:T(8,128)(2,1)}, bf16[256,1024]{1,0:T(8,128)(2,1)S(1)}, u32[]{:S(2)}, u32[]{:S(2)}) collective-permute-start(bf16[256,1024]{1,0:T(8,128)(2,1)} %get-tuple-element.50), channel_id=1, source_target_pairs={{0,16},{8,24},{16,0},{24,8},{1,17},{9,25},{17,1},{25,9},{2,18},{10... | collective-permute-start | bytes 1572872 | tf_op jit(solution)/shard_map/ppermute | solution.py:695
  12.9 0.7 collective-permute-start.4
  14.9 1.0 %shard_map.123 = (f32[8,16,128]{2,1,0:T(8,128)}, f32[1,128]{1,0:T(1,128)S(1)}, s32[1,128]{1,0:T(1,128)S(1)}, s32[1]{0:T(128)}, s32[1]{0:T(128)}) custom-call(s32[1,1]{1,0:T(1,128)} %bitcast.9.donor_ref, s32[1,1]{1,0:T(1,128)} %bitcast.10.take_ref, f32[8,1024]{1,0:T(8,128)S(1)} %get-tuple-element.36.after_ref.refs_0_, ...), custom_call_target="tpu_custom_call" | custom-call | tf_op jit(solution)/shard_map/pallas_call | solution.py:651
  15.9 4.9 %all-to-all-start = ((f32[8,16,128]{2,1,0:T(8,128)}), f32[8,16,128]{2,1,0:T(8,128)S(1)}, u32[]{:S(2)}, u32[]{:S(2)}) async-start(f32[8,16,128]{2,1,0:T(8,128)} %get-tuple-element.44), calls=%async_computation | async-start | bytes 131072 | tf_op jit(solution)/shard_map/all_to_all | solution.py:666
  20.8 0.0 copy-start
  20.8 4.0 %shard_map.124 = (bf16[2048,640]{1,0:T(8,128)(2,1)S(1)}, bf16[256,1024]{1,0:T(8,128)(2,1)}, bf16[256,1024]{1,0:T(8,128)(2,1)}) custom-call(bf16[2048,128]{1,0:T(8,128)(2,1)} %coeff_hbm.1, f32[3,1024]{1,0:T(4,128)} %refs_1_.1, f32[1,1024,1024]{2,1,0:T(8,128)} %inverse_hbm.9, f32[1,128]{1,0:T(1,128)S(1)} %get-tuple-element.45.after_ref.weight_ref), custom_call_target="tpu_custom_call" | custom-call | flops 2097152 | bytes 5767168 | tf_op jit(solution)/shard_map/pallas_call | solution.py:670
  24.8 1.9 %all-to-all-done.refs_1_.refs_0_ = f32[8,16,128]{2,1,0:T(8,128)S(1)} async-done(((f32[8,16,128]{2,1,0:T(8,128)}), f32[8,16,128]{2,1,0:T(8,128)S(1)}, u32[]{:S(2)}, u32[]{:S(2)}) %all-to-all-start) | async-done | bytes 65568 | tf_op jit(solution)/shard_map/all_to_all | solution.py:666
  26.7 0.0 collective-permute-done.3.got_a
  26.7 0.0 collective-permute-done.4.got_b
  26.7 3.1 %shard_map.125 = (bf16[256,1024]{1,0:T(8,128)(2,1)S(1)}, bf16[256,1024]{1,0:T(8,128)(2,1)}, f32[8,128]{1,0:T(8,128)S(1)}) custom-call(s32[1]{0:T(128)} %get-tuple-element.47.flag_ref, bf16[256,1024]{1,0:T(8,128)(2,1)} %get-tuple-element.48.own_a.own_b, ...), custom_call_target="tpu_custom_call", output_to_operand_aliasing={{0}: (3, {}), {1}: (4, {})} | custom-call | tf_op jit(solution)/shard_map/pallas_call | solution.py:698
  29.9 0.1 collective-permute-start.5
  29.9 0.1 collective-permute-start.6
  30.0 0.0 copy-done
  30.0 6.4 %shard_map.126.refs_0_ = bf16[8,176,128]{2,1,0:T(8,128)(2,1)} custom-call(f32[8,16,128]{2,1,0:T(8,128)S(1)} %all-to-all-done.refs_1_.refs_0_, f32[3,1024]{1,0:T(4,128)S(1)} %copy-done, bf16[2048,640]{1,0:T(8,128)(2,1)S(1)} %get-tuple-element.46.refs_0_.refs_2_, f32[8,128]{1,0:T(8,128)S(1)} %get-tuple-element.52.refs_3_), custom_call_target="tpu_custom_call" | custom-call | flops 738197504 | bytes 3145728 | tf_op jit(solution)/shard_map/pallas_call | solution.py:738
  36.4 3.4 %all-to-all-start.1 = ((bf16[8,176,128]{2,1,0:T(8,128)(2,1)}), bf16[8,176,128]{2,1,0:T(8,128)(2,1)S(1)}, u32[]{:S(2)}, u32[]{:S(2)}) async-start(bf16[8,176,128]{2,1,0:T(8,128)(2,1)} %shard_map.126.refs_0_), calls=%async_computation.1 | async-start | bytes 720896 | tf_op jit(solution)/shard_map/all_to_all | solution.py:763
  39.9 2.6 %collective-permute-done.5.got_a = bf16[256,1024]{1,0:T(8,128)(2,1)} collective-permute-done((bf16[256,1024]{1,0:T(8,128)(2,1)}, bf16[256,1024]{1,0:T(8,128)(2,1)}, u32[]{:S(2)}, u32[]{:S(2)}) %collective-permute-start.5) | collective-permute-done | bytes 524320 | tf_op jit(solution)/shard_map/ppermute | solution.py:695
  42.5 1.2 %collective-permute-done.6.got_b = bf16[256,1024]{1,0:T(8,128)(2,1)} collective-permute-done((bf16[256,1024]{1,0:T(8,128)(2,1)S(1)}, bf16[256,1024]{1,0:T(8,128)(2,1)}, u32[]{:S(2)}, u32[]{:S(2)}) %collective-permute-start.6) | collective-permute-done | bytes 524320 | tf_op jit(solution)/shard_map/ppermute | solution.py:694
  43.7 2.7 %shard_map.127 = (bf16[256,1024]{1,0:T(8,128)(2,1)}, bf16[256,1024]{1,0:T(8,128)(2,1)}, f32[8,128]{1,0:T(8,128)S(1)}) custom-call(s32[1]{0:T(128)} %get-tuple-element.47.flag_ref, bf16[256,1024]{1,0:T(8,128)(2,1)} %get-tuple-element.49.own_b.own_a, bf16[256,1024]{1,0:T(8,128)(2,1)} %get-tuple-element.48.own_a.own_b, ...), custom_call_target="tpu_custom_call", output_to_operand_aliasing={{0}: (3, {}), {1}: (4, {})} | custom-call | tf_op jit(solution)/shard_map/pallas_call | solution.py:698
  46.5 0.1 collective-permute-start.8
  46.6 0.1 collective-permute-start.7
  46.6 2.5 %shard_map.128.refs_1_ = bf16[1024,128]{1,0:T(8,128)(2,1)S(1)} custom-call(f32[1,1024,1024]{2,1,0:T(8,128)} %inverse_hbm.9, s32[2,128]{1,0:T(2,128)S(1)} %get-tuple-element.37.refs_4_.moved_ref, f32[8,128]{1,0:T(8,128)S(1)} %get-tuple-element.55.after_ref), custom_call_target="tpu_custom_call" | custom-call | flops 268435456 | bytes 4194304 | tf_op jit(solution)/shard_map/pallas_call | solution.py:782
  49.2 2.5 %all-to-all-done.1.refs_0_ = bf16[8,176,128]{2,1,0:T(8,128)(2,1)S(1)} async-done(((bf16[8,176,128]{2,1,0:T(8,128)(2,1)}), bf16[8,176,128]{2,1,0:T(8,128)(2,1)S(1)}, u32[]{:S(2)}, u32[]{:S(2)}) %all-to-all-start.1) | async-done | bytes 360480 | tf_op jit(solution)/shard_map/all_to_all | solution.py:763
  51.7 1.4 %shard_map.129 = (f32[3,1,16]{2,1,0:T(1,128)S(1)}, f32[1,1,16]{2,1,0:T(1,128)S(1)}, bf16[96,1024]{1,0:T(8,128)(2,1)S(1)}) custom-call(s32[1]{0:T(128)} %bitcast.4.me_ref, bf16[8,176,128]{2,1,0:T(8,128)(2,1)S(1)} %all-to-all-done.1.refs_0_, bf16[1024,128]{1,0:T(8,128)(2,1)S(1)} %shard_map.128.refs_1_), custom_call_target="tpu_custom_call" | custom-call | flops 46137344 | bytes 720896 | tf_op jit(solution)/shard_map/pallas_call | solution.py:797
  53.1 3.0 %shard_map.130 = (bf16[2,256,128]{2,1,0:T(8,128)(2,1)S(1)}, f32[96,128]{1,0:T(8,128)S(1)}, f32[32,1024]{1,0:T(8,128)S(1)}) custom-call(s32[1]{0:T(128)} %get-tuple-element.42.role_ref, s32[1,128]{1,0:T(1,128)S(1)} %get-tuple-element.43.number_ref, bf16[96,1024]{1,0:T(8,128)(2,1)S(1)} %get-tuple-element.56.later_ref, f32[1,1024,1024]{2,1,0:T(8,128)} %inverse_hbm.9, ...), custom_call_target="tpu_custom_call" | custom-call | flops 33554432 | bytes 1048576 | tf_op jit(solution)/shard_map/pallas_call | solution.py:813
  56.0 2.6 %collective-permute-done.8.refs_5_ = bf16[256,1024]{1,0:T(8,128)(2,1)S(1)} collective-permute-done((bf16[256,1024]{1,0:T(8,128)(2,1)}, bf16[256,1024]{1,0:T(8,128)(2,1)S(1)}, u32[]{:S(2)}, u32[]{:S(2)}) %collective-permute-start.8) | collective-permute-done | bytes 524320 | tf_op jit(solution)/shard_map/ppermute | solution.py:695
  58.7 1.5 %collective-permute-done.7.refs_4_ = bf16[256,1024]{1,0:T(8,128)(2,1)S(1)} collective-permute-done((bf16[256,1024]{1,0:T(8,128)(2,1)}, bf16[256,1024]{1,0:T(8,128)(2,1)S(1)}, u32[]{:S(2)}, u32[]{:S(2)}) %collective-permute-start.7) | collective-permute-done | bytes 524320 | tf_op jit(solution)/shard_map/ppermute | solution.py:694
  60.1 7.8 %shard_map.131 = (f32[1024,1024]{1,0:T(8,128)}, f32[6,1,16]{2,1,0:T(1,128)}, f32[2,1,16]{2,1,0:T(1,128)}, f32[1,128]{1,0:T(1,128)}) custom-call(s32[1]{0:T(128)} %get-tuple-element.42.role_ref, s32[1,128]{1,0:T(1,128)S(1)} %get-tuple-element.43.number_ref, bf16[96,1024]{1,0:T(8,128)(2,1)S(1)} %get-tuple-element.56.later_ref, ...), custom_call_target="tpu_custom_call" | custom-call | flops 134217728 | bytes 6291456 | tf_op jit(solution)/shard_map/pallas_call | solution.py:832
  (1 shorter events, 0.0 us)
Async XLA Ops:
  3.0 7.0 %collective-permute-start.2 = (f32[8,1024]{1,0:T(8,128)S(1)}, f32[8,1024]{1,0:T(8,128)S(1)}, u32[]{:S(2)}, u32[]{:S(2)}) collective-permute-start(f32[8,1024]{1,0:T(8,128)S(1)} %get-tuple-element.36.after_ref.refs_0_), channel_id=1, source_target_pairs={{0,24},{8,16},{16,8},{24,0},{1,25},{9,17},{17,9},{25,1},{2,26},{10... | collective-permute-start | bytes 98312 | tf_op jit(solution)/shard_map/ppermute | solution.py:617
  7.0 3.9 %collective-permute-start.1 = (f32[8,1024]{1,0:T(8,128)S(1)}, f32[8,1024]{1,0:T(8,128)S(1)}, u32[]{:S(2)}, u32[]{:S(2)}) collective-permute-start(f32[8,1024]{1,0:T(8,128)S(1)} %get-tuple-element.36.after_ref.refs_0_), channel_id=1, source_target_pairs={{0,16},{8,24},{16,0},{24,8},{1,17},{9,25},{17,1},{25,9},{2,18},{10... | collective-permute-start | bytes 98312 | tf_op jit(solution)/shard_map/ppermute | solution.py:617
  7.5 3.9 %collective-permute-start = (f32[8,1024]{1,0:T(8,128)S(1)}, f32[8,1024]{1,0:T(8,128)S(1)}, u32[]{:S(2)}, u32[]{:S(2)}) collective-permute-start(f32[8,1024]{1,0:T(8,128)S(1)} %get-tuple-element.36.after_ref.refs_0_), channel_id=1, source_target_pairs={{0,8},{8,0},{16,24},{24,16},{1,9},{9,1},{17,25},{25,17},{2,10},{10... | collective-permute-start | bytes 98312 | tf_op jit(solution)/shard_map/ppermute | solution.py:617
  11.4 15.3 %collective-permute-start.3 = (bf16[256,1024]{1,0:T(8,128)(2,1)}, bf16[256,1024]{1,0:T(8,128)(2,1)S(1)}, u32[]{:S(2)}, u32[]{:S(2)}) collective-permute-start(bf16[256,1024]{1,0:T(8,128)(2,1)} %get-tuple-element.50), channel_id=1, source_target_pairs={{0,16},{8,24},{16,0},{24,8},{1,17},{9,25},{17,1},{25,9},{2,18},{10... | collective-permute-start | bytes 1572872 | tf_op jit(solution)/shard_map/ppermute | solution.py:695
  12.9 13.8 %collective-permute-start.4 = (bf16[256,1024]{1,0:T(8,128)(2,1)}, bf16[256,1024]{1,0:T(8,128)(2,1)}, u32[]{:S(2)}, u32[]{:S(2)}) collective-permute-start(bf16[256,1024]{1,0:T(8,128)(2,1)} %get-tuple-element.51), channel_id=1, source_target_pairs={{0,8},{8,0},{16,24},{24,16},{1,9},{9,1},{17,25},{25,17},{2,10},{10... | collective-permute-start | bytes 1572872 | tf_op jit(solution)/shard_map/ppermute | solution.py:694
  15.9 10.8 %all-to-all-start = ((f32[8,16,128]{2,1,0:T(8,128)}), f32[8,16,128]{2,1,0:T(8,128)S(1)}, u32[]{:S(2)}, u32[]{:S(2)}) async-start(f32[8,16,128]{2,1,0:T(8,128)} %get-tuple-element.44), calls=%async_computation | async-start | bytes 131072 | tf_op jit(solution)/shard_map/all_to_all | solution.py:666
  20.8 9.2 %copy-start = (f32[3,1024]{1,0:T(4,128)S(1)}, f32[3,1024]{1,0:T(4,128)}, u32[]{:S(2)}) copy-start(f32[3,1024]{1,0:T(4,128)} %refs_1_.1) | copy-start | bytes 36868
  29.9 12.6 %collective-permute-start.5 = (bf16[256,1024]{1,0:T(8,128)(2,1)}, bf16[256,1024]{1,0:T(8,128)(2,1)}, u32[]{:S(2)}, u32[]{:S(2)}) collective-permute-start(bf16[256,1024]{1,0:T(8,128)(2,1)} %get-tuple-element.53.refs_0_), channel_id=1, source_target_pairs={{0,16},{8,24},{16,0},{24,8},{1,17},{9,25},{17,1},{25,9},{2,18},{10... | collective-permute-start | bytes 1572872 | tf_op jit(solution)/shard_map/ppermute | solution.py:695
  29.9 13.8 %collective-permute-start.6 = (bf16[256,1024]{1,0:T(8,128)(2,1)S(1)}, bf16[256,1024]{1,0:T(8,128)(2,1)}, u32[]{:S(2)}, u32[]{:S(2)}) collective-permute-start(bf16[256,1024]{1,0:T(8,128)(2,1)S(1)} %get-tuple-element.54.refs_2_), channel_id=1, source_target_pairs={{0,8},{8,0},{16,24},{24,16},{1,9},{9,1},{17,25},{25,17},{2,10},{10... | collective-permute-start | bytes 1572872 | tf_op jit(solution)/shard_map/ppermute | solution.py:694
  36.4 15.2 %all-to-all-start.1 = ((bf16[8,176,128]{2,1,0:T(8,128)(2,1)}), bf16[8,176,128]{2,1,0:T(8,128)(2,1)S(1)}, u32[]{:S(2)}, u32[]{:S(2)}) async-start(bf16[8,176,128]{2,1,0:T(8,128)(2,1)} %shard_map.126.refs_0_), calls=%async_computation.1 | async-start | bytes 720896 | tf_op jit(solution)/shard_map/all_to_all | solution.py:763
  46.5 12.2 %collective-permute-start.8 = (bf16[256,1024]{1,0:T(8,128)(2,1)}, bf16[256,1024]{1,0:T(8,128)(2,1)S(1)}, u32[]{:S(2)}, u32[]{:S(2)}) collective-permute-start(bf16[256,1024]{1,0:T(8,128)(2,1)} %get-tuple-element.59.refs_1_), channel_id=1, source_target_pairs={{0,16},{8,24},{16,0},{24,8},{1,17},{9,25},{17,1},{25,9},{2,18},{10... | collective-permute-start | bytes 1572872 | tf_op jit(solution)/shard_map/ppermute | solution.py:695
  46.6 13.6 %collective-permute-start.7 = (bf16[256,1024]{1,0:T(8,128)(2,1)}, bf16[256,1024]{1,0:T(8,128)(2,1)S(1)}, u32[]{:S(2)}, u32[]{:S(2)}) collective-permute-start(bf16[256,1024]{1,0:T(8,128)(2,1)} %get-tuple-element.60.refs_3_), channel_id=1, source_target_pairs={{0,8},{8,0},{16,24},{24,16},{1,9},{9,1},{17,25},{25,17},{2,10},{10... | collective-permute-start | bytes 1572872 | tf_op jit(solution)/shard_map/ppermute | solution.py:694

commit v11 on v10

--- a/solution.py
+++ b/solution.py
@@ -446,46 +446,28 @@
     return chunk
 
 
-def load_slots(plan, slots, role, inverse_hbm, inputs, parent, staged, sem):
-    depth = parent.shape[1]
+def load_slots(plan, slots, role, inputs, parent, sem):
     for slot in slots:
-        own = pltpu.make_async_copy(
-            rows_of(inverse_hbm, plan[0][slot][0], depth), staged.at[slot], sem.at[slot]
-        )
-        pl.when(role == 0)(own.start)
-        for which in range(1, len(plan)):
-            sent = pltpu.make_async_copy(
+        for which in range(len(plan)):
+            load = pltpu.make_async_copy(
                 inputs[plan[which][slot][1]], parent.at[slot], sem.at[slot]
             )
-            pl.when(role == which)(sent.start)
-
-
-def settle_slots(plan, slots, role, inverse_hbm, inputs, parent, staged, sem):
-    depth = parent.shape[1]
+            pl.when(role == which)(load.start)
+
+
+def wait_slots(slots, inputs, parent, sem):
     for slot in slots:
-        own = pltpu.make_async_copy(
-            rows_of(inverse_hbm, plan[0][slot][0], depth), staged.at[slot], sem.at[slot]
-        )
-        sent = pltpu.make_async_copy(inputs[0], parent.at[slot], sem.at[slot])
-
-        @pl.when(role == 0)
-        def _():
-            own.wait()
-            parent[slot] = staged[slot].astype(BF16)
-
-        @pl.when(role != 0)
-        def _():
-            sent.wait()
-
-
-def early_kernel(count, plan, role_ref, number_ref, later_ref, inverse_hbm, *refs):
-    inputs = refs[:-6]
-    columns_ref, products_ref, total_ref, parent, staged, sem = refs[-6:]
+        pltpu.make_async_copy(inputs[0], parent.at[slot], sem.at[slot]).wait()
+
+
+def early_kernel(count, plan, role_ref, number_ref, later_ref, *refs):
+    inputs = refs[:-5]
+    columns_ref, products_ref, total_ref, parent, sem = refs[-5:]
     slots, depth, electrons = parent.shape
     role = role_ref[0]
-    load_slots(plan, range(slots), role, inverse_hbm, inputs, parent, staged, sem)
+    load_slots(plan, range(slots), role, inputs, parent, sem)
     pick = pick_from(number_ref, electrons)
-    settle_slots(plan, range(slots), role, inverse_hbm, inputs, parent, staged, sem)
+    wait_slots(range(slots), inputs, parent, sem)
     products, total = None, None
     for slot in range(slots):
         columns = dot(parent[slot], pick).astype(BF16)
@@ -515,17 +497,25 @@
     inverse_hbm,
     *refs,
 ):
-    inputs = refs[:-8]
-    out_ref, drift_ref, lap_ref, out_weight_ref, parent, staged, in_sem, out_sem = refs[-8:]
+    inputs = refs[:-9]
+    out_ref, drift_ref, lap_ref, out_weight_ref = refs[-9:-5]
+    parent, staged, in_sem, own_sem, out_sem = refs[-5:]
     chunks, depth, electrons = parent.shape
     done = early_ref.shape[0]
     late = range(done, chunks)
     size = 2 * count
     role = role_ref[0]
-    loads = (role, inverse_hbm, inputs, parent, staged, in_sem)
-    load_slots(plan, list(late) + list(range(done)), *loads)
+    own = [
+        pltpu.make_async_copy(
+            rows_of(inverse_hbm, plan[0][slot][0], depth), staged.at[slot], own_sem.at[slot]
+        )
+        for slot in range(chunks)
+    ]
+    load_slots(plan, list(late) + list(range(done)), role, inputs, parent, in_sem)
+    for load in own:
+        pl.when(role == 0)(load.start)
     pick = pick_from(number_ref, electrons)
-    settle_slots(plan, late, *loads)
+    wait_slots(late, inputs, parent, in_sem)
     columns = [early_ref[slot] for slot in range(done)]
     products = products_ref[...]
     rows = []
@@ -544,7 +534,7 @@
     rounded = total.astype(BF16)
     solved = dot(halves, jnp.concatenate([rounded, rounded], 0)).astype(BF16)
     solved = jnp.concatenate([solved, jnp.zeros((LANES - size, electrons), BF16)], 0)
-    settle_slots(plan, range(done), *loads)
+    wait_slots(range(done), inputs, parent, in_sem)
     copies = []
     for slot in list(late) + list(range(done)):
         at = pl.multiple_of(chunk_at(plan, role, slot) * depth, depth)
@@ -553,12 +543,16 @@
         )
         copies.append((slot, copy))
 
+    def kept(slot):
+        own[slot].wait()
+        return staged[slot]
+
     def write(before):
         for slot, copy in copies:
             staged[slot] = before(slot) - dot(columns[slot], solved)
             copy.start()
 
-    pl.when(role == 0)(lambda: write(lambda slot: staged[slot]))
+    pl.when(role == 0)(lambda: write(kept))
     pl.when(role != 0)(lambda: write(lambda slot: parent[slot].astype(F32)))
     sums = moved_sums(products, ratio, inverse, count)
     drift_ref[0:3] = drift_in[...]
@@ -689,7 +683,7 @@
     for chunk, ready in zip(middle, prepared):
         own[chunk] = ready
 
-    arrays = []
+    arrays = list(own)
     if n_grp == 4:
         send_x = lambda block: lax.ppermute(block, "grp", pairs(n_grp, 1))
         send_y = lambda block: lax.ppermute(block, "grp", pairs(n_grp, 2))
@@ -701,9 +695,9 @@
                 [SM] + [ANY] * (4 + len(first)),
                 (ANY, ANY, VM),
                 scratch=[
-                    pltpu.VMEM((8, depth // 4, electrons), BF16),
-                    pltpu.SemaphoreType.DMA((8,)),
-                    pltpu.SemaphoreType.DMA((8,)),
+                    pltpu.VMEM((2, depth, electrons), BF16),
+                    pltpu.SemaphoreType.DMA((2,)),
+                    pltpu.SemaphoreType.DMA((2,)),
                 ],
                 aliases={3: 0, 4: 1},
                 vmem=2,
@@ -714,7 +708,7 @@
         x2, y2 = send_x(y1), send_y(x1)
     else:
         token_1 = token_2 = jnp.zeros((8, LANES), F32)
-        plan = [tuple((chunk, 0) for chunk in range(chunks))]
+        plan = [tuple((chunk, chunk) for chunk in range(chunks))]
         for step in range(1, n_grp):
             plan.append(tuple((chunk, len(arrays) + chunk) for chunk in range(chunks)))
             arrays += [lax.ppermute(block, "grp", pairs(n_grp, step)) for block in own]
@@ -768,16 +762,16 @@
     if n_grp == 4:
         y2, x2, token_2 = relay((own[2], own[1]), (y2, x2), (computed,))
         x3, y3 = send_x(y2), send_y(x2)
-        arrays = [x1, x2, y1, y2, x3, y3]
-        a1, a2, b1, b2, a3, b3 = range(6)
+        arrays = own + [x1, x2, y1, y2, x3, y3]
+        a1, a2, b1, b2, a3, b3 = range(chunks, chunks + 6)
         first, second, third, fourth = range(chunks)
         plan = [
-            tuple((chunk, 0) for chunk in range(chunks)),
+            tuple((chunk, chunk) for chunk in range(chunks)),
             ((first, a1), (second, a2), (third, a3), (fourth, b3)),
             ((fourth, b1), (third, b2), (first, a3), (second, b3)),
             ((fourth, a2), (first, b2), (third, a3), (second, b3)),
         ]
-        settled = 4
+        settled = chunks + 4
 
     columns = call(
         functools.partial(columns_kernel, count),
@@ -817,17 +811,16 @@
             shape((6 * count, LANES), F32),
             shape((2 * count, electrons), F32),
         ),
-        [SM, VM, VM, HBM] + [ANY] * settled,
+        [SM, VM, VM] + [ANY] * settled,
         (VM, VM, VM),
         scratch=[
             pltpu.VMEM((early, depth, electrons), BF16),
-            pltpu.VMEM((early, depth, electrons), F32),
             pltpu.SemaphoreType.DMA((early,)),
         ],
         flops=early * depth * work,
         moved=2 * early * depth * electrons,
         vmem=8,
-    )(role, number, later, *in_hbm(inverse), *arrays[:settled])
+    )(role, number, later, *in_hbm(*own), *arrays[chunks:settled])
 
     updated, drift, laplacian, new_weight = call(
         functools.partial(finish_kernel, count, plan),
@@ -842,6 +835,7 @@
         scratch=[
             pltpu.VMEM((chunks, depth, electrons), BF16),
             pltpu.VMEM((chunks, depth, electrons), F32),
+            pltpu.SemaphoreType.DMA((chunks,)),
             pltpu.SemaphoreType.DMA((chunks,)),
             pltpu.SemaphoreType.DMA((chunks,)),
         ],
@@ -858,8 +852,8 @@
         early_columns,
         products,
         total,
-        *in_hbm(inverse),
-        *arrays,
+        *in_hbm(inverse, *own),
+        *arrays[chunks:],
     )
 
     return updated[None], drift.reshape(2, 1, 3, count), laplacian, new_weight[0, :1]

time: 68.2 us -> 67.3 us (0.987)
  Pallas kernels: 36.2 us -> 34.9 us
  starting transfers between devices: 15.4 us -> 16.2 us
    ppermute x3, waiting for transfers between devices: 5.23 us -> 1.76 us  [per_device(): send_y = lambda block: lax.ppermute(block, 'grp', pairs(n_grp, 2))]
    ppermute x3, waiting for transfers between devices: 2.71 us -> 4.26 us  [per_device(): send_x = lambda block: lax.ppermute(block, 'grp', pairs(n_grp, 1))]
    all_to_all x1, waiting for transfers between devices: 2.51 us -> 3.78 us  [per_device(): lax.all_to_all(values, 'orb', split_axis=0, concat_axis=0, tiled=True)]
    all_to_all x1, starting transfers between devices: 3.44 us -> 4.25 us  [per_device(): lax.all_to_all(values, 'orb', split_axis=0, concat_axis=0, tiled=True)]
where the time goes in v11:
time: 67.3 us; the launch traced here: 66.8 us
  Pallas kernels  34.9 us (52%)
  starting transfers between devices  16.2 us (24%)
  waiting for transfers between devices  13 us (19%)
  between operations  2.69 us (4%)
    pallas_call x1, Pallas kernels, per_device(): call(functools.partial(finish_kernel, count, plan), (shape((electrons, el...  7.37 us
    pallas_call x1, Pallas kernels, per_device(): pl.pallas_call(functools.partial(evaluate_kernel, count, sources, targets...  6.42 us
    pallas_call x2, Pallas kernels, relay(): call(relay_kernel, (kept, kept, token), [SM] + [ANY] * (4 + len(first)),...  5.38 us
    all_to_all x1, starting transfers between devices, per_device(): lax.all_to_all(points, 'orb', split_axis=0, concat_axis=0, tiled=True)  4.89 us
    ppermute x3, starting transfers between devices, per_device(): lax.ppermute(record, 'grp', pairs(n_grp, s))  4.6 us
    ppermute x3, waiting for transfers between devices, per_device(): send_x = lambda block: lax.ppermute(block, 'grp', pairs(n_grp, 1))  4.26 us
    all_to_all x1, starting transfers between devices, per_device(): lax.all_to_all(values, 'orb', split_axis=0, concat_axis=0, tiled=True)  4.25 us
    pallas_call x1, Pallas kernels, per_device(): call(functools.partial(prepare_kernel, middle), (shape((plane, 5 * width)...  4.05 us
  transfers between devices with their start and end apart: 11, of which 8 were waited for; matrix products, arithmetic and copies ran while one was open for 0% of the time, Pallas kernels for 35%

profile of v11, /device:TPU:0, one launch (start us, length us, event | category | flops | bytes accessed | tf_op | source)
XLA Modules:
  0.0 66.8 jit_solution(12051354806673974490)
XLA Ops:
  1.3 1.7 %shard_map.120 = (f32[8,1024]{1,0:T(8,128)S(1)}, s32[2,128]{1,0:T(2,128)S(1)}, f32[2,8,128]{2,1,0:T(8,128)S(1)}) custom-call(f32[3,1,1024]{2,1,0:T(1,128)} %bitcast.11, s32[2,1,16]{2,1,0:T(1,128)} %moved_hbm.1, f32[6,1,16]{2,1,0:T(1,128)} %bitcast.12, f32[1]{0:T(128)S(6)} %copy.27.weight_ref), custom_call_target="tpu_custom_call" | custom-call | tf_op jit(solution)/shard_map/pallas_call | solution.py:588
  3.0 4.0 %collective-permute-start.2 = (f32[8,1024]{1,0:T(8,128)S(1)}, f32[8,1024]{1,0:T(8,128)S(1)}, u32[]{:S(2)}, u32[]{:S(2)}) collective-permute-start(f32[8,1024]{1,0:T(8,128)S(1)} %get-tuple-element.36.after_ref.refs_0_), channel_id=1, source_target_pairs={{0,24},{8,16},{16,8},{24,0},{1,25},{9,17},{17,9},{25,1},{2,26},{10... | collective-permute-start | bytes 98312 | tf_op jit(solution)/shard_map/ppermute | solution.py:611
  7.0 0.5 collective-permute-start.1
  7.5 0.1 collective-permute-start
  7.6 2.4 %shard_map.121 = (bf16[256,1024]{1,0:T(8,128)(2,1)}, bf16[256,1024]{1,0:T(8,128)(2,1)}) custom-call(f32[1,1024,1024]{2,1,0:T(8,128)} %inverse_hbm.7, f32[8,1024]{1,0:T(8,128)S(1)} %get-tuple-element.36.after_ref.refs_0_), custom_call_target="tpu_custom_call" | custom-call | bytes 3145728 | tf_op jit(solution)/shard_map/pallas_call | solution.py:619
  10.0 0.0 collective-permute-done.2.refs_4_.refs_3_
  10.0 0.8 %collective-permute-done.1.refs_3_.refs_2_ = f32[8,1024]{1,0:T(8,128)S(1)} collective-permute-done((f32[8,1024]{1,0:T(8,128)S(1)}, f32[8,1024]{1,0:T(8,128)S(1)}, u32[]{:S(2)}, u32[]{:S(2)}) %collective-permute-start.1) | collective-permute-done | bytes 32800 | tf_op jit(solution)/shard_map/ppermute | solution.py:611
  10.9 0.5 collective-permute-done.refs_2_.refs_1_
  11.4 1.5 %collective-permute-start.3 = (bf16[256,1024]{1,0:T(8,128)(2,1)}, bf16[256,1024]{1,0:T(8,128)(2,1)S(1)}, u32[]{:S(2)}, u32[]{:S(2)}) collective-permute-start(bf16[256,1024]{1,0:T(8,128)(2,1)} %get-tuple-element.50.refs_3_), channel_id=1, source_target_pairs={{0,16},{8,24},{16,0},{24,8},{1,17},{9,25},{17,1},{25,9},{2,18},{10... | collective-permute-start | bytes 1572872 | tf_op jit(solution)/shard_map/ppermute | solution.py:689
  12.9 0.6 collective-permute-start.4
  14.8 1.0 %shard_map.123 = (f32[8,16,128]{2,1,0:T(8,128)}, f32[1,128]{1,0:T(1,128)S(1)}, s32[1,128]{1,0:T(1,128)S(1)}, s32[1]{0:T(128)}, s32[1]{0:T(128)}) custom-call(s32[1,1]{1,0:T(1,128)} %bitcast.9.donor_ref, s32[1,1]{1,0:T(1,128)} %bitcast.10.take_ref, f32[8,1024]{1,0:T(8,128)S(1)} %get-tuple-element.36.after_ref.refs_0_, ...), custom_call_target="tpu_custom_call" | custom-call | tf_op jit(solution)/shard_map/pallas_call | solution.py:645
  15.9 4.9 %all-to-all-start = ((f32[8,16,128]{2,1,0:T(8,128)}), f32[8,16,128]{2,1,0:T(8,128)S(1)}, u32[]{:S(2)}, u32[]{:S(2)}) async-start(f32[8,16,128]{2,1,0:T(8,128)} %get-tuple-element.44), calls=%async_computation | async-start | bytes 131072 | tf_op jit(solution)/shard_map/all_to_all | solution.py:660
  20.8 0.0 copy-start
  20.8 4.0 %shard_map.124 = (bf16[2048,640]{1,0:T(8,128)(2,1)S(1)}, bf16[256,1024]{1,0:T(8,128)(2,1)}, bf16[256,1024]{1,0:T(8,128)(2,1)}) custom-call(bf16[2048,128]{1,0:T(8,128)(2,1)} %coeff_hbm.1, f32[3,1024]{1,0:T(4,128)} %refs_1_.1, f32[1,1024,1024]{2,1,0:T(8,128)} %inverse_hbm.7, f32[1,128]{1,0:T(1,128)S(1)} %get-tuple-element.45.after_ref.weight_ref), custom_call_target="tpu_custom_call" | custom-call | flops 2097152 | bytes 5767168 | tf_op jit(solution)/shard_map/pallas_call | solution.py:664
  24.8 1.9 %all-to-all-done.refs_1_.refs_0_ = f32[8,16,128]{2,1,0:T(8,128)S(1)} async-done(((f32[8,16,128]{2,1,0:T(8,128)}), f32[8,16,128]{2,1,0:T(8,128)S(1)}, u32[]{:S(2)}, u32[]{:S(2)}) %all-to-all-start) | async-done | bytes 65568 | tf_op jit(solution)/shard_map/all_to_all | solution.py:660
  26.7 0.0 collective-permute-done.3.got_a
  26.7 0.0 collective-permute-done.4.got_b
  26.7 2.7 %shard_map.125 = (bf16[256,1024]{1,0:T(8,128)(2,1)S(1)}, bf16[256,1024]{1,0:T(8,128)(2,1)}, f32[8,128]{1,0:T(8,128)S(1)}) custom-call(s32[1]{0:T(128)} %get-tuple-element.47.flag_ref, bf16[256,1024]{1,0:T(8,128)(2,1)} %get-tuple-element.48.own_a.own_b.refs_1_, ...), custom_call_target="tpu_custom_call", output_to_operand_aliasing={{0}: (3, {}), {1}: (4, {})} | custom-call | tf_op jit(solution)/shard_map/pallas_call | solution.py:692
  29.4 0.1 collective-permute-start.5
  29.5 0.1 collective-permute-start.6
  29.5 0.0 copy-done
  29.6 6.4 %shard_map.126.refs_0_ = bf16[8,176,128]{2,1,0:T(8,128)(2,1)} custom-call(f32[8,16,128]{2,1,0:T(8,128)S(1)} %all-to-all-done.refs_1_.refs_0_, f32[3,1024]{1,0:T(4,128)S(1)} %copy-done, bf16[2048,640]{1,0:T(8,128)(2,1)S(1)} %get-tuple-element.46.refs_0_.refs_2_, f32[8,128]{1,0:T(8,128)S(1)} %get-tuple-element.52.refs_3_), custom_call_target="tpu_custom_call" | custom-call | flops 738197504 | bytes 3145728 | tf_op jit(solution)/shard_map/pallas_call | solution.py:732
  36.0 4.2 %all-to-all-start.1 = ((bf16[8,176,128]{2,1,0:T(8,128)(2,1)}), bf16[8,176,128]{2,1,0:T(8,128)(2,1)S(1)}, u32[]{:S(2)}, u32[]{:S(2)}) async-start(bf16[8,176,128]{2,1,0:T(8,128)(2,1)} %shard_map.126.refs_0_), calls=%async_computation.1 | async-start | bytes 720896 | tf_op jit(solution)/shard_map/all_to_all | solution.py:757
  40.2 1.0 %collective-permute-done.5.got_a = bf16[256,1024]{1,0:T(8,128)(2,1)} collective-permute-done((bf16[256,1024]{1,0:T(8,128)(2,1)}, bf16[256,1024]{1,0:T(8,128)(2,1)}, u32[]{:S(2)}, u32[]{:S(2)}) %collective-permute-start.5) | collective-permute-done | bytes 524320 | tf_op jit(solution)/shard_map/ppermute | solution.py:689
  41.3 1.7 %collective-permute-done.6.got_b = bf16[256,1024]{1,0:T(8,128)(2,1)} collective-permute-done((bf16[256,1024]{1,0:T(8,128)(2,1)S(1)}, bf16[256,1024]{1,0:T(8,128)(2,1)}, u32[]{:S(2)}, u32[]{:S(2)}) %collective-permute-start.6) | collective-permute-done | bytes 524320 | tf_op jit(solution)/shard_map/ppermute | solution.py:688
  42.9 2.7 %shard_map.127 = (bf16[256,1024]{1,0:T(8,128)(2,1)}, bf16[256,1024]{1,0:T(8,128)(2,1)}, f32[8,128]{1,0:T(8,128)S(1)}) custom-call(s32[1]{0:T(128)} %get-tuple-element.47.flag_ref, bf16[256,1024]{1,0:T(8,128)(2,1)} %get-tuple-element.49.own_b.own_a.refs_2_, ...), custom_call_target="tpu_custom_call", output_to_operand_aliasing={{0}: (3, {}), {1}: (4, {})} | custom-call | tf_op jit(solution)/shard_map/pallas_call | solution.py:692
  45.6 0.1 collective-permute-start.8
  45.7 0.1 collective-permute-start.7
  45.8 2.5 %shard_map.128.refs_1_ = bf16[1024,128]{1,0:T(8,128)(2,1)S(1)} custom-call(f32[1,1024,1024]{2,1,0:T(8,128)} %inverse_hbm.7, s32[2,128]{1,0:T(2,128)S(1)} %get-tuple-element.37.refs_4_.moved_ref, f32[8,128]{1,0:T(8,128)S(1)} %get-tuple-element.55.after_ref), custom_call_target="tpu_custom_call" | custom-call | flops 268435456 | bytes 4194304 | tf_op jit(solution)/shard_map/pallas_call | solution.py:776
  48.3 3.8 %all-to-all-done.1.refs_0_ = bf16[8,176,128]{2,1,0:T(8,128)(2,1)S(1)} async-done(((bf16[8,176,128]{2,1,0:T(8,128)(2,1)}), bf16[8,176,128]{2,1,0:T(8,128)(2,1)S(1)}, u32[]{:S(2)}, u32[]{:S(2)}) %all-to-all-start.1) | async-done | bytes 360480 | tf_op jit(solution)/shard_map/all_to_all | solution.py:757
  52.1 1.4 %shard_map.129 = (f32[3,1,16]{2,1,0:T(1,128)S(1)}, f32[1,1,16]{2,1,0:T(1,128)S(1)}, bf16[96,1024]{1,0:T(8,128)(2,1)S(1)}) custom-call(s32[1]{0:T(128)} %bitcast.4.me_ref, bf16[8,176,128]{2,1,0:T(8,128)(2,1)S(1)} %all-to-all-done.1.refs_0_, bf16[1024,128]{1,0:T(8,128)(2,1)S(1)} %shard_map.128.refs_1_), custom_call_target="tpu_custom_call" | custom-call | flops 46137344 | bytes 720896 | tf_op jit(solution)/shard_map/pallas_call | solution.py:791
  53.5 2.6 %shard_map.130 = (bf16[2,256,128]{2,1,0:T(8,128)(2,1)S(1)}, f32[96,128]{1,0:T(8,128)S(1)}, f32[32,1024]{1,0:T(8,128)S(1)}) custom-call(s32[1]{0:T(128)} %get-tuple-element.42.role_ref, s32[1,128]{1,0:T(1,128)S(1)} %get-tuple-element.43.number_ref, bf16[96,1024]{1,0:T(8,128)(2,1)S(1)} %get-tuple-element.56.later_ref, ...), custom_call_target="tpu_custom_call" | custom-call | flops 33554432 | bytes 1048576 | tf_op jit(solution)/shard_map/pallas_call | solution.py:807
  56.1 0.7 %collective-permute-done.8.refs_9_ = bf16[256,1024]{1,0:T(8,128)(2,1)S(1)} collective-permute-done((bf16[256,1024]{1,0:T(8,128)(2,1)}, bf16[256,1024]{1,0:T(8,128)(2,1)S(1)}, u32[]{:S(2)}, u32[]{:S(2)}) %collective-permute-start.8) | collective-permute-done | bytes 524320 | tf_op jit(solution)/shard_map/ppermute | solution.py:689
  56.8 2.6 %collective-permute-done.7.refs_8_ = bf16[256,1024]{1,0:T(8,128)(2,1)S(1)} collective-permute-done((bf16[256,1024]{1,0:T(8,128)(2,1)}, bf16[256,1024]{1,0:T(8,128)(2,1)S(1)}, u32[]{:S(2)}, u32[]{:S(2)}) %collective-permute-start.7) | collective-permute-done | bytes 524320 | tf_op jit(solution)/shard_map/ppermute | solution.py:688
  59.4 7.4 %shard_map.131 = (f32[1024,1024]{1,0:T(8,128)}, f32[6,1,16]{2,1,0:T(1,128)}, f32[2,1,16]{2,1,0:T(1,128)}, f32[1,128]{1,0:T(1,128)}) custom-call(s32[1]{0:T(128)} %get-tuple-element.42.role_ref, s32[1,128]{1,0:T(1,128)S(1)} %get-tuple-element.43.number_ref, bf16[96,1024]{1,0:T(8,128)(2,1)S(1)} %get-tuple-element.56.later_ref, ...), custom_call_target="tpu_custom_call" | custom-call | flops 134217728 | bytes 6291456 | tf_op jit(solution)/shard_map/pallas_call | solution.py:825
  (1 shorter events, 0.0 us)
Async XLA Ops:
  3.0 7.0 %collective-permute-start.2 = (f32[8,1024]{1,0:T(8,128)S(1)}, f32[8,1024]{1,0:T(8,128)S(1)}, u32[]{:S(2)}, u32[]{:S(2)}) collective-permute-start(f32[8,1024]{1,0:T(8,128)S(1)} %get-tuple-element.36.after_ref.refs_0_), channel_id=1, source_target_pairs={{0,24},{8,16},{16,8},{24,0},{1,25},{9,17},{17,9},{25,1},{2,26},{10... | collective-permute-start | bytes 98312 | tf_op jit(solution)/shard_map/ppermute | solution.py:611
  7.0 3.9 %collective-permute-start.1 = (f32[8,1024]{1,0:T(8,128)S(1)}, f32[8,1024]{1,0:T(8,128)S(1)}, u32[]{:S(2)}, u32[]{:S(2)}) collective-permute-start(f32[8,1024]{1,0:T(8,128)S(1)} %get-tuple-element.36.after_ref.refs_0_), channel_id=1, source_target_pairs={{0,16},{8,24},{16,0},{24,8},{1,17},{9,25},{17,1},{25,9},{2,18},{10... | collective-permute-start | bytes 98312 | tf_op jit(solution)/shard_map/ppermute | solution.py:611
  7.5 3.9 %collective-permute-start = (f32[8,1024]{1,0:T(8,128)S(1)}, f32[8,1024]{1,0:T(8,128)S(1)}, u32[]{:S(2)}, u32[]{:S(2)}) collective-permute-start(f32[8,1024]{1,0:T(8,128)S(1)} %get-tuple-element.36.after_ref.refs_0_), channel_id=1, source_target_pairs={{0,8},{8,0},{16,24},{24,16},{1,9},{9,1},{17,25},{25,17},{2,10},{10... | collective-permute-start | bytes 98312 | tf_op jit(solution)/shard_map/ppermute | solution.py:611
  11.4 15.3 %collective-permute-start.3 = (bf16[256,1024]{1,0:T(8,128)(2,1)}, bf16[256,1024]{1,0:T(8,128)(2,1)S(1)}, u32[]{:S(2)}, u32[]{:S(2)}) collective-permute-start(bf16[256,1024]{1,0:T(8,128)(2,1)} %get-tuple-element.50.refs_3_), channel_id=1, source_target_pairs={{0,16},{8,24},{16,0},{24,8},{1,17},{9,25},{17,1},{25,9},{2,18},{10... | collective-permute-start | bytes 1572872 | tf_op jit(solution)/shard_map/ppermute | solution.py:689
  12.9 13.8 %collective-permute-start.4 = (bf16[256,1024]{1,0:T(8,128)(2,1)}, bf16[256,1024]{1,0:T(8,128)(2,1)}, u32[]{:S(2)}, u32[]{:S(2)}) collective-permute-start(bf16[256,1024]{1,0:T(8,128)(2,1)} %get-tuple-element.51.refs_0_), channel_id=1, source_target_pairs={{0,8},{8,0},{16,24},{24,16},{1,9},{9,1},{17,25},{25,17},{2,10},{10... | collective-permute-start | bytes 1572872 | tf_op jit(solution)/shard_map/ppermute | solution.py:688
  15.9 10.8 %all-to-all-start = ((f32[8,16,128]{2,1,0:T(8,128)}), f32[8,16,128]{2,1,0:T(8,128)S(1)}, u32[]{:S(2)}, u32[]{:S(2)}) async-start(f32[8,16,128]{2,1,0:T(8,128)} %get-tuple-element.44), calls=%async_computation | async-start | bytes 131072 | tf_op jit(solution)/shard_map/all_to_all | solution.py:660
  20.8 8.8 %copy-start = (f32[3,1024]{1,0:T(4,128)S(1)}, f32[3,1024]{1,0:T(4,128)}, u32[]{:S(2)}) copy-start(f32[3,1024]{1,0:T(4,128)} %refs_1_.1) | copy-start | bytes 36868
  29.4 11.9 %collective-permute-start.5 = (bf16[256,1024]{1,0:T(8,128)(2,1)}, bf16[256,1024]{1,0:T(8,128)(2,1)}, u32[]{:S(2)}, u32[]{:S(2)}) collective-permute-start(bf16[256,1024]{1,0:T(8,128)(2,1)} %get-tuple-element.53.refs_4_), channel_id=1, source_target_pairs={{0,16},{8,24},{16,0},{24,8},{1,17},{9,25},{17,1},{25,9},{2,18},{10... | collective-permute-start | bytes 1572872 | tf_op jit(solution)/shard_map/ppermute | solution.py:689
  29.5 13.5 %collective-permute-start.6 = (bf16[256,1024]{1,0:T(8,128)(2,1)S(1)}, bf16[256,1024]{1,0:T(8,128)(2,1)}, u32[]{:S(2)}, u32[]{:S(2)}) collective-permute-start(bf16[256,1024]{1,0:T(8,128)(2,1)S(1)} %get-tuple-element.54.refs_6_), channel_id=1, source_target_pairs={{0,8},{8,0},{16,24},{24,16},{1,9},{9,1},{17,25},{25,17},{2,10},{10... | collective-permute-start | bytes 1572872 | tf_op jit(solution)/shard_map/ppermute | solution.py:688
  36.0 16.1 %all-to-all-start.1 = ((bf16[8,176,128]{2,1,0:T(8,128)(2,1)}), bf16[8,176,128]{2,1,0:T(8,128)(2,1)S(1)}, u32[]{:S(2)}, u32[]{:S(2)}) async-start(bf16[8,176,128]{2,1,0:T(8,128)(2,1)} %shard_map.126.refs_0_), calls=%async_computation.1 | async-start | bytes 720896 | tf_op jit(solution)/shard_map/all_to_all | solution.py:757
  45.6 11.1 %collective-permute-start.8 = (bf16[256,1024]{1,0:T(8,128)(2,1)}, bf16[256,1024]{1,0:T(8,128)(2,1)S(1)}, u32[]{:S(2)}, u32[]{:S(2)}) collective-permute-start(bf16[256,1024]{1,0:T(8,128)(2,1)} %get-tuple-element.59.refs_5_), channel_id=1, source_target_pairs={{0,16},{8,24},{16,0},{24,8},{1,17},{9,25},{17,1},{25,9},{2,18},{10... | collective-permute-start | bytes 1572872 | tf_op jit(solution)/shard_map/ppermute | solution.py:689
  45.7 13.7 %collective-permute-start.7 = (bf16[256,1024]{1,0:T(8,128)(2,1)}, bf16[256,1024]{1,0:T(8,128)(2,1)S(1)}, u32[]{:S(2)}, u32[]{:S(2)}) collective-permute-start(bf16[256,1024]{1,0:T(8,128)(2,1)} %get-tuple-element.60.refs_7_), channel_id=1, source_target_pairs={{0,8},{8,0},{16,24},{24,16},{1,9},{9,1},{17,25},{25,17},{2,10},{10... | collective-permute-start | bytes 1572872 | tf_op jit(solution)/shard_map/ppermute | solution.py:688

commit v12 on v11

--- a/solution.py
+++ b/solution.py
@@ -185,15 +185,11 @@
     token_ref[...] = jnp.zeros(token_ref.shape, F32)
 
 
-def points_kernel(count, others, donor_ref, take_ref, *refs):
+def points_kernel(count, others, role_ref, *refs):
     own_ref = refs[0]
     received = refs[1 : 1 + others]
-    moved_ref, disp_ref, after_ref, points_ref, weight_ref, number_ref = refs[1 + others : -2]
-    role_ref, apart_ref = refs[-2:]
-    apart = distance(others + 1, lax.axis_index("grp"), donor_ref[0, 0])
-    role = jnp.where(take_ref[0, 0] == 1, apart, 0)
-    apart_ref[0] = apart
-    role_ref[0] = role
+    moved_ref, disp_ref, after_ref, points_ref, weight_ref, number_ref = refs[1 + others :]
+    role = role_ref[0]
     parent = own_ref[...]
     for step in range(others):
         parent = jnp.where(role == step + 1, received[step][...], parent)
@@ -275,8 +271,8 @@
 def evaluate_kernel(count, sources, targets, *refs):
     points = refs[:sources]
     wave_ref, table_ref = refs[sources : sources + 2]
-    outs = refs[sources + 3 : -3]
-    diff, new, gathered = refs[-3:]
+    outs = refs[sources + 3 : -4]
+    diff, new, gathered, spread = refs[-4:]
     walkers = gathered.shape[0]
     for w in range(walkers):
         gathered[w] = points[w][...] if sources > 1 else points[0][w, 0:8]
@@ -286,26 +282,27 @@
 
     def one(w, carry):
         column = jnp.transpose(gathered[w])
-        xs = [column[0 : 6 * count, a : a + 1] for a in range(3)]
+        for a in range(3):
+            spread[a] = jnp.broadcast_to(column[0 : 6 * count, a : a + 1], (6 * count, step))
         row_d = pl.multiple_of(w * (3 * count), count)
         row_n = pl.multiple_of(w * (2 * count), count)
         for at in range(0, waves, step):
             ks = [wave_ref[a : a + 1, at : at + step] * (0.5 / math.pi) for a in range(3)]
-            turn = xs[0] * ks[0] + xs[1] * ks[1] + xs[2] * ks[2]
-            r = turn - jnp.floor(turn + 0.5)
-            u = r * r
-            s = r * horner(SIN_HALF, u)
-            c = horner(COS_HALF, u)
-            for value, base in ((1.0 - s * s, 0), (s * c, waves)):
-                where = slice(base + at, base + at + step)
-                kept = value.astype(BF16)
-                wide = kept.astype(F32)
-                part = [wide[i * count : (i + 1) * count] for i in range(6)]
-                diff[pl.ds(row_d, count), where] = (part[3] - part[2]).astype(BF16)
-                diff[pl.ds(row_d + count, count), where] = (part[5] - part[4]).astype(BF16)
-                diff[pl.ds(row_d + 2 * count, count), where] = (part[1] - part[0]).astype(BF16)
-                new[pl.ds(row_n, count), where] = kept[5 * count : 6 * count]
-                new[pl.ds(row_n + count, count), where] = kept[count : 2 * count]
+            for pair, diff_at, new_at in ((0, 2, 1), (1, 0, None), (2, 1, 0)):
+                rows = slice(2 * pair * count, 2 * (pair + 1) * count)
+                turn = spread[0, rows] * ks[0] + spread[1, rows] * ks[1] + spread[2, rows] * ks[2]
+                r = turn - jnp.floor(turn + 0.5)
+                u = r * r
+                s = r * horner(SIN_HALF, u)
+                c = horner(COS_HALF, u)
+                for value, base in ((1.0 - s * s, 0), (s * c, waves)):
+                    where = slice(base + at, base + at + step)
+                    kept = value.astype(BF16)
+                    wide = kept.astype(F32)
+                    change = (wide[count:] - wide[:count]).astype(BF16)
+                    diff[pl.ds(row_d + diff_at * count, count), where] = change
+                    if new_at is not None:
+                        new[pl.ds(row_n + new_at * count, count), where] = kept[count:]
         return carry
 
     lax.fori_loop(0, walkers, one, 0)
@@ -411,9 +408,40 @@
         out_ref[chunk * depth : (chunk + 1) * depth] = found.astype(BF16)
 
 
-def first_kernel(count, sources, me_ref, *refs):
+def pick_from(number_ref, electrons):
+    return (iota((electrons, LANES), 0) == number_ref[...]).astype(F32).astype(BF16)
+
+
+def chunk_at(plan, role, slot):
+    chunk = jnp.int32(plan[0][slot][0])
+    for which in range(1, len(plan)):
+        chunk = jnp.where(role == which, plan[which][slot][0], chunk)
+    return chunk
+
+
+def load_slots(plan, slots, role, inputs, parent, sem):
+    for slot in slots:
+        for which in range(len(plan)):
+            load = pltpu.make_async_copy(
+                inputs[plan[which][slot][1]], parent.at[slot], sem.at[slot]
+            )
+            pl.when(role == which)(load.start)
+
+
+def wait_slots(slots, inputs, parent, sem):
+    for slot in slots:
+        pltpu.make_async_copy(inputs[0], parent.at[slot], sem.at[slot]).wait()
+
+
+def middle_kernel(count, sources, plan, me_ref, role_ref, number_ref, *refs):
     values = refs[:sources]
-    columns, drift_ref, lap_ref, later_ref, vals = refs[sources:]
+    own_columns = refs[sources]
+    inputs = refs[sources + 1 : -9]
+    drift_ref, lap_ref, later_ref, columns_ref, products_ref, total_ref = refs[-9:-3]
+    vals, parent, sem = refs[-3:]
+    slots, depth, electrons = parent.shape
+    role = role_ref[0]
+    load_slots(plan, range(slots), role, inputs, parent, sem)
     rows = later_ref.shape[0]
     if sources > 1:
         width = values[0].shape[1]
@@ -427,59 +455,26 @@
             where = slice(piece * width, (piece + 1) * width)
             later_ref[:, where] = values[0][piece, 0:rows]
             vals[:, where] = values[0][piece, rows:]
-    products = dot(vals[...], columns[...])
-    ratio, inverse, _ = ratio_of(products, count)
-    sums = moved_sums(products, ratio, inverse, count)
-    for a in range(3):
-        drift_ref[a] = sums[:, a * count : (a + 1) * count]
-    lap_ref[0] = sums[:, 3 * count : 4 * count]
-
-
-def pick_from(number_ref, electrons):
-    return (iota((electrons, LANES), 0) == number_ref[...]).astype(F32).astype(BF16)
-
-
-def chunk_at(plan, role, slot):
-    chunk = jnp.int32(plan[0][slot][0])
-    for which in range(1, len(plan)):
-        chunk = jnp.where(role == which, plan[which][slot][0], chunk)
-    return chunk
-
-
-def load_slots(plan, slots, role, inputs, parent, sem):
-    for slot in slots:
-        for which in range(len(plan)):
-            load = pltpu.make_async_copy(
-                inputs[plan[which][slot][1]], parent.at[slot], sem.at[slot]
-            )
-            pl.when(role == which)(load.start)
-
-
-def wait_slots(slots, inputs, parent, sem):
-    for slot in slots:
-        pltpu.make_async_copy(inputs[0], parent.at[slot], sem.at[slot]).wait()
-
-
-def early_kernel(count, plan, role_ref, number_ref, later_ref, *refs):
-    inputs = refs[:-5]
-    columns_ref, products_ref, total_ref, parent, sem = refs[-5:]
-    slots, depth, electrons = parent.shape
-    role = role_ref[0]
-    load_slots(plan, range(slots), role, inputs, parent, sem)
     pick = pick_from(number_ref, electrons)
     wait_slots(range(slots), inputs, parent, sem)
+    own = dot(vals[...], own_columns[...])
     products, total = None, None
     for slot in range(slots):
         columns = dot(parent[slot], pick).astype(BF16)
         columns_ref[slot] = columns
         at = pl.multiple_of(chunk_at(plan, role, slot) * depth, depth)
-        rows = later_ref[:, pl.ds(at, depth)]
-        part = dot(rows, columns)
-        more = dot(rows[0 : 2 * count], parent[slot])
-        products = part if slot == 0 else products + part
+        part = later_ref[:, pl.ds(at, depth)]
+        product = dot(part, columns)
+        more = dot(part[0 : 2 * count], parent[slot])
+        products = product if slot == 0 else products + product
         total = more if slot == 0 else total + more
     products_ref[...] = products
     total_ref[...] = total
+    ratio, inverse, _ = ratio_of(own, count)
+    sums = moved_sums(own, ratio, inverse, count)
+    for a in range(3):
+        drift_ref[a] = sums[:, a * count : (a + 1) * count]
+    lap_ref[0] = sums[:, 3 * count : 4 * count]
 
 
 def finish_kernel(
@@ -585,6 +580,10 @@
     others = n_grp - 1
     chunks = 4
 
+    apart = distance(n_grp, lax.axis_index("grp"), donor[0])
+    role = jnp.where(take[0] == 1, apart, 0).astype(jnp.int32).reshape(1)
+    apart = apart.astype(jnp.int32).reshape(1)
+
     record, tiled, disp = call(
         functools.partial(start_kernel, count),
         (
@@ -642,18 +641,16 @@
     few = is_power(n_orb) and local % LANES == 0
     direct = few and DIRECT_POINTS
     sources = n_orb if direct else 1
-    points, weight, number, role, apart = call(
+    points, weight, number = call(
         functools.partial(points_kernel, count, others),
         (
             shape((8, LANES) if direct else (n_orb, ROWS, LANES), F32),
             shape((1, LANES), F32),
             shape((1, LANES), jnp.int32),
-            shape((1,), jnp.int32),
-            shape((1,), jnp.int32),
         ),
-        [VM, VM] + [VM] * (others + 3) + [ANY],
-        (VM, VM, VM, SM, SM),
-    )(donor.reshape(1, 1), take.reshape(1, 1), record, *records, tiled, disp, token_0)
+        [SM] + [VM] * (others + 3) + [ANY],
+        (VM, VM, VM),
+    )(role, record, *records, tiled, disp, token_0)
     if direct:
         points = [points] + [lax.ppermute(points, "orb", pairs(n_orb, s)) for s in range(1, n_orb)]
     else:
@@ -695,9 +692,9 @@
                 [SM] + [ANY] * (4 + len(first)),
                 (ANY, ANY, VM),
                 scratch=[
-                    pltpu.VMEM((2, depth, electrons), BF16),
-                    pltpu.SemaphoreType.DMA((2,)),
-                    pltpu.SemaphoreType.DMA((2,)),
+                    pltpu.VMEM((4, depth // 2, electrons), BF16),
+                    pltpu.SemaphoreType.DMA((4,)),
+                    pltpu.SemaphoreType.DMA((4,)),
                 ],
                 aliases={3: 0, 4: 1},
                 vmem=2,
@@ -739,6 +736,7 @@
             pltpu.VMEM((block * 3 * count, plane), BF16),
             pltpu.VMEM((block * 2 * count, plane), BF16),
             pltpu.VMEM((block, 8, LANES), F32),
+            pltpu.VMEM((3, 6 * count, LANES), F32),
         ],
         compiler_params=pltpu.CompilerParams(vmem_limit_bytes=8 * MIB),
         cost_estimate=pl.CostEstimate(
@@ -788,39 +786,29 @@
     )(*in_hbm(inverse), tiled, token_2)
 
     here = lax.axis_index("orb").astype(jnp.int32).reshape(1)
-    drift, laplacian, later = call(
-        functools.partial(first_kernel, count, targets),
+    early = 2
+    work = 2 * electrons * 2 * count
+    drift, laplacian, later, early_columns, products, total = call(
+        functools.partial(middle_kernel, count, targets, plan),
         (
             shape((3, 1, count), F32),
             shape((1, 1, count), F32),
             shape((6 * count, electrons), BF16),
-        ),
-        [SM] + [VM] * (targets + 1),
-        (VM, VM, VM),
-        scratch=[pltpu.VMEM((5 * count, electrons), BF16)],
-        flops=2 * electrons * 11 * count * LANES,
-        moved=44 * count * electrons,
-    )(here, *values, columns)
-
-    early = 2
-    work = 2 * electrons * 2 * count
-    early_columns, products, total = call(
-        functools.partial(early_kernel, count, plan),
-        (
             shape((early, depth, LANES), BF16),
             shape((6 * count, LANES), F32),
             shape((2 * count, electrons), F32),
         ),
-        [SM, VM, VM] + [ANY] * settled,
-        (VM, VM, VM),
+        [SM, SM, VM] + [VM] * (targets + 1) + [ANY] * settled,
+        (VM,) * 6,
         scratch=[
+            pltpu.VMEM((5 * count, electrons), BF16),
             pltpu.VMEM((early, depth, electrons), BF16),
             pltpu.SemaphoreType.DMA((early,)),
         ],
         flops=early * depth * work,
-        moved=2 * early * depth * electrons,
+        moved=2 * early * depth * electrons + 44 * count * electrons,
         vmem=8,
-    )(role, number, later, *in_hbm(*own), *arrays[chunks:settled])
+    )(here, role, number, *values, columns, *in_hbm(*own), *arrays[chunks:settled])
 
     updated, drift, laplacian, new_weight = call(
         functools.partial(finish_kernel, count, plan),

time: 67.3 us -> 64.8 us (0.963)
  Pallas kernels: 34.9 us -> 27.9 us
  starting transfers between devices: 16.2 us -> 22.4 us
  waiting for transfers between devices: 13 us -> 10.8 us
    pallas_call x2, Pallas kernels: 5.38 us -> 0.15 us  [relay(): call(relay_kernel, (kept, kept, token), [SM] + [ANY] * (4 + len(first)),...]
    ppermute x3, starting transfers between devices: 0.79 us -> 5.69 us  [per_device(): send_x = lambda block: lax.ppermute(block, 'grp', pairs(n_grp, 1))]
    ppermute x3, starting transfers between devices: 1.66 us -> 3.82 us  [per_device(): send_y = lambda block: lax.ppermute(block, 'grp', pairs(n_grp, 2))]
    pallas_call x2 -> x1, Pallas kernels: 3.97 us -> 2.89 us  [per_device(): call(functools.partial(middle_kernel, count, targets, plan), (shape((3, 1...]
    ppermute x3, waiting for transfers between devices: 4.26 us -> 3.22 us  [per_device(): send_x = lambda block: lax.ppermute(block, 'grp', pairs(n_grp, 1))]
    all_to_all x1, starting transfers between devices: 4.25 us -> 3.44 us  [per_device(): lax.all_to_all(values, 'orb', split_axis=0, concat_axis=0, tiled=True)]
  transfers between devices with their start and end apart: 11 -> 11, of which waited for: 8 -> 8; matrix products, arithmetic and copies ran while one was open for 0% -> 0% of each run, Pallas kernels for 35% -> 30%
where the time goes in v12:
time: 64.8 us; the launch traced here: 63.8 us
  Pallas kernels  27.9 us (43%)
  starting transfers between devices  22.4 us (35%)
  waiting for transfers between devices  10.8 us (17%)
  between operations  2.67 us (4%)
    pallas_call x1, Pallas kernels, per_device(): call(functools.partial(finish_kernel, count, plan), (shape((electrons, el...  6.73 us
    pallas_call x1, Pallas kernels, per_device(): pl.pallas_call(functools.partial(evaluate_kernel, count, sources, targets...  6.44 us
    ppermute x3, starting transfers between devices, per_device(): send_x = lambda block: lax.ppermute(block, 'grp', pairs(n_grp, 1))  5.69 us
    all_to_all x1, starting transfers between devices, per_device(): lax.all_to_all(points, 'orb', split_axis=0, concat_axis=0, tiled=True)  4.88 us
    ppermute x3, starting transfers between devices, per_device(): lax.ppermute(record, 'grp', pairs(n_grp, s))  4.6 us
    pallas_call x1, Pallas kernels, per_device(): call(functools.partial(prepare_kernel, middle), (shape((plane, 5 * width)...  4.05 us
    ppermute x3, starting transfers between devices, per_device(): send_y = lambda block: lax.ppermute(block, 'grp', pairs(n_grp, 2))  3.82 us
    all_to_all x1, starting transfers between devices, per_device(): lax.all_to_all(values, 'orb', split_axis=0, concat_axis=0, tiled=True)  3.44 us
  transfers between devices with their start and end apart: 11, of which 8 were waited for; matrix products, arithmetic and copies ran while one was open for 0% of the time, Pallas kernels for 30%

profile of v12, /device:TPU:0, one launch (start us, length us, event | category | flops | bytes accessed | tf_op | source)
XLA Modules:
  0.0 63.8 jit_solution(476011840172091811)
XLA Ops:
  1.3 1.7 %shard_map.120 = (f32[8,1024]{1,0:T(8,128)S(1)}, s32[2,128]{1,0:T(2,128)S(1)}, f32[2,8,128]{2,1,0:T(8,128)S(1)}) custom-call(f32[3,1,1024]{2,1,0:T(1,128)} %bitcast.12, s32[2,1,16]{2,1,0:T(1,128)} %moved_hbm.1, f32[6,1,16]{2,1,0:T(1,128)} %bitcast.13, f32[1]{0:T(128)S(6)} %copy.27.weight_ref), custom_call_target="tpu_custom_call" | custom-call | tf_op jit(solution)/shard_map/pallas_call | solution.py:587
  3.0 4.0 %collective-permute-start.2 = (f32[8,1024]{1,0:T(8,128)S(1)}, f32[8,1024]{1,0:T(8,128)S(1)}, u32[]{:S(2)}, u32[]{:S(2)}) collective-permute-start(f32[8,1024]{1,0:T(8,128)S(1)} %get-tuple-element.34.after_ref.refs_0_), channel_id=1, source_target_pairs={{0,24},{8,16},{16,8},{24,0},{1,25},{9,17},{17,9},{25,1},{2,26},{10... | collective-permute-start | bytes 98312 | tf_op jit(solution)/shard_map/ppermute | solution.py:610
  7.0 0.5 collective-permute-start.1
  7.5 0.1 collective-permute-start
  7.6 2.4 %shard_map.121 = (bf16[256,1024]{1,0:T(8,128)(2,1)}, bf16[256,1024]{1,0:T(8,128)(2,1)}) custom-call(f32[1,1024,1024]{2,1,0:T(8,128)} %inverse_hbm.7, f32[8,1024]{1,0:T(8,128)S(1)} %get-tuple-element.34.after_ref.refs_0_), custom_call_target="tpu_custom_call" | custom-call | bytes 3145728 | tf_op jit(solution)/shard_map/pallas_call | solution.py:618
  10.0 0.0 collective-permute-done.2.refs_4_.refs_3_
  10.0 0.8 %collective-permute-done.1.refs_3_.refs_2_ = f32[8,1024]{1,0:T(8,128)S(1)} collective-permute-done((f32[8,1024]{1,0:T(8,128)S(1)}, f32[8,1024]{1,0:T(8,128)S(1)}, u32[]{:S(2)}, u32[]{:S(2)}) %collective-permute-start.1) | collective-permute-done | bytes 32800 | tf_op jit(solution)/shard_map/ppermute | solution.py:610
  10.9 0.5 collective-permute-done.refs_2_.refs_1_
  11.4 1.5 %collective-permute-start.3 = (bf16[256,1024]{1,0:T(8,128)(2,1)}, bf16[256,1024]{1,0:T(8,128)(2,1)S(1)}, u32[]{:S(2)}, u32[]{:S(2)}) collective-permute-start(bf16[256,1024]{1,0:T(8,128)(2,1)} %get-tuple-element.46.refs_5_.refs_3_), channel_id=1, source_target_pairs={{0,16},{8,24},{16,0},{24,8},{1,17},{9,25},{17,1},{25,9},{2,18},{10... | collective-permute-start | bytes 1572872 | tf_op jit(solution)/shard_map/ppermute | solution.py:686
  12.9 0.6 collective-permute-start.4
  14.8 1.0 %shard_map.123 = (f32[8,16,128]{2,1,0:T(8,128)}, f32[1,128]{1,0:T(1,128)S(1)}, s32[1,128]{1,0:T(1,128)S(1)}) custom-call(s32[1]{0:T(128)} %bitcast.2.role_ref, f32[8,1024]{1,0:T(8,128)S(1)} %get-tuple-element.34.after_ref.refs_0_, f32[8,1024]{1,0:T(8,128)S(1)} %collective-permute-done.refs_2_.refs_1_, f32[8,1024]{1,0:T(8,128)S(1)} %collective-permute-done.1.refs_3_.refs_2_, ...), custom_call_target="tpu_custom_call" | custom-call | tf_op jit(solution)/shard_map/pallas_call | solution.py:644
  15.8 4.9 %all-to-all-start = ((f32[8,16,128]{2,1,0:T(8,128)}), f32[8,16,128]{2,1,0:T(8,128)S(1)}, u32[]{:S(2)}, u32[]{:S(2)}) async-start(f32[8,16,128]{2,1,0:T(8,128)} %get-tuple-element.41), calls=%async_computation | async-start | bytes 131072 | tf_op jit(solution)/shard_map/all_to_all | solution.py:657
  20.7 0.0 copy-start
  20.7 4.1 %shard_map.124 = (bf16[2048,640]{1,0:T(8,128)(2,1)S(1)}, bf16[256,1024]{1,0:T(8,128)(2,1)}, bf16[256,1024]{1,0:T(8,128)(2,1)}) custom-call(bf16[2048,128]{1,0:T(8,128)(2,1)} %coeff_hbm.1, f32[3,1024]{1,0:T(4,128)} %refs_1_.1, f32[1,1024,1024]{2,1,0:T(8,128)} %inverse_hbm.7, f32[1,128]{1,0:T(1,128)S(1)} %get-tuple-element.42.after_ref.weight_ref), custom_call_target="tpu_custom_call" | custom-call | flops 2097152 | bytes 5767168 | tf_op jit(solution)/shard_map/pallas_call | solution.py:661
  24.8 1.9 %all-to-all-done.refs_1_.refs_0_ = f32[8,16,128]{2,1,0:T(8,128)S(1)} async-done(((f32[8,16,128]{2,1,0:T(8,128)}), f32[8,16,128]{2,1,0:T(8,128)S(1)}, u32[]{:S(2)}, u32[]{:S(2)}) %all-to-all-start) | async-done | bytes 65568 | tf_op jit(solution)/shard_map/all_to_all | solution.py:657
  26.6 0.0 collective-permute-done.3.got_a
  26.6 0.0 collective-permute-done.4.got_b
  26.7 0.1 shard_map.125
  26.7 0.6 collective-permute-start.5
  27.3 2.9 %collective-permute-start.6 = (bf16[256,1024]{1,0:T(8,128)(2,1)S(1)}, bf16[256,1024]{1,0:T(8,128)(2,1)}, u32[]{:S(2)}, u32[]{:S(2)}) collective-permute-start(bf16[256,1024]{1,0:T(8,128)(2,1)S(1)} %get-tuple-element.50.refs_8_.refs_6_), channel_id=1, source_target_pairs={{0,8},{8,0},{16,24},{24,16},{1,9},{9,1},{17,25},{25,17},{2,10},{10... | collective-permute-start | bytes 1572872 | tf_op jit(solution)/shard_map/ppermute | solution.py:685
  30.2 0.0 copy-done
  30.2 6.4 %shard_map.126.refs_0_ = bf16[8,176,128]{2,1,0:T(8,128)(2,1)} custom-call(f32[8,16,128]{2,1,0:T(8,128)S(1)} %all-to-all-done.refs_1_.refs_0_, f32[3,1024]{1,0:T(4,128)S(1)} %copy-done, bf16[2048,640]{1,0:T(8,128)(2,1)S(1)} %get-tuple-element.43.refs_0_.refs_2_, f32[8,128]{1,0:T(8,128)S(1)} %get-tuple-element.48.refs_3_), custom_call_target="tpu_custom_call" | custom-call | flops 738197504 | bytes 3145728 | tf_op jit(solution)/shard_map/pallas_call | solution.py:729
  36.6 3.4 %all-to-all-start.1 = ((bf16[8,176,128]{2,1,0:T(8,128)(2,1)}), bf16[8,176,128]{2,1,0:T(8,128)(2,1)S(1)}, u32[]{:S(2)}, u32[]{:S(2)}) async-start(bf16[8,176,128]{2,1,0:T(8,128)(2,1)} %shard_map.126.refs_0_), calls=%async_computation.1 | async-start | bytes 720896 | tf_op jit(solution)/shard_map/all_to_all | solution.py:755
  40.1 0.5 collective-permute-done.5.got_a
  40.6 1.4 %collective-permute-done.6.got_b = bf16[256,1024]{1,0:T(8,128)(2,1)} collective-permute-done((bf16[256,1024]{1,0:T(8,128)(2,1)S(1)}, bf16[256,1024]{1,0:T(8,128)(2,1)}, u32[]{:S(2)}, u32[]{:S(2)}) %collective-permute-start.6) | collective-permute-done | bytes 524320 | tf_op jit(solution)/shard_map/ppermute | solution.py:685
  42.0 0.1 shard_map.127
  42.1 1.7 %collective-permute-start.8 = (bf16[256,1024]{1,0:T(8,128)(2,1)}, bf16[256,1024]{1,0:T(8,128)(2,1)S(1)}, u32[]{:S(2)}, u32[]{:S(2)}) collective-permute-start(bf16[256,1024]{1,0:T(8,128)(2,1)} %get-tuple-element.52.refs_7_.refs_5_), channel_id=1, source_target_pairs={{0,16},{8,24},{16,0},{24,8},{1,17},{9,25},{17,1},{25,9},{2,18},{10... | collective-permute-start | bytes 1572872 | tf_op jit(solution)/shard_map/ppermute | solution.py:686
  43.8 2.2 %collective-permute-start.7 = (bf16[256,1024]{1,0:T(8,128)(2,1)}, bf16[256,1024]{1,0:T(8,128)(2,1)S(1)}, u32[]{:S(2)}, u32[]{:S(2)}) collective-permute-start(bf16[256,1024]{1,0:T(8,128)(2,1)} %get-tuple-element.53.refs_9_.refs_7_), channel_id=1, source_target_pairs={{0,8},{8,0},{16,24},{24,16},{1,9},{9,1},{17,25},{25,17},{2,10},{10... | collective-permute-start | bytes 1572872 | tf_op jit(solution)/shard_map/ppermute | solution.py:685
  46.0 2.5 %shard_map.128.refs_1_ = bf16[1024,128]{1,0:T(8,128)(2,1)S(1)} custom-call(f32[1,1024,1024]{2,1,0:T(8,128)} %inverse_hbm.7, s32[2,128]{1,0:T(2,128)S(1)} %get-tuple-element.35.refs_4_.moved_ref, f32[8,128]{1,0:T(8,128)S(1)} %get-tuple-element.51.after_ref), custom_call_target="tpu_custom_call" | custom-call | flops 268435456 | bytes 4194304 | tf_op jit(solution)/shard_map/pallas_call | solution.py:774
  48.5 3.3 %all-to-all-done.1.refs_0_ = bf16[8,176,128]{2,1,0:T(8,128)(2,1)S(1)} async-done(((bf16[8,176,128]{2,1,0:T(8,128)(2,1)}), bf16[8,176,128]{2,1,0:T(8,128)(2,1)S(1)}, u32[]{:S(2)}, u32[]{:S(2)}) %all-to-all-start.1) | async-done | bytes 360480 | tf_op jit(solution)/shard_map/all_to_all | solution.py:755
  51.8 2.9 %shard_map.129 = (f32[3,1,16]{2,1,0:T(1,128)S(1)}, f32[1,1,16]{2,1,0:T(1,128)S(1)}, bf16[96,1024]{1,0:T(8,128)(2,1)S(1)}, bf16[2,256,128]{2,1,0:T(8,128)(2,1)S(1...) custom-call(s32[1]{0:T(128)} %bitcast.5.me_ref, s32[1]{0:T(128)} %bitcast.2.role_ref, ...), custom_call_target="tpu_custom_call" | custom-call | flops 33554432 | bytes 1769472 | tf_op jit(solution)/shard_map/pallas_call | solution.py:791
  54.7 0.6 collective-permute-done.8.refs_9_
  55.3 1.8 %collective-permute-done.7.refs_8_ = bf16[256,1024]{1,0:T(8,128)(2,1)S(1)} collective-permute-done((bf16[256,1024]{1,0:T(8,128)(2,1)}, bf16[256,1024]{1,0:T(8,128)(2,1)S(1)}, u32[]{:S(2)}, u32[]{:S(2)}) %collective-permute-start.7) | collective-permute-done | bytes 524320 | tf_op jit(solution)/shard_map/ppermute | solution.py:685
  57.1 6.7 %shard_map.130 = (f32[1024,1024]{1,0:T(8,128)}, f32[6,1,16]{2,1,0:T(1,128)}, f32[2,1,16]{2,1,0:T(1,128)}, f32[1,128]{1,0:T(1,128)}) custom-call(s32[1]{0:T(128)} %bitcast.2.role_ref, s32[1,128]{1,0:T(1,128)S(1)} %get-tuple-element.40.number_ref, bf16[96,1024]{1,0:T(8,128)(2,1)S(1)} %get-tuple-element.54.later_ref, ...), custom_call_target="tpu_custom_call" | custom-call | flops 134217728 | bytes 6291456 | tf_op jit(solution)/shard_map/pallas_call | solution.py:813
  (1 shorter events, 0.0 us)
Async XLA Ops:
  3.0 7.0 %collective-permute-start.2 = (f32[8,1024]{1,0:T(8,128)S(1)}, f32[8,1024]{1,0:T(8,128)S(1)}, u32[]{:S(2)}, u32[]{:S(2)}) collective-permute-start(f32[8,1024]{1,0:T(8,128)S(1)} %get-tuple-element.34.after_ref.refs_0_), channel_id=1, source_target_pairs={{0,24},{8,16},{16,8},{24,0},{1,25},{9,17},{17,9},{25,1},{2,26},{10... | collective-permute-start | bytes 98312 | tf_op jit(solution)/shard_map/ppermute | solution.py:610
  7.0 3.9 %collective-permute-start.1 = (f32[8,1024]{1,0:T(8,128)S(1)}, f32[8,1024]{1,0:T(8,128)S(1)}, u32[]{:S(2)}, u32[]{:S(2)}) collective-permute-start(f32[8,1024]{1,0:T(8,128)S(1)} %get-tuple-element.34.after_ref.refs_0_), channel_id=1, source_target_pairs={{0,16},{8,24},{16,0},{24,8},{1,17},{9,25},{17,1},{25,9},{2,18},{10... | collective-permute-start | bytes 98312 | tf_op jit(solution)/shard_map/ppermute | solution.py:610
  7.5 3.9 %collective-permute-start = (f32[8,1024]{1,0:T(8,128)S(1)}, f32[8,1024]{1,0:T(8,128)S(1)}, u32[]{:S(2)}, u32[]{:S(2)}) collective-permute-start(f32[8,1024]{1,0:T(8,128)S(1)} %get-tuple-element.34.after_ref.refs_0_), channel_id=1, source_target_pairs={{0,8},{8,0},{16,24},{24,16},{1,9},{9,1},{17,25},{25,17},{2,10},{10... | collective-permute-start | bytes 98312 | tf_op jit(solution)/shard_map/ppermute | solution.py:610
  11.4 15.3 %collective-permute-start.3 = (bf16[256,1024]{1,0:T(8,128)(2,1)}, bf16[256,1024]{1,0:T(8,128)(2,1)S(1)}, u32[]{:S(2)}, u32[]{:S(2)}) collective-permute-start(bf16[256,1024]{1,0:T(8,128)(2,1)} %get-tuple-element.46.refs_5_.refs_3_), channel_id=1, source_target_pairs={{0,16},{8,24},{16,0},{24,8},{1,17},{9,25},{17,1},{25,9},{2,18},{10... | collective-permute-start | bytes 1572872 | tf_op jit(solution)/shard_map/ppermute | solution.py:686
  12.9 13.7 %collective-permute-start.4 = (bf16[256,1024]{1,0:T(8,128)(2,1)}, bf16[256,1024]{1,0:T(8,128)(2,1)}, u32[]{:S(2)}, u32[]{:S(2)}) collective-permute-start(bf16[256,1024]{1,0:T(8,128)(2,1)} %get-tuple-element.47.refs_2_.refs_0_), channel_id=1, source_target_pairs={{0,8},{8,0},{16,24},{24,16},{1,9},{9,1},{17,25},{25,17},{2,10},{10... | collective-permute-start | bytes 1572872 | tf_op jit(solution)/shard_map/ppermute | solution.py:685
  15.8 10.8 %all-to-all-start = ((f32[8,16,128]{2,1,0:T(8,128)}), f32[8,16,128]{2,1,0:T(8,128)S(1)}, u32[]{:S(2)}, u32[]{:S(2)}) async-start(f32[8,16,128]{2,1,0:T(8,128)} %get-tuple-element.41), calls=%async_computation | async-start | bytes 131072 | tf_op jit(solution)/shard_map/all_to_all | solution.py:657
  20.7 9.4 %copy-start = (f32[3,1024]{1,0:T(4,128)S(1)}, f32[3,1024]{1,0:T(4,128)}, u32[]{:S(2)}) copy-start(f32[3,1024]{1,0:T(4,128)} %refs_1_.1) | copy-start | bytes 36868
  26.7 13.9 %collective-permute-start.5 = (bf16[256,1024]{1,0:T(8,128)(2,1)}, bf16[256,1024]{1,0:T(8,128)(2,1)}, u32[]{:S(2)}, u32[]{:S(2)}) collective-permute-start(bf16[256,1024]{1,0:T(8,128)(2,1)} %get-tuple-element.49.refs_6_.refs_4_), channel_id=1, source_target_pairs={{0,16},{8,24},{16,0},{24,8},{1,17},{9,25},{17,1},{25,9},{2,18},{10... | collective-permute-start | bytes 1572872 | tf_op jit(solution)/shard_map/ppermute | solution.py:686
  27.3 14.7 %collective-permute-start.6 = (bf16[256,1024]{1,0:T(8,128)(2,1)S(1)}, bf16[256,1024]{1,0:T(8,128)(2,1)}, u32[]{:S(2)}, u32[]{:S(2)}) collective-permute-start(bf16[256,1024]{1,0:T(8,128)(2,1)S(1)} %get-tuple-element.50.refs_8_.refs_6_), channel_id=1, source_target_pairs={{0,8},{8,0},{16,24},{24,16},{1,9},{9,1},{17,25},{25,17},{2,10},{10... | collective-permute-start | bytes 1572872 | tf_op jit(solution)/shard_map/ppermute | solution.py:685
  36.6 15.2 %all-to-all-start.1 = ((bf16[8,176,128]{2,1,0:T(8,128)(2,1)}), bf16[8,176,128]{2,1,0:T(8,128)(2,1)S(1)}, u32[]{:S(2)}, u32[]{:S(2)}) async-start(bf16[8,176,128]{2,1,0:T(8,128)(2,1)} %shard_map.126.refs_0_), calls=%async_computation.1 | async-start | bytes 720896 | tf_op jit(solution)/shard_map/all_to_all | solution.py:755
  42.1 13.2 %collective-permute-start.8 = (bf16[256,1024]{1,0:T(8,128)(2,1)}, bf16[256,1024]{1,0:T(8,128)(2,1)S(1)}, u32[]{:S(2)}, u32[]{:S(2)}) collective-permute-start(bf16[256,1024]{1,0:T(8,128)(2,1)} %get-tuple-element.52.refs_7_.refs_5_), channel_id=1, source_target_pairs={{0,16},{8,24},{16,0},{24,8},{1,17},{9,25},{17,1},{25,9},{2,18},{10... | collective-permute-start | bytes 1572872 | tf_op jit(solution)/shard_map/ppermute | solution.py:686
  43.8 13.3 %collective-permute-start.7 = (bf16[256,1024]{1,0:T(8,128)(2,1)}, bf16[256,1024]{1,0:T(8,128)(2,1)S(1)}, u32[]{:S(2)}, u32[]{:S(2)}) collective-permute-start(bf16[256,1024]{1,0:T(8,128)(2,1)} %get-tuple-element.53.refs_9_.refs_7_), channel_id=1, source_target_pairs={{0,8},{8,0},{16,24},{24,16},{1,9},{9,1},{17,25},{25,17},{2,10},{10... | collective-permute-start | bytes 1572872 | tf_op jit(solution)/shard_map/ppermute | solution.py:685

commit v13 on v12

--- a/solution.py
+++ b/solution.py
@@ -25,6 +25,17 @@
     return lax.dot_general(
         a, b, (dims, ((), ())), precision=precise if exact else None, preferred_element_type=F32
     )
+
+
+def exact_dot(a, pick, dims=((1,), (0,))):
+    high = a.astype(BF16)
+    rest = a - high.astype(F32)
+    middle = rest.astype(BF16)
+    low = (rest - middle.astype(F32)).astype(BF16)
+    rows = a.shape[0]
+    parts = jnp.concatenate([high, middle, low], 0)
+    found = dot(parts, pick, dims)
+    return (found[0:rows] + found[rows : 2 * rows]) + found[2 * rows :]
 
 
 def iota(shape, dim):
@@ -109,7 +120,7 @@
     loads[0].wait()
     tiled = jnp.concatenate([moved_ref[:, 0, :]] * copies, 1)
     tiled_ref[...] = tiled
-    pick = (iota((electrons, LANES), 0) == tiled[0:1, :]).astype(F32)
+    pick = (iota((electrons, LANES), 0) == tiled[0:1, :]).astype(F32).astype(BF16)
     block = iota((8, LANES), 1) // count
     zeros = jnp.zeros((5, LANES), F32)
     loads[1].wait()
@@ -118,11 +129,11 @@
         shift_ref[update] = jnp.concatenate([shift, zeros], 0)
     loads[2].wait()
     pos = jnp.concatenate([pos_ref[:, 0, :], jnp.zeros((5, electrons), F32)], 0)
-    old = dot(pos, pick, exact=True)
+    old = exact_dot(pos, pick)
     disp = shift_ref[0]
     points = old + jnp.where(block % 2 == 1, disp, 0.0)
     first = jnp.where(block == 0, disp, 0.0)
-    out_ref[...] = pos + dot(first, pick, ((1,), (1,)), exact=True)
+    out_ref[...] = pos + exact_dot(first, pick, ((1,), (1,)))
     out_ref[3:6, 0:LANES] = points[0:3]
     out_ref[6:7, 0:LANES] = tiled[0:1, :].astype(F32)
     out_ref[7:8, 0:LANES] = jnp.full((1, LANES), weight_ref[0], F32)
@@ -194,9 +205,9 @@
     for step in range(others):
         parent = jnp.where(role == step + 1, received[step][...], parent)
     electrons = parent.shape[1]
-    pick = (iota((electrons, LANES), 0) == moved_ref[1:2, :]).astype(F32)
+    pick = (iota((electrons, LANES), 0) == moved_ref[1:2, :]).astype(F32).astype(BF16)
     block = iota((8, LANES), 1) // count
-    old = dot(parent, pick, exact=True)
+    old = exact_dot(parent, pick)
     later = old + jnp.where(block % 2 == 1, disp_ref[1], 0.0)
     zeros = jnp.zeros((5, LANES), F32)
     mine = jnp.concatenate([own_ref[3:6, 0:LANES], zeros], 0)
@@ -248,15 +259,15 @@
         )
         load.start()
         loads.append(load)
-    wave_load.wait()
-    coeff_load.wait()
-    derive(coeff_ref, wave_ref, table_ref)
     for slot, out in enumerate(outs):
         loads[slot].wait()
         rounded[slot] = staged[slot].astype(BF16)
         store = pltpu.make_async_copy(rounded.at[slot], out, out_sem.at[slot])
         store.start()
         stores.append(store)
+    wave_load.wait()
+    coeff_load.wait()
+    derive(coeff_ref, wave_ref, table_ref)
     for store in stores:
         store.wait()
 
@@ -507,10 +518,10 @@
         for slot in range(chunks)
     ]
     load_slots(plan, list(late) + list(range(done)), role, inputs, parent, in_sem)
-    for load in own:
-        pl.when(role == 0)(load.start)
     pick = pick_from(number_ref, electrons)
     wait_slots(late, inputs, parent, in_sem)
+    for load in own[done:] + own[:done]:
+        pl.when(role == 0)(load.start)
     columns = [early_ref[slot] for slot in range(done)]
     products = products_ref[...]
     rows = []

time: 64.8 us -> 64.6 us (level)
  starting transfers between devices: 22.4 us -> 17.1 us
  waiting for transfers between devices: 10.8 us -> 14 us
  Pallas kernels: 27.9 us -> 30.4 us
    ppermute x3, starting transfers between devices: 5.69 us -> 0.78 us  [per_device(): send_x = lambda block: lax.ppermute(block, 'grp', pairs(n_grp, 1))]
    pallas_call x2, Pallas kernels: 0.15 us -> 3.95 us  [relay(): call(relay_kernel, (kept, kept, token), [SM] + [ANY] * (4 + len(first)),...]
    ppermute x3, starting transfers between devices: 3.82 us -> 1.66 us  [per_device(): send_y = lambda block: lax.ppermute(block, 'grp', pairs(n_grp, 2))]
    all_to_all x1, waiting for transfers between devices: 3.29 us -> 5.14 us  [per_device(): lax.all_to_all(values, 'orb', split_axis=0, concat_axis=0, tiled=True)]
    all_to_all x1, starting transfers between devices: 3.44 us -> 5.22 us  [per_device(): lax.all_to_all(values, 'orb', split_axis=0, concat_axis=0, tiled=True)]
    ppermute x3, waiting for transfers between devices: 1.12 us -> 2.3 us  [per_device(): send_y = lambda block: lax.ppermute(block, 'grp', pairs(n_grp, 2))]
    all_to_all x1, waiting for transfers between devices: 1.85 us -> 2.51 us  [per_device(): lax.all_to_all(points, 'orb', split_axis=0, concat_axis=0, tiled=True)]
    pallas_call x1, Pallas kernels: 4.05 us -> 3.4 us  [per_device(): call(functools.partial(prepare_kernel, middle), (shape((plane, 5 * width)...]
  transfers between devices with their start and end apart: 11 -> 11, of which waited for: 8 -> 8; matrix products, arithmetic and copies ran while one was open for 0% -> 0% of each run, Pallas kernels for 30% -> 32%
where the time goes in v13:
time: 64.6 us; the launch traced here: 64.2 us
  Pallas kernels  30.4 us (47%)
  starting transfers between devices  17.1 us (26%)
  waiting for transfers between devices  14 us (22%)
  between operations  2.7 us (4%)
    pallas_call x1, Pallas kernels, per_device(): call(functools.partial(finish_kernel, count, plan), (shape((electrons, el...  6.75 us
    pallas_call x1, Pallas kernels, per_device(): pl.pallas_call(functools.partial(evaluate_kernel, count, sources, targets...  6.44 us
    all_to_all x1, starting transfers between devices, per_device(): lax.all_to_all(values, 'orb', split_axis=0, concat_axis=0, tiled=True)  5.22 us
    all_to_all x1, waiting for transfers between devices, per_device(): lax.all_to_all(values, 'orb', split_axis=0, concat_axis=0, tiled=True)  5.14 us
    all_to_all x1, starting transfers between devices, per_device(): lax.all_to_all(points, 'orb', split_axis=0, concat_axis=0, tiled=True)  4.88 us
    ppermute x3, starting transfers between devices, per_device(): lax.ppermute(record, 'grp', pairs(n_grp, s))  4.6 us
    pallas_call x2, Pallas kernels, relay(): call(relay_kernel, (kept, kept, token), [SM] + [ANY] * (4 + len(first)),...  3.95 us
    pallas_call x1, Pallas kernels, per_device(): call(functools.partial(prepare_kernel, middle), (shape((plane, 5 * width)...  3.4 us
  transfers between devices with their start and end apart: 11, of which 8 were waited for; matrix products, arithmetic and copies ran while one was open for 0% of the time, Pallas kernels for 32%

profile of v13, /device:TPU:0, one launch (start us, length us, event | category | flops | bytes accessed | tf_op | source)
XLA Modules:
  0.0 64.2 jit_solution(15029408156765689967)
XLA Ops:
  1.3 1.2 %shard_map.120 = (f32[8,1024]{1,0:T(8,128)S(1)}, s32[2,128]{1,0:T(2,128)S(1)}, f32[2,8,128]{2,1,0:T(8,128)S(1)}) custom-call(f32[3,1,1024]{2,1,0:T(1,128)} %bitcast.12, s32[2,1,16]{2,1,0:T(1,128)} %moved_hbm.1, f32[6,1,16]{2,1,0:T(1,128)} %bitcast.13, f32[1]{0:T(128)S(6)} %copy.27.weight_ref), custom_call_target="tpu_custom_call" | custom-call | tf_op jit(solution)/shard_map/pallas_call | solution.py:598
  2.5 4.0 %collective-permute-start.2 = (f32[8,1024]{1,0:T(8,128)S(1)}, f32[8,1024]{1,0:T(8,128)S(1)}, u32[]{:S(2)}, u32[]{:S(2)}) collective-permute-start(f32[8,1024]{1,0:T(8,128)S(1)} %get-tuple-element.34.after_ref.refs_0_), channel_id=1, source_target_pairs={{0,24},{8,16},{16,8},{24,0},{1,25},{9,17},{17,9},{25,1},{2,26},{10... | collective-permute-start | bytes 98312 | tf_op jit(solution)/shard_map/ppermute | solution.py:621
  6.4 0.5 collective-permute-start.1
  6.9 0.1 collective-permute-start
  7.1 2.4 %shard_map.121 = (bf16[256,1024]{1,0:T(8,128)(2,1)}, bf16[256,1024]{1,0:T(8,128)(2,1)}) custom-call(f32[1,1024,1024]{2,1,0:T(8,128)} %inverse_hbm.7, f32[8,1024]{1,0:T(8,128)S(1)} %get-tuple-element.34.after_ref.refs_0_), custom_call_target="tpu_custom_call" | custom-call | bytes 3145728 | tf_op jit(solution)/shard_map/pallas_call | solution.py:629
  9.5 0.0 collective-permute-done.2.refs_4_.refs_3_
  9.5 0.8 %collective-permute-done.1.refs_3_.refs_2_ = f32[8,1024]{1,0:T(8,128)S(1)} collective-permute-done((f32[8,1024]{1,0:T(8,128)S(1)}, f32[8,1024]{1,0:T(8,128)S(1)}, u32[]{:S(2)}, u32[]{:S(2)}) %collective-permute-start.1) | collective-permute-done | bytes 32800 | tf_op jit(solution)/shard_map/ppermute | solution.py:621
  10.4 0.5 collective-permute-done.refs_2_.refs_1_
  10.9 1.5 %collective-permute-start.3 = (bf16[256,1024]{1,0:T(8,128)(2,1)}, bf16[256,1024]{1,0:T(8,128)(2,1)S(1)}, u32[]{:S(2)}, u32[]{:S(2)}) collective-permute-start(bf16[256,1024]{1,0:T(8,128)(2,1)} %get-tuple-element.46.refs_5_.refs_3_), channel_id=1, source_target_pairs={{0,16},{8,24},{16,0},{24,8},{1,17},{9,25},{17,1},{25,9},{2,18},{10... | collective-permute-start | bytes 1572872 | tf_op jit(solution)/shard_map/ppermute | solution.py:697
  12.4 0.6 collective-permute-start.4
  14.3 0.8 %shard_map.123 = (f32[8,16,128]{2,1,0:T(8,128)}, f32[1,128]{1,0:T(1,128)S(1)}, s32[1,128]{1,0:T(1,128)S(1)}) custom-call(s32[1]{0:T(128)} %bitcast.2.role_ref, f32[8,1024]{1,0:T(8,128)S(1)} %get-tuple-element.34.after_ref.refs_0_, f32[8,1024]{1,0:T(8,128)S(1)} %collective-permute-done.refs_2_.refs_1_, f32[8,1024]{1,0:T(8,128)S(1)} %collective-permute-done.1.refs_3_.refs_2_, ...), custom_call_target="tpu_custom_call" | custom-call | tf_op jit(solution)/shard_map/pallas_call | solution.py:655
  15.1 4.9 %all-to-all-start = ((f32[8,16,128]{2,1,0:T(8,128)}), f32[8,16,128]{2,1,0:T(8,128)S(1)}, u32[]{:S(2)}, u32[]{:S(2)}) async-start(f32[8,16,128]{2,1,0:T(8,128)} %get-tuple-element.41), calls=%async_computation | async-start | bytes 131072 | tf_op jit(solution)/shard_map/all_to_all | solution.py:668
  20.0 0.0 copy-start
  20.0 3.4 %shard_map.124 = (bf16[2048,640]{1,0:T(8,128)(2,1)S(1)}, bf16[256,1024]{1,0:T(8,128)(2,1)}, bf16[256,1024]{1,0:T(8,128)(2,1)}) custom-call(bf16[2048,128]{1,0:T(8,128)(2,1)} %coeff_hbm.1, f32[3,1024]{1,0:T(4,128)} %refs_1_.1, f32[1,1024,1024]{2,1,0:T(8,128)} %inverse_hbm.7, f32[1,128]{1,0:T(1,128)S(1)} %get-tuple-element.42.after_ref.weight_ref), custom_call_target="tpu_custom_call" | custom-call | flops 2097152 | bytes 5767168 | tf_op jit(solution)/shard_map/pallas_call | solution.py:672
  23.4 2.5 %all-to-all-done.refs_1_.refs_0_ = f32[8,16,128]{2,1,0:T(8,128)S(1)} async-done(((f32[8,16,128]{2,1,0:T(8,128)}), f32[8,16,128]{2,1,0:T(8,128)S(1)}, u32[]{:S(2)}, u32[]{:S(2)}) %all-to-all-start) | async-done | bytes 65568 | tf_op jit(solution)/shard_map/all_to_all | solution.py:668
  25.9 0.0 collective-permute-done.3.got_a
  25.9 0.0 collective-permute-done.4.got_b
  25.9 2.0 %shard_map.125 = (bf16[256,1024]{1,0:T(8,128)(2,1)S(1)}, bf16[256,1024]{1,0:T(8,128)(2,1)}, f32[8,128]{1,0:T(8,128)S(1)}) custom-call(s32[1]{0:T(128)} %bitcast.6.flag_ref, bf16[256,1024]{1,0:T(8,128)(2,1)} %get-tuple-element.44.own_a.own_b.refs_3_.refs_1_, ...), custom_call_target="tpu_custom_call", output_to_operand_aliasing={{0}: (3, {}), {1}: (4, {})} | custom-call | tf_op jit(solution)/shard_map/pallas_call | solution.py:700
  27.9 0.1 collective-permute-start.5
  28.0 0.1 collective-permute-start.6
  28.1 0.0 copy-done
  28.1 6.4 %shard_map.126.refs_0_ = bf16[8,176,128]{2,1,0:T(8,128)(2,1)} custom-call(f32[8,16,128]{2,1,0:T(8,128)S(1)} %all-to-all-done.refs_1_.refs_0_, f32[3,1024]{1,0:T(4,128)S(1)} %copy-done, bf16[2048,640]{1,0:T(8,128)(2,1)S(1)} %get-tuple-element.43.refs_0_.refs_2_, f32[8,128]{1,0:T(8,128)S(1)} %get-tuple-element.48.refs_3_), custom_call_target="tpu_custom_call" | custom-call | flops 738197504 | bytes 3145728 | tf_op jit(solution)/shard_map/pallas_call | solution.py:740
  34.5 5.2 %all-to-all-start.1 = ((bf16[8,176,128]{2,1,0:T(8,128)(2,1)}), bf16[8,176,128]{2,1,0:T(8,128)(2,1)S(1)}, u32[]{:S(2)}, u32[]{:S(2)}) async-start(bf16[8,176,128]{2,1,0:T(8,128)(2,1)} %shard_map.126.refs_0_), calls=%async_computation.1 | async-start | bytes 720896 | tf_op jit(solution)/shard_map/all_to_all | solution.py:766
  39.7 0.8 %collective-permute-done.5.got_a = bf16[256,1024]{1,0:T(8,128)(2,1)} collective-permute-done((bf16[256,1024]{1,0:T(8,128)(2,1)}, bf16[256,1024]{1,0:T(8,128)(2,1)}, u32[]{:S(2)}, u32[]{:S(2)}) %collective-permute-start.5) | collective-permute-done | bytes 524320 | tf_op jit(solution)/shard_map/ppermute | solution.py:697
  40.6 1.2 %collective-permute-done.6.got_b = bf16[256,1024]{1,0:T(8,128)(2,1)} collective-permute-done((bf16[256,1024]{1,0:T(8,128)(2,1)S(1)}, bf16[256,1024]{1,0:T(8,128)(2,1)}, u32[]{:S(2)}, u32[]{:S(2)}) %collective-permute-start.6) | collective-permute-done | bytes 524320 | tf_op jit(solution)/shard_map/ppermute | solution.py:696
  41.8 2.0 %shard_map.127 = (bf16[256,1024]{1,0:T(8,128)(2,1)}, bf16[256,1024]{1,0:T(8,128)(2,1)}, f32[8,128]{1,0:T(8,128)S(1)}) custom-call(s32[1]{0:T(128)} %bitcast.6.flag_ref, bf16[256,1024]{1,0:T(8,128)(2,1)} %get-tuple-element.45.own_b.own_a.refs_4_.refs_2_, ...), custom_call_target="tpu_custom_call", output_to_operand_aliasing={{0}: (3, {}), {1}: (4, {})} | custom-call | tf_op jit(solution)/shard_map/pallas_call | solution.py:700
  43.8 0.1 collective-permute-start.8
  43.9 0.1 collective-permute-start.7
  44.0 2.5 %shard_map.128.refs_1_ = bf16[1024,128]{1,0:T(8,128)(2,1)S(1)} custom-call(f32[1,1024,1024]{2,1,0:T(8,128)} %inverse_hbm.7, s32[2,128]{1,0:T(2,128)S(1)} %get-tuple-element.35.refs_4_.moved_ref, f32[8,128]{1,0:T(8,128)S(1)} %get-tuple-element.51.after_ref), custom_call_target="tpu_custom_call" | custom-call | flops 268435456 | bytes 4194304 | tf_op jit(solution)/shard_map/pallas_call | solution.py:785
  46.5 5.1 %all-to-all-done.1.refs_0_ = bf16[8,176,128]{2,1,0:T(8,128)(2,1)S(1)} async-done(((bf16[8,176,128]{2,1,0:T(8,128)(2,1)}), bf16[8,176,128]{2,1,0:T(8,128)(2,1)S(1)}, u32[]{:S(2)}, u32[]{:S(2)}) %all-to-all-start.1) | async-done | bytes 360480 | tf_op jit(solution)/shard_map/all_to_all | solution.py:766
  51.6 2.9 %shard_map.129 = (f32[3,1,16]{2,1,0:T(1,128)S(1)}, f32[1,1,16]{2,1,0:T(1,128)S(1)}, bf16[96,1024]{1,0:T(8,128)(2,1)S(1)}, bf16[2,256,128]{2,1,0:T(8,128)(2,1)S(1...) custom-call(s32[1]{0:T(128)} %bitcast.5.me_ref, s32[1]{0:T(128)} %bitcast.2.role_ref, ...), custom_call_target="tpu_custom_call" | custom-call | flops 33554432 | bytes 1769472 | tf_op jit(solution)/shard_map/pallas_call | solution.py:802
  54.5 1.5 %collective-permute-done.8.refs_9_ = bf16[256,1024]{1,0:T(8,128)(2,1)S(1)} collective-permute-done((bf16[256,1024]{1,0:T(8,128)(2,1)}, bf16[256,1024]{1,0:T(8,128)(2,1)S(1)}, u32[]{:S(2)}, u32[]{:S(2)}) %collective-permute-start.8) | collective-permute-done | bytes 524320 | tf_op jit(solution)/shard_map/ppermute | solution.py:697
  56.0 1.5 %collective-permute-done.7.refs_8_ = bf16[256,1024]{1,0:T(8,128)(2,1)S(1)} collective-permute-done((bf16[256,1024]{1,0:T(8,128)(2,1)}, bf16[256,1024]{1,0:T(8,128)(2,1)S(1)}, u32[]{:S(2)}, u32[]{:S(2)}) %collective-permute-start.7) | collective-permute-done | bytes 524320 | tf_op jit(solution)/shard_map/ppermute | solution.py:696
  57.4 6.8 %shard_map.130 = (f32[1024,1024]{1,0:T(8,128)}, f32[6,1,16]{2,1,0:T(1,128)}, f32[2,1,16]{2,1,0:T(1,128)}, f32[1,128]{1,0:T(1,128)}) custom-call(s32[1]{0:T(128)} %bitcast.2.role_ref, s32[1,128]{1,0:T(1,128)S(1)} %get-tuple-element.40.number_ref, bf16[96,1024]{1,0:T(8,128)(2,1)S(1)} %get-tuple-element.54.later_ref, ...), custom_call_target="tpu_custom_call" | custom-call | flops 134217728 | bytes 6291456 | tf_op jit(solution)/shard_map/pallas_call | solution.py:824
  (1 shorter events, 0.0 us)
Async XLA Ops:
  2.5 7.0 %collective-permute-start.2 = (f32[8,1024]{1,0:T(8,128)S(1)}, f32[8,1024]{1,0:T(8,128)S(1)}, u32[]{:S(2)}, u32[]{:S(2)}) collective-permute-start(f32[8,1024]{1,0:T(8,128)S(1)} %get-tuple-element.34.after_ref.refs_0_), channel_id=1, source_target_pairs={{0,24},{8,16},{16,8},{24,0},{1,25},{9,17},{17,9},{25,1},{2,26},{10... | collective-permute-start | bytes 98312 | tf_op jit(solution)/shard_map/ppermute | solution.py:621
  6.4 3.9 %collective-permute-start.1 = (f32[8,1024]{1,0:T(8,128)S(1)}, f32[8,1024]{1,0:T(8,128)S(1)}, u32[]{:S(2)}, u32[]{:S(2)}) collective-permute-start(f32[8,1024]{1,0:T(8,128)S(1)} %get-tuple-element.34.after_ref.refs_0_), channel_id=1, source_target_pairs={{0,16},{8,24},{16,0},{24,8},{1,17},{9,25},{17,1},{25,9},{2,18},{10... | collective-permute-start | bytes 98312 | tf_op jit(solution)/shard_map/ppermute | solution.py:621
  6.9 3.9 %collective-permute-start = (f32[8,1024]{1,0:T(8,128)S(1)}, f32[8,1024]{1,0:T(8,128)S(1)}, u32[]{:S(2)}, u32[]{:S(2)}) collective-permute-start(f32[8,1024]{1,0:T(8,128)S(1)} %get-tuple-element.34.after_ref.refs_0_), channel_id=1, source_target_pairs={{0,8},{8,0},{16,24},{24,16},{1,9},{9,1},{17,25},{25,17},{2,10},{10... | collective-permute-start | bytes 98312 | tf_op jit(solution)/shard_map/ppermute | solution.py:621
  10.9 15.1 %collective-permute-start.3 = (bf16[256,1024]{1,0:T(8,128)(2,1)}, bf16[256,1024]{1,0:T(8,128)(2,1)S(1)}, u32[]{:S(2)}, u32[]{:S(2)}) collective-permute-start(bf16[256,1024]{1,0:T(8,128)(2,1)} %get-tuple-element.46.refs_5_.refs_3_), channel_id=1, source_target_pairs={{0,16},{8,24},{16,0},{24,8},{1,17},{9,25},{17,1},{25,9},{2,18},{10... | collective-permute-start | bytes 1572872 | tf_op jit(solution)/shard_map/ppermute | solution.py:697
  12.4 13.6 %collective-permute-start.4 = (bf16[256,1024]{1,0:T(8,128)(2,1)}, bf16[256,1024]{1,0:T(8,128)(2,1)}, u32[]{:S(2)}, u32[]{:S(2)}) collective-permute-start(bf16[256,1024]{1,0:T(8,128)(2,1)} %get-tuple-element.47.refs_2_.refs_0_), channel_id=1, source_target_pairs={{0,8},{8,0},{16,24},{24,16},{1,9},{9,1},{17,25},{25,17},{2,10},{10... | collective-permute-start | bytes 1572872 | tf_op jit(solution)/shard_map/ppermute | solution.py:696
  15.1 10.8 %all-to-all-start = ((f32[8,16,128]{2,1,0:T(8,128)}), f32[8,16,128]{2,1,0:T(8,128)S(1)}, u32[]{:S(2)}, u32[]{:S(2)}) async-start(f32[8,16,128]{2,1,0:T(8,128)} %get-tuple-element.41), calls=%async_computation | async-start | bytes 131072 | tf_op jit(solution)/shard_map/all_to_all | solution.py:668
  20.0 8.1 %copy-start = (f32[3,1024]{1,0:T(4,128)S(1)}, f32[3,1024]{1,0:T(4,128)}, u32[]{:S(2)}) copy-start(f32[3,1024]{1,0:T(4,128)} %refs_1_.1) | copy-start | bytes 36868
  27.9 12.6 %collective-permute-start.5 = (bf16[256,1024]{1,0:T(8,128)(2,1)}, bf16[256,1024]{1,0:T(8,128)(2,1)}, u32[]{:S(2)}, u32[]{:S(2)}) collective-permute-start(bf16[256,1024]{1,0:T(8,128)(2,1)} %get-tuple-element.49.refs_6_.refs_4_), channel_id=1, source_target_pairs={{0,16},{8,24},{16,0},{24,8},{1,17},{9,25},{17,1},{25,9},{2,18},{10... | collective-permute-start | bytes 1572872 | tf_op jit(solution)/shard_map/ppermute | solution.py:697
  28.0 13.8 %collective-permute-start.6 = (bf16[256,1024]{1,0:T(8,128)(2,1)S(1)}, bf16[256,1024]{1,0:T(8,128)(2,1)}, u32[]{:S(2)}, u32[]{:S(2)}) collective-permute-start(bf16[256,1024]{1,0:T(8,128)(2,1)S(1)} %get-tuple-element.50.refs_8_.refs_6_), channel_id=1, source_target_pairs={{0,8},{8,0},{16,24},{24,16},{1,9},{9,1},{17,25},{25,17},{2,10},{10... | collective-permute-start | bytes 1572872 | tf_op jit(solution)/shard_map/ppermute | solution.py:696
  34.5 17.1 %all-to-all-start.1 = ((bf16[8,176,128]{2,1,0:T(8,128)(2,1)}), bf16[8,176,128]{2,1,0:T(8,128)(2,1)S(1)}, u32[]{:S(2)}, u32[]{:S(2)}) async-start(bf16[8,176,128]{2,1,0:T(8,128)(2,1)} %shard_map.126.refs_0_), calls=%async_computation.1 | async-start | bytes 720896 | tf_op jit(solution)/shard_map/all_to_all | solution.py:766
  43.8 12.2 %collective-permute-start.8 = (bf16[256,1024]{1,0:T(8,128)(2,1)}, bf16[256,1024]{1,0:T(8,128)(2,1)S(1)}, u32[]{:S(2)}, u32[]{:S(2)}) collective-permute-start(bf16[256,1024]{1,0:T(8,128)(2,1)} %get-tuple-element.52.refs_7_.refs_5_), channel_id=1, source_target_pairs={{0,16},{8,24},{16,0},{24,8},{1,17},{9,25},{17,1},{25,9},{2,18},{10... | collective-permute-start | bytes 1572872 | tf_op jit(solution)/shard_map/ppermute | solution.py:697
  43.9 13.6 %collective-permute-start.7 = (bf16[256,1024]{1,0:T(8,128)(2,1)}, bf16[256,1024]{1,0:T(8,128)(2,1)S(1)}, u32[]{:S(2)}, u32[]{:S(2)}) collective-permute-start(bf16[256,1024]{1,0:T(8,128)(2,1)} %get-tuple-element.53.refs_9_.refs_7_), channel_id=1, source_target_pairs={{0,8},{8,0},{16,24},{24,16},{1,9},{9,1},{17,25},{25,17},{2,10},{10... | collective-permute-start | bytes 1572872 | tf_op jit(solution)/shard_map/ppermute | solution.py:696

commit v14 on v13

--- a/solution.py
+++ b/solution.py
@@ -196,6 +196,32 @@
     token_ref[...] = jnp.zeros(token_ref.shape, F32)
 
 
+def near_kernel(own_a, own_b, after_ref, near_a, near_b, sems):
+    copies = [
+        pltpu.make_async_copy(own_a, near_a, sems.at[0]),
+        pltpu.make_async_copy(own_b, near_b, sems.at[1]),
+    ]
+    for copy in copies:
+        copy.start()
+    for copy in copies:
+        copy.wait()
+
+
+def near_relay_kernel(flag_ref, own_a, own_b, got_a, got_b, out_a, out_b, token_ref, sems):
+    @pl.when(flag_ref[0] == 0)
+    def _():
+        copies = [
+            pltpu.make_async_copy(own_a, out_a, sems.at[0]),
+            pltpu.make_async_copy(own_b, out_b, sems.at[1]),
+        ]
+        for copy in copies:
+            copy.start()
+        for copy in copies:
+            copy.wait()
+
+    token_ref[...] = jnp.zeros(token_ref.shape, F32)
+
+
 def points_kernel(count, others, role_ref, *refs):
     own_ref = refs[0]
     received = refs[1 : 1 + others]
@@ -430,9 +456,9 @@
     return chunk
 
 
-def load_slots(plan, slots, role, inputs, parent, sem):
+def load_slots(plan, slots, role, inputs, parent, sem, first=0):
     for slot in slots:
-        for which in range(len(plan)):
+        for which in range(first, len(plan)):
             load = pltpu.make_async_copy(
                 inputs[plan[which][slot][1]], parent.at[slot], sem.at[slot]
             )
@@ -517,11 +543,12 @@
         )
         for slot in range(chunks)
     ]
-    load_slots(plan, list(late) + list(range(done)), role, inputs, parent, in_sem)
+    load_slots(plan, late, role, inputs, parent, in_sem)
+    for load in own[done:] + own[:done]:
+        pl.when(role == 0)(load.start)
+    load_slots(plan, range(done), role, inputs, parent, in_sem, 1)
     pick = pick_from(number_ref, electrons)
     wait_slots(late, inputs, parent, in_sem)
-    for load in own[done:] + own[:done]:
-        pl.when(role == 0)(load.start)
     columns = [early_ref[slot] for slot in range(done)]
     products = products_ref[...]
     rows = []
@@ -540,7 +567,6 @@
     rounded = total.astype(BF16)
     solved = dot(halves, jnp.concatenate([rounded, rounded], 0)).astype(BF16)
     solved = jnp.concatenate([solved, jnp.zeros((LANES - size, electrons), BF16)], 0)
-    wait_slots(range(done), inputs, parent, in_sem)
     copies = []
     for slot in list(late) + list(range(done)):
         at = pl.multiple_of(chunk_at(plan, role, slot) * depth, depth)
@@ -558,8 +584,13 @@
             staged[slot] = before(slot) - dot(columns[slot], solved)
             copy.start()
 
+    def sent(slot):
+        if slot < done:
+            wait_slots([slot], inputs, parent, in_sem)
+        return parent[slot].astype(F32)
+
     pl.when(role == 0)(lambda: write(kept))
-    pl.when(role != 0)(lambda: write(lambda slot: parent[slot].astype(F32)))
+    pl.when(role != 0)(lambda: write(sent))
     sums = moved_sums(products, ratio, inverse, count)
     drift_ref[0:3] = drift_in[...]
     lap_ref[0:1] = lap_in[...]
@@ -769,7 +800,23 @@
         values = [values]
 
     if n_grp == 4:
-        y2, x2, token_2 = relay((own[2], own[1]), (y2, x2), (computed,))
+        near = call(
+            near_kernel,
+            (kept, kept),
+            [HBM, HBM, ANY],
+            (VM, VM),
+            scratch=[pltpu.SemaphoreType.DMA((2,))],
+            vmem=3,
+        )(*in_hbm(own[2], own[1]), computed)
+        y2, x2, token_2 = call(
+            near_relay_kernel,
+            (kept, kept, token),
+            [SM, VM, VM, ANY, ANY],
+            (ANY, ANY, VM),
+            scratch=[pltpu.SemaphoreType.DMA((2,))],
+            aliases={3: 0, 4: 1},
+            vmem=3,
+        )(apart, *near, y2, x2)
         x3, y3 = send_x(y2), send_y(x2)
         arrays = own + [x1, x2, y1, y2, x3, y3]
         a1, a2, b1, b2, a3, b3 = range(chunks, chunks + 6)

time: 64.6 us -> 63.4 us (0.981)
  starting transfers between devices: 17.1 us -> 20.9 us
  Pallas kernels: 30.4 us -> 26.7 us
  waiting for transfers between devices: 14 us -> 12.2 us
    pallas_call x2 -> x1, Pallas kernels: 3.95 us -> 0.08 us  [relay(): call(relay_kernel, (kept, kept, token), [SM] + [ANY] * (4 + len(first)),...]
    ppermute x3, starting transfers between devices: 0.78 us -> 3.78 us  [per_device(): send_x = lambda block: lax.ppermute(block, 'grp', pairs(n_grp, 1))]
    ppermute x3, starting transfers between devices: 1.66 us -> 3.82 us  [per_device(): send_y = lambda block: lax.ppermute(block, 'grp', pairs(n_grp, 2))]
    ppermute x3, waiting for transfers between devices: 2.71 us -> 0.88 us  [per_device(): send_x = lambda block: lax.ppermute(block, 'grp', pairs(n_grp, 1))]
    all_to_all x1, starting transfers between devices: 5.22 us -> 3.85 us  [per_device(): lax.all_to_all(values, 'orb', split_axis=0, concat_axis=0, tiled=True)]
    pallas_call x0 -> x2, Pallas kernels: none -> 1.23 us  [the longest x1 1.22 us: per_device(): call(near_kernel, (kept, kept), [HBM, HBM, ANY], (VM, VM), scratch=[pltpu...]
    pallas_call x1, Pallas kernels: 6.75 us -> 5.72 us  [per_device(): call(functools.partial(finish_kernel, count, plan), (shape((electrons, el...]
  transfers between devices with their start and end apart: 11 -> 11, of which waited for: 8 -> 7; matrix products, arithmetic and copies ran while one was open for 0% -> 0% of each run, Pallas kernels for 32% -> 31%
where the time goes in v14:
time: 63.4 us; the launch traced here: 62.5 us
  Pallas kernels  26.7 us (42%)
  starting transfers between devices  20.9 us (33%)
  waiting for transfers between devices  12.2 us (19%)
  between operations  2.68 us (4%)
    pallas_call x1, Pallas kernels, per_device(): pl.pallas_call(functools.partial(evaluate_kernel, count, sources, targets...  6.44 us
    pallas_call x1, Pallas kernels, per_device(): call(functools.partial(finish_kernel, count, plan), (shape((electrons, el...  5.72 us
    all_to_all x1, waiting for transfers between devices, per_device(): lax.all_to_all(values, 'orb', split_axis=0, concat_axis=0, tiled=True)  5.39 us
    all_to_all x1, starting transfers between devices, per_device(): lax.all_to_all(points, 'orb', split_axis=0, concat_axis=0, tiled=True)  4.88 us
    ppermute x3, starting transfers between devices, per_device(): lax.ppermute(record, 'grp', pairs(n_grp, s))  4.6 us
    all_to_all x1, starting transfers between devices, per_device(): lax.all_to_all(values, 'orb', split_axis=0, concat_axis=0, tiled=True)  3.85 us
    ppermute x3, starting transfers between devices, per_device(): send_y = lambda block: lax.ppermute(block, 'grp', pairs(n_grp, 2))  3.82 us
    ppermute x3, starting transfers between devices, per_device(): send_x = lambda block: lax.ppermute(block, 'grp', pairs(n_grp, 1))  3.78 us
  transfers between devices with their start and end apart: 11, of which 7 were waited for; matrix products, arithmetic and copies ran while one was open for 0% of the time, Pallas kernels for 31%

profile of v14, /device:TPU:0, one launch (start us, length us, event | category | flops | bytes accessed | tf_op | source)
XLA Modules:
  0.0 62.5 jit_solution(2185384944213406924)
XLA Ops:
  1.3 1.2 %shard_map.120 = (f32[8,1024]{1,0:T(8,128)S(1)}, s32[2,128]{1,0:T(2,128)S(1)}, f32[2,8,128]{2,1,0:T(8,128)S(1)}) custom-call(f32[3,1,1024]{2,1,0:T(1,128)} %bitcast.12, s32[2,1,16]{2,1,0:T(1,128)} %moved_hbm.1, f32[6,1,16]{2,1,0:T(1,128)} %bitcast.13, f32[1]{0:T(128)S(6)} %copy.27.weight_ref), custom_call_target="tpu_custom_call" | custom-call | tf_op jit(solution)/shard_map/pallas_call | solution.py:629
  2.5 4.0 %collective-permute-start.2 = (f32[8,1024]{1,0:T(8,128)S(1)}, f32[8,1024]{1,0:T(8,128)S(1)}, u32[]{:S(2)}, u32[]{:S(2)}) collective-permute-start(f32[8,1024]{1,0:T(8,128)S(1)} %get-tuple-element.36.after_ref.refs_0_), channel_id=1, source_target_pairs={{0,24},{8,16},{16,8},{24,0},{1,25},{9,17},{17,9},{25,1},{2,26},{10... | collective-permute-start | bytes 98312 | tf_op jit(solution)/shard_map/ppermute | solution.py:652
  6.4 0.5 collective-permute-start.1
  6.9 0.1 collective-permute-start
  7.1 2.4 %shard_map.121 = (bf16[256,1024]{1,0:T(8,128)(2,1)}, bf16[256,1024]{1,0:T(8,128)(2,1)}) custom-call(f32[1,1024,1024]{2,1,0:T(8,128)} %inverse_hbm.7, f32[8,1024]{1,0:T(8,128)S(1)} %get-tuple-element.36.after_ref.refs_0_), custom_call_target="tpu_custom_call" | custom-call | bytes 3145728 | tf_op jit(solution)/shard_map/pallas_call | solution.py:660
  9.5 0.0 collective-permute-done.2.refs_4_.refs_3_
  9.5 0.8 %collective-permute-done.1.refs_3_.refs_2_ = f32[8,1024]{1,0:T(8,128)S(1)} collective-permute-done((f32[8,1024]{1,0:T(8,128)S(1)}, f32[8,1024]{1,0:T(8,128)S(1)}, u32[]{:S(2)}, u32[]{:S(2)}) %collective-permute-start.1) | collective-permute-done | bytes 32800 | tf_op jit(solution)/shard_map/ppermute | solution.py:652
  10.4 0.5 collective-permute-done.refs_2_.refs_1_
  10.9 1.5 %collective-permute-start.3 = (bf16[256,1024]{1,0:T(8,128)(2,1)}, bf16[256,1024]{1,0:T(8,128)(2,1)S(1)}, u32[]{:S(2)}, u32[]{:S(2)}) collective-permute-start(bf16[256,1024]{1,0:T(8,128)(2,1)} %get-tuple-element.48.refs_5_.refs_3_), channel_id=1, source_target_pairs={{0,16},{8,24},{16,0},{24,8},{1,17},{9,25},{17,1},{25,9},{2,18},{10... | collective-permute-start | bytes 1572872 | tf_op jit(solution)/shard_map/ppermute | solution.py:728
  12.4 0.6 %collective-permute-start.4 = (bf16[256,1024]{1,0:T(8,128)(2,1)}, bf16[256,1024]{1,0:T(8,128)(2,1)}, u32[]{:S(2)}, u32[]{:S(2)}) collective-permute-start(bf16[256,1024]{1,0:T(8,128)(2,1)} %get-tuple-element.49.refs_2_.refs_0_), channel_id=1, source_target_pairs={{0,8},{8,0},{16,24},{24,16},{1,9},{9,1},{17,25},{25,17},{2,10},{10... | collective-permute-start | bytes 1572872 | tf_op jit(solution)/shard_map/ppermute | solution.py:727
  14.3 0.8 %shard_map.123 = (f32[8,16,128]{2,1,0:T(8,128)}, f32[1,128]{1,0:T(1,128)S(1)}, s32[1,128]{1,0:T(1,128)S(1)}) custom-call(s32[1]{0:T(128)} %bitcast.2.role_ref, f32[8,1024]{1,0:T(8,128)S(1)} %get-tuple-element.36.after_ref.refs_0_, f32[8,1024]{1,0:T(8,128)S(1)} %collective-permute-done.refs_2_.refs_1_, f32[8,1024]{1,0:T(8,128)S(1)} %collective-permute-done.1.refs_3_.refs_2_, ...), custom_call_target="tpu_custom_call" | custom-call | tf_op jit(solution)/shard_map/pallas_call | solution.py:686
  15.1 4.9 %all-to-all-start = ((f32[8,16,128]{2,1,0:T(8,128)}), f32[8,16,128]{2,1,0:T(8,128)S(1)}, u32[]{:S(2)}, u32[]{:S(2)}) async-start(f32[8,16,128]{2,1,0:T(8,128)} %get-tuple-element.43), calls=%async_computation | async-start | bytes 131072 | tf_op jit(solution)/shard_map/all_to_all | solution.py:699
  20.0 0.0 copy-start
  20.0 3.4 %shard_map.124 = (bf16[2048,640]{1,0:T(8,128)(2,1)S(1)}, bf16[256,1024]{1,0:T(8,128)(2,1)}, bf16[256,1024]{1,0:T(8,128)(2,1)}) custom-call(bf16[2048,128]{1,0:T(8,128)(2,1)} %coeff_hbm.1, f32[3,1024]{1,0:T(4,128)} %refs_1_.1, f32[1,1024,1024]{2,1,0:T(8,128)} %inverse_hbm.7, f32[1,128]{1,0:T(1,128)S(1)} %get-tuple-element.44.after_ref.weight_ref), custom_call_target="tpu_custom_call" | custom-call | flops 2097152 | bytes 5767168 | tf_op jit(solution)/shard_map/pallas_call | solution.py:703
  23.4 2.5 %all-to-all-done.refs_1_.refs_0_ = f32[8,16,128]{2,1,0:T(8,128)S(1)} async-done(((f32[8,16,128]{2,1,0:T(8,128)}), f32[8,16,128]{2,1,0:T(8,128)S(1)}, u32[]{:S(2)}, u32[]{:S(2)}) %all-to-all-start) | async-done | bytes 65568 | tf_op jit(solution)/shard_map/all_to_all | solution.py:699
  25.9 0.0 collective-permute-done.3.got_a
  25.9 0.0 collective-permute-done.4.got_b
  25.9 0.1 shard_map.125
  26.0 0.6 collective-permute-start.5
  26.6 2.9 %collective-permute-start.6 = (bf16[256,1024]{1,0:T(8,128)(2,1)S(1)}, bf16[256,1024]{1,0:T(8,128)(2,1)}, u32[]{:S(2)}, u32[]{:S(2)}) collective-permute-start(bf16[256,1024]{1,0:T(8,128)(2,1)S(1)} %get-tuple-element.54.refs_8_.refs_6_), channel_id=1, source_target_pairs={{0,8},{8,0},{16,24},{24,16},{1,9},{9,1},{17,25},{25,17},{2,10},{10... | collective-permute-start | bytes 1572872 | tf_op jit(solution)/shard_map/ppermute | solution.py:727
  29.5 0.0 copy-done
  29.5 6.4 %shard_map.126.after_ref = bf16[8,176,128]{2,1,0:T(8,128)(2,1)} custom-call(f32[8,16,128]{2,1,0:T(8,128)S(1)} %all-to-all-done.refs_1_.refs_0_, f32[3,1024]{1,0:T(4,128)S(1)} %copy-done, bf16[2048,640]{1,0:T(8,128)(2,1)S(1)} %get-tuple-element.45.refs_0_.refs_2_, f32[8,128]{1,0:T(8,128)S(1)} %get-tuple-element.50.refs_3_), custom_call_target="tpu_custom_call" | custom-call | flops 738197504 | bytes 3145728 | tf_op jit(solution)/shard_map/pallas_call | solution.py:771
  35.9 3.9 %all-to-all-start.1 = ((bf16[8,176,128]{2,1,0:T(8,128)(2,1)}), bf16[8,176,128]{2,1,0:T(8,128)(2,1)S(1)}, u32[]{:S(2)}, u32[]{:S(2)}) async-start(bf16[8,176,128]{2,1,0:T(8,128)(2,1)} %shard_map.126.after_ref), calls=%async_computation.1 | async-start | bytes 720896 | tf_op jit(solution)/shard_map/all_to_all | solution.py:797
  39.8 1.2 %shard_map.127 = (bf16[256,1024]{1,0:T(8,128)(2,1)S(1)}, bf16[256,1024]{1,0:T(8,128)(2,1)S(1)}) custom-call(bf16[256,1024]{1,0:T(8,128)(2,1)} %get-tuple-element.47.own_b.own_a.refs_4_.refs_2_, bf16[256,1024]{1,0:T(8,128)(2,1)} %get-tuple-element.46.own_a.own_b.refs_3_.refs_1_, bf16[8,176,128]{2,1,0:T(8,128)(2,1)} %shard_map.126.after_ref), custom_call_target="tpu_custom_call" | custom-call | tf_op jit(solution)/shard_map/pallas_call | solution.py:803
  41.0 0.0 collective-permute-done.5.got_a
  41.0 0.7 %collective-permute-done.6.got_b = bf16[256,1024]{1,0:T(8,128)(2,1)} collective-permute-done((bf16[256,1024]{1,0:T(8,128)(2,1)S(1)}, bf16[256,1024]{1,0:T(8,128)(2,1)}, u32[]{:S(2)}, u32[]{:S(2)}) %collective-permute-start.6) | collective-permute-done | bytes 524320 | tf_op jit(solution)/shard_map/ppermute | solution.py:727
  41.7 1.7 %collective-permute-start.8 = (bf16[256,1024]{1,0:T(8,128)(2,1)}, bf16[256,1024]{1,0:T(8,128)(2,1)S(1)}, u32[]{:S(2)}, u32[]{:S(2)}) collective-permute-start(bf16[256,1024]{1,0:T(8,128)(2,1)} %get-tuple-element.56.refs_7_.refs_5_), channel_id=1, source_target_pairs={{0,16},{8,24},{16,0},{24,8},{1,17},{9,25},{17,1},{25,9},{2,18},{10... | collective-permute-start | bytes 1572872 | tf_op jit(solution)/shard_map/ppermute | solution.py:728
  43.4 0.3 collective-permute-start.7
  43.7 2.5 %shard_map.129.refs_1_ = bf16[1024,128]{1,0:T(8,128)(2,1)S(1)} custom-call(f32[1,1024,1024]{2,1,0:T(8,128)} %inverse_hbm.7, s32[2,128]{1,0:T(2,128)S(1)} %get-tuple-element.37.refs_4_.moved_ref, f32[8,128]{1,0:T(8,128)S(1)} %get-tuple-element.55.after_ref), custom_call_target="tpu_custom_call" | custom-call | flops 268435456 | bytes 4194304 | tf_op jit(solution)/shard_map/pallas_call | solution.py:832
  46.2 5.4 %all-to-all-done.1.refs_0_ = bf16[8,176,128]{2,1,0:T(8,128)(2,1)S(1)} async-done(((bf16[8,176,128]{2,1,0:T(8,128)(2,1)}), bf16[8,176,128]{2,1,0:T(8,128)(2,1)S(1)}, u32[]{:S(2)}, u32[]{:S(2)}) %all-to-all-start.1) | async-done | bytes 360480 | tf_op jit(solution)/shard_map/all_to_all | solution.py:797
  51.6 2.9 %shard_map.130 = (f32[3,1,16]{2,1,0:T(1,128)S(1)}, f32[1,1,16]{2,1,0:T(1,128)S(1)}, bf16[96,1024]{1,0:T(8,128)(2,1)S(1)}, bf16[2,256,128]{2,1,0:T(8,128)(2,1)S(1...) custom-call(s32[1]{0:T(128)} %bitcast.5.me_ref, s32[1]{0:T(128)} %bitcast.2.role_ref, ...), custom_call_target="tpu_custom_call" | custom-call | flops 33554432 | bytes 1769472 | tf_op jit(solution)/shard_map/pallas_call | solution.py:849
  54.5 2.1 %collective-permute-done.8.refs_9_ = bf16[256,1024]{1,0:T(8,128)(2,1)S(1)} collective-permute-done((bf16[256,1024]{1,0:T(8,128)(2,1)}, bf16[256,1024]{1,0:T(8,128)(2,1)S(1)}, u32[]{:S(2)}, u32[]{:S(2)}) %collective-permute-start.8) | collective-permute-done | bytes 524320 | tf_op jit(solution)/shard_map/ppermute | solution.py:728
  56.6 0.2 collective-permute-done.7.refs_8_
  56.8 5.7 %shard_map.131 = (f32[1024,1024]{1,0:T(8,128)}, f32[6,1,16]{2,1,0:T(1,128)}, f32[2,1,16]{2,1,0:T(1,128)}, f32[1,128]{1,0:T(1,128)}) custom-call(s32[1]{0:T(128)} %bitcast.2.role_ref, s32[1,128]{1,0:T(1,128)S(1)} %get-tuple-element.42.number_ref, bf16[96,1024]{1,0:T(8,128)(2,1)S(1)} %get-tuple-element.58.later_ref, ...), custom_call_target="tpu_custom_call" | custom-call | flops 134217728 | bytes 6291456 | tf_op jit(solution)/shard_map/pallas_call | solution.py:871
  (2 shorter events, 0.0 us)
Async XLA Ops:
  2.5 7.0 %collective-permute-start.2 = (f32[8,1024]{1,0:T(8,128)S(1)}, f32[8,1024]{1,0:T(8,128)S(1)}, u32[]{:S(2)}, u32[]{:S(2)}) collective-permute-start(f32[8,1024]{1,0:T(8,128)S(1)} %get-tuple-element.36.after_ref.refs_0_), channel_id=1, source_target_pairs={{0,24},{8,16},{16,8},{24,0},{1,25},{9,17},{17,9},{25,1},{2,26},{10... | collective-permute-start | bytes 98312 | tf_op jit(solution)/shard_map/ppermute | solution.py:652
  6.4 3.9 %collective-permute-start.1 = (f32[8,1024]{1,0:T(8,128)S(1)}, f32[8,1024]{1,0:T(8,128)S(1)}, u32[]{:S(2)}, u32[]{:S(2)}) collective-permute-start(f32[8,1024]{1,0:T(8,128)S(1)} %get-tuple-element.36.after_ref.refs_0_), channel_id=1, source_target_pairs={{0,16},{8,24},{16,0},{24,8},{1,17},{9,25},{17,1},{25,9},{2,18},{10... | collective-permute-start | bytes 98312 | tf_op jit(solution)/shard_map/ppermute | solution.py:652
  6.9 3.9 %collective-permute-start = (f32[8,1024]{1,0:T(8,128)S(1)}, f32[8,1024]{1,0:T(8,128)S(1)}, u32[]{:S(2)}, u32[]{:S(2)}) collective-permute-start(f32[8,1024]{1,0:T(8,128)S(1)} %get-tuple-element.36.after_ref.refs_0_), channel_id=1, source_target_pairs={{0,8},{8,0},{16,24},{24,16},{1,9},{9,1},{17,25},{25,17},{2,10},{10... | collective-permute-start | bytes 98312 | tf_op jit(solution)/shard_map/ppermute | solution.py:652
  10.9 15.1 %collective-permute-start.3 = (bf16[256,1024]{1,0:T(8,128)(2,1)}, bf16[256,1024]{1,0:T(8,128)(2,1)S(1)}, u32[]{:S(2)}, u32[]{:S(2)}) collective-permute-start(bf16[256,1024]{1,0:T(8,128)(2,1)} %get-tuple-element.48.refs_5_.refs_3_), channel_id=1, source_target_pairs={{0,16},{8,24},{16,0},{24,8},{1,17},{9,25},{17,1},{25,9},{2,18},{10... | collective-permute-start | bytes 1572872 | tf_op jit(solution)/shard_map/ppermute | solution.py:728
  12.4 13.6 %collective-permute-start.4 = (bf16[256,1024]{1,0:T(8,128)(2,1)}, bf16[256,1024]{1,0:T(8,128)(2,1)}, u32[]{:S(2)}, u32[]{:S(2)}) collective-permute-start(bf16[256,1024]{1,0:T(8,128)(2,1)} %get-tuple-element.49.refs_2_.refs_0_), channel_id=1, source_target_pairs={{0,8},{8,0},{16,24},{24,16},{1,9},{9,1},{17,25},{25,17},{2,10},{10... | collective-permute-start | bytes 1572872 | tf_op jit(solution)/shard_map/ppermute | solution.py:727
  15.1 10.8 %all-to-all-start = ((f32[8,16,128]{2,1,0:T(8,128)}), f32[8,16,128]{2,1,0:T(8,128)S(1)}, u32[]{:S(2)}, u32[]{:S(2)}) async-start(f32[8,16,128]{2,1,0:T(8,128)} %get-tuple-element.43), calls=%async_computation | async-start | bytes 131072 | tf_op jit(solution)/shard_map/all_to_all | solution.py:699
  20.0 9.5 %copy-start = (f32[3,1024]{1,0:T(4,128)S(1)}, f32[3,1024]{1,0:T(4,128)}, u32[]{:S(2)}) copy-start(f32[3,1024]{1,0:T(4,128)} %refs_1_.1) | copy-start | bytes 36868
  26.0 15.0 %collective-permute-start.5 = (bf16[256,1024]{1,0:T(8,128)(2,1)}, bf16[256,1024]{1,0:T(8,128)(2,1)}, u32[]{:S(2)}, u32[]{:S(2)}) collective-permute-start(bf16[256,1024]{1,0:T(8,128)(2,1)} %get-tuple-element.53.refs_6_.refs_4_), channel_id=1, source_target_pairs={{0,16},{8,24},{16,0},{24,8},{1,17},{9,25},{17,1},{25,9},{2,18},{10... | collective-permute-start | bytes 1572872 | tf_op jit(solution)/shard_map/ppermute | solution.py:728
  26.6 15.1 %collective-permute-start.6 = (bf16[256,1024]{1,0:T(8,128)(2,1)S(1)}, bf16[256,1024]{1,0:T(8,128)(2,1)}, u32[]{:S(2)}, u32[]{:S(2)}) collective-permute-start(bf16[256,1024]{1,0:T(8,128)(2,1)S(1)} %get-tuple-element.54.refs_8_.refs_6_), channel_id=1, source_target_pairs={{0,8},{8,0},{16,24},{24,16},{1,9},{9,1},{17,25},{25,17},{2,10},{10... | collective-permute-start | bytes 1572872 | tf_op jit(solution)/shard_map/ppermute | solution.py:727
  35.9 15.7 %all-to-all-start.1 = ((bf16[8,176,128]{2,1,0:T(8,128)(2,1)}), bf16[8,176,128]{2,1,0:T(8,128)(2,1)S(1)}, u32[]{:S(2)}, u32[]{:S(2)}) async-start(bf16[8,176,128]{2,1,0:T(8,128)(2,1)} %shard_map.126.after_ref), calls=%async_computation.1 | async-start | bytes 720896 | tf_op jit(solution)/shard_map/all_to_all | solution.py:797
  41.7 14.9 %collective-permute-start.8 = (bf16[256,1024]{1,0:T(8,128)(2,1)}, bf16[256,1024]{1,0:T(8,128)(2,1)S(1)}, u32[]{:S(2)}, u32[]{:S(2)}) collective-permute-start(bf16[256,1024]{1,0:T(8,128)(2,1)} %get-tuple-element.56.refs_7_.refs_5_), channel_id=1, source_target_pairs={{0,16},{8,24},{16,0},{24,8},{1,17},{9,25},{17,1},{25,9},{2,18},{10... | collective-permute-start | bytes 1572872 | tf_op jit(solution)/shard_map/ppermute | solution.py:728
  43.4 13.4 %collective-permute-start.7 = (bf16[256,1024]{1,0:T(8,128)(2,1)}, bf16[256,1024]{1,0:T(8,128)(2,1)S(1)}, u32[]{:S(2)}, u32[]{:S(2)}) collective-permute-start(bf16[256,1024]{1,0:T(8,128)(2,1)} %get-tuple-element.57.refs_9_.refs_7_), channel_id=1, source_target_pairs={{0,8},{8,0},{16,24},{24,16},{1,9},{9,1},{17,25},{25,17},{2,10},{10... | collective-permute-start | bytes 1572872 | tf_op jit(solution)/shard_map/ppermute | solution.py:727

commit v15 on v14

--- a/solution.py
+++ b/solution.py
@@ -16,6 +16,8 @@
 DIRECT_VALUES = False
 MIB = 1024 * 1024
 precise = lax.Precision.HIGHEST
+
+WHOLE = 1.5 * 2.0**23
 
 SIN_HALF = (4.4428679, -7.30744342, 3.59478808, -0.78437403)
 COS_HALF = (1.4142135, -6.97885099, 5.73946117, -1.88356299, 0.31069819)
@@ -328,7 +330,7 @@
             for pair, diff_at, new_at in ((0, 2, 1), (1, 0, None), (2, 1, 0)):
                 rows = slice(2 * pair * count, 2 * (pair + 1) * count)
                 turn = spread[0, rows] * ks[0] + spread[1, rows] * ks[1] + spread[2, rows] * ks[2]
-                r = turn - jnp.floor(turn + 0.5)
+                r = turn - ((turn + WHOLE) - WHOLE)
                 u = r * r
                 s = r * horner(SIN_HALF, u)
                 c = horner(COS_HALF, u)
@@ -456,9 +458,9 @@
     return chunk
 
 
-def load_slots(plan, slots, role, inputs, parent, sem, first=0):
+def load_slots(plan, slots, role, inputs, parent, sem):
     for slot in slots:
-        for which in range(first, len(plan)):
+        for which in range(len(plan)):
             load = pltpu.make_async_copy(
                 inputs[plan[which][slot][1]], parent.at[slot], sem.at[slot]
             )
@@ -470,15 +472,23 @@
         pltpu.make_async_copy(inputs[0], parent.at[slot], sem.at[slot]).wait()
 
 
-def middle_kernel(count, sources, plan, me_ref, role_ref, number_ref, *refs):
+def middle_kernel(count, sources, plan, me_ref, role_ref, number_ref, inverse_hbm, *refs):
     values = refs[:sources]
     own_columns = refs[sources]
-    inputs = refs[sources + 1 : -9]
-    drift_ref, lap_ref, later_ref, columns_ref, products_ref, total_ref = refs[-9:-3]
-    vals, parent, sem = refs[-3:]
+    inputs = refs[sources + 1 : -11]
+    drift_ref, lap_ref, later_ref, columns_ref, products_ref, total_ref, held_ref = refs[-11:-4]
+    vals, parent, sem, own_sem = refs[-4:]
     slots, depth, electrons = parent.shape
     role = role_ref[0]
     load_slots(plan, range(slots), role, inputs, parent, sem)
+    wide = [
+        pltpu.make_async_copy(
+            rows_of(inverse_hbm, plan[0][slot][0], depth), held_ref.at[slot], own_sem.at[slot]
+        )
+        for slot in range(slots)
+    ]
+    for load in wide:
+        pl.when(role == 0)(load.start)
     rows = later_ref.shape[0]
     if sources > 1:
         width = values[0].shape[1]
@@ -507,6 +517,17 @@
         total = more if slot == 0 else total + more
     products_ref[...] = products
     total_ref[...] = total
+
+    @pl.when(role == 0)
+    def _():
+        for load in wide:
+            load.wait()
+
+    @pl.when(role != 0)
+    def _():
+        for slot in range(slots):
+            held_ref[slot] = parent[slot].astype(F32)
+
     ratio, inverse, _ = ratio_of(own, count)
     sums = moved_sums(own, ratio, inverse, count)
     for a in range(3):
@@ -526,6 +547,7 @@
     early_ref,
     products_ref,
     total_ref,
+    held_ref,
     inverse_hbm,
     *refs,
 ):
@@ -544,9 +566,8 @@
         for slot in range(chunks)
     ]
     load_slots(plan, late, role, inputs, parent, in_sem)
-    for load in own[done:] + own[:done]:
-        pl.when(role == 0)(load.start)
-    load_slots(plan, range(done), role, inputs, parent, in_sem, 1)
+    for slot in late:
+        pl.when(role == 0)(own[slot].start)
     pick = pick_from(number_ref, electrons)
     wait_slots(late, inputs, parent, in_sem)
     columns = [early_ref[slot] for slot in range(done)]
@@ -568,29 +589,26 @@
     solved = dot(halves, jnp.concatenate([rounded, rounded], 0)).astype(BF16)
     solved = jnp.concatenate([solved, jnp.zeros((LANES - size, electrons), BF16)], 0)
     copies = []
-    for slot in list(late) + list(range(done)):
+    for slot in range(chunks):
         at = pl.multiple_of(chunk_at(plan, role, slot) * depth, depth)
-        copy = pltpu.make_async_copy(
-            staged.at[slot], out_ref.at[pl.ds(at, depth)], out_sem.at[slot]
+        copies.append(
+            pltpu.make_async_copy(
+                staged.at[slot], out_ref.at[pl.ds(at, depth)], out_sem.at[slot]
+            )
         )
-        copies.append((slot, copy))
+
+    def write(slots, before):
+        for slot in slots:
+            staged[slot] = before(slot) - dot(columns[slot], solved)
+            copies[slot].start()
 
     def kept(slot):
         own[slot].wait()
         return staged[slot]
 
-    def write(before):
-        for slot, copy in copies:
-            staged[slot] = before(slot) - dot(columns[slot], solved)
-            copy.start()
-
-    def sent(slot):
-        if slot < done:
-            wait_slots([slot], inputs, parent, in_sem)
-        return parent[slot].astype(F32)
-
-    pl.when(role == 0)(lambda: write(kept))
-    pl.when(role != 0)(lambda: write(sent))
+    write(range(done), lambda slot: held_ref[slot])
+    pl.when(role == 0)(lambda: write(late, kept))
+    pl.when(role != 0)(lambda: write(late, lambda slot: parent[slot].astype(F32)))
     sums = moved_sums(products, ratio, inverse, count)
     drift_ref[0:3] = drift_in[...]
     lap_ref[0:1] = lap_in[...]
@@ -598,7 +616,7 @@
         drift_ref[3 + a] = sums[:, a * count : (a + 1) * count]
     lap_ref[1] = sums[:, 3 * count : 4 * count]
     out_weight_ref[...] = weight_ref[...] + log
-    for _, copy in copies:
+    for copy in copies:
         copy.wait()
 
 
@@ -846,7 +864,7 @@
     here = lax.axis_index("orb").astype(jnp.int32).reshape(1)
     early = 2
     work = 2 * electrons * 2 * count
-    drift, laplacian, later, early_columns, products, total = call(
+    drift, laplacian, later, early_columns, products, total, held = call(
         functools.partial(middle_kernel, count, targets, plan),
         (
             shape((3, 1, count), F32),
@@ -855,18 +873,20 @@
             shape((early, depth, LANES), BF16),
             shape((6 * count, LANES), F32),
             shape((2 * count, electrons), F32),
+            shape((early, depth, electrons), F32),
         ),
-        [SM, SM, VM] + [VM] * (targets + 1) + [ANY] * settled,
-        (VM,) * 6,
+        [SM, SM, VM, HBM] + [VM] * (targets + 1) + [ANY] * settled,
+        (VM,) * 7,
         scratch=[
             pltpu.VMEM((5 * count, electrons), BF16),
             pltpu.VMEM((early, depth, electrons), BF16),
             pltpu.SemaphoreType.DMA((early,)),
+            pltpu.SemaphoreType.DMA((early,)),
         ],
         flops=early * depth * work,
-        moved=2 * early * depth * electrons + 44 * count * electrons,
-        vmem=8,
-    )(here, role, number, *values, columns, *in_hbm(*own), *arrays[chunks:settled])
+        moved=8 * early * depth * electrons + 44 * count * electrons,
+        vmem=10,
+    )(here, role, number, *in_hbm(inverse), *values, columns, *in_hbm(*own), *arrays[chunks:settled])
 
     updated, drift, laplacian, new_weight = call(
         functools.partial(finish_kernel, count, plan),
@@ -876,7 +896,7 @@
             shape((2, 1, count), F32),
             shape((1, LANES), F32),
         ),
-        [SM] + [VM] * 8 + [HBM] + [ANY] * len(arrays),
+        [SM] + [VM] * 9 + [HBM] + [ANY] * len(arrays),
         (HBM, VM, VM, VM),
         scratch=[
             pltpu.VMEM((chunks, depth, electrons), BF16),
@@ -898,6 +918,7 @@
         early_columns,
         products,
         total,
+        held,
         *in_hbm(inverse, *own),
         *arrays[chunks:],
     )

time: 63.4 us -> 64.1 us (1.011)
  Pallas kernels: 26.7 us -> 30.9 us
  starting transfers between devices: 20.9 us -> 16.7 us
  waiting for transfers between devices: 12.2 us -> 13.3 us
    ppermute x3, waiting for transfers between devices: 0.88 us -> 3.85 us  [per_device(): send_x = lambda block: lax.ppermute(block, 'grp', pairs(n_grp, 1))]
    ppermute x3, starting transfers between devices: 3.82 us -> 1.66 us  [per_device(): send_y = lambda block: lax.ppermute(block, 'grp', pairs(n_grp, 2))]
    ppermute x3, starting transfers between devices: 3.78 us -> 1.82 us  [per_device(): send_x = lambda block: lax.ppermute(block, 'grp', pairs(n_grp, 1))]
    pallas_call x1, Pallas kernels: 0.08 us -> 1.98 us  [relay(): call(relay_kernel, (kept, kept, token), [SM] + [ANY] * (4 + len(first)),...]
    all_to_all x1, waiting for transfers between devices: 5.39 us -> 4 us  [per_device(): lax.all_to_all(values, 'orb', split_axis=0, concat_axis=0, tiled=True)]
    pallas_call x1, Pallas kernels: 5.72 us -> 6.7 us  [per_device(): call(functools.partial(finish_kernel, count, plan), (shape((electrons, el...]
    pallas_call x1, Pallas kernels: 0.02 us -> 0.99 us  [per_device(): call(near_relay_kernel, (kept, kept, token), [SM, VM, VM, ANY, ANY], (ANY...]
  transfers between devices with their start and end apart: 11 -> 11, of which waited for: 7 -> 8; matrix products, arithmetic and copies ran while one was open for 0% -> 0% of each run, Pallas kernels for 31% -> 33%
where the time goes in v15:
time: 64.1 us; the launch traced here: 63.6 us
  Pallas kernels  30.9 us (48%)
  starting transfers between devices  16.7 us (26%)
  waiting for transfers between devices  13.3 us (21%)
  between operations  2.7 us (4%)
    pallas_call x1, Pallas kernels, per_device(): call(functools.partial(finish_kernel, count, plan), (shape((electrons, el...  6.7 us
    pallas_call x1, Pallas kernels, per_device(): pl.pallas_call(functools.partial(evaluate_kernel, count, sources, targets...  6.45 us
    all_to_all x1, starting transfers between devices, per_device(): lax.all_to_all(points, 'orb', split_axis=0, concat_axis=0, tiled=True)  4.88 us
    ppermute x3, starting transfers between devices, per_device(): lax.ppermute(record, 'grp', pairs(n_grp, s))  4.6 us
    all_to_all x1, waiting for transfers between devices, per_device(): lax.all_to_all(values, 'orb', split_axis=0, concat_axis=0, tiled=True)  4 us
    ppermute x3, waiting for transfers between devices, per_device(): send_x = lambda block: lax.ppermute(block, 'grp', pairs(n_grp, 1))  3.85 us
    all_to_all x1, starting transfers between devices, per_device(): lax.all_to_all(values, 'orb', split_axis=0, concat_axis=0, tiled=True)  3.77 us
    pallas_call x1, Pallas kernels, per_device(): call(functools.partial(prepare_kernel, middle), (shape((plane, 5 * width)...  3.4 us
  transfers between devices with their start and end apart: 11, of which 8 were waited for; matrix products, arithmetic and copies ran while one was open for 0% of the time, Pallas kernels for 33%

profile of v15, /device:TPU:0, one launch (start us, length us, event | category | flops | bytes accessed | tf_op | source)
XLA Modules:
  0.0 63.6 jit_solution(786465548825826389)
XLA Ops:
  1.3 1.2 %shard_map.120 = (f32[8,1024]{1,0:T(8,128)S(1)}, s32[2,128]{1,0:T(2,128)S(1)}, f32[2,8,128]{2,1,0:T(8,128)S(1)}) custom-call(f32[3,1,1024]{2,1,0:T(1,128)} %bitcast.12, s32[2,1,16]{2,1,0:T(1,128)} %moved_hbm.1, f32[6,1,16]{2,1,0:T(1,128)} %bitcast.13, f32[1]{0:T(128)S(6)} %copy.27.weight_ref), custom_call_target="tpu_custom_call" | custom-call | tf_op jit(solution)/shard_map/pallas_call | solution.py:647
  2.5 4.0 %collective-permute-start.2 = (f32[8,1024]{1,0:T(8,128)S(1)}, f32[8,1024]{1,0:T(8,128)S(1)}, u32[]{:S(2)}, u32[]{:S(2)}) collective-permute-start(f32[8,1024]{1,0:T(8,128)S(1)} %get-tuple-element.37.after_ref.refs_0_), channel_id=1, source_target_pairs={{0,24},{8,16},{16,8},{24,0},{1,25},{9,17},{17,9},{25,1},{2,26},{10... | collective-permute-start | bytes 98312 | tf_op jit(solution)/shard_map/ppermute | solution.py:670
  6.4 0.5 collective-permute-start.1
  6.9 0.1 collective-permute-start
  7.1 2.4 %shard_map.121 = (bf16[256,1024]{1,0:T(8,128)(2,1)}, bf16[256,1024]{1,0:T(8,128)(2,1)}) custom-call(f32[1,1024,1024]{2,1,0:T(8,128)} %inverse_hbm.9, f32[8,1024]{1,0:T(8,128)S(1)} %get-tuple-element.37.after_ref.refs_0_), custom_call_target="tpu_custom_call" | custom-call | bytes 3145728 | tf_op jit(solution)/shard_map/pallas_call | solution.py:678
  9.5 0.0 collective-permute-done.2.refs_4_.refs_3_
  9.5 0.8 %collective-permute-done.1.refs_3_.refs_2_ = f32[8,1024]{1,0:T(8,128)S(1)} collective-permute-done((f32[8,1024]{1,0:T(8,128)S(1)}, f32[8,1024]{1,0:T(8,128)S(1)}, u32[]{:S(2)}, u32[]{:S(2)}) %collective-permute-start.1) | collective-permute-done | bytes 32800 | tf_op jit(solution)/shard_map/ppermute | solution.py:670
  10.4 0.5 collective-permute-done.refs_2_.refs_1_
  10.9 1.5 %collective-permute-start.3 = (bf16[256,1024]{1,0:T(8,128)(2,1)}, bf16[256,1024]{1,0:T(8,128)(2,1)S(1)}, u32[]{:S(2)}, u32[]{:S(2)}) collective-permute-start(bf16[256,1024]{1,0:T(8,128)(2,1)} %get-tuple-element.49.refs_5_.refs_3_), channel_id=1, source_target_pairs={{0,16},{8,24},{16,0},{24,8},{1,17},{9,25},{17,1},{25,9},{2,18},{10... | collective-permute-start | bytes 1572872 | tf_op jit(solution)/shard_map/ppermute | solution.py:746
  12.4 0.6 collective-permute-start.4
  14.3 0.8 %shard_map.123 = (f32[8,16,128]{2,1,0:T(8,128)}, f32[1,128]{1,0:T(1,128)S(1)}, s32[1,128]{1,0:T(1,128)S(1)}) custom-call(s32[1]{0:T(128)} %bitcast.2.role_ref, f32[8,1024]{1,0:T(8,128)S(1)} %get-tuple-element.37.after_ref.refs_0_, f32[8,1024]{1,0:T(8,128)S(1)} %collective-permute-done.refs_2_.refs_1_, f32[8,1024]{1,0:T(8,128)S(1)} %collective-permute-done.1.refs_3_.refs_2_, ...), custom_call_target="tpu_custom_call" | custom-call | tf_op jit(solution)/shard_map/pallas_call | solution.py:704
  15.1 4.9 %all-to-all-start = ((f32[8,16,128]{2,1,0:T(8,128)}), f32[8,16,128]{2,1,0:T(8,128)S(1)}, u32[]{:S(2)}, u32[]{:S(2)}) async-start(f32[8,16,128]{2,1,0:T(8,128)} %get-tuple-element.44), calls=%async_computation | async-start | bytes 131072 | tf_op jit(solution)/shard_map/all_to_all | solution.py:717
  20.0 0.0 copy-start
  20.0 3.4 %shard_map.124 = (bf16[2048,640]{1,0:T(8,128)(2,1)S(1)}, bf16[256,1024]{1,0:T(8,128)(2,1)}, bf16[256,1024]{1,0:T(8,128)(2,1)}) custom-call(bf16[2048,128]{1,0:T(8,128)(2,1)} %coeff_hbm.1, f32[3,1024]{1,0:T(4,128)} %refs_1_.1, f32[1,1024,1024]{2,1,0:T(8,128)} %inverse_hbm.9, f32[1,128]{1,0:T(1,128)S(1)} %get-tuple-element.45.after_ref.weight_ref), custom_call_target="tpu_custom_call" | custom-call | flops 2097152 | bytes 5767168 | tf_op jit(solution)/shard_map/pallas_call | solution.py:721
  23.4 2.5 %all-to-all-done.refs_1_.refs_0_ = f32[8,16,128]{2,1,0:T(8,128)S(1)} async-done(((f32[8,16,128]{2,1,0:T(8,128)}), f32[8,16,128]{2,1,0:T(8,128)S(1)}, u32[]{:S(2)}, u32[]{:S(2)}) %all-to-all-start) | async-done | bytes 65568 | tf_op jit(solution)/shard_map/all_to_all | solution.py:717
  25.9 0.0 collective-permute-done.3.got_a
  25.9 0.0 collective-permute-done.4.got_b
  25.9 2.0 %shard_map.125 = (bf16[256,1024]{1,0:T(8,128)(2,1)S(1)}, bf16[256,1024]{1,0:T(8,128)(2,1)}, f32[8,128]{1,0:T(8,128)S(1)}) custom-call(s32[1]{0:T(128)} %bitcast.6.flag_ref, bf16[256,1024]{1,0:T(8,128)(2,1)} %get-tuple-element.47.own_a.own_b.refs_3_.refs_1_, ...), custom_call_target="tpu_custom_call", output_to_operand_aliasing={{0}: (3, {}), {1}: (4, {})} | custom-call | tf_op jit(solution)/shard_map/pallas_call | solution.py:749
  27.9 0.1 collective-permute-start.5
  28.0 0.1 collective-permute-start.6
  28.1 0.0 copy-done
  28.1 6.4 %shard_map.126.after_ref = bf16[8,176,128]{2,1,0:T(8,128)(2,1)} custom-call(f32[8,16,128]{2,1,0:T(8,128)S(1)} %all-to-all-done.refs_1_.refs_0_, f32[3,1024]{1,0:T(4,128)S(1)} %copy-done, bf16[2048,640]{1,0:T(8,128)(2,1)S(1)} %get-tuple-element.46.refs_0_.refs_2_, f32[8,128]{1,0:T(8,128)S(1)} %get-tuple-element.51.refs_3_), custom_call_target="tpu_custom_call" | custom-call | flops 738197504 | bytes 3145728 | tf_op jit(solution)/shard_map/pallas_call | solution.py:789
  34.5 3.8 %all-to-all-start.1 = ((bf16[8,176,128]{2,1,0:T(8,128)(2,1)}), bf16[8,176,128]{2,1,0:T(8,128)(2,1)S(1)}, u32[]{:S(2)}, u32[]{:S(2)}) async-start(bf16[8,176,128]{2,1,0:T(8,128)(2,1)} %shard_map.126.after_ref), calls=%async_computation.1 | async-start | bytes 720896 | tf_op jit(solution)/shard_map/all_to_all | solution.py:815
  38.3 1.2 %shard_map.127 = (bf16[256,1024]{1,0:T(8,128)(2,1)S(1)}, bf16[256,1024]{1,0:T(8,128)(2,1)S(1)}) custom-call(bf16[256,1024]{1,0:T(8,128)(2,1)} %get-tuple-element.48.own_b.own_a.refs_4_.refs_2_, bf16[256,1024]{1,0:T(8,128)(2,1)} %get-tuple-element.47.own_a.own_b.refs_3_.refs_1_, bf16[8,176,128]{2,1,0:T(8,128)(2,1)} %shard_map.126.after_ref), custom_call_target="tpu_custom_call" | custom-call | tf_op jit(solution)/shard_map/pallas_call | solution.py:821
  39.5 0.4 collective-permute-done.5.got_a
  39.9 1.6 %collective-permute-done.6.got_b = bf16[256,1024]{1,0:T(8,128)(2,1)} collective-permute-done((bf16[256,1024]{1,0:T(8,128)(2,1)S(1)}, bf16[256,1024]{1,0:T(8,128)(2,1)}, u32[]{:S(2)}, u32[]{:S(2)}) %collective-permute-start.6) | collective-permute-done | bytes 524320 | tf_op jit(solution)/shard_map/ppermute | solution.py:745
  41.5 1.0 %shard_map.128 = (bf16[256,1024]{1,0:T(8,128)(2,1)}, bf16[256,1024]{1,0:T(8,128)(2,1)}, f32[8,128]{1,0:T(8,128)S(1)}) custom-call(s32[1]{0:T(128)} %bitcast.6.flag_ref, bf16[256,1024]{1,0:T(8,128)(2,1)S(1)} %get-tuple-element.52.own_a, bf16[256,1024]{1,0:T(8,128)(2,1)S(1)} %get-tuple-element.53.own_b, ...), custom_call_target="tpu_custom_call", output_to_operand_aliasing={{0}: (3, {}), {1}: (4, {})} | custom-call | tf_op jit(solution)/shard_map/pallas_call | solution.py:829
  42.5 0.1 collective-permute-start.8
  42.5 1.1 %collective-permute-start.7 = (bf16[256,1024]{1,0:T(8,128)(2,1)}, bf16[256,1024]{1,0:T(8,128)(2,1)S(1)}, u32[]{:S(2)}, u32[]{:S(2)}) collective-permute-start(bf16[256,1024]{1,0:T(8,128)(2,1)} %get-tuple-element.58.refs_9_.refs_7_), channel_id=1, source_target_pairs={{0,8},{8,0},{16,24},{24,16},{1,9},{9,1},{17,25},{25,17},{2,10},{10... | collective-permute-start | bytes 1572872 | tf_op jit(solution)/shard_map/ppermute | solution.py:745
  43.7 2.5 %shard_map.129.refs_1_ = bf16[1024,128]{1,0:T(8,128)(2,1)S(1)} custom-call(f32[1,1024,1024]{2,1,0:T(8,128)} %inverse_hbm.9, s32[2,128]{1,0:T(2,128)S(1)} %get-tuple-element.38.refs_4_.moved_ref, f32[8,128]{1,0:T(8,128)S(1)} %get-tuple-element.56.after_ref), custom_call_target="tpu_custom_call" | custom-call | flops 268435456 | bytes 4194304 | tf_op jit(solution)/shard_map/pallas_call | solution.py:850
  46.2 4.0 %all-to-all-done.1.refs_0_ = bf16[8,176,128]{2,1,0:T(8,128)(2,1)S(1)} async-done(((bf16[8,176,128]{2,1,0:T(8,128)(2,1)}), bf16[8,176,128]{2,1,0:T(8,128)(2,1)S(1)}, u32[]{:S(2)}, u32[]{:S(2)}) %all-to-all-start.1) | async-done | bytes 360480 | tf_op jit(solution)/shard_map/all_to_all | solution.py:815
  50.2 3.2 %shard_map.130 = (f32[3,1,16]{2,1,0:T(1,128)S(1)}, f32[1,1,16]{2,1,0:T(1,128)S(1)}, bf16[96,1024]{1,0:T(8,128)(2,1)S(1)}, bf16[2,256,128]{2,1,0:T(8,128)(2,1)S(1...) custom-call(s32[1]{0:T(128)} %bitcast.5.me_ref, s32[1]{0:T(128)} %bitcast.2.role_ref, ...), custom_call_target="tpu_custom_call" | custom-call | flops 33554432 | bytes 4915200 | tf_op jit(solution)/shard_map/pallas_call | solution.py:867
  53.4 1.2 %collective-permute-done.8.refs_9_ = bf16[256,1024]{1,0:T(8,128)(2,1)S(1)} collective-permute-done((bf16[256,1024]{1,0:T(8,128)(2,1)}, bf16[256,1024]{1,0:T(8,128)(2,1)S(1)}, u32[]{:S(2)}, u32[]{:S(2)}) %collective-permute-start.8) | collective-permute-done | bytes 524320 | tf_op jit(solution)/shard_map/ppermute | solution.py:746
  54.6 2.3 %collective-permute-done.7.refs_8_ = bf16[256,1024]{1,0:T(8,128)(2,1)S(1)} collective-permute-done((bf16[256,1024]{1,0:T(8,128)(2,1)}, bf16[256,1024]{1,0:T(8,128)(2,1)S(1)}, u32[]{:S(2)}, u32[]{:S(2)}) %collective-permute-start.7) | collective-permute-done | bytes 524320 | tf_op jit(solution)/shard_map/ppermute | solution.py:745
  56.9 6.7 %shard_map.131 = (f32[1024,1024]{1,0:T(8,128)}, f32[6,1,16]{2,1,0:T(1,128)}, f32[2,1,16]{2,1,0:T(1,128)}, f32[1,128]{1,0:T(1,128)}) custom-call(s32[1]{0:T(128)} %bitcast.2.role_ref, s32[1,128]{1,0:T(1,128)S(1)} %get-tuple-element.43.number_ref, bf16[96,1024]{1,0:T(8,128)(2,1)S(1)} %get-tuple-element.59.later_ref, ...), custom_call_target="tpu_custom_call" | custom-call | flops 134217728 | bytes 6291456 | tf_op jit(solution)/shard_map/pallas_call | solution.py:891
  (1 shorter events, 0.0 us)
Async XLA Ops:
  2.5 7.0 %collective-permute-start.2 = (f32[8,1024]{1,0:T(8,128)S(1)}, f32[8,1024]{1,0:T(8,128)S(1)}, u32[]{:S(2)}, u32[]{:S(2)}) collective-permute-start(f32[8,1024]{1,0:T(8,128)S(1)} %get-tuple-element.37.after_ref.refs_0_), channel_id=1, source_target_pairs={{0,24},{8,16},{16,8},{24,0},{1,25},{9,17},{17,9},{25,1},{2,26},{10... | collective-permute-start | bytes 98312 | tf_op jit(solution)/shard_map/ppermute | solution.py:670
  6.4 3.9 %collective-permute-start.1 = (f32[8,1024]{1,0:T(8,128)S(1)}, f32[8,1024]{1,0:T(8,128)S(1)}, u32[]{:S(2)}, u32[]{:S(2)}) collective-permute-start(f32[8,1024]{1,0:T(8,128)S(1)} %get-tuple-element.37.after_ref.refs_0_), channel_id=1, source_target_pairs={{0,16},{8,24},{16,0},{24,8},{1,17},{9,25},{17,1},{25,9},{2,18},{10... | collective-permute-start | bytes 98312 | tf_op jit(solution)/shard_map/ppermute | solution.py:670
  6.9 3.9 %collective-permute-start = (f32[8,1024]{1,0:T(8,128)S(1)}, f32[8,1024]{1,0:T(8,128)S(1)}, u32[]{:S(2)}, u32[]{:S(2)}) collective-permute-start(f32[8,1024]{1,0:T(8,128)S(1)} %get-tuple-element.37.after_ref.refs_0_), channel_id=1, source_target_pairs={{0,8},{8,0},{16,24},{24,16},{1,9},{9,1},{17,25},{25,17},{2,10},{10... | collective-permute-start | bytes 98312 | tf_op jit(solution)/shard_map/ppermute | solution.py:670
  10.9 15.1 %collective-permute-start.3 = (bf16[256,1024]{1,0:T(8,128)(2,1)}, bf16[256,1024]{1,0:T(8,128)(2,1)S(1)}, u32[]{:S(2)}, u32[]{:S(2)}) collective-permute-start(bf16[256,1024]{1,0:T(8,128)(2,1)} %get-tuple-element.49.refs_5_.refs_3_), channel_id=1, source_target_pairs={{0,16},{8,24},{16,0},{24,8},{1,17},{9,25},{17,1},{25,9},{2,18},{10... | collective-permute-start | bytes 1572872 | tf_op jit(solution)/shard_map/ppermute | solution.py:746
  12.4 13.6 %collective-permute-start.4 = (bf16[256,1024]{1,0:T(8,128)(2,1)}, bf16[256,1024]{1,0:T(8,128)(2,1)}, u32[]{:S(2)}, u32[]{:S(2)}) collective-permute-start(bf16[256,1024]{1,0:T(8,128)(2,1)} %get-tuple-element.50.refs_2_.refs_0_), channel_id=1, source_target_pairs={{0,8},{8,0},{16,24},{24,16},{1,9},{9,1},{17,25},{25,17},{2,10},{10... | collective-permute-start | bytes 1572872 | tf_op jit(solution)/shard_map/ppermute | solution.py:745
  15.1 10.8 %all-to-all-start = ((f32[8,16,128]{2,1,0:T(8,128)}), f32[8,16,128]{2,1,0:T(8,128)S(1)}, u32[]{:S(2)}, u32[]{:S(2)}) async-start(f32[8,16,128]{2,1,0:T(8,128)} %get-tuple-element.44), calls=%async_computation | async-start | bytes 131072 | tf_op jit(solution)/shard_map/all_to_all | solution.py:717
  20.0 8.1 %copy-start = (f32[3,1024]{1,0:T(4,128)S(1)}, f32[3,1024]{1,0:T(4,128)}, u32[]{:S(2)}) copy-start(f32[3,1024]{1,0:T(4,128)} %refs_1_.1) | copy-start | bytes 36868
  27.9 12.0 %collective-permute-start.5 = (bf16[256,1024]{1,0:T(8,128)(2,1)}, bf16[256,1024]{1,0:T(8,128)(2,1)}, u32[]{:S(2)}, u32[]{:S(2)}) collective-permute-start(bf16[256,1024]{1,0:T(8,128)(2,1)} %get-tuple-element.54.refs_6_.refs_4_), channel_id=1, source_target_pairs={{0,16},{8,24},{16,0},{24,8},{1,17},{9,25},{17,1},{25,9},{2,18},{10... | collective-permute-start | bytes 1572872 | tf_op jit(solution)/shard_map/ppermute | solution.py:746
  28.0 13.5 %collective-permute-start.6 = (bf16[256,1024]{1,0:T(8,128)(2,1)S(1)}, bf16[256,1024]{1,0:T(8,128)(2,1)}, u32[]{:S(2)}, u32[]{:S(2)}) collective-permute-start(bf16[256,1024]{1,0:T(8,128)(2,1)S(1)} %get-tuple-element.55.refs_8_.refs_6_), channel_id=1, source_target_pairs={{0,8},{8,0},{16,24},{24,16},{1,9},{9,1},{17,25},{25,17},{2,10},{10... | collective-permute-start | bytes 1572872 | tf_op jit(solution)/shard_map/ppermute | solution.py:745
  34.5 15.6 %all-to-all-start.1 = ((bf16[8,176,128]{2,1,0:T(8,128)(2,1)}), bf16[8,176,128]{2,1,0:T(8,128)(2,1)S(1)}, u32[]{:S(2)}, u32[]{:S(2)}) async-start(bf16[8,176,128]{2,1,0:T(8,128)(2,1)} %shard_map.126.after_ref), calls=%async_computation.1 | async-start | bytes 720896 | tf_op jit(solution)/shard_map/all_to_all | solution.py:815
  42.5 12.2 %collective-permute-start.8 = (bf16[256,1024]{1,0:T(8,128)(2,1)}, bf16[256,1024]{1,0:T(8,128)(2,1)S(1)}, u32[]{:S(2)}, u32[]{:S(2)}) collective-permute-start(bf16[256,1024]{1,0:T(8,128)(2,1)} %get-tuple-element.57.refs_7_.refs_5_), channel_id=1, source_target_pairs={{0,16},{8,24},{16,0},{24,8},{1,17},{9,25},{17,1},{25,9},{2,18},{10... | collective-permute-start | bytes 1572872 | tf_op jit(solution)/shard_map/ppermute | solution.py:746
  42.5 14.4 %collective-permute-start.7 = (bf16[256,1024]{1,0:T(8,128)(2,1)}, bf16[256,1024]{1,0:T(8,128)(2,1)S(1)}, u32[]{:S(2)}, u32[]{:S(2)}) collective-permute-start(bf16[256,1024]{1,0:T(8,128)(2,1)} %get-tuple-element.58.refs_9_.refs_7_), channel_id=1, source_target_pairs={{0,8},{8,0},{16,24},{24,16},{1,9},{9,1},{17,25},{25,17},{2,10},{10... | collective-permute-start | bytes 1572872 | tf_op jit(solution)/shard_map/ppermute | solution.py:745

commit v16 on v15

--- a/solution.py
+++ b/solution.py
@@ -11,7 +11,7 @@
 F32 = jnp.float32
 BF16 = jnp.bfloat16
 LANES = 128
-ROWS = 16
+ROWS = 64
 DIRECT_POINTS = False
 DIRECT_VALUES = False
 MIB = 1024 * 1024
@@ -458,9 +458,9 @@
     return chunk
 
 
-def load_slots(plan, slots, role, inputs, parent, sem):
+def load_slots(plan, slots, role, inputs, parent, sem, first=0):
     for slot in slots:
-        for which in range(len(plan)):
+        for which in range(first, len(plan)):
             load = pltpu.make_async_copy(
                 inputs[plan[which][slot][1]], parent.at[slot], sem.at[slot]
             )
@@ -475,9 +475,9 @@
 def middle_kernel(count, sources, plan, me_ref, role_ref, number_ref, inverse_hbm, *refs):
     values = refs[:sources]
     own_columns = refs[sources]
-    inputs = refs[sources + 1 : -11]
-    drift_ref, lap_ref, later_ref, columns_ref, products_ref, total_ref, held_ref = refs[-11:-4]
-    vals, parent, sem, own_sem = refs[-4:]
+    inputs = refs[sources + 1 : -13]
+    drift_ref, lap_ref, later_ref, columns_ref, products_ref, total_ref = refs[-13:-7]
+    held_ref, near_ref, vals, parent, sem, own_sem, near_sem = refs[-7:]
     slots, depth, electrons = parent.shape
     role = role_ref[0]
     load_slots(plan, range(slots), role, inputs, parent, sem)
@@ -486,6 +486,12 @@
             rows_of(inverse_hbm, plan[0][slot][0], depth), held_ref.at[slot], own_sem.at[slot]
         )
         for slot in range(slots)
+    ]
+    wide += [
+        pltpu.make_async_copy(
+            inputs[plan[0][slots + slot][1]], near_ref.at[slot], near_sem.at[slot]
+        )
+        for slot in range(near_ref.shape[0])
     ]
     for load in wide:
         pl.when(role == 0)(load.start)
@@ -548,6 +554,7 @@
     products_ref,
     total_ref,
     held_ref,
+    near_ref,
     inverse_hbm,
     *refs,
 ):
@@ -565,8 +572,12 @@
         )
         for slot in range(chunks)
     ]
-    load_slots(plan, late, role, inputs, parent, in_sem)
+    load_slots(plan, late, role, inputs, parent, in_sem, 1)
     for slot in late:
+        close = pltpu.make_async_copy(
+            near_ref.at[slot - done], parent.at[slot], in_sem.at[slot]
+        )
+        pl.when(role == 0)(close.start)
         pl.when(role == 0)(own[slot].start)
     pick = pick_from(number_ref, electrons)
     wait_slots(late, inputs, parent, in_sem)
@@ -761,7 +772,7 @@
             )(apart, *in_hbm(*mine), *got, *first)
 
         x1, y1 = send_x(own[0]), send_y(own[3])
-        y1, x1, token_1 = relay((own[1], own[2]), (y1, x1), (derived, *points))
+        y1, x1, token_1 = relay((own[1], own[2]), (y1, x1), (derived,))
         x2, y2 = send_x(y1), send_y(x1)
     else:
         token_1 = token_2 = jnp.zeros((8, LANES), F32)
@@ -864,7 +875,7 @@
     here = lax.axis_index("orb").astype(jnp.int32).reshape(1)
     early = 2
     work = 2 * electrons * 2 * count
-    drift, laplacian, later, early_columns, products, total, held = call(
+    drift, laplacian, later, early_columns, products, total, held, near_own = call(
         functools.partial(middle_kernel, count, targets, plan),
         (
             shape((3, 1, count), F32),
@@ -874,14 +885,16 @@
             shape((6 * count, LANES), F32),
             shape((2 * count, electrons), F32),
             shape((early, depth, electrons), F32),
+            shape((chunks - early, depth, electrons), BF16),
         ),
         [SM, SM, VM, HBM] + [VM] * (targets + 1) + [ANY] * settled,
-        (VM,) * 7,
+        (VM,) * 8,
         scratch=[
             pltpu.VMEM((5 * count, electrons), BF16),
             pltpu.VMEM((early, depth, electrons), BF16),
             pltpu.SemaphoreType.DMA((early,)),
             pltpu.SemaphoreType.DMA((early,)),
+            pltpu.SemaphoreType.DMA((chunks - early,)),
         ],
         flops=early * depth * work,
         moved=8 * early * depth * electrons + 44 * count * electrons,
@@ -896,7 +909,7 @@
             shape((2, 1, count), F32),
             shape((1, LANES), F32),
         ),
-        [SM] + [VM] * 9 + [HBM] + [ANY] * len(arrays),
+        [SM] + [VM] * 10 + [HBM] + [ANY] * len(arrays),
         (HBM, VM, VM, VM),
         scratch=[
             pltpu.VMEM((chunks, depth, electrons), BF16),
@@ -919,6 +932,7 @@
         products,
         total,
         held,
+        near_own,
         *in_hbm(inverse, *own),
         *arrays[chunks:],
     )

time: 64.1 us -> 62.9 us (0.981)
  Pallas kernels: 30.9 us -> 27.2 us
  starting transfers between devices: 16.7 us -> 19.3 us
    ppermute x3, starting transfers between devices: 1.66 us -> 5.54 us  [per_device(): send_y = lambda block: lax.ppermute(block, 'grp', pairs(n_grp, 2))]
    all_to_all x1, waiting for transfers between devices: 4 us -> 6.14 us  [per_device(): lax.all_to_all(values, 'orb', split_axis=0, concat_axis=0, tiled=True)]
    pallas_call x1, Pallas kernels: 1.98 us -> 0.07 us  [relay(): call(relay_kernel, (kept, kept, token), [SM] + [ANY] * (4 + len(first)),...]
    ppermute x3, waiting for transfers between devices: 3.85 us -> 2.26 us  [per_device(): send_x = lambda block: lax.ppermute(block, 'grp', pairs(n_grp, 1))]
    pallas_call x1, Pallas kernels: 6.7 us -> 5.65 us  [per_device(): call(functools.partial(finish_kernel, count, plan), (shape((electrons, el...]
    ppermute x3, starting transfers between devices: 1.82 us -> 0.8 us  [per_device(): send_x = lambda block: lax.ppermute(block, 'grp', pairs(n_grp, 1))]
    pallas_call x1, Pallas kernels: 0.99 us -> 0.03 us  [per_device(): call(near_relay_kernel, (kept, kept, token), [SM, VM, VM, ANY, ANY], (ANY...]
    ppermute x3, waiting for transfers between devices: 1.61 us -> 0.67 us  [per_device(): send_y = lambda block: lax.ppermute(block, 'grp', pairs(n_grp, 2))]
  transfers between devices with their start and end apart: 11 -> 11, of which waited for: 8 -> 7; matrix products, arithmetic and copies ran while one was open for 0% -> 0% of each run, Pallas kernels for 33% -> 33%
where the time goes in v16:
time: 62.9 us; the launch traced here: 62.5 us
  Pallas kernels  27.2 us (43%)
  starting transfers between devices  19.3 us (31%)
  waiting for transfers between devices  13.2 us (21%)
  between operations  2.69 us (4%)
    pallas_call x1, Pallas kernels, per_device(): pl.pallas_call(functools.partial(evaluate_kernel, count, sources, targets...  6.45 us
    all_to_all x1, waiting for transfers between devices, per_device(): lax.all_to_all(values, 'orb', split_axis=0, concat_axis=0, tiled=True)  6.14 us
    pallas_call x1, Pallas kernels, per_device(): call(functools.partial(finish_kernel, count, plan), (shape((electrons, el...  5.65 us
    ppermute x3, starting transfers between devices, per_device(): send_y = lambda block: lax.ppermute(block, 'grp', pairs(n_grp, 2))  5.54 us
    all_to_all x1, starting transfers between devices, per_device(): lax.all_to_all(points, 'orb', split_axis=0, concat_axis=0, tiled=True)  4.88 us
    ppermute x3, starting transfers between devices, per_device(): lax.ppermute(record, 'grp', pairs(n_grp, s))  4.6 us
    all_to_all x1, starting transfers between devices, per_device(): lax.all_to_all(values, 'orb', split_axis=0, concat_axis=0, tiled=True)  3.49 us
    pallas_call x1, Pallas kernels, per_device(): call(functools.partial(middle_kernel, count, targets, plan), (shape((3, 1...  3.41 us
  transfers between devices with their start and end apart: 11, of which 7 were waited for; matrix products, arithmetic and copies ran while one was open for 0% of the time, Pallas kernels for 33%

profile of v16, /device:TPU:0, one launch (start us, length us, event | category | flops | bytes accessed | tf_op | source)
XLA Modules:
  0.0 62.5 jit_solution(3042144349282949010)
XLA Ops:
  1.3 1.2 %shard_map.120 = (f32[8,1024]{1,0:T(8,128)S(1)}, s32[2,128]{1,0:T(2,128)S(1)}, f32[2,8,128]{2,1,0:T(8,128)S(1)}) custom-call(f32[3,1,1024]{2,1,0:T(1,128)} %bitcast.12, s32[2,1,16]{2,1,0:T(1,128)} %moved_hbm.1, f32[6,1,16]{2,1,0:T(1,128)} %bitcast.13, f32[1]{0:T(128)S(6)} %copy.27.weight_ref), custom_call_target="tpu_custom_call" | custom-call | tf_op jit(solution)/shard_map/pallas_call | solution.py:658
  2.5 4.0 %collective-permute-start.2 = (f32[8,1024]{1,0:T(8,128)S(1)}, f32[8,1024]{1,0:T(8,128)S(1)}, u32[]{:S(2)}, u32[]{:S(2)}) collective-permute-start(f32[8,1024]{1,0:T(8,128)S(1)} %get-tuple-element.38.after_ref.refs_0_), channel_id=1, source_target_pairs={{0,24},{8,16},{16,8},{24,0},{1,25},{9,17},{17,9},{25,1},{2,26},{10... | collective-permute-start | bytes 98312 | tf_op jit(solution)/shard_map/ppermute | solution.py:681
  6.4 0.5 collective-permute-start.1
  6.9 0.1 collective-permute-start
  7.1 2.4 %shard_map.121 = (bf16[256,1024]{1,0:T(8,128)(2,1)}, bf16[256,1024]{1,0:T(8,128)(2,1)}) custom-call(f32[1,1024,1024]{2,1,0:T(8,128)} %inverse_hbm.9, f32[8,1024]{1,0:T(8,128)S(1)} %get-tuple-element.38.after_ref.refs_0_), custom_call_target="tpu_custom_call" | custom-call | bytes 3145728 | tf_op jit(solution)/shard_map/pallas_call | solution.py:689
  9.5 0.0 collective-permute-done.2.refs_4_.refs_3_
  9.5 0.8 %collective-permute-done.1.refs_3_.refs_2_ = f32[8,1024]{1,0:T(8,128)S(1)} collective-permute-done((f32[8,1024]{1,0:T(8,128)S(1)}, f32[8,1024]{1,0:T(8,128)S(1)}, u32[]{:S(2)}, u32[]{:S(2)}) %collective-permute-start.1) | collective-permute-done | bytes 32800 | tf_op jit(solution)/shard_map/ppermute | solution.py:681
  10.4 0.5 collective-permute-done.refs_2_.refs_1_
  10.9 1.5 %collective-permute-start.3 = (bf16[256,1024]{1,0:T(8,128)(2,1)}, bf16[256,1024]{1,0:T(8,128)(2,1)S(1)}, u32[]{:S(2)}, u32[]{:S(2)}) collective-permute-start(bf16[256,1024]{1,0:T(8,128)(2,1)} %get-tuple-element.50.refs_5_.refs_3_), channel_id=1, source_target_pairs={{0,16},{8,24},{16,0},{24,8},{1,17},{9,25},{17,1},{25,9},{2,18},{10... | collective-permute-start | bytes 1572872 | tf_op jit(solution)/shard_map/ppermute | solution.py:757
  12.4 0.6 %collective-permute-start.4 = (bf16[256,1024]{1,0:T(8,128)(2,1)}, bf16[256,1024]{1,0:T(8,128)(2,1)}, u32[]{:S(2)}, u32[]{:S(2)}) collective-permute-start(bf16[256,1024]{1,0:T(8,128)(2,1)} %get-tuple-element.51.refs_2_.refs_0_), channel_id=1, source_target_pairs={{0,8},{8,0},{16,24},{24,16},{1,9},{9,1},{17,25},{25,17},{2,10},{10... | collective-permute-start | bytes 1572872 | tf_op jit(solution)/shard_map/ppermute | solution.py:756
  14.3 0.9 %shard_map.123 = (f32[8,64,128]{2,1,0:T(8,128)}, f32[1,128]{1,0:T(1,128)S(1)}, s32[1,128]{1,0:T(1,128)S(1)}) custom-call(s32[1]{0:T(128)} %bitcast.2.role_ref, f32[8,1024]{1,0:T(8,128)S(1)} %get-tuple-element.38.after_ref.refs_0_, f32[8,1024]{1,0:T(8,128)S(1)} %collective-permute-done.refs_2_.refs_1_, f32[8,1024]{1,0:T(8,128)S(1)} %collective-permute-done.1.refs_3_.refs_2_, ...), custom_call_target="tpu_custom_call" | custom-call | tf_op jit(solution)/shard_map/pallas_call | solution.py:715
  15.2 4.9 %all-to-all-start = ((f32[8,64,128]{2,1,0:T(8,128)}), f32[8,64,128]{2,1,0:T(8,128)S(1)}, u32[]{:S(2)}, u32[]{:S(2)}) async-start(f32[8,64,128]{2,1,0:T(8,128)} %get-tuple-element.45), calls=%async_computation | async-start | bytes 524288 | tf_op jit(solution)/shard_map/all_to_all | solution.py:728
  20.1 0.0 copy-start
  20.1 3.4 %shard_map.124 = (bf16[2048,640]{1,0:T(8,128)(2,1)S(1)}, bf16[256,1024]{1,0:T(8,128)(2,1)}, bf16[256,1024]{1,0:T(8,128)(2,1)}) custom-call(bf16[2048,128]{1,0:T(8,128)(2,1)} %coeff_hbm.1, f32[3,1024]{1,0:T(4,128)} %refs_1_.1, f32[1,1024,1024]{2,1,0:T(8,128)} %inverse_hbm.9, f32[1,128]{1,0:T(1,128)S(1)} %get-tuple-element.46.after_ref.weight_ref), custom_call_target="tpu_custom_call" | custom-call | flops 2097152 | bytes 5767168 | tf_op jit(solution)/shard_map/pallas_call | solution.py:732
  23.5 0.0 collective-permute-done.3.got_a
  23.5 1.2 %collective-permute-done.4.got_b = bf16[256,1024]{1,0:T(8,128)(2,1)} collective-permute-done((bf16[256,1024]{1,0:T(8,128)(2,1)}, bf16[256,1024]{1,0:T(8,128)(2,1)}, u32[]{:S(2)}, u32[]{:S(2)}) %collective-permute-start.4) | collective-permute-done | bytes 524320 | tf_op jit(solution)/shard_map/ppermute | solution.py:756
  24.7 0.1 shard_map.125
  24.7 2.3 %collective-permute-start.5 = (bf16[256,1024]{1,0:T(8,128)(2,1)}, bf16[256,1024]{1,0:T(8,128)(2,1)}, u32[]{:S(2)}, u32[]{:S(2)}) collective-permute-start(bf16[256,1024]{1,0:T(8,128)(2,1)} %get-tuple-element.55.refs_6_.refs_4_), channel_id=1, source_target_pairs={{0,16},{8,24},{16,0},{24,8},{1,17},{9,25},{17,1},{25,9},{2,18},{10... | collective-permute-start | bytes 1572872 | tf_op jit(solution)/shard_map/ppermute | solution.py:757
  27.0 0.0 collective-permute-start.6
  27.0 2.8 %all-to-all-done.refs_0_ = f32[8,64,128]{2,1,0:T(8,128)S(1)} async-done(((f32[8,64,128]{2,1,0:T(8,128)}), f32[8,64,128]{2,1,0:T(8,128)S(1)}, u32[]{:S(2)}, u32[]{:S(2)}) %all-to-all-start) | async-done | bytes 262176 | tf_op jit(solution)/shard_map/all_to_all | solution.py:728
  29.8 0.0 copy-done
  29.8 6.4 %shard_map.126.after_ref = bf16[8,176,128]{2,1,0:T(8,128)(2,1)} custom-call(f32[8,64,128]{2,1,0:T(8,128)S(1)} %all-to-all-done.refs_0_, f32[3,1024]{1,0:T(4,128)S(1)} %copy-done, bf16[2048,640]{1,0:T(8,128)(2,1)S(1)} %get-tuple-element.47.refs_0_.refs_2_, f32[8,128]{1,0:T(8,128)S(1)} %get-tuple-element.52.refs_3_), custom_call_target="tpu_custom_call" | custom-call | flops 738197504 | bytes 3145728 | tf_op jit(solution)/shard_map/pallas_call | solution.py:800
  36.3 3.5 %all-to-all-start.1 = ((bf16[8,176,128]{2,1,0:T(8,128)(2,1)}), bf16[8,176,128]{2,1,0:T(8,128)(2,1)S(1)}, u32[]{:S(2)}, u32[]{:S(2)}) async-start(bf16[8,176,128]{2,1,0:T(8,128)(2,1)} %shard_map.126.after_ref), calls=%async_computation.1 | async-start | bytes 720896 | tf_op jit(solution)/shard_map/all_to_all | solution.py:826
  39.8 1.2 %shard_map.127 = (bf16[256,1024]{1,0:T(8,128)(2,1)S(1)}, bf16[256,1024]{1,0:T(8,128)(2,1)S(1)}) custom-call(bf16[256,1024]{1,0:T(8,128)(2,1)} %get-tuple-element.49.own_b.own_a.refs_4_.refs_2_, bf16[256,1024]{1,0:T(8,128)(2,1)} %get-tuple-element.48.own_a.own_b.refs_3_.refs_1_, bf16[8,176,128]{2,1,0:T(8,128)(2,1)} %shard_map.126.after_ref), custom_call_target="tpu_custom_call" | custom-call | tf_op jit(solution)/shard_map/pallas_call | solution.py:832
  41.0 0.0 collective-permute-done.5.got_a
  41.0 0.0 collective-permute-done.6.got_b
  41.1 1.8 %collective-permute-start.8 = (bf16[256,1024]{1,0:T(8,128)(2,1)}, bf16[256,1024]{1,0:T(8,128)(2,1)S(1)}, u32[]{:S(2)}, u32[]{:S(2)}) collective-permute-start(bf16[256,1024]{1,0:T(8,128)(2,1)} %get-tuple-element.58.refs_7_.refs_5_), channel_id=1, source_target_pairs={{0,16},{8,24},{16,0},{24,8},{1,17},{9,25},{17,1},{25,9},{2,18},{10... | collective-permute-start | bytes 1572872 | tf_op jit(solution)/shard_map/ppermute | solution.py:757
  42.8 0.2 collective-permute-start.7
  43.0 2.5 %shard_map.129.refs_1_ = bf16[1024,128]{1,0:T(8,128)(2,1)S(1)} custom-call(f32[1,1024,1024]{2,1,0:T(8,128)} %inverse_hbm.9, s32[2,128]{1,0:T(2,128)S(1)} %get-tuple-element.39.refs_4_.moved_ref, f32[8,128]{1,0:T(8,128)S(1)} %get-tuple-element.57.after_ref), custom_call_target="tpu_custom_call" | custom-call | flops 268435456 | bytes 4194304 | tf_op jit(solution)/shard_map/pallas_call | solution.py:861
  45.5 6.1 %all-to-all-done.1.refs_0_ = bf16[8,176,128]{2,1,0:T(8,128)(2,1)S(1)} async-done(((bf16[8,176,128]{2,1,0:T(8,128)(2,1)}), bf16[8,176,128]{2,1,0:T(8,128)(2,1)S(1)}, u32[]{:S(2)}, u32[]{:S(2)}) %all-to-all-start.1) | async-done | bytes 360480 | tf_op jit(solution)/shard_map/all_to_all | solution.py:826
  51.6 3.4 %shard_map.130 = (f32[3,1,16]{2,1,0:T(1,128)S(1)}, f32[1,1,16]{2,1,0:T(1,128)S(1)}, bf16[96,1024]{1,0:T(8,128)(2,1)S(1)}, bf16[2,256,128]{2,1,0:T(8,128)(2,1)S(1...) custom-call(s32[1]{0:T(128)} %bitcast.5.me_ref, ...), custom_call_target="tpu_custom_call" | custom-call | flops 33554432 | bytes 4915200 | tf_op jit(solution)/shard_map/pallas_call | solution.py:878
  55.0 0.7 %collective-permute-done.8.refs_9_ = bf16[256,1024]{1,0:T(8,128)(2,1)S(1)} collective-permute-done((bf16[256,1024]{1,0:T(8,128)(2,1)}, bf16[256,1024]{1,0:T(8,128)(2,1)S(1)}, u32[]{:S(2)}, u32[]{:S(2)}) %collective-permute-start.8) | collective-permute-done | bytes 524320 | tf_op jit(solution)/shard_map/ppermute | solution.py:757
  55.7 1.1 %collective-permute-done.7.refs_8_ = bf16[256,1024]{1,0:T(8,128)(2,1)} collective-permute-done((bf16[256,1024]{1,0:T(8,128)(2,1)}, bf16[256,1024]{1,0:T(8,128)(2,1)}, u32[]{:S(2)}, u32[]{:S(2)}) %collective-permute-start.7) | collective-permute-done | bytes 524320 | tf_op jit(solution)/shard_map/ppermute | solution.py:756
  56.8 5.6 %shard_map.131 = (f32[1024,1024]{1,0:T(8,128)}, f32[6,1,16]{2,1,0:T(1,128)}, f32[2,1,16]{2,1,0:T(1,128)}, f32[1,128]{1,0:T(1,128)}) custom-call(s32[1]{0:T(128)} %bitcast.2.role_ref, s32[1,128]{1,0:T(1,128)S(1)} %get-tuple-element.44.number_ref, bf16[96,1024]{1,0:T(8,128)(2,1)S(1)} %get-tuple-element.60.later_ref, ...), custom_call_target="tpu_custom_call" | custom-call | flops 134217728 | bytes 6291456 | tf_op jit(solution)/shard_map/pallas_call | solution.py:904
  (2 shorter events, 0.0 us)
Async XLA Ops:
  2.5 7.0 %collective-permute-start.2 = (f32[8,1024]{1,0:T(8,128)S(1)}, f32[8,1024]{1,0:T(8,128)S(1)}, u32[]{:S(2)}, u32[]{:S(2)}) collective-permute-start(f32[8,1024]{1,0:T(8,128)S(1)} %get-tuple-element.38.after_ref.refs_0_), channel_id=1, source_target_pairs={{0,24},{8,16},{16,8},{24,0},{1,25},{9,17},{17,9},{25,1},{2,26},{10... | collective-permute-start | bytes 98312 | tf_op jit(solution)/shard_map/ppermute | solution.py:681
  6.4 3.9 %collective-permute-start.1 = (f32[8,1024]{1,0:T(8,128)S(1)}, f32[8,1024]{1,0:T(8,128)S(1)}, u32[]{:S(2)}, u32[]{:S(2)}) collective-permute-start(f32[8,1024]{1,0:T(8,128)S(1)} %get-tuple-element.38.after_ref.refs_0_), channel_id=1, source_target_pairs={{0,16},{8,24},{16,0},{24,8},{1,17},{9,25},{17,1},{25,9},{2,18},{10... | collective-permute-start | bytes 98312 | tf_op jit(solution)/shard_map/ppermute | solution.py:681
  6.9 3.9 %collective-permute-start = (f32[8,1024]{1,0:T(8,128)S(1)}, f32[8,1024]{1,0:T(8,128)S(1)}, u32[]{:S(2)}, u32[]{:S(2)}) collective-permute-start(f32[8,1024]{1,0:T(8,128)S(1)} %get-tuple-element.38.after_ref.refs_0_), channel_id=1, source_target_pairs={{0,8},{8,0},{16,24},{24,16},{1,9},{9,1},{17,25},{25,17},{2,10},{10... | collective-permute-start | bytes 98312 | tf_op jit(solution)/shard_map/ppermute | solution.py:681
  10.9 12.6 %collective-permute-start.3 = (bf16[256,1024]{1,0:T(8,128)(2,1)}, bf16[256,1024]{1,0:T(8,128)(2,1)S(1)}, u32[]{:S(2)}, u32[]{:S(2)}) collective-permute-start(bf16[256,1024]{1,0:T(8,128)(2,1)} %get-tuple-element.50.refs_5_.refs_3_), channel_id=1, source_target_pairs={{0,16},{8,24},{16,0},{24,8},{1,17},{9,25},{17,1},{25,9},{2,18},{10... | collective-permute-start | bytes 1572872 | tf_op jit(solution)/shard_map/ppermute | solution.py:757
  12.4 12.3 %collective-permute-start.4 = (bf16[256,1024]{1,0:T(8,128)(2,1)}, bf16[256,1024]{1,0:T(8,128)(2,1)}, u32[]{:S(2)}, u32[]{:S(2)}) collective-permute-start(bf16[256,1024]{1,0:T(8,128)(2,1)} %get-tuple-element.51.refs_2_.refs_0_), channel_id=1, source_target_pairs={{0,8},{8,0},{16,24},{24,16},{1,9},{9,1},{17,25},{25,17},{2,10},{10... | collective-permute-start | bytes 1572872 | tf_op jit(solution)/shard_map/ppermute | solution.py:756
  15.2 14.6 %all-to-all-start = ((f32[8,64,128]{2,1,0:T(8,128)}), f32[8,64,128]{2,1,0:T(8,128)S(1)}, u32[]{:S(2)}, u32[]{:S(2)}) async-start(f32[8,64,128]{2,1,0:T(8,128)} %get-tuple-element.45), calls=%async_computation | async-start | bytes 524288 | tf_op jit(solution)/shard_map/all_to_all | solution.py:728
  20.1 9.7 %copy-start = (f32[3,1024]{1,0:T(4,128)S(1)}, f32[3,1024]{1,0:T(4,128)}, u32[]{:S(2)}) copy-start(f32[3,1024]{1,0:T(4,128)} %refs_1_.1) | copy-start | bytes 36868
  24.7 16.3 %collective-permute-start.5 = (bf16[256,1024]{1,0:T(8,128)(2,1)}, bf16[256,1024]{1,0:T(8,128)(2,1)}, u32[]{:S(2)}, u32[]{:S(2)}) collective-permute-start(bf16[256,1024]{1,0:T(8,128)(2,1)} %get-tuple-element.55.refs_6_.refs_4_), channel_id=1, source_target_pairs={{0,16},{8,24},{16,0},{24,8},{1,17},{9,25},{17,1},{25,9},{2,18},{10... | collective-permute-start | bytes 1572872 | tf_op jit(solution)/shard_map/ppermute | solution.py:757
  27.0 14.0 %collective-permute-start.6 = (bf16[256,1024]{1,0:T(8,128)(2,1)S(1)}, bf16[256,1024]{1,0:T(8,128)(2,1)}, u32[]{:S(2)}, u32[]{:S(2)}) collective-permute-start(bf16[256,1024]{1,0:T(8,128)(2,1)S(1)} %get-tuple-element.56.refs_8_.refs_6_), channel_id=1, source_target_pairs={{0,8},{8,0},{16,24},{24,16},{1,9},{9,1},{17,25},{25,17},{2,10},{10... | collective-permute-start | bytes 1572872 | tf_op jit(solution)/shard_map/ppermute | solution.py:756
  36.3 15.3 %all-to-all-start.1 = ((bf16[8,176,128]{2,1,0:T(8,128)(2,1)}), bf16[8,176,128]{2,1,0:T(8,128)(2,1)S(1)}, u32[]{:S(2)}, u32[]{:S(2)}) async-start(bf16[8,176,128]{2,1,0:T(8,128)(2,1)} %shard_map.126.after_ref), calls=%async_computation.1 | async-start | bytes 720896 | tf_op jit(solution)/shard_map/all_to_all | solution.py:826
  41.1 14.7 %collective-permute-start.8 = (bf16[256,1024]{1,0:T(8,128)(2,1)}, bf16[256,1024]{1,0:T(8,128)(2,1)S(1)}, u32[]{:S(2)}, u32[]{:S(2)}) collective-permute-start(bf16[256,1024]{1,0:T(8,128)(2,1)} %get-tuple-element.58.refs_7_.refs_5_), channel_id=1, source_target_pairs={{0,16},{8,24},{16,0},{24,8},{1,17},{9,25},{17,1},{25,9},{2,18},{10... | collective-permute-start | bytes 1572872 | tf_op jit(solution)/shard_map/ppermute | solution.py:757
  42.8 14.0 %collective-permute-start.7 = (bf16[256,1024]{1,0:T(8,128)(2,1)}, bf16[256,1024]{1,0:T(8,128)(2,1)}, u32[]{:S(2)}, u32[]{:S(2)}) collective-permute-start(bf16[256,1024]{1,0:T(8,128)(2,1)} %get-tuple-element.59.refs_9_.refs_7_), channel_id=1, source_target_pairs={{0,8},{8,0},{16,24},{24,16},{1,9},{9,1},{17,25},{25,17},{2,10},{10... | collective-permute-start | bytes 1572872 | tf_op jit(solution)/shard_map/ppermute | solution.py:756
